TPU v7x, 512 devices: a whole 4x4x16 slice. The times are simulated.
512 devices in a mesh: gx: 4 (over x), gy: 8 (over z_lo), gz: 16 (over y, z_hi, core).
Axes of the slice: x: 4, y: 4, z: 16 (z_hi: 2, z_lo: 8; z = z_hi * 8 + z_lo), core: 2. Of those that a mesh axis runs over, the one named last changes fastest.
Arguments:
- volume: bfloat16 [32, 64, 128, 128], P('gx', 'gy', 'gz'), may hold values from -6 to 6
- fine_weight: bfloat16 [27, 128, 128], replicated, may hold values from -0.109375 to 0.109375
- coarse_weight: bfloat16 [27, 128, 128], replicated, may hold values from -0.3125 to 0.3125
- cotangent: bfloat16 [16, 32, 64, 128], P('gx', 'gy', 'gz'), may hold values from -144 to 144
Outputs:
- coarse_out: bfloat16 [16, 32, 64, 128], P('gx', 'gy', 'gz')
- grad_volume: bfloat16 [32, 64, 128, 128], P('gx', 'gy', 'gz')
- grad_fine_weight: bfloat16 [27, 128, 128], replicated
- grad_coarse_weight: bfloat16 [27, 128, 128], replicated
All inputs are finite; a program needn't handle non-finite values.
Results may differ from a plain program's by a relative error of at most 0.018.
Values may be sent and summed in bfloat16 or wider, within the bound.
No kernel may reach another device: no remote copies, remote signals or barrier semaphores. Data moves between devices by JAX's collectives and lax.ppermute only.
A program may use at most 64 MiB of HBM per device.

v0:
```python
import math

import jax
import jax.numpy as jnp
from jax import lax
from jax.sharding import PartitionSpec as P


def extended(x, sides, width):
    for axis, dim in sides:
        peers, length = (lax.axis_size(axis), x.shape[dim])
        up = [(i, (i + 1) % peers) for i in range(peers - 1)]
        down = [(j, i) for i, j in up]
        last = lax.slice_in_dim(x, length - width, length, axis=dim)
        leading = lax.slice_in_dim(x, 0, width, axis=dim)
        before = lax.ppermute(last, axis, up)
        after = lax.ppermute(leading, axis, down)
        x = jnp.concatenate([before, x, after], axis=dim)
    return x


def gather_taps(padded, extent, reverse):
    rows_x, rows_y, rows_z = extent
    pieces = []
    for i in range(3):
        for j in range(3):
            for k in range(3):
                if reverse:
                    start_x, start_y, start_z = (2 - i, 2 - j, 2 - k)
                else:
                    start_x, start_y, start_z = (i, j, k)
                pieces.append(
                    padded[
                        start_x : start_x + rows_x,
                        start_y : start_y + rows_y,
                        start_z : start_z + rows_z,
                        :,
                    ]
                )
    stacked = jnp.concatenate(pieces, axis=3)
    return stacked.reshape(rows_x * rows_y * rows_z, stacked.shape[3])


def forward_taps(patches, weights):
    flat = weights.reshape(weights.shape[0] * weights.shape[1], weights.shape[2])
    return jnp.dot(patches, flat, preferred_element_type=jnp.float32)


def backward_taps(padded_grad, extent, weights):
    patches = gather_taps(padded_grad, extent, True)
    turned = jnp.transpose(weights, (0, 2, 1))
    flat = turned.reshape(turned.shape[0] * turned.shape[1], turned.shape[2])
    return jnp.dot(patches, flat, preferred_element_type=jnp.float32)


def weight_terms(patches, grads):
    return lax.dot_general(
        patches, grads, (((0,), (0,)), ((), ())), preferred_element_type=jnp.float32
    )


def silu_slope(values):
    sigma = jax.nn.sigmoid(values)
    return sigma * (1.0 + values * (1.0 - sigma))


def pool_mean(values):
    sx, sy, sz, chans = values.shape
    blocks = values.reshape(sx // 2, 2, sy // 2, 2, sz // 2, 2, chans)
    return jnp.mean(blocks, axis=(1, 3, 5))


def spread_back(values):
    sx, sy, sz, chans = values.shape
    wide = jnp.broadcast_to(values[:, None, :, None, :, None, :], (sx, 2, sy, 2, sz, 2, chans))
    return wide.reshape(sx * 2, sy * 2, sz * 2, chans)


def local(volume, fine_weight, coarse_weight, cotangent):
    fine_extent = volume.shape[:3]
    chans = volume.shape[3]
    coarse_extent = (fine_extent[0] // 2, fine_extent[1] // 2, fine_extent[2] // 2)
    coarse_chans = coarse_weight.shape[2]
    padded = extended(volume, (("gx", 0), ("gy", 1), ("gz", 2)), 1)
    fine_patches = gather_taps(padded, fine_extent, False)
    hidden = forward_taps(fine_patches, fine_weight)
    pooled = pool_mean(jax.nn.silu(hidden).reshape(fine_extent + (chans,))).astype(jnp.bfloat16)
    pooled_pad = extended(pooled, (("gx", 0), ("gy", 1), ("gz", 2)), 1)
    coarse_patches = gather_taps(pooled_pad, coarse_extent, False)
    coarse = forward_taps(coarse_patches, coarse_weight)
    coarse_out = jax.nn.silu(coarse).astype(jnp.bfloat16).reshape(coarse_extent + (coarse_chans,))
    incoming = cotangent.reshape(coarse.shape).astype(jnp.float32)
    coarse_grad = (incoming * silu_slope(coarse)).astype(jnp.bfloat16)
    coarse_sum = weight_terms(coarse_patches, coarse_grad)
    grad_pad = extended(
        coarse_grad.reshape(coarse_extent + (coarse_chans,)), (("gx", 0), ("gy", 1), ("gz", 2)), 1
    )
    back_pooled = backward_taps(grad_pad, coarse_extent, coarse_weight)
    spread = spread_back(back_pooled.reshape(coarse_extent + (chans,))) * 0.125
    fine_grad = (spread.reshape(hidden.shape) * silu_slope(hidden)).astype(jnp.bfloat16)
    fine_sum = weight_terms(fine_patches, fine_grad)
    fine_pad = extended(
        fine_grad.reshape(fine_extent + (chans,)), (("gx", 0), ("gy", 1), ("gz", 2)), 1
    )
    grad_volume = (
        backward_taps(fine_pad, fine_extent, fine_weight)
        .astype(jnp.bfloat16)
        .reshape(fine_extent + (chans,))
    )
    devices = lax.axis_size("gx") * lax.axis_size("gy") * lax.axis_size("gz")
    cells_fine = fine_extent[0] * fine_extent[1] * fine_extent[2] * devices
    fine_scale = 1.0 / math.sqrt(cells_fine)
    coarse_scale = 1.0 / math.sqrt(cells_fine // 8)
    fine_total, coarse_total = lax.psum((fine_sum, coarse_sum), ("gx", "gy", "gz"))
    fine_done = (fine_total * fine_scale).astype(jnp.bfloat16)
    coarse_done = (coarse_total * coarse_scale).astype(jnp.bfloat16)
    grad_fine_weight = fine_done.reshape(fine_weight.shape)
    grad_coarse_weight = coarse_done.reshape(coarse_weight.shape)
    return (coarse_out, grad_volume, grad_fine_weight, grad_coarse_weight)


def solution(mesh):
    return jax.shard_map(
        local,
        mesh=mesh,
        in_specs=(P("gx", "gy", "gz", None), P(), P(), P("gx", "gy", "gz", None)),
        out_specs=(P("gx", "gy", "gz", None), P("gx", "gy", "gz", None), P(), P()),
        check_vma=False,
    )
```

profile of v0, /device:TPU:1, one launch (start us, length us, event | category | flops | bytes accessed | tf_op | source)
XLA Modules:
  0.0 636.0 jit_solution(15636615781726683696)
XLA Ops:
  8.0 3.9 collective-permute-start
  14.2 2.2 collective-permute-done.1
  16.4 3.5 collective-permute-start.2
  21.3 3.4 collective-permute-done.3
  24.8 17.8 %collective-permute-start.4 = (bf16[10,10,1,128]{3,2,1,0:T(2,128)(2,1)S(1)}, bf16[10,10,1,128]{3,2,1,0:T(2,128)(2,1)S(1)}, u32[]{:S(2)}, u32[]{:S(2)}) collective-permute-start(bf16[10,10,1,128]{3,2,1,0:T(2,128)(2,1)S(1)} %get-tuple-element.31), channel_id=1, source_target_pairs={{0,1},{1,2},{2,3},{3,4},{4,5},{5,6},{6,7},{7,8},{8,9},{9,10},{10,1... | collective-permute-start | bytes 76808 | tf_op jit(solution)/shard_map/ppermute | solution.py:16
  45.2 11.5 %collective-permute-done.5 = bf16[10,10,1,128]{3,2,1,0:T(2,128)(2,1)S(1)} collective-permute-done((bf16[10,10,1,128]{3,2,1,0:T(2,128)(2,1)S(1)}, bf16[10,10,1,128]{3,2,1,0:T(2,128)(2,1)S(1)}, u32[]{:S(2)}, u32[]{:S(2)}) %collective-permute-start.5) | collective-permute-done | bytes 25632 | tf_op jit(solution)/shard_map/ppermute | solution.py:17
  62.5 3.1 collective-permute-start.6
  66.9 3.0 collective-permute-done.7
  70.0 2.6 collective-permute-start.8
  73.9 3.1 collective-permute-done.9
  77.1 4.7 collective-permute-start.10
  81.8 1.9 collective-permute-start.11
  83.8 11.8 %collective-permute-done.11 = bf16[6,6,1,128]{3,2,1,0:T(2,128)(2,1)S(1)} collective-permute-done((bf16[6,6,1,128]{3,2,1,0:T(2,128)(2,1)S(1)}, bf16[6,6,1,128]{3,2,1,0:T(2,128)(2,1)S(1)}, u32[]{:S(2)}, u32[]{:S(2)}) %collective-permute-start.11) | collective-permute-done | bytes 9248 | tf_op jit(solution)/shard_map/ppermute | solution.py:17
  97.4 2.8 collective-permute-start.12
  104.6 3.4 collective-permute-start.14
  112.6 1.9 collective-permute-start.16
  114.6 12.4 %collective-permute-start.17 = (bf16[6,6,1,128]{3,2,1,0:T(2,128)(2,1)S(1)}, bf16[6,6,1,128]{3,2,1,0:T(2,128)(2,1)S(1)}, u32[]{:S(2)}, u32[]{:S(2)}) collective-permute-start(bf16[6,6,1,128]{3,2,1,0:T(2,128)(2,1)S(1)} %get-tuple-element.52), channel_id=1, source_target_pairs={{0,1},{1,2},{2,3},{3,4},{4,5},{5,6},{6,7},{7,8},{8,9},{9,10},{10,1... | collective-permute-start | bytes 27656 | tf_op jit(solution)/shard_map/ppermute | solution.py:16
  129.1 3.8 collective-permute-start.18
  134.1 2.3 fusion.19
  137.6 3.1 collective-permute-start.20
  142.0 3.2 collective-permute-done.21
  147.2 15.8 %collective-permute-start.23 = (bf16[10,10,1,128]{3,2,1,0:T(2,128)(2,1)S(1)}, bf16[10,10,1,128]{3,2,1,0:T(2,128)(2,1)S(1)}, u32[]{:S(2)}, u32[]{:S(2)}) collective-permute-start(bf16[10,10,1,128]{3,2,1,0:T(2,128)(2,1)S(1)} %get-tuple-element.26), channel_id=1, source_target_pairs={{0,1},{1,2},{2,3},{3,4},{4,5},{5,6},{6,7},{7,8},{8,9},{9,10},{10,1... | collective-permute-start | bytes 76808 | tf_op jit(solution)/shard_map/ppermute | solution.py:16
  167.8 457.8 %all-reduce.3.cloned.1.call-done = (f32[3456,128]{1,0:T(8,128)}, f32[3456,128]{1,0:T(8,128)}) async-done(((f32[3456,128]{1,0:T(8,128)}, f32[3456,128]{1,0:T(8,128)}), (f32[3456,128]{1,0:T(8,128)}, f32[3456,128]{1,0:T(8,128)})) %all-reduce.3.cloned.1.call-update) | async-done | bytes 3538960 | tf_op jit(solution)/shard_map/psum | solution.py:114
  625.6 3.6 multiply_convert_fusion
  (188 shorter events, 38.1 us)
Async XLA Ops:
  7.2 618.4 %all-reduce.3.cloned.1.call-start = ((), (), s32[]{:S(2)}) async-start(), calls=%async_computation | async-start | bytes 7077888 | tf_op jit(solution)/shard_map/psum | solution.py:114
  8.0 5.2 collective-permute-start
  11.9 4.5 collective-permute-start.1
  16.4 4.9 collective-permute-start.2
  20.0 4.7 collective-permute-start.3
  24.8 20.5 %collective-permute-start.4 = (bf16[10,10,1,128]{3,2,1,0:T(2,128)(2,1)S(1)}, bf16[10,10,1,128]{3,2,1,0:T(2,128)(2,1)S(1)}, u32[]{:S(2)}, u32[]{:S(2)}) collective-permute-start(bf16[10,10,1,128]{3,2,1,0:T(2,128)(2,1)S(1)} %get-tuple-element.31), channel_id=1, source_target_pairs={{0,1},{1,2},{2,3},{3,4},{4,5},{5,6},{6,7},{7,8},{8,9},{9,10},{10,1... | collective-permute-start | bytes 76808 | tf_op jit(solution)/shard_map/ppermute | solution.py:16
  42.6 14.1 %collective-permute-start.5 = (bf16[10,10,1,128]{3,2,1,0:T(2,128)(2,1)S(1)}, bf16[10,10,1,128]{3,2,1,0:T(2,128)(2,1)S(1)}, u32[]{:S(2)}, u32[]{:S(2)}) collective-permute-start(bf16[10,10,1,128]{3,2,1,0:T(2,128)(2,1)S(1)} %get-tuple-element.30), channel_id=1, source_target_pairs={{1,0},{2,1},{3,2},{4,3},{5,4},{6,5},{7,6},{8,7},{9,8},{10,9},{11,1... | collective-permute-start | bytes 76808 | tf_op jit(solution)/shard_map/ppermute | solution.py:17
  62.5 4.4 collective-permute-start.6
  65.6 4.4 collective-permute-start.7
  72.6 4.4 collective-permute-start.9
  77.1 6.7 %collective-permute-start.10 = (bf16[6,6,1,128]{3,2,1,0:T(2,128)(2,1)S(1)}, bf16[6,6,1,128]{3,2,1,0:T(2,128)(2,1)S(1)}, u32[]{:S(2)}, u32[]{:S(2)}) collective-permute-start(bf16[6,6,1,128]{3,2,1,0:T(2,128)(2,1)S(1)} %get-tuple-element.57), channel_id=1, source_target_pairs={{0,1},{1,2},{2,3},{3,4},{4,5},{5,6},{6,7},{7,8},{8,9},{9,10},{10,1... | collective-permute-start | bytes 27656 | tf_op jit(solution)/shard_map/ppermute | solution.py:16
  81.8 13.8 %collective-permute-start.11 = (bf16[6,6,1,128]{3,2,1,0:T(2,128)(2,1)S(1)}, bf16[6,6,1,128]{3,2,1,0:T(2,128)(2,1)S(1)}, u32[]{:S(2)}, u32[]{:S(2)}) collective-permute-start(bf16[6,6,1,128]{3,2,1,0:T(2,128)(2,1)S(1)} %get-tuple-element.56), channel_id=1, source_target_pairs={{1,0},{2,1},{3,2},{4,3},{5,4},{6,5},{7,6},{8,7},{9,8},{10,9},{11,1... | collective-permute-start | bytes 27656 | tf_op jit(solution)/shard_map/ppermute | solution.py:17
  97.4 6.8 %collective-permute-start.12 = (bf16[1,4,4,128]{3,2,1,0:T(4,128)(2,1)S(1)}, bf16[1,4,4,128]{3,2,1,0:T(4,128)(2,1)S(1)}, u32[]{:S(2)}, u32[]{:S(2)}) collective-permute-start(bf16[1,4,4,128]{3,2,1,0:T(4,128)(2,1)S(1)} %bitcast.225), channel_id=1, source_target_pairs={{0,128},{128,256},{256,384},{1,129},{129,257},{257,385},{2,130},{1... | collective-permute-start | bytes 12296 | tf_op jit(solution)/shard_map/ppermute | solution.py:16
  100.2 4.4 collective-permute-start.13
  104.6 6.4 %collective-permute-start.14 = (bf16[6,1,4,128]{3,2,1,0:T(4,128)(2,1)S(1)}, bf16[6,1,4,128]{3,2,1,0:T(4,128)(2,1)S(1)}, u32[]{:S(2)}, u32[]{:S(2)}) collective-permute-start(bf16[6,1,4,128]{3,2,1,0:T(4,128)(2,1)S(1)} %get-tuple-element.62), channel_id=1, source_target_pairs={{0,16},{16,32},{32,48},{48,64},{64,80},{80,96},{96,112},{1,17},{17... | collective-permute-start | bytes 18440 | tf_op jit(solution)/shard_map/ppermute | solution.py:16
  108.0 4.5 collective-permute-start.15
  112.6 14.4 %collective-permute-start.16 = (bf16[6,6,1,128]{3,2,1,0:T(2,128)(2,1)S(1)}, bf16[6,6,1,128]{3,2,1,0:T(2,128)(2,1)S(1)}, u32[]{:S(2)}, u32[]{:S(2)}) collective-permute-start(bf16[6,6,1,128]{3,2,1,0:T(2,128)(2,1)S(1)} %get-tuple-element.53), channel_id=1, source_target_pairs={{1,0},{2,1},{3,2},{4,3},{5,4},{6,5},{7,6},{8,7},{9,8},{10,9},{11,1... | collective-permute-start | bytes 27656 | tf_op jit(solution)/shard_map/ppermute | solution.py:17
  114.6 13.2 %collective-permute-start.17 = (bf16[6,6,1,128]{3,2,1,0:T(2,128)(2,1)S(1)}, bf16[6,6,1,128]{3,2,1,0:T(2,128)(2,1)S(1)}, u32[]{:S(2)}, u32[]{:S(2)}) collective-permute-start(bf16[6,6,1,128]{3,2,1,0:T(2,128)(2,1)S(1)} %get-tuple-element.52), channel_id=1, source_target_pairs={{0,1},{1,2},{2,3},{3,4},{4,5},{5,6},{6,7},{7,8},{8,9},{9,10},{10,1... | collective-permute-start | bytes 27656 | tf_op jit(solution)/shard_map/ppermute | solution.py:16
  129.1 7.4 %collective-permute-start.18 = (bf16[1,8,8,128]{3,2,1,0:T(8,128)(2,1)S(1)}, bf16[1,8,8,128]{3,2,1,0:T(8,128)(2,1)S(1)}, u32[]{:S(2)}, u32[]{:S(2)}) collective-permute-start(bf16[1,8,8,128]{3,2,1,0:T(8,128)(2,1)S(1)} %get-tuple-element.46), channel_id=1, source_target_pairs={{0,128},{128,256},{256,384},{1,129},{129,257},{257,385},{2,130},{1... | collective-permute-start | bytes 49160 | tf_op jit(solution)/shard_map/ppermute | solution.py:16
  132.8 4.8 collective-permute-start.19
  137.6 4.4 collective-permute-start.20
  140.7 4.5 collective-permute-start.21
  145.3 17.9 %collective-permute-start.22 = (bf16[10,10,1,128]{3,2,1,0:T(2,128)(2,1)S(1)}, bf16[10,10,1,128]{3,2,1,0:T(2,128)(2,1)S(1)}, u32[]{:S(2)}, u32[]{:S(2)}) collective-permute-start(bf16[10,10,1,128]{3,2,1,0:T(2,128)(2,1)S(1)} %get-tuple-element.27), channel_id=1, source_target_pairs={{1,0},{2,1},{3,2},{4,3},{5,4},{6,5},{7,6},{8,7},{9,8},{10,9},{11,1... | collective-permute-start | bytes 76808 | tf_op jit(solution)/shard_map/ppermute | solution.py:17
  147.2 17.0 %collective-permute-start.23 = (bf16[10,10,1,128]{3,2,1,0:T(2,128)(2,1)S(1)}, bf16[10,10,1,128]{3,2,1,0:T(2,128)(2,1)S(1)}, u32[]{:S(2)}, u32[]{:S(2)}) collective-permute-start(bf16[10,10,1,128]{3,2,1,0:T(2,128)(2,1)S(1)} %get-tuple-element.26), channel_id=1, source_target_pairs={{0,1},{1,2},{2,3},{3,4},{4,5},{5,6},{6,7},{7,8},{8,9},{9,10},{10,1... | collective-permute-start | bytes 76808 | tf_op jit(solution)/shard_map/ppermute | solution.py:16
  (7 other events, 161.9 us)
Sparse Core Ops, SparseCore 0:
  136.6 488.9 all-reduce.2
where the time goes:
time: 637 us; the launch traced here: 636 us
  waiting for transfers between devices  502 us (79%)
  starting transfers between devices  95 us (15%)
  between operations  15.2 us (2%)
  local copies, waits for them, and re-layouts  9.84 us (2%)
  matrix products  8.1 us (1%)
    psum x1, waiting for transfers between devices, local(): lax.psum((fine_sum, coarse_sum), ('gx', 'gy', 'gz'))  458 us
    ppermute x12, starting transfers between devices, extended(): before = lax.ppermute(last, axis, up)  76.9 us
    ppermute x12, waiting for transfers between devices, extended(): after = lax.ppermute(leading, axis, down)  41.2 us
    ppermute x12, starting transfers between devices, extended(): after = lax.ppermute(leading, axis, down)  18 us
  transfers between devices with their start and end apart: 25, of which 14 were waited for; matrix products, arithmetic and copies ran while one was open for 2% of the time, Pallas kernels for 0%

commit v1 on v0

v1 whole, which is shorter than its diff:
```python
import math

import jax
import jax.numpy as jnp
from jax import lax
from jax.sharding import Mesh, PartitionSpec as P

AXES = ("gx", "gy", "y", "zh", "core")
WIDTH = ("y", "zh", "core")
PLANE = ("gx", "y")
LINE = ("gy", "zh")


def line(count, step):
    return [(i, i + step) for i in range(count) if 0 <= i + step < count]


def beside(last, leading, axis, count):
    before = lax.ppermute(last, axis, line(count, 1))
    after = lax.ppermute(leading, axis, line(count, -1))
    return before, after


def extended(x, axis, count, dim, width):
    length = x.shape[dim]
    last = lax.slice_in_dim(x, length - width, length, axis=dim)
    leading = lax.slice_in_dim(x, 0, width, axis=dim)
    before, after = beside(last, leading, axis, count)
    return jnp.concatenate([before, x, after], axis=dim)


def valid_conv(x, weights):
    kernel = weights.reshape(3, 3, 3, weights.shape[1], weights.shape[2])
    result = lax.conv_general_dilated(
        x[None],
        kernel,
        (1, 1, 1),
        "VALID",
        dimension_numbers=("NDHWC", "DHWIO", "NDHWC"),
        preferred_element_type=jnp.float32,
    )
    return result[0]


def valid_conv_back(x, weights):
    return valid_conv(x, jnp.transpose(weights[::-1], (0, 2, 1)))


def gather_taps(padded, extent):
    rows_x, rows_y, rows_z = extent
    pieces = []
    for i in range(3):
        for j in range(3):
            for k in range(3):
                pieces.append(padded[i : i + rows_x, j : j + rows_y, k : k + rows_z, :])
    stacked = jnp.concatenate(pieces, axis=3)
    return stacked.reshape(rows_x * rows_y * rows_z, stacked.shape[3])


def weight_terms(padded, grads):
    patches = gather_taps(padded, grads.shape[:3])
    flat = grads.reshape(-1, grads.shape[3])
    return lax.dot_general(
        patches, flat, (((0,), (0,)), ((), ())), preferred_element_type=jnp.float32
    )


def silu_slope(values):
    sigma = jax.nn.sigmoid(values)
    return sigma * (1.0 + values * (1.0 - sigma))


def pool_mean(values):
    sx, sy, sz, chans = values.shape
    blocks = values.reshape(sx // 2, 2, sy // 2, 2, sz // 2, 2, chans)
    return jnp.mean(blocks, axis=(1, 3, 5))


def spread_back(values):
    sx, sy, sz, chans = values.shape
    wide = jnp.broadcast_to(values[:, None, :, None, :, None, :], (sx, 2, sy, 2, sz, 2, chans))
    return wide.reshape(sx * 2, sy * 2, sz * 2, chans)


def inside(extent, starts, sizes):
    keep = None
    for dim in range(3):
        at = starts[dim] + lax.broadcasted_iota(jnp.int32, extent + (1,), dim)
        ok = (at >= 0) & (at < sizes[dim])
        keep = ok if keep is None else keep & ok
    return keep


def spread_rows(terms, axes, peers):
    rows, chans = terms.shape
    parts = terms.astype(jnp.bfloat16).reshape(peers, rows // peers, chans)
    got = lax.all_to_all(parts, axes, 0, 0, tiled=True)
    return jnp.sum(got.astype(jnp.float32), axis=0)


def gathered_rows(part, axes, peers):
    rows, chans = part.shape
    parts = jnp.broadcast_to(part[None], (peers, rows, chans))
    return lax.all_to_all(parts, axes, 0, 0, tiled=True).reshape(peers * rows, chans)


def total_over_slice(terms, scale, plane, along):
    rows, chans = terms.shape
    half = rows // 2
    core = lax.axis_index("core")
    swap = [(0, 1), (1, 0)]
    halves = terms.reshape(2, half, chans)
    mine = lax.dynamic_index_in_dim(halves, core, 0, keepdims=False)
    other = lax.dynamic_index_in_dim(halves, 1 - core, 0, keepdims=False)
    mine = mine + lax.ppermute(other.astype(jnp.bfloat16), "core", swap).astype(jnp.float32)

    part = spread_rows(mine, PLANE, plane)
    length = half // plane
    padded = -(-length // (16 * along)) * 16 * along
    part = jnp.pad(part, ((0, padded - length), (0, 0)))
    part = spread_rows(part, LINE, along)

    part = gathered_rows(part.astype(jnp.bfloat16), LINE, along)[:length].astype(jnp.float32)
    part = (part * scale).astype(jnp.bfloat16)
    mine = gathered_rows(part, PLANE, plane)
    other = lax.ppermute(mine, "core", swap)
    first = jnp.where(core == 0, mine, other)
    second = jnp.where(core == 0, other, mine)
    return jnp.concatenate([first, second], axis=0)


def local(volume, fine_weight, coarse_weight, cotangent):
    chans = volume.shape[3]
    sizes = {axis: lax.axis_size(axis) for axis in AXES}
    plane, along = (sizes["gx"] * sizes["y"], sizes["gy"] * sizes["zh"])
    place = [lax.axis_index("gx"), lax.axis_index("gy"), lax.axis_index(WIDTH)]
    peers = [sizes["gx"], sizes["gy"], sizes["y"] * sizes["zh"] * 2]
    fine_sizes = [8 * n for n in peers]
    coarse_sizes = [4 * n for n in peers]

    packed = jnp.concatenate([volume.reshape(512, chans), cotangent.reshape(64, chans)], axis=0)
    first = lax.axis_index("core") == 0
    near = [(i, i ^ 1) for i in range(peers[2])]
    far = [(i, i - 1 + 2 * (i % 2)) for i in range(1, peers[2] - 1)]
    inner = lax.ppermute(packed, WIDTH, near)
    outer = lax.ppermute(packed, WIDTH, far)
    before = jnp.where(first, outer, inner)
    after = jnp.where(first, inner, outer)
    wide = jnp.concatenate(
        [
            before[:512].reshape(8, 8, 8, chans)[:, :, 1:],
            volume,
            after[:512].reshape(8, 8, 8, chans)[:, :, :7],
        ],
        axis=2,
    )
    incoming = jnp.concatenate(
        [
            before[512:].reshape(4, 4, 4, chans)[:, :, 2:],
            cotangent,
            after[512:].reshape(4, 4, 4, chans)[:, :, :2],
        ],
        axis=2,
    ).astype(jnp.float32)
    wide = extended(wide, "gy", peers[1], 1, 3)
    wide = extended(wide, "gx", peers[0], 0, 3)

    hidden = valid_conv(wide, fine_weight)
    pooled = pool_mean(jax.nn.silu(hidden))
    starts = [4 * place[0] - 1, 4 * place[1] - 1, 4 * place[2] - 3]
    keep = inside((6, 6, 10), starts, coarse_sizes)
    pooled = jnp.where(keep, pooled, 0.0).astype(jnp.bfloat16)
    coarse = valid_conv(pooled, coarse_weight)
    coarse_out = jax.nn.silu(coarse[:, :, 2:6]).astype(jnp.bfloat16)
    coarse_grad = (incoming * silu_slope(coarse)).astype(jnp.bfloat16)
    coarse_sum = weight_terms(pooled[:, :, 2:8], coarse_grad[:, :, 2:6])

    around = extended(coarse_grad, "gy", peers[1], 1, 2)
    around = extended(around, "gx", peers[0], 0, 2)
    back_pooled = valid_conv_back(around, coarse_weight)
    spread = spread_back(back_pooled)[1:11, 1:11, 1:11] * 0.125
    fine_grad = spread * silu_slope(hidden[1:11, 1:11, 5:15])
    keep = inside((10, 10, 10), [8 * p - 1 for p in place], fine_sizes)
    fine_grad = jnp.where(keep, fine_grad, 0.0).astype(jnp.bfloat16)
    fine_sum = weight_terms(wide[2:12, 2:12, 6:16], fine_grad[1:9, 1:9, 1:9])
    grad_volume = valid_conv_back(fine_grad, fine_weight).astype(jnp.bfloat16)

    cells_fine = fine_sizes[0] * fine_sizes[1] * fine_sizes[2]
    fine_scale = 1.0 / math.sqrt(cells_fine)
    coarse_scale = 1.0 / math.sqrt(cells_fine // 8)
    pieces = 2 * plane
    rows = fine_sum.shape[0] // pieces
    both = jnp.concatenate(
        [fine_sum.reshape(pieces, rows, chans), coarse_sum.reshape(pieces, rows, chans)], axis=1
    )
    scale = jnp.where(
        lax.broadcasted_iota(jnp.int32, (2 * rows, 1), 0) < rows, fine_scale, coarse_scale
    )
    done = total_over_slice(both.reshape(-1, chans), scale, plane, along)
    done = done.reshape(pieces, 2 * rows, chans)
    grad_fine_weight = done[:, :rows].reshape(fine_weight.shape)
    grad_coarse_weight = done[:, rows:].reshape(coarse_weight.shape)
    return (coarse_out, grad_volume, grad_fine_weight, grad_coarse_weight)


def solution(mesh):
    shape = mesh.devices.shape
    inner = Mesh(mesh.devices.reshape(shape[0], shape[1], shape[2] // 4, 2, 2), AXES)
    cells = P("gx", "gy", WIDTH, None)
    return jax.shard_map(
        local,
        mesh=inner,
        in_specs=(cells, P(), P(), cells),
        out_specs=(cells, cells, P(), P()),
        check_vma=False,
    )
```

time: 637 us -> 234 us (0.37)
  waiting for transfers between devices: 502 us -> 35.5 us
  blocking collectives: 0 us -> 51 us
  starting transfers between devices: 95 us -> 61.5 us
  local copies, waits for them, and re-layouts: 9.84 us -> 43.3 us
  other arithmetic: 6.3 us -> 21.3 us
  between operations: 15.2 us -> 1.4 us
  matrix products: 8.1 us -> 19 us
    psum x1 -> x0, waiting for transfers between devices: 458 us -> none  [local(): lax.psum((fine_sum, coarse_sum), ('gx', 'gy', 'gz'))]
    all_to_all x0 -> x2, blocking collectives: none -> 51 us  [spread_rows(): got = lax.all_to_all(parts, axes, 0, 0, tiled=True)]
    ppermute x24 -> x12, starting transfers between devices: 95 us -> 53.8 us  [the longest x4 20.5 us: beside(): before = lax.ppermute(last, axis, line(count, 1))]
    ppermute x24 -> x12, waiting for transfers between devices: 43.7 us -> 13 us  [the longest x4 7.65 us: beside(): after = lax.ppermute(leading, axis, line(count, -1))]
    all_to_all x0 -> x2, waiting for transfers between devices: none -> 22.5 us  [gathered_rows(): lax.all_to_all(parts, axes, 0, 0, tiled=True).reshape(peers * rows, chans)]
    conv_general_dilated x0 -> x4, matrix products: none -> 14.1 us  [valid_conv(): lax.conv_general_dilated(x[None], kernel, (1, 1, 1), 'VALID', dimension_n...]
    unnamed x107 -> x79, local copies, waits for them, and re-layouts: 8.04 us -> 16.6 us
    all_to_all x0 -> x2, starting transfers between devices: none -> 7.74 us  [gathered_rows(): lax.all_to_all(parts, axes, 0, 0, tiled=True).reshape(peers * rows, chans)]
  transfers between devices with their start and end apart: 25 -> 14, of which waited for: 14 -> 8; matrix products, arithmetic and copies ran while one was open for 2% -> 8% of each run, Pallas kernels for 0% -> 0%
where the time goes in v1:
time: 234 us; the launch traced here: 233 us
  starting transfers between devices  61.5 us (26%)
  blocking collectives  51 us (22%)
  local copies, waits for them, and re-layouts  43.3 us (19%)
  waiting for transfers between devices  35.5 us (15%)
  other arithmetic  21.3 us (9%)
  matrix products  19 us (8%)
    all_to_all x2, blocking collectives, spread_rows(): got = lax.all_to_all(parts, axes, 0, 0, tiled=True)  51 us
    all_to_all x2, waiting for transfers between devices, gathered_rows(): lax.all_to_all(parts, axes, 0, 0, tiled=True).reshape(peers * rows, chans)  22.5 us
    ppermute x4, starting transfers between devices, beside(): before = lax.ppermute(last, axis, line(count, 1))  20.5 us
    ppermute x1, starting transfers between devices, local(): outer = lax.ppermute(packed, WIDTH, far)  16.8 us
    unnamed x79, local copies, waits for them, and re-layouts  16.6 us
    conv_general_dilated x4, matrix products, valid_conv(): lax.conv_general_dilated(x[None], kernel, (1, 1, 1), 'VALID', dimension_n...  14.1 us
    all_to_all x2, starting transfers between devices, gathered_rows(): lax.all_to_all(parts, axes, 0, 0, tiled=True).reshape(peers * rows, chans)  7.74 us
    ppermute x4, waiting for transfers between devices, beside(): after = lax.ppermute(leading, axis, line(count, -1))  7.65 us
  transfers between devices with their start and end apart: 14, of which 8 were waited for; matrix products, arithmetic and copies ran while one was open for 8% of the time, Pallas kernels for 0%

profile of v1, /device:TPU:1, one launch (start us, length us, event | category | flops | bytes accessed | tf_op | source)
XLA Modules:
  0.0 233.0 jit_solution(15804758266611430640)
XLA Ops:
  1.7 16.8 %collective-permute-start = (bf16[576,128]{1,0:T(8,128)(2,1)S(1)}, bf16[576,128]{1,0:T(8,128)(2,1)S(1)}, u32[]{:S(2)}, u32[]{:S(2)}) collective-permute-start(bf16[576,128]{1,0:T(8,128)(2,1)S(1)} %pad_maximum_fusion.11), channel_id=1, source_target_pairs={{1,2},{2,1},{3,4},{4,3},{5,6},{6,5},{7,8},{8,7},{9,10},{10,9},{11,... | collective-permute-start | bytes 442376 | tf_op jit(solution)/shard_map/ppermute | solution.py:146
  23.4 11.5 %collective-permute-start.2 = (bf16[8,3,22,128]{3,2,1,0:T(8,128)(2,1)S(1)}, bf16[8,3,22,128]{3,2,1,0:T(8,128)(2,1)S(1)}, u32[]{:S(2)}, u32[]{:S(2)}) collective-permute-start(bf16[8,3,22,128]{3,2,1,0:T(8,128)(2,1)S(1)} %get-tuple-element.14), channel_id=1, source_target_pairs={{0,16},{16,32},{32,48},{48,64},{64,80},{80,96},{96,112},{1,17},{17... | collective-permute-start | bytes 405512 | tf_op jit(solution)/shard_map/ppermute | solution.py:19
  37.0 3.8 %collective-permute-done.3 = bf16[8,3,22,128]{3,2,1,0:T(8,128)(2,1)S(1)} collective-permute-done((bf16[8,3,22,128]{3,2,1,0:T(8,128)(2,1)S(1)}, bf16[8,3,22,128]{3,2,1,0:T(8,128)(2,1)S(1)}, u32[]{:S(2)}, u32[]{:S(2)}) %collective-permute-start.3) | collective-permute-done | bytes 135200 | tf_op jit(solution)/shard_map/ppermute | solution.py:20
  41.8 3.4 %collective-permute-start.4 = (bf16[3,14,22,128]{3,2,1,0:T(8,128)(2,1)S(1)}, bf16[3,14,22,128]{3,2,1,0:T(8,128)(2,1)S(1)}, u32[]{:S(2)}, u32[]{:S(2)}) collective-permute-start(bf16[3,14,22,128]{3,2,1,0:T(8,128)(2,1)S(1)} %get-tuple-element.12), channel_id=1, source_target_pairs={{0,128},{128,256},{256,384},{1,129},{129,257},{257,385},{2,130},{1... | collective-permute-start | bytes 709640 | tf_op jit(solution)/shard_map/ppermute | solution.py:19
  48.5 3.8 %collective-permute-done.5 = bf16[3,14,22,128]{3,2,1,0:T(8,128)(2,1)S(1)} collective-permute-done((bf16[3,14,22,128]{3,2,1,0:T(8,128)(2,1)S(1)}, bf16[3,14,22,128]{3,2,1,0:T(8,128)(2,1)S(1)}, u32[]{:S(2)}, u32[]{:S(2)}) %collective-permute-start.5) | collective-permute-done | bytes 236576 | tf_op jit(solution)/shard_map/ppermute | solution.py:20
  54.7 7.0 %fusion.10 = f32[12,12,8,3,128]{4,2,3,1,0:T(8,128)S(1)} fusion(bf16[3,3,3,128,128]{4,3,2,1,0:T(8,128)(2,1)S(1)} %bitcast.94, bf16[14,14,1,7,2,128]{5,3,4,1,0,2:T(8,128)(2,1)S(1)} %slice.409, bf16[14,14,1,8,3,128]{5,3,4,1,0,2:T(8,128)(2,1)S(1)} %copy.43, pred[8,3]{0,1:T(4,128)(4,1)S(1)} %copy-done.15), kind=kOutput, calls=%fused_computation.15 | convolution fusion | flops 3064111104 | bytes 4560920 | tf_op jit(solution)/shard_map/conv_general_dilated | solution.py:34
  62.4 2.4 %reshape.149 = f32[12,12,1,24,128]{4,3,1,0,2:T(8,128)} reshape(f32[12,12,8,3,128]{4,3,2,1,0:T(4,128)S(1)} %copy.44) | data formatting | bytes 3538944 | tf_op jit(solution)/shard_map/conv_general_dilated | solution.py:34
  64.7 3.1 %slice_bitcast_fusion = (f32[12,12,20,128]{3,2,1,0:T(8,128)}, f32[12,12,1,20,128]{4,3,1,0,2:T(8,128)S(1)}) fusion(f32[12,12,1,24,128]{4,3,1,0,2:T(8,128)} %reshape.149), kind=kLoop, calls=%fused_computation.132 | loop fusion | bytes 4423680 | tf_op jit(solution)/shard_map/squeeze | solution.py:42
  69.9 3.4 %fusion.9 = f32[6,6,10,128]{3,2,1,0:T(8,128)S(1)} fusion(f32[6,2,6,2,10,2,128]{6,5,4,3,2,1,0:T(2,128)} %squeeze.14), kind=kLoop, calls=%fused_computation.14 | loop fusion | flops 1797120 | bytes 1658880 | tf_op jit(solution)/shard_map/reduce_sum | solution.py:76
  100.3 2.0 dot_general.18
  105.5 3.7 %collective-permute-start.8 = (bf16[2,8,8,128]{3,2,1,0:T(8,128)(2,1)}, bf16[2,8,8,128]{3,2,1,0:T(8,128)(2,1)}, u32[]{:S(2)}, u32[]{:S(2)}) collective-permute-start(bf16[2,8,8,128]{3,2,1,0:T(8,128)(2,1)} %get-tuple-element.18), channel_id=1, source_target_pairs={{0,128},{128,256},{256,384},{1,129},{129,257},{257,385},{2,130},{1... | collective-permute-start | bytes 98312 | tf_op jit(solution)/shard_map/ppermute | solution.py:19
  111.2 4.4 %copy.49 = bf16[512,3456]{0,1:T(8,128)(2,1)S(1)} copy(bf16[512,3456]{1,0:T(8,128)(2,1)} %bitcast.20) | data formatting | bytes 7077888 | tf_op jit(solution)/shard_map/reshape | solution.py:57
  115.6 2.5 %dot_general.15 = bf16[32,108,512]{2,1,0:T(8,128)(2,1)} reshape(bf16[3456,512]{1,0:T(8,128)(2,1)S(1)} %bitcast.85) | data formatting | bytes 7077888 | tf_op jit(solution)/shard_map/dot_general | solution.py:63
  118.9 2.4 %fusion.21 = f32[1,6,6,6,128]{4,0,3,2,1:T(1,128)S(1)} fusion(bf16[3,3,3,128,128]{3,4,2,1,0:T(8,128)(2,1)} %bitcast.95, bf16[1,8,8,8,128]{4,3,2,1,0:T(8,128)(2,1)S(1)} %maximum_bitcast_fusion.1), kind=kOutput, calls=%fused_computation.32 | convolution fusion | flops 191102976 | bytes 1126400 | tf_op jit(solution)/shard_map/conv_general_dilated | solution.py:34
  125.0 3.1 %fusion.37 = f32[32,108,128]{2,1,0:T(8,128)S(1)} fusion(bf16[32,108,512]{2,1,0:T(8,128)(2,1)} %dot_general.15, bf16[512,128,1]{1,0,2:T(8,128)(2,1)S(1)} %bitcast.99), kind=kOutput, calls=%fused_computation.136 | convolution fusion | flops 452984832 | bytes 5439488 | tf_op jit(solution)/shard_map/dot_general | solution.py:63
  131.3 2.7 %collective-permute-done.10 = bf16[3456,128]{1,0:T(8,128)(2,1)} collective-permute-done((bf16[3456,128]{1,0:T(8,128)(2,1)}, bf16[3456,128]{1,0:T(8,128)(2,1)}, u32[]{:S(2)}, u32[]{:S(2)}) %collective-permute-start.10) | collective-permute-done | bytes 884768 | tf_op jit(solution)/shard_map/ppermute | solution.py:115
  135.4 25.9 %all_to_all.20 = bf16[16,216,128]{2,1,0:T(8,128)(2,1)S(1)} all-to-all(bf16[16,216,128]{2,1,0:T(8,128)(2,1)S(1)} %bitcast.91), channel_id=1, replica_groups=mesh['gx'=4,'gy'=8,'y'=4,'zh'=2,'core'=2] {'gx','y'}, dimensions={0} | all-to-all | bytes 1769472 | tf_op jit(solution)/shard_map/all_to_all | solution.py:97
  161.5 25.1 %all_to_all.21 = bf16[16,16,128]{2,1,0:T(8,128)(2,1)S(1)} all-to-all(bf16[16,16,128]{2,1,0:T(8,128)(2,1)S(1)} %bitcast.101), channel_id=1, replica_groups=mesh['gx'=4,'gy'=8,'y'=4,'zh'=2,'core'=2] {'gy','zh'}, dimensions={0} | all-to-all | bytes 131072 | tf_op jit(solution)/shard_map/all_to_all | solution.py:97
  187.2 3.5 %all-to-all-start.2 = ((bf16[16,16,128]{2,1,0:T(8,128)(2,1)}), bf16[16,16,128]{2,1,0:T(8,128)(2,1)S(1)}, u32[]{:S(2)}, u32[]{:S(2)}) async-start(bf16[16,16,128]{2,1,0:T(8,128)(2,1)} %broadcast_in_dim.76), calls=%async_computation.2 | async-start | bytes 131072 | tf_op jit(solution)/shard_map/all_to_all | solution.py:104
  190.7 11.6 %all-to-all-done.2 = bf16[16,16,128]{2,1,0:T(8,128)(2,1)S(1)} async-done(((bf16[16,16,128]{2,1,0:T(8,128)(2,1)}), bf16[16,16,128]{2,1,0:T(8,128)(2,1)S(1)}, u32[]{:S(2)}, u32[]{:S(2)}) %all-to-all-start.2) | async-done | bytes 65568 | tf_op jit(solution)/shard_map/all_to_all | solution.py:104
  203.4 4.2 %all-to-all-start.3 = ((bf16[16,216,128]{2,1,0:T(8,128)(2,1)}), bf16[16,216,128]{2,1,0:T(8,128)(2,1)S(1)}, u32[]{:S(2)}, u32[]{:S(2)}) async-start(bf16[16,216,128]{2,1,0:T(8,128)(2,1)} %broadcast_in_dim.79), calls=%async_computation.3 | async-start | bytes 1769472 | tf_op jit(solution)/shard_map/all_to_all | solution.py:104
  207.8 10.9 %all-to-all-done.3 = bf16[16,216,128]{2,1,0:T(8,128)(2,1)S(1)} async-done(((bf16[16,216,128]{2,1,0:T(8,128)(2,1)}), bf16[16,216,128]{2,1,0:T(8,128)(2,1)S(1)}, u32[]{:S(2)}, u32[]{:S(2)}) %all-to-all-start.3) | async-done | bytes 884768 | tf_op jit(solution)/shard_map/all_to_all | solution.py:104
  218.7 7.5 %collective-permute-start.11 = (bf16[3456,128]{1,0:T(8,128)(2,1)S(1)}, bf16[3456,128]{1,0:T(8,128)(2,1)S(1)}, u32[]{:S(2)}, u32[]{:S(2)}) collective-permute-start(bf16[3456,128]{1,0:T(8,128)(2,1)S(1)} %bitcast.90), channel_id=1, source_target_pairs={{0,1},{1,0},{2,3},{3,2},{4,5},{5,4},{6,7},{7,6},{8,9},{9,8},{10,11... | collective-permute-start | bytes 2654216 | tf_op jit(solution)/shard_map/ppermute | solution.py:126
  226.8 2.8 %convolution_convert_fusion = bf16[1,8,8,8,128]{4,0,3,2,1:T(2,128)(2,1)S(1)} fusion(bf16[3,3,3,128,128]{3,4,2,1,0:T(8,128)(2,1)S(1)} %bitcast.96, bf16[1,10,10,10,128]{4,3,2,1,0:T(8,128)(2,1)S(1)} %bitcast.97), kind=kOutput, calls=%fused_computation.17 | convolution fusion | flops 453050368 | bytes 1271808 | tf_op jit(solution)/shard_map/conv_general_dilated | solution.py:34
  (163 shorter events, 64.0 us)
Async XLA Ops:
  0.6 52.4 %copy-start = (bf16[8,8,8,128]{3,2,1,0:T(8,128)(2,1)S(1)}, bf16[8,8,8,128]{3,2,1,0:T(8,128)(2,1)}, u32[]{:S(2)}) copy-start(bf16[8,8,8,128]{3,2,1,0:T(8,128)(2,1)} %param.4) | copy-start | bytes 393220
  0.6 46.1 %copy-start.4 = (bf16[27,128,128]{2,1,0:T(8,128)(2,1)S(1)}, bf16[27,128,128]{2,1,0:T(8,128)(2,1)}, u32[]{:S(2)}) copy-start(bf16[27,128,128]{2,1,0:T(8,128)(2,1)} %param.6) | copy-start | bytes 2654212
  1.7 20.7 %collective-permute-start = (bf16[576,128]{1,0:T(8,128)(2,1)S(1)}, bf16[576,128]{1,0:T(8,128)(2,1)S(1)}, u32[]{:S(2)}, u32[]{:S(2)}) collective-permute-start(bf16[576,128]{1,0:T(8,128)(2,1)S(1)} %pad_maximum_fusion.11), channel_id=1, source_target_pairs={{1,2},{2,1},{3,4},{4,3},{5,6},{6,5},{7,8},{8,7},{9,10},{10,9},{11,... | collective-permute-start | bytes 442376 | tf_op jit(solution)/shard_map/ppermute | solution.py:146
  18.5 3.8 %collective-permute-start.1 = (bf16[576,128]{1,0:T(8,128)(2,1)S(1)}, bf16[576,128]{1,0:T(8,128)(2,1)S(1)}, u32[]{:S(2)}, u32[]{:S(2)}) collective-permute-start(bf16[576,128]{1,0:T(8,128)(2,1)S(1)} %pad_maximum_fusion.11), channel_id=1, source_target_pairs={{0,1},{1,0},{2,3},{3,2},{4,5},{5,4},{6,7},{7,6},{8,9},{9,8},{10,11... | collective-permute-start | bytes 442376 | tf_op jit(solution)/shard_map/ppermute | solution.py:145
  23.4 13.6 %collective-permute-start.2 = (bf16[8,3,22,128]{3,2,1,0:T(8,128)(2,1)S(1)}, bf16[8,3,22,128]{3,2,1,0:T(8,128)(2,1)S(1)}, u32[]{:S(2)}, u32[]{:S(2)}) collective-permute-start(bf16[8,3,22,128]{3,2,1,0:T(8,128)(2,1)S(1)} %get-tuple-element.14), channel_id=1, source_target_pairs={{0,16},{16,32},{32,48},{48,64},{64,80},{80,96},{96,112},{1,17},{17... | collective-permute-start | bytes 405512 | tf_op jit(solution)/shard_map/ppermute | solution.py:19
  34.9 5.9 %collective-permute-start.3 = (bf16[8,3,22,128]{3,2,1,0:T(8,128)(2,1)S(1)}, bf16[8,3,22,128]{3,2,1,0:T(8,128)(2,1)S(1)}, u32[]{:S(2)}, u32[]{:S(2)}) collective-permute-start(bf16[8,3,22,128]{3,2,1,0:T(8,128)(2,1)S(1)} %get-tuple-element.15), channel_id=1, source_target_pairs={{16,0},{32,16},{48,32},{64,48},{80,64},{96,80},{112,96},{17,1},{33... | collective-permute-start | bytes 405512 | tf_op jit(solution)/shard_map/ppermute | solution.py:20
  41.8 6.7 %collective-permute-start.4 = (bf16[3,14,22,128]{3,2,1,0:T(8,128)(2,1)S(1)}, bf16[3,14,22,128]{3,2,1,0:T(8,128)(2,1)S(1)}, u32[]{:S(2)}, u32[]{:S(2)}) collective-permute-start(bf16[3,14,22,128]{3,2,1,0:T(8,128)(2,1)S(1)} %get-tuple-element.12), channel_id=1, source_target_pairs={{0,128},{128,256},{256,384},{1,129},{129,257},{257,385},{2,130},{1... | collective-permute-start | bytes 709640 | tf_op jit(solution)/shard_map/ppermute | solution.py:19
  45.2 7.1 %collective-permute-start.5 = (bf16[3,14,22,128]{3,2,1,0:T(8,128)(2,1)S(1)}, bf16[3,14,22,128]{3,2,1,0:T(8,128)(2,1)S(1)}, u32[]{:S(2)}, u32[]{:S(2)}) collective-permute-start(bf16[3,14,22,128]{3,2,1,0:T(8,128)(2,1)S(1)} %get-tuple-element.13), channel_id=1, source_target_pairs={{128,0},{256,128},{384,256},{129,1},{257,129},{385,257},{130,2},{2... | collective-permute-start | bytes 709640 | tf_op jit(solution)/shard_map/ppermute | solution.py:20
  67.8 7.8 %copy-start.13 = (bf16[4,4,4,128]{3,2,1,0:T(4,128)(2,1)S(1)}, bf16[4,4,4,128]{3,2,1,0:T(4,128)(2,1)}, u32[]{:S(2)}) copy-start(bf16[4,4,4,128]{3,2,1,0:T(4,128)(2,1)} %param.7) | copy-start | bytes 49156
  67.8 8.4 %copy-start.3 = (bf16[3,14,22,128]{3,2,1,0:T(8,128)(2,1)S(1)}, bf16[3,14,22,128]{3,2,1,0:T(8,128)(2,1)}, u32[]{:S(2)}) copy-start(bf16[3,14,22,128]{3,2,1,0:T(8,128)(2,1)} %copy-done.2) | copy-start | bytes 709636
  75.7 29.2 %copy-start.9 = (bf16[4,4,8,128]{3,2,1,0:T(8,128)(2,1)}, bf16[4,4,8,128]{3,2,1,0:T(8,128)(2,1)S(1)}, u32[]{:S(2)}) copy-start(bf16[4,4,8,128]{3,2,1,0:T(8,128)(2,1)S(1)} %multiply_convert_fusion.1) | copy-start | bytes 98308
  96.3 8.5 %collective-permute-start.6 = (bf16[4,2,8,128]{3,2,1,0:T(8,128)(2,1)S(1)}, bf16[4,2,8,128]{3,2,1,0:T(8,128)(2,1)S(1)}, u32[]{:S(2)}, u32[]{:S(2)}) collective-permute-start(bf16[4,2,8,128]{3,2,1,0:T(8,128)(2,1)S(1)} %get-tuple-element.20), channel_id=1, source_target_pairs={{0,16},{16,32},{32,48},{48,64},{64,80},{80,96},{96,112},{1,17},{17... | collective-permute-start | bytes 49160 | tf_op jit(solution)/shard_map/ppermute | solution.py:19
  98.2 6.6 %collective-permute-start.7 = (bf16[4,2,8,128]{3,2,1,0:T(8,128)(2,1)S(1)}, bf16[4,2,8,128]{3,2,1,0:T(8,128)(2,1)S(1)}, u32[]{:S(2)}, u32[]{:S(2)}) collective-permute-start(bf16[4,2,8,128]{3,2,1,0:T(8,128)(2,1)S(1)} %get-tuple-element.21), channel_id=1, source_target_pairs={{16,0},{32,16},{48,32},{64,48},{80,64},{96,80},{112,96},{17,1},{33... | collective-permute-start | bytes 49160 | tf_op jit(solution)/shard_map/ppermute | solution.py:20
  104.9 6.3 %copy-start.14 = (bf16[4,2,8,128]{3,2,1,0:T(8,128)(2,1)}, bf16[4,2,8,128]{3,2,1,0:T(8,128)(2,1)S(1)}, u32[]{:S(2)}) copy-start(bf16[4,2,8,128]{3,2,1,0:T(8,128)(2,1)S(1)} %collective-permute-done.7) | copy-start | bytes 49156
  105.5 12.6 %collective-permute-start.8 = (bf16[2,8,8,128]{3,2,1,0:T(8,128)(2,1)}, bf16[2,8,8,128]{3,2,1,0:T(8,128)(2,1)}, u32[]{:S(2)}, u32[]{:S(2)}) collective-permute-start(bf16[2,8,8,128]{3,2,1,0:T(8,128)(2,1)} %get-tuple-element.18), channel_id=1, source_target_pairs={{0,128},{128,256},{256,384},{1,129},{129,257},{257,385},{2,130},{1... | collective-permute-start | bytes 98312 | tf_op jit(solution)/shard_map/ppermute | solution.py:19
  109.2 8.9 %collective-permute-start.9 = (bf16[2,8,8,128]{3,2,1,0:T(8,128)(2,1)}, bf16[2,8,8,128]{3,2,1,0:T(8,128)(2,1)}, u32[]{:S(2)}, u32[]{:S(2)}) collective-permute-start(bf16[2,8,8,128]{3,2,1,0:T(8,128)(2,1)} %get-tuple-element.19), channel_id=1, source_target_pairs={{128,0},{256,128},{384,256},{129,1},{257,129},{385,257},{130,2},{2... | collective-permute-start | bytes 98312 | tf_op jit(solution)/shard_map/ppermute | solution.py:20
  122.3 5.9 %copy-start.1 = (f32[32,108,128]{2,1,0:T(8,128)S(1)}, f32[32,108,128]{2,1,0:T(8,128)}, u32[]{:S(2)}) copy-start(f32[32,108,128]{2,1,0:T(8,128)} %fusion.18) | copy-start | bytes 5308420
  129.4 4.7 %collective-permute-start.10 = (bf16[3456,128]{1,0:T(8,128)(2,1)}, bf16[3456,128]{1,0:T(8,128)(2,1)}, u32[]{:S(2)}, u32[]{:S(2)}) collective-permute-start(bf16[3456,128]{1,0:T(8,128)(2,1)} %fusion.14), channel_id=1, source_target_pairs={{0,1},{1,0},{2,3},{3,2},{4,5},{5,4},{6,7},{7,6},{8,9},{9,8},{10,11... | collective-permute-start | bytes 2654216 | tf_op jit(solution)/shard_map/ppermute | solution.py:115
  135.4 72.3 %copy-start.6 = (bf16[27,128,128]{2,1,0:T(8,128)(2,1)S(1)}, bf16[27,128,128]{2,1,0:T(8,128)(2,1)}, u32[]{:S(2)}) copy-start(bf16[27,128,128]{2,1,0:T(8,128)(2,1)} %param.5) | copy-start | bytes 2654212
  135.4 90.7 %copy-start.11 = (f32[1,4,4,8,128]{4,0,3,2,1:T(1,128)S(1)}, f32[1,4,4,8,128]{4,0,3,2,1:T(1,128)}, u32[]{:S(2)}) copy-start(f32[1,4,4,8,128]{4,0,3,2,1:T(1,128)} %copy-done.10) | copy-start | bytes 196612
  135.4 91.4 %copy-start.8 = (bf16[10,10,10,128]{3,2,1,0:T(8,128)(2,1)S(1)}, bf16[10,10,10,128]{3,2,1,0:T(8,128)(2,1)}, u32[]{:S(2)}) copy-start(bf16[10,10,10,128]{3,2,1,0:T(8,128)(2,1)} %copy-done.7) | copy-start | bytes 768004
  187.2 15.1 %all-to-all-start.2 = ((bf16[16,16,128]{2,1,0:T(8,128)(2,1)}), bf16[16,16,128]{2,1,0:T(8,128)(2,1)S(1)}, u32[]{:S(2)}, u32[]{:S(2)}) async-start(bf16[16,16,128]{2,1,0:T(8,128)(2,1)} %broadcast_in_dim.76), calls=%async_computation.2 | async-start | bytes 131072 | tf_op jit(solution)/shard_map/all_to_all | solution.py:104
  203.4 15.2 %all-to-all-start.3 = ((bf16[16,216,128]{2,1,0:T(8,128)(2,1)}), bf16[16,216,128]{2,1,0:T(8,128)(2,1)S(1)}, u32[]{:S(2)}, u32[]{:S(2)}) async-start(bf16[16,216,128]{2,1,0:T(8,128)(2,1)} %broadcast_in_dim.79), calls=%async_computation.3 | async-start | bytes 1769472 | tf_op jit(solution)/shard_map/all_to_all | solution.py:104
  218.7 11.6 %collective-permute-start.11 = (bf16[3456,128]{1,0:T(8,128)(2,1)S(1)}, bf16[3456,128]{1,0:T(8,128)(2,1)S(1)}, u32[]{:S(2)}, u32[]{:S(2)}) collective-permute-start(bf16[3456,128]{1,0:T(8,128)(2,1)S(1)} %bitcast.90), channel_id=1, source_target_pairs={{0,1},{1,0},{2,3},{3,2},{4,5},{5,4},{6,7},{7,6},{8,9},{9,8},{10,11... | collective-permute-start | bytes 2654216 | tf_op jit(solution)/shard_map/ppermute | solution.py:126
  (6 other events, 7.7 us)

commit v2 on v1

v2 whole, which is shorter than its diff:
```python
import math

import jax
import jax.numpy as jnp
from jax import lax
from jax.experimental import pallas as pl
from jax.experimental.pallas import tpu as pltpu
from jax.sharding import Mesh, PartitionSpec as P

AXES = ("gx", "gy", "y", "zh", "core")
WIDTH = ("y", "zh", "core")
PLANE = ("gx", "y")
LINE = ("gy", "zh")
C = 128
F32 = jnp.float32
BF16 = jnp.bfloat16


def silu_slope(values):
    sigma = 1.0 / (1.0 + jnp.exp(-values))
    return sigma * (1.0 + values * (1.0 - sigma))


def inside(shape, starts, sizes):
    keep = None
    for dim in range(3):
        at = starts[dim] + lax.broadcasted_iota(jnp.int32, shape, dim)
        ok = (at >= 0) & (at < sizes[dim])
        keep = ok if keep is None else keep & ok
    return keep


def taps():
    return [(i, j, k) for i in range(3) for j in range(3) for k in range(3)]


def flat(values):
    return values.reshape(-1, C).astype(BF16)


def front_kernel(
    sizes, place, own, below, above, left, right, weights, coarse_weights, incoming,
    coarse_ref, grad_ref, pooled_ref, hidden_ref, core_ref,
    wide, patches, hidden, pairs,
):
    for x in range(8):
        wide[3 + x, 3:11, :24] = own[x].astype(F32).reshape(8, 24, C)
        wide[3 + x, :3, :24] = below[x].astype(F32).reshape(3, 24, C)
        wide[3 + x, 11:, :24] = above[x].astype(F32).reshape(3, 24, C)
    for x in range(3):
        wide[x, :, :24] = left[x].astype(F32).reshape(14, 24, C)
        wide[11 + x, :, :24] = right[x].astype(F32).reshape(14, 24, C)

    def gather(x, carry):
        for k in range(3):
            line = wide[x, :, k + 1 : k + 25]
            for j in range(3):
                at = (3 * j + k) * C
                patches[x, :, at : at + C] = flat(line[j : j + 12])
        return carry

    lax.fori_loop(0, 14, gather, 0)

    def convolve(part, carry):
        total = jnp.zeros((1152, C), F32)
        for i in range(3):
            cells = patches[pl.ds(part * 4 + i, 4)].reshape(1152, 9 * C)
            total = total + jnp.dot(
                cells, weights[9 * C * i : 9 * C * (i + 1)], preferred_element_type=F32
            )
        hidden[pl.ds(part * 4, 4)] = total.reshape(4, 12, 24, C)
        return carry

    lax.fori_loop(0, 3, convolve, 0)

    for x in range(6):
        value = hidden[2 * x : 2 * x + 2]
        active = value / (1.0 + jnp.exp(-value))
        active = active[0] + active[1]
        active = active.reshape(6, 2, 24, C)
        pairs[...] = active[:, 0] + active[:, 1]
        mean = (pairs[:, pl.ds(0, 12, 2)] + pairs[:, pl.ds(1, 12, 2)]) * 0.125
        starts = [4 * place[0] - 1 + x, 4 * place[1] - 1, 4 * place[2] - 3]
        keep = inside((1, 6, 12, C), starts, sizes)[0]
        pooled_ref[x, :, :12] = jnp.where(keep, mean, 0.0)
        pooled_ref[x, :, 12:] = jnp.zeros((6, 4, C), F32)

    cells = jnp.concatenate(
        [flat(pooled_ref[i : i + 4, j : j + 4, k : k + 8]) for i, j, k in taps()], axis=1
    )
    coarse = jnp.dot(cells, coarse_weights[...], preferred_element_type=F32)
    coarse_ref[...] = coarse
    grad_ref[...] = (incoming[...] * silu_slope(coarse)).astype(BF16)

    for x in range(10):
        hidden_ref[x] = hidden[1 + x, 1:11, 4:20]
        core_ref[x] = wide[2 + x, 2:12, 7:23]


def side_kernel(sizes, place, pooled, grad, hidden, sum_ref, slope_ref):
    at = lax.broadcasted_iota(jnp.int32, (C, C), 0) % 8
    mine = jnp.where((at >= 2) & (at < 6), grad[...].astype(F32), 0.0)
    turned = mine.T.astype(BF16)
    for i in range(3):
        cells = jnp.concatenate(
            [
                flat(pooled[i : i + 4, j : j + 4, k : k + 8])
                for j in range(3)
                for k in range(3)
            ],
            axis=1,
        )
        terms = jnp.dot(turned, cells, preferred_element_type=F32)
        for t in range(9):
            row = (9 * i + t) * C
            sum_ref[row : row + C] = terms[:, t * C : (t + 1) * C].T.astype(BF16)
    for x in range(10):
        starts = [8 * place[0] - 1 + x, 8 * place[1] - 1, 8 * place[2] - 2]
        keep = inside((1, 10, 16, C), starts, sizes)[0]
        slope_ref[x] = jnp.where(keep, silu_slope(hidden[x]) * 0.125, 0.0)


def back_kernel(around, coarse_weights, slope, core, sum_ref, grad_ref, wide, spread):
    for x in range(8):
        wide[x, :, :8] = around[64 * x : 64 * x + 64].astype(F32).reshape(8, 8, C)
    cells = jnp.concatenate(
        [flat(wide[2 - i : 8 - i, 2 - j : 8 - j, 2 - k : 10 - k]) for i, j, k in taps()], axis=1
    )
    turned = jnp.concatenate([coarse_weights[t] for t in range(27)], axis=1)
    back = lax.dot_general(cells, turned, (((1,), (1,)), ((), ())), preferred_element_type=F32)
    back = back.reshape(6, 6, 8, C)
    spread[:, :, pl.ds(0, 8, 2)] = back
    spread[:, :, pl.ds(1, 8, 2)] = back
    for x in range(10):
        for y in range(10):
            grad_ref[x, y] = spread[(x + 1) // 2, (y + 1) // 2] * slope[x, y]
    turned = grad_ref[1:9, 1:9, 2:10].reshape(512, C).T.astype(BF16)
    for i in range(3):
        cells = jnp.concatenate(
            [
                flat(core[i : i + 8, j : j + 8, k : k + 8])
                for j in range(3)
                for k in range(3)
            ],
            axis=1,
        )
        terms = jnp.dot(turned, cells, preferred_element_type=F32)
        for t in range(9):
            row = (9 * i + t) * C
            sum_ref[row : row + C] = terms[:, t * C : (t + 1) * C].T.astype(BF16)


def volume_kernel(grad, weights, out_ref):
    total = jnp.zeros((512, C), F32)
    for i in range(3):
        cells = jnp.concatenate(
            [
                flat(grad[2 - i : 10 - i, 2 - j : 10 - j, 3 - k : 11 - k])
                for j in range(3)
                for k in range(3)
            ],
            axis=1,
        )
        turned = jnp.concatenate([weights[9 * i + t] for t in range(9)], axis=1)
        total = total + lax.dot_general(
            cells, turned, (((1,), (1,)), ((), ())), preferred_element_type=F32
        )
    out_ref[...] = total.astype(BF16)


def call(kernel, outs, inputs, scratch=(), scalars=0, flops=0):
    in_specs = [
        pl.BlockSpec(memory_space=pltpu.SMEM if n < scalars else pltpu.VMEM)
        for n in range(len(inputs))
    ]
    moved = sum(a.size * a.dtype.itemsize for a in inputs)
    moved += sum(math.prod(s) * jnp.dtype(t).itemsize for s, t in outs)
    return pl.pallas_call(
        kernel,
        out_shape=[jax.ShapeDtypeStruct(s, t) for s, t in outs],
        in_specs=in_specs,
        out_specs=[pl.BlockSpec(memory_space=pltpu.VMEM) for _ in outs],
        scratch_shapes=[pltpu.VMEM(s, t) for s, t in scratch],
        compiler_params=pltpu.CompilerParams(vmem_limit_bytes=40 * 1024 * 1024),
        cost_estimate=pl.CostEstimate(flops=flops, bytes_accessed=moved, transcendentals=0),
    )(*inputs)


def line(count, step):
    return [(i, i + step) for i in range(count) if 0 <= i + step < count]


def beside(last, leading, axis, count):
    before = lax.ppermute(last, axis, line(count, 1))
    after = lax.ppermute(leading, axis, line(count, -1))
    return before, after


def spread_rows(terms, axes, peers):
    rows = terms.shape[0]
    parts = terms.astype(BF16).reshape(peers, rows // peers, C)
    got = lax.all_to_all(parts, axes, 0, 0, tiled=True)
    return jnp.sum(got.astype(F32), axis=0)


def gathered_rows(part, axes, peers):
    rows = part.shape[0]
    parts = jnp.broadcast_to(part[None], (peers, rows, C))
    return lax.all_to_all(parts, axes, 0, 0, tiled=True).reshape(peers * rows, C)


def totals(fine_sum, coarse_sum, fine_scale, coarse_scale, plane, along):
    first = lax.axis_index("core") == 0
    swap = [(0, 1), (1, 0)]
    mine = jnp.where(first, fine_sum, coarse_sum).astype(F32)
    other = jnp.where(first, coarse_sum, fine_sum)
    mine = mine + lax.ppermute(other, "core", swap).astype(F32)

    part = spread_rows(mine, PLANE, plane)
    length = part.shape[0]
    padded = -(-length // (16 * along)) * 16 * along
    part = jnp.pad(part, ((0, padded - length), (0, 0)))
    part = spread_rows(part, LINE, along) * jnp.where(first, fine_scale, coarse_scale)

    part = gathered_rows(part.astype(BF16), LINE, along)[:length]
    mine = gathered_rows(part, PLANE, plane)
    other = lax.ppermute(mine, "core", swap)
    return jnp.where(first, mine, other), jnp.where(first, other, mine)


def local(volume, fine_weight, coarse_weight, cotangent):
    sizes = {axis: lax.axis_size(axis) for axis in AXES}
    plane, along = (sizes["gx"] * sizes["y"], sizes["gy"] * sizes["zh"])
    peers = [sizes["gx"], sizes["gy"], sizes["y"] * sizes["zh"] * 2]
    place = [lax.axis_index("gx"), lax.axis_index("gy"), lax.axis_index(WIDTH)]
    place = jnp.stack([p.astype(jnp.int32) for p in place])
    fine_sizes = [8 * n for n in peers]
    coarse_sizes = [4 * n for n in peers]
    fine_rows = fine_weight.reshape(27 * C, C)
    coarse_rows = coarse_weight.reshape(27 * C, C)

    packed = jnp.concatenate([volume.reshape(512, C), cotangent.reshape(64, C)], axis=0)
    first = lax.axis_index("core") == 0
    near = [(i, i ^ 1) for i in range(peers[2])]
    far = [(i, i - 1 + 2 * (i % 2)) for i in range(1, peers[2] - 1)]
    inner = lax.ppermute(packed, WIDTH, near)
    outer = lax.ppermute(packed, WIDTH, far)
    before = jnp.where(first, outer, inner)
    after = jnp.where(first, inner, outer)
    own = jnp.concatenate(
        [before[:512].reshape(8, 8, 8, C), volume, after[:512].reshape(8, 8, 8, C)], axis=2
    )
    incoming = jnp.concatenate(
        [
            before[512:].reshape(4, 4, 4, C)[:, :, 2:],
            cotangent,
            after[512:].reshape(4, 4, 4, C)[:, :, :2],
        ],
        axis=2,
    ).astype(F32)
    below, above = beside(own[:, 5:], own[:, :3], "gy", peers[1])
    sides = [
        jnp.concatenate([below[at], own[at], above[at]], axis=1)
        for at in (slice(5, 8), slice(0, 3))
    ]
    left, right = beside(sides[0], sides[1], "gx", peers[0])

    coarse, coarse_grad, pooled, hidden, core = call(
        lambda *refs: front_kernel(coarse_sizes, *refs),
        [
            ((128, C), F32),
            ((128, C), BF16),
            ((6, 6, 16, C), F32),
            ((10, 10, 16, C), F32),
            ((10, 10, 16, C), F32),
        ],
        [
            place,
            own.reshape(8, 192, C),
            below.reshape(8, 72, C),
            above.reshape(8, 72, C),
            left.reshape(3, 336, C),
            right.reshape(3, 336, C),
            fine_rows,
            coarse_rows,
            incoming.reshape(128, C),
        ],
        scratch=[
            ((14, 14, 32, C), F32),
            ((14, 288, 9 * C), BF16),
            ((12, 12, 24, C), F32),
            ((6, 24, C), F32),
        ],
        scalars=1,
        flops=2 * 3600 * 27 * C * C,
    )
    coarse_out = jax.nn.silu(coarse.reshape(4, 4, 8, C)[:, :, 2:6]).astype(BF16)

    grads = coarse_grad.reshape(4, 4, 8, C)
    below, above = beside(grads[:, 2:], grads[:, :2], "gy", peers[1])
    grads = jnp.concatenate([below, grads, above], axis=1)
    left, right = beside(grads[2:], grads[:2], "gx", peers[0])
    around = jnp.concatenate([left, grads, right], axis=0)

    coarse_sum, slope = call(
        lambda *refs: side_kernel(fine_sizes, *refs),
        [((27 * C, C), BF16), ((10, 10, 16, C), F32)],
        [place, pooled, coarse_grad, hidden],
        scalars=1,
        flops=2 * 128 * 27 * C * C,
    )
    fine_sum, fine_grad = call(
        back_kernel,
        [((27 * C, C), BF16), ((10, 10, 16, C), F32)],
        [around.reshape(512, C), coarse_weight, slope, core],
        scratch=[((8, 8, 16, C), F32), ((6, 6, 16, C), F32)],
        flops=2 * 800 * 27 * C * C,
    )
    (grad_volume,) = call(
        volume_kernel, [((512, C), BF16)], [fine_grad, fine_weight], flops=2 * 512 * 27 * C * C
    )

    cells_fine = fine_sizes[0] * fine_sizes[1] * fine_sizes[2]
    fine_scale = 1.0 / math.sqrt(cells_fine)
    coarse_scale = 1.0 / math.sqrt(cells_fine // 8)
    fine_done, coarse_done = totals(
        fine_sum, coarse_sum, fine_scale, coarse_scale, plane, along
    )
    return (
        coarse_out,
        grad_volume.reshape(8, 8, 8, C),
        fine_done.reshape(27, C, C),
        coarse_done.reshape(27, C, C),
    )


def solution(mesh):
    shape = mesh.devices.shape
    inner = Mesh(mesh.devices.reshape(shape[0], shape[1], shape[2] // 4, 2, 2), AXES)
    cells = P("gx", "gy", WIDTH, None)
    return jax.shard_map(
        local,
        mesh=inner,
        in_specs=(cells, P(), P(), cells),
        out_specs=(cells, cells, P(), P()),
        check_vma=False,
    )
```

time: 234 us -> 175 us (0.75)
  local copies, waits for them, and re-layouts: 43.3 us -> 0.94 us
  matrix products: 19 us -> 0 us
  other arithmetic: 21.3 us -> 3.92 us
  Pallas kernels: 0 us -> 15.1 us
  starting transfers between devices: 61.5 us -> 69.8 us
  waiting for transfers between devices: 35.5 us -> 27.4 us
  blocking collectives: 51 us -> 56.3 us
    all_to_all x0 -> x2, blocking collectives: none -> 28.9 us  [gathered_rows(): lax.all_to_all(parts, axes, 0, 0, tiled=True).reshape(peers * rows, C)]
    all_to_all x2 -> x1, blocking collectives: 51 us -> 27.4 us  [spread_rows(): got = lax.all_to_all(parts, axes, 0, 0, tiled=True)]
    unnamed x79 -> x8, local copies, waits for them, and re-layouts: 16.6 us -> 0.02 us
    pallas_call x0 -> x4, Pallas kernels: none -> 15.1 us  [call(): pl.pallas_call(kernel, out_shape=[jax.ShapeDtypeStruct(s, t) for s, t in...]
    conv_general_dilated x4 -> x0, matrix products: 14.1 us -> none  [valid_conv(): lax.conv_general_dilated(x[None], kernel, (1, 1, 1), 'VALID', dimension_n...]
    all_to_all x2 -> x1, waiting for transfers between devices: 22.5 us -> 12.1 us  [spread_rows(): got = lax.all_to_all(parts, axes, 0, 0, tiled=True)]
    reshape x5 -> x0, local copies, waits for them, and re-layouts: 7.21 us -> none  [the longest x2 4.47 us: gather_taps(): return stacked.reshape(rows_x * rows_y * rows_z, stacked.shape[3])]
    all_to_all x2 -> x1, starting transfers between devices: 7.74 us -> 13.8 us  [spread_rows(): got = lax.all_to_all(parts, axes, 0, 0, tiled=True)]
  transfers between devices with their start and end apart: 14 -> 13, of which waited for: 8 -> 7; matrix products, arithmetic and copies ran while one was open for 8% -> 0% of each run, Pallas kernels for 0% -> 2%
where the time goes in v2:
time: 175 us; the launch traced here: 174 us
  starting transfers between devices  69.8 us (40%)
  blocking collectives  56.3 us (32%)
  waiting for transfers between devices  27.4 us (16%)
  Pallas kernels  15.1 us (9%)
  other arithmetic  3.92 us (2%)
    all_to_all x2, blocking collectives, gathered_rows(): lax.all_to_all(parts, axes, 0, 0, tiled=True).reshape(peers * rows, C)  28.9 us
    all_to_all x1, blocking collectives, spread_rows(): got = lax.all_to_all(parts, axes, 0, 0, tiled=True)  27.4 us
    ppermute x4, starting transfers between devices, beside(): before = lax.ppermute(last, axis, line(count, 1))  22.7 us
    ppermute x1, starting transfers between devices, local(): outer = lax.ppermute(packed, WIDTH, far)  16.8 us
    pallas_call x4, Pallas kernels, call(): pl.pallas_call(kernel, out_shape=[jax.ShapeDtypeStruct(s, t) for s, t in...  15.1 us
    all_to_all x1, starting transfers between devices, spread_rows(): got = lax.all_to_all(parts, axes, 0, 0, tiled=True)  13.8 us
    all_to_all x1, waiting for transfers between devices, spread_rows(): got = lax.all_to_all(parts, axes, 0, 0, tiled=True)  12.1 us
    ppermute x4, waiting for transfers between devices, beside(): after = lax.ppermute(leading, axis, line(count, -1))  8.35 us
  transfers between devices with their start and end apart: 13, of which 7 were waited for; matrix products, arithmetic and copies ran while one was open for 0% of the time, Pallas kernels for 2%

profile of v2, /device:TPU:1, one launch (start us, length us, event | category | flops | bytes accessed | tf_op | source)
XLA Modules:
  0.0 174.4 jit_solution(17616052564616515839)
XLA Ops:
  1.6 16.8 %collective-permute-start = (bf16[576,128]{1,0:T(8,128)(2,1)S(1)}, bf16[576,128]{1,0:T(8,128)(2,1)S(1)}, u32[]{:S(2)}, u32[]{:S(2)}) collective-permute-start(bf16[576,128]{1,0:T(8,128)(2,1)S(1)} %pad_maximum_fusion.3), channel_id=1, source_target_pairs={{1,2},{2,1},{3,4},{4,3},{5,6},{6,5},{7,8},{8,7},{9,10},{10,9},{11,... | collective-permute-start | bytes 442376 | tf_op jit(solution)/shard_map/ppermute | solution.py:247
  18.5 1.9 %collective-permute-start.1 = (bf16[576,128]{1,0:T(8,128)(2,1)S(1)}, bf16[576,128]{1,0:T(8,128)(2,1)S(1)}, u32[]{:S(2)}, u32[]{:S(2)}) collective-permute-start(bf16[576,128]{1,0:T(8,128)(2,1)S(1)} %pad_maximum_fusion.3), channel_id=1, source_target_pairs={{0,1},{1,0},{2,3},{3,2},{4,5},{5,4},{6,7},{7,6},{8,9},{9,8},{10,11... | collective-permute-start | bytes 442376 | tf_op jit(solution)/shard_map/ppermute | solution.py:246
  20.5 1.8 %collective-permute-done = bf16[576,128]{1,0:T(8,128)(2,1)S(1)} collective-permute-done((bf16[576,128]{1,0:T(8,128)(2,1)S(1)}, bf16[576,128]{1,0:T(8,128)(2,1)S(1)}, u32[]{:S(2)}, u32[]{:S(2)}) %collective-permute-start) | collective-permute-done | bytes 147488 | tf_op jit(solution)/shard_map/ppermute | solution.py:247
  22.5 11.5 %collective-permute-start.2 = (bf16[8,3,24,128]{3,2,1,0:T(8,128)(2,1)S(1)}, bf16[8,3,24,128]{3,2,1,0:T(8,128)(2,1)S(1)}, u32[]{:S(2)}, u32[]{:S(2)}) collective-permute-start(bf16[8,3,24,128]{3,2,1,0:T(8,128)(2,1)S(1)} %get-tuple-element.27), channel_id=1, source_target_pairs={{0,16},{16,32},{32,48},{48,64},{64,80},{80,96},{96,112},{1,17},{17... | collective-permute-start | bytes 442376 | tf_op jit(solution)/shard_map/ppermute | solution.py:194
  34.0 1.3 collective-permute-start.3
  35.4 4.5 %collective-permute-done.3 = bf16[8,3,24,128]{3,2,1,0:T(8,128)(2,1)S(1)} collective-permute-done((bf16[8,3,24,128]{3,2,1,0:T(8,128)(2,1)S(1)}, bf16[8,3,24,128]{3,2,1,0:T(8,128)(2,1)S(1)}, u32[]{:S(2)}, u32[]{:S(2)}) %collective-permute-start.3) | collective-permute-done | bytes 147488 | tf_op jit(solution)/shard_map/ppermute | solution.py:195
  40.0 3.2 %collective-permute-start.4 = (bf16[3,14,24,128]{3,2,1,0:T(8,128)(2,1)S(1)}, bf16[3,14,24,128]{3,2,1,0:T(8,128)(2,1)S(1)}, u32[]{:S(2)}, u32[]{:S(2)}) collective-permute-start(bf16[3,14,24,128]{3,2,1,0:T(8,128)(2,1)S(1)} %pad_maximum_fusion.1), channel_id=1, source_target_pairs={{0,128},{128,256},{256,384},{1,129},{129,257},{257,385},{2,130},{1... | collective-permute-start | bytes 774152 | tf_op jit(solution)/shard_map/ppermute | solution.py:194
  44.6 1.8 %collective-permute-done.4 = bf16[3,14,24,128]{3,2,1,0:T(8,128)(2,1)S(1)} collective-permute-done((bf16[3,14,24,128]{3,2,1,0:T(8,128)(2,1)S(1)}, bf16[3,14,24,128]{3,2,1,0:T(8,128)(2,1)S(1)}, u32[]{:S(2)}, u32[]{:S(2)}) %collective-permute-start.4) | collective-permute-done | bytes 258080 | tf_op jit(solution)/shard_map/ppermute | solution.py:194
  46.5 3.9 %collective-permute-done.5 = bf16[3,14,24,128]{3,2,1,0:T(8,128)(2,1)S(1)} collective-permute-done((bf16[3,14,24,128]{3,2,1,0:T(8,128)(2,1)S(1)}, bf16[3,14,24,128]{3,2,1,0:T(8,128)(2,1)S(1)}, u32[]{:S(2)}, u32[]{:S(2)}) %collective-permute-start.5) | collective-permute-done | bytes 258080 | tf_op jit(solution)/shard_map/ppermute | solution.py:195
  50.3 9.5 %shard_map.75 = (f32[128,128]{1,0:T(8,128)S(1)}, bf16[128,128]{1,0:T(8,128)(2,1)S(1)}, f32[6,6,16,128]{3,2,1,0:T(8,128)S(1)}, f32[10,10,16,128]{3,2,1,0:T(8,128)S(1)}, f32[10,10,16,128]{3,2,1,0:T(8,128)S(1)}) custom-call(s32[3]{0:T(128)S(1)} %pad_add_fusion.refs_0_, bf16[8,192,128]{2,1,0:T(8,128)(2,1)S(1)} %bitcast.31, bf16[8,72,128]{2,1,0:T(8,128)(2,1)S(1)} %bitcast.38, ...), custom_call_target="tpu_custom_call" | custom-call | flops 3185049600 | bytes 5070860 | tf_op jit(solution)/shard_map/pallas_call | solution.py:178
  61.1 4.0 %collective-permute-start.6 = (bf16[4,2,8,128]{3,2,1,0:T(8,128)(2,1)S(1)}, bf16[4,2,8,128]{3,2,1,0:T(8,128)(2,1)S(1)}, u32[]{:S(2)}, u32[]{:S(2)}) collective-permute-start(bf16[4,2,8,128]{3,2,1,0:T(8,128)(2,1)S(1)} %get-tuple-element.36), channel_id=1, source_target_pairs={{0,16},{16,32},{32,48},{48,64},{64,80},{80,96},{96,112},{1,17},{17... | collective-permute-start | bytes 49160 | tf_op jit(solution)/shard_map/ppermute | solution.py:194
  67.3 4.0 %collective-permute-start.8 = (bf16[2,8,8,128]{3,2,1,0:T(8,128)(2,1)S(1)}, bf16[2,8,8,128]{3,2,1,0:T(8,128)(2,1)S(1)}, u32[]{:S(2)}, u32[]{:S(2)}) collective-permute-start(bf16[2,8,8,128]{3,2,1,0:T(8,128)(2,1)S(1)} %get-tuple-element.34), channel_id=1, source_target_pairs={{0,128},{128,256},{256,384},{1,129},{129,257},{257,385},{2,130},{1... | collective-permute-start | bytes 98312 | tf_op jit(solution)/shard_map/ppermute | solution.py:194
  71.3 1.4 shard_map.76
  72.8 2.4 %shard_map.77 = (bf16[3456,128]{1,0:T(8,128)(2,1)S(1)}, f32[10,10,16,128]{3,2,1,0:T(8,128)S(1)}) custom-call(bf16[512,128]{1,0:T(8,128)(2,1)S(1)} %bitcast.37, bf16[27,128,128]{2,1,0:T(8,128)(2,1)S(1)} %copy-done.1, f32[10,10,16,128]{3,2,1,0:T(8,128)S(1)} %get-tuple-element.17.slope, f32[10,10,16,128]{3,2,1,0:T(8,128)S(1)} %get-tuple-element.18.core), custom_call_target="tpu_custom_call" | custom-call | flops 707788800 | bytes 4358144 | tf_op jit(solution)/shard_map/pallas_call | solution.py:178
  75.3 1.9 %collective-permute-start.10 = (bf16[3456,128]{1,0:T(8,128)(2,1)S(1)}, bf16[3456,128]{1,0:T(8,128)(2,1)S(1)}, u32[]{:S(2)}, u32[]{:S(2)}) collective-permute-start(bf16[3456,128]{1,0:T(8,128)(2,1)S(1)} %broadcast_select_fusion.2), channel_id=1, source_target_pairs={{0,1},{1,0},{2,3},{3,2},{4,5},{5,4},{6,7},{7,6},{8,9},{9,8},{10,11... | collective-permute-start | bytes 2654216 | tf_op jit(solution)/shard_map/ppermute | solution.py:217
  77.3 2.4 %collective-permute-done.10 = bf16[3456,128]{1,0:T(8,128)(2,1)S(1)} collective-permute-done((bf16[3456,128]{1,0:T(8,128)(2,1)S(1)}, bf16[3456,128]{1,0:T(8,128)(2,1)S(1)}, u32[]{:S(2)}, u32[]{:S(2)}) %collective-permute-start.10) | collective-permute-done | bytes 884768 | tf_op jit(solution)/shard_map/ppermute | solution.py:217
  80.0 27.4 %all_to_all.20 = bf16[16,216,128]{2,1,0:T(8,128)(2,1)S(1)} all-to-all(bf16[16,216,128]{2,1,0:T(8,128)(2,1)S(1)} %bitcast.44), channel_id=1, replica_groups=mesh['gx'=4,'gy'=8,'y'=4,'zh'=2,'core'=2] {'gx','y'}, dimensions={0} | all-to-all | bytes 1769472 | tf_op jit(solution)/shard_map/all_to_all | solution.py:202
  108.2 13.8 %all-to-all-start.1 = ((bf16[16,16,128]{2,1,0:T(8,128)(2,1)}), bf16[16,16,128]{2,1,0:T(8,128)(2,1)S(1)}, u32[]{:S(2)}, u32[]{:S(2)}) async-start(bf16[16,16,128]{2,1,0:T(8,128)(2,1)} %bitcast.22), calls=%async_computation.1 | async-start | bytes 131072 | tf_op jit(solution)/shard_map/all_to_all | solution.py:202
  122.0 12.1 %all-to-all-done.1 = bf16[16,16,128]{2,1,0:T(8,128)(2,1)S(1)} async-done(((bf16[16,16,128]{2,1,0:T(8,128)(2,1)}), bf16[16,16,128]{2,1,0:T(8,128)(2,1)S(1)}, u32[]{:S(2)}, u32[]{:S(2)}) %all-to-all-start.1) | async-done | bytes 65568 | tf_op jit(solution)/shard_map/all_to_all | solution.py:202
  134.2 14.2 %all_to_all.21 = bf16[16,16,128]{2,1,0:T(8,128)(2,1)S(1)} all-to-all(bf16[16,16,128]{2,1,0:T(8,128)(2,1)S(1)} %broadcast_in_dim.4), channel_id=1, replica_groups=mesh['gx'=4,'gy'=8,'y'=4,'zh'=2,'core'=2] {'gy','zh'}, dimensions={0} | all-to-all | bytes 131072 | tf_op jit(solution)/shard_map/all_to_all | solution.py:209
  148.5 14.7 %all_to_all.22 = bf16[16,216,128]{2,1,0:T(8,128)(2,1)S(1)} all-to-all(bf16[16,216,128]{2,1,0:T(8,128)(2,1)S(1)} %broadcast_in_dim.5), channel_id=1, replica_groups=mesh['gx'=4,'gy'=8,'y'=4,'zh'=2,'core'=2] {'gx','y'}, dimensions={0} | all-to-all | bytes 1769472 | tf_op jit(solution)/shard_map/all_to_all | solution.py:209
  163.2 7.5 %collective-permute-start.11 = (bf16[3456,128]{1,0:T(8,128)(2,1)S(1)}, bf16[3456,128]{1,0:T(8,128)(2,1)S(1)}, u32[]{:S(2)}, u32[]{:S(2)}) collective-permute-start(bf16[3456,128]{1,0:T(8,128)(2,1)S(1)} %bitcast.43), channel_id=1, source_target_pairs={{0,1},{1,0},{2,3},{3,2},{4,5},{5,4},{6,7},{7,6},{8,9},{9,8},{10,11... | collective-permute-start | bytes 2654216 | tf_op jit(solution)/shard_map/ppermute | solution.py:227
  171.3 1.7 shard_map.78
  173.0 1.4 broadcast_select_fusion
  (50 shorter events, 8.2 us)
Async XLA Ops:
  0.6 21.8 %copy-start.2 = (bf16[8,8,8,128]{3,2,1,0:T(8,128)(2,1)S(1)}, bf16[8,8,8,128]{3,2,1,0:T(8,128)(2,1)}, u32[]{:S(2)}) copy-start(bf16[8,8,8,128]{3,2,1,0:T(8,128)(2,1)} %param.4) | copy-start | bytes 393220
  1.6 20.7 %collective-permute-start = (bf16[576,128]{1,0:T(8,128)(2,1)S(1)}, bf16[576,128]{1,0:T(8,128)(2,1)S(1)}, u32[]{:S(2)}, u32[]{:S(2)}) collective-permute-start(bf16[576,128]{1,0:T(8,128)(2,1)S(1)} %pad_maximum_fusion.3), channel_id=1, source_target_pairs={{1,2},{2,1},{3,4},{4,3},{5,6},{6,5},{7,8},{8,7},{9,10},{10,9},{11,... | collective-permute-start | bytes 442376 | tf_op jit(solution)/shard_map/ppermute | solution.py:247
  18.5 3.8 %collective-permute-start.1 = (bf16[576,128]{1,0:T(8,128)(2,1)S(1)}, bf16[576,128]{1,0:T(8,128)(2,1)S(1)}, u32[]{:S(2)}, u32[]{:S(2)}) collective-permute-start(bf16[576,128]{1,0:T(8,128)(2,1)S(1)} %pad_maximum_fusion.3), channel_id=1, source_target_pairs={{0,1},{1,0},{2,3},{3,2},{4,5},{5,4},{6,7},{7,6},{8,9},{9,8},{10,11... | collective-permute-start | bytes 442376 | tf_op jit(solution)/shard_map/ppermute | solution.py:246
  22.5 17.4 %collective-permute-start.2 = (bf16[8,3,24,128]{3,2,1,0:T(8,128)(2,1)S(1)}, bf16[8,3,24,128]{3,2,1,0:T(8,128)(2,1)S(1)}, u32[]{:S(2)}, u32[]{:S(2)}) collective-permute-start(bf16[8,3,24,128]{3,2,1,0:T(8,128)(2,1)S(1)} %get-tuple-element.27), channel_id=1, source_target_pairs={{0,16},{16,32},{32,48},{48,64},{64,80},{80,96},{96,112},{1,17},{17... | collective-permute-start | bytes 442376 | tf_op jit(solution)/shard_map/ppermute | solution.py:194
  34.0 5.9 %collective-permute-start.3 = (bf16[8,3,24,128]{3,2,1,0:T(8,128)(2,1)S(1)}, bf16[8,3,24,128]{3,2,1,0:T(8,128)(2,1)S(1)}, u32[]{:S(2)}, u32[]{:S(2)}) collective-permute-start(bf16[8,3,24,128]{3,2,1,0:T(8,128)(2,1)S(1)} %get-tuple-element.26), channel_id=1, source_target_pairs={{16,0},{32,16},{48,32},{64,48},{80,64},{96,80},{112,96},{17,1},{33... | collective-permute-start | bytes 442376 | tf_op jit(solution)/shard_map/ppermute | solution.py:195
  35.4 15.0 %copy-start.1 = (bf16[27,128,128]{2,1,0:T(8,128)(2,1)S(1)}, bf16[27,128,128]{2,1,0:T(8,128)(2,1)}, u32[]{:S(2)}) copy-start(bf16[27,128,128]{2,1,0:T(8,128)(2,1)} %coarse_weights.1) | copy-start | bytes 2654212
  35.4 9.1 %copy-start.3 = (bf16[4,4,4,128]{3,2,1,0:T(4,128)(2,1)S(1)}, bf16[4,4,4,128]{3,2,1,0:T(4,128)(2,1)}, u32[]{:S(2)}) copy-start(bf16[4,4,4,128]{3,2,1,0:T(4,128)(2,1)} %param.7) | copy-start | bytes 49156
  35.4 14.9 %copy-start = (bf16[27,128,128]{2,1,0:T(8,128)(2,1)S(1)}, bf16[27,128,128]{2,1,0:T(8,128)(2,1)}, u32[]{:S(2)}) copy-start(bf16[27,128,128]{2,1,0:T(8,128)(2,1)} %weights.1) | copy-start | bytes 2654212
  40.0 6.4 %collective-permute-start.4 = (bf16[3,14,24,128]{3,2,1,0:T(8,128)(2,1)S(1)}, bf16[3,14,24,128]{3,2,1,0:T(8,128)(2,1)S(1)}, u32[]{:S(2)}, u32[]{:S(2)}) collective-permute-start(bf16[3,14,24,128]{3,2,1,0:T(8,128)(2,1)S(1)} %pad_maximum_fusion.1), channel_id=1, source_target_pairs={{0,128},{128,256},{256,384},{1,129},{129,257},{257,385},{2,130},{1... | collective-permute-start | bytes 774152 | tf_op jit(solution)/shard_map/ppermute | solution.py:194
  43.3 7.1 %collective-permute-start.5 = (bf16[3,14,24,128]{3,2,1,0:T(8,128)(2,1)S(1)}, bf16[3,14,24,128]{3,2,1,0:T(8,128)(2,1)S(1)}, u32[]{:S(2)}, u32[]{:S(2)}) collective-permute-start(bf16[3,14,24,128]{3,2,1,0:T(8,128)(2,1)S(1)} %pad_maximum_fusion.2), channel_id=1, source_target_pairs={{128,0},{256,128},{384,256},{129,1},{257,129},{385,257},{130,2},{2... | collective-permute-start | bytes 774152 | tf_op jit(solution)/shard_map/ppermute | solution.py:195
  59.8 5.3 %collective-permute-start.7 = (bf16[4,2,8,128]{3,2,1,0:T(8,128)(2,1)S(1)}, bf16[4,2,8,128]{3,2,1,0:T(8,128)(2,1)S(1)}, u32[]{:S(2)}, u32[]{:S(2)}) collective-permute-start(bf16[4,2,8,128]{3,2,1,0:T(8,128)(2,1)S(1)} %get-tuple-element.37), channel_id=1, source_target_pairs={{16,0},{32,16},{48,32},{64,48},{80,64},{96,80},{112,96},{17,1},{33... | collective-permute-start | bytes 49160 | tf_op jit(solution)/shard_map/ppermute | solution.py:195
  61.1 4.8 %collective-permute-start.6 = (bf16[4,2,8,128]{3,2,1,0:T(8,128)(2,1)S(1)}, bf16[4,2,8,128]{3,2,1,0:T(8,128)(2,1)S(1)}, u32[]{:S(2)}, u32[]{:S(2)}) collective-permute-start(bf16[4,2,8,128]{3,2,1,0:T(8,128)(2,1)S(1)} %get-tuple-element.36), channel_id=1, source_target_pairs={{0,16},{16,32},{32,48},{48,64},{64,80},{80,96},{96,112},{1,17},{17... | collective-permute-start | bytes 49160 | tf_op jit(solution)/shard_map/ppermute | solution.py:194
  66.0 6.7 %collective-permute-start.9 = (bf16[2,8,8,128]{3,2,1,0:T(8,128)(2,1)S(1)}, bf16[2,8,8,128]{3,2,1,0:T(8,128)(2,1)S(1)}, u32[]{:S(2)}, u32[]{:S(2)}) collective-permute-start(bf16[2,8,8,128]{3,2,1,0:T(8,128)(2,1)S(1)} %get-tuple-element.35), channel_id=1, source_target_pairs={{128,0},{256,128},{384,256},{129,1},{257,129},{385,257},{130,2},{2... | collective-permute-start | bytes 98312 | tf_op jit(solution)/shard_map/ppermute | solution.py:195
  67.3 5.5 %collective-permute-start.8 = (bf16[2,8,8,128]{3,2,1,0:T(8,128)(2,1)S(1)}, bf16[2,8,8,128]{3,2,1,0:T(8,128)(2,1)S(1)}, u32[]{:S(2)}, u32[]{:S(2)}) collective-permute-start(bf16[2,8,8,128]{3,2,1,0:T(8,128)(2,1)S(1)} %get-tuple-element.34), channel_id=1, source_target_pairs={{0,128},{128,256},{256,384},{1,129},{129,257},{257,385},{2,130},{1... | collective-permute-start | bytes 98312 | tf_op jit(solution)/shard_map/ppermute | solution.py:194
  75.3 4.3 %collective-permute-start.10 = (bf16[3456,128]{1,0:T(8,128)(2,1)S(1)}, bf16[3456,128]{1,0:T(8,128)(2,1)S(1)}, u32[]{:S(2)}, u32[]{:S(2)}) collective-permute-start(bf16[3456,128]{1,0:T(8,128)(2,1)S(1)} %broadcast_select_fusion.2), channel_id=1, source_target_pairs={{0,1},{1,0},{2,3},{3,2},{4,5},{5,4},{6,7},{7,6},{8,9},{9,8},{10,11... | collective-permute-start | bytes 2654216 | tf_op jit(solution)/shard_map/ppermute | solution.py:217
  108.2 25.9 %all-to-all-start.1 = ((bf16[16,16,128]{2,1,0:T(8,128)(2,1)}), bf16[16,16,128]{2,1,0:T(8,128)(2,1)S(1)}, u32[]{:S(2)}, u32[]{:S(2)}) async-start(bf16[16,16,128]{2,1,0:T(8,128)(2,1)} %bitcast.22), calls=%async_computation.1 | async-start | bytes 131072 | tf_op jit(solution)/shard_map/all_to_all | solution.py:202
  163.2 9.9 %collective-permute-start.11 = (bf16[3456,128]{1,0:T(8,128)(2,1)S(1)}, bf16[3456,128]{1,0:T(8,128)(2,1)S(1)}, u32[]{:S(2)}, u32[]{:S(2)}) collective-permute-start(bf16[3456,128]{1,0:T(8,128)(2,1)S(1)} %bitcast.43), channel_id=1, source_target_pairs={{0,1},{1,0},{2,3},{3,2},{4,5},{5,4},{6,7},{7,6},{8,9},{9,8},{10,11... | collective-permute-start | bytes 2654216 | tf_op jit(solution)/shard_map/ppermute | solution.py:227

commit v3 on v2

v3 whole, which is shorter than its diff:
```python
import math

import jax
import jax.numpy as jnp
from jax import lax
from jax.experimental import pallas as pl
from jax.experimental.pallas import tpu as pltpu
from jax.sharding import Mesh, PartitionSpec as P

AXES = ("gx", "gy", "y", "zh", "core")
WIDTH = ("y", "zh", "core")
PLANE = ("gx", "y")
LINE = ("gy", "zh")
C = 128
F32 = jnp.float32
BF16 = jnp.bfloat16


def silu_slope(values):
    sigma = 1.0 / (1.0 + jnp.exp(-values))
    return sigma * (1.0 + values * (1.0 - sigma))


def inside(shape, starts, sizes):
    keep = None
    for dim in range(3):
        at = starts[dim] + lax.broadcasted_iota(jnp.int32, shape, dim)
        ok = (at >= 0) & (at < sizes[dim])
        keep = ok if keep is None else keep & ok
    return keep


def taps():
    return [(i, j, k) for i in range(3) for j in range(3) for k in range(3)]


def flat(values):
    return values.reshape(-1, C).astype(BF16)


def weight_terms(turned, cells, sum_ref, at):
    terms = jnp.dot(turned, cells, preferred_element_type=F32)
    for t in range(9):
        row = (at + t) * C
        sum_ref[row : row + C] = terms[:, t * C : (t + 1) * C].T.astype(BF16)


def back_conv(grads, weights):
    cells = jnp.concatenate(
        [flat(grads[2 - i : 8 - i, 2 - j : 8 - j, 2 - k : 10 - k]) for i, j, k in taps()], axis=1
    )
    turned = jnp.concatenate([weights[t] for t in range(27)], axis=1)
    back = lax.dot_general(cells, turned, (((1,), (1,)), ((), ())), preferred_element_type=F32)
    return back.reshape(6, 6, 8, C)


def front_kernel(
    fine_sizes, coarse_sizes, place, own, below, above, left, right, weights, coarse_weights, incoming,
    coarse_ref, grad_ref, slope_ref, fine_ref, coarse_sum_ref,
    wide, patches, hidden, pairs, pooled, grads, spread, shares,
):
    wide[:, :, 16:] = jnp.zeros((14, 14, 8, C), F32)
    for x in range(8):
        wide[3 + x, 3:11, :16] = own[x].astype(F32).reshape(8, 16, C)
        wide[3 + x, :3, :16] = below[x].astype(F32).reshape(3, 16, C)
        wide[3 + x, 11:, :16] = above[x].astype(F32).reshape(3, 16, C)
    for x in range(3):
        wide[x, :, :16] = left[x].astype(F32).reshape(14, 16, C)
        wide[11 + x, :, :16] = right[x].astype(F32).reshape(14, 16, C)

    def gather(x, carry):
        for k in range(3):
            line = wide[x, :, k + 1 : k + 17]
            for j in range(3):
                at = (3 * j + k) * C
                patches[x, :, at : at + C] = flat(line[j : j + 12])
        return carry

    lax.fori_loop(0, 14, gather, 0)

    def convolve(part, carry):
        total = jnp.zeros((768, C), F32)
        for i in range(3):
            cells = patches[pl.ds(part * 4 + i, 4)].reshape(768, 9 * C)
            total = total + jnp.dot(
                cells, weights[9 * C * i : 9 * C * (i + 1)], preferred_element_type=F32
            )
        hidden[pl.ds(part * 4, 4)] = total.reshape(4, 12, 16, C)
        return carry

    lax.fori_loop(0, 3, convolve, 0)

    used = lax.broadcasted_iota(jnp.int32, (1, 12, 16, C), 2) < 12
    for x in range(6):
        active = None
        for half in range(2):
            value = hidden[2 * x + half]
            sigma = 1.0 / (1.0 + jnp.exp(-value))
            slope = sigma * (1.0 + value * (1.0 - sigma)) * 0.125
            starts = [8 * place[0] - 2 + 2 * x + half, 8 * place[1] - 2, 8 * place[2] - 2]
            keep = (inside((1, 12, 16, C), starts, fine_sizes) & used)[0]
            slope_ref[2 * x + half] = jnp.where(keep, slope, 0.0)
            value = value * sigma
            active = value if active is None else active + value
        active = active.reshape(6, 2, 16, C)
        pairs[...] = active[:, 0] + active[:, 1]
        mean = (pairs[:, pl.ds(0, 8, 2)] + pairs[:, pl.ds(1, 8, 2)]) * 0.125
        starts = [4 * place[0] - 1 + x, 4 * place[1] - 1, 4 * place[2] - 1]
        keep = inside((1, 6, 8, C), starts, coarse_sizes)[0]
        pooled[x, :, :8] = jnp.where(keep, mean, 0.0)
        pooled[x, :, 8:] = jnp.zeros((6, 8, C), F32)

    cells = [flat(pooled[i : i + 4, j : j + 4, k : k + 8]) for i, j, k in taps()]
    coarse = jnp.dot(
        jnp.concatenate(cells, axis=1), coarse_weights[...].reshape(27 * C, C), preferred_element_type=F32
    )
    coarse_ref[...] = coarse
    grad = (incoming[...] * silu_slope(coarse)).astype(BF16)
    grad_ref[...] = grad
    grad = grad.astype(F32)

    grads[...] = jnp.zeros((8, 8, 16, C), F32)
    grads[2:6, 2:6, 2:10] = grad.reshape(4, 4, 8, C)
    back = back_conv(grads, coarse_weights)
    spread[:, :, pl.ds(0, 8, 2)] = back
    spread[:, :, pl.ds(1, 8, 2)] = back
    for x in range(12):
        for y in range(12):
            shares[x, y] = spread[x // 2, y // 2] * slope_ref[x, y]
    turned = shares[...].reshape(2304, C).T.astype(BF16)
    for i in range(3):
        weight_terms(turned, patches[i : i + 12].reshape(2304, 9 * C), fine_ref, 9 * i)
    turned = grad.T.astype(BF16)
    for i in range(3):
        weight_terms(
            turned, jnp.concatenate(cells[9 * i : 9 * i + 9], axis=1), coarse_sum_ref, 9 * i
        )


def volume_kernel(around, coarse_weights, slope, weights, out_ref, grads, spread, fine):
    for x in range(8):
        grads[x, :, :8] = around[64 * x : 64 * x + 64].astype(F32).reshape(8, 8, C)
    back = back_conv(grads, coarse_weights)
    spread[:, :, pl.ds(0, 8, 2)] = back
    spread[:, :, pl.ds(1, 8, 2)] = back
    for x in range(10):
        for y in range(10):
            fine[x, y] = spread[(x + 1) // 2, (y + 1) // 2] * slope[x + 1, y + 1]
    total = jnp.zeros((512, C), F32)
    for i in range(3):
        cells = jnp.concatenate(
            [
                flat(fine[2 - i : 10 - i, 2 - j : 10 - j, 3 - k : 11 - k])
                for j in range(3)
                for k in range(3)
            ],
            axis=1,
        )
        turned = jnp.concatenate([weights[9 * i + t] for t in range(9)], axis=1)
        total = total + lax.dot_general(
            cells, turned, (((1,), (1,)), ((), ())), preferred_element_type=F32
        )
    out_ref[...] = total.astype(BF16)


def call(kernel, outs, inputs, scratch=(), scalars=0, flops=0):
    in_specs = [
        pl.BlockSpec(memory_space=pltpu.SMEM if n < scalars else pltpu.VMEM)
        for n in range(len(inputs))
    ]
    moved = sum(a.size * a.dtype.itemsize for a in inputs)
    moved += sum(math.prod(s) * jnp.dtype(t).itemsize for s, t in outs)
    return pl.pallas_call(
        kernel,
        out_shape=[jax.ShapeDtypeStruct(s, t) for s, t in outs],
        in_specs=in_specs,
        out_specs=[pl.BlockSpec(memory_space=pltpu.VMEM) for _ in outs],
        scratch_shapes=[pltpu.VMEM(s, t) for s, t in scratch],
        compiler_params=pltpu.CompilerParams(vmem_limit_bytes=40 * 1024 * 1024),
        cost_estimate=pl.CostEstimate(flops=flops, bytes_accessed=moved, transcendentals=0),
    )(*inputs)


def line(count, step):
    return [(i, i + step) for i in range(count) if 0 <= i + step < count]


def beside(last, leading, axis, count):
    before = lax.ppermute(last, axis, line(count, 1))
    after = lax.ppermute(leading, axis, line(count, -1))
    return before, after


def along_width(x, count):
    outer = lax.ppermute(x, WIDTH, [(i, i - 1 + 2 * (i % 2)) for i in range(1, count - 1)])
    inner = lax.ppermute(x, WIDTH, [(i, i ^ 1) for i in range(count)])
    return outer, inner


def in_order(outer, inner):
    first = lax.axis_index("core") == 0
    return jnp.where(first, outer, inner), jnp.where(first, inner, outer)


def spread_rows(terms, axes, peers):
    rows = terms.shape[0]
    parts = terms.astype(BF16).reshape(peers, rows // peers, C)
    return lax.all_to_all(parts, axes, 0, 0, tiled=True)


def gathered_rows(part, axes, peers):
    rows = part.shape[0]
    parts = jnp.broadcast_to(part[None], (peers, rows, C))
    return lax.all_to_all(parts, axes, 0, 0, tiled=True)


def summed(parts):
    return jnp.sum(parts.astype(F32), axis=0)


def joined(parts):
    return parts.reshape(-1, C)


def local(volume, fine_weight, coarse_weight, cotangent):
    sizes = {axis: lax.axis_size(axis) for axis in AXES}
    plane, along = (sizes["gx"] * sizes["y"], sizes["gy"] * sizes["zh"])
    peers = [sizes["gx"], sizes["gy"], sizes["y"] * sizes["zh"] * 2]
    place = [lax.axis_index("gx"), lax.axis_index("gy"), lax.axis_index(WIDTH)]
    place = jnp.stack([p.astype(jnp.int32) for p in place])
    fine_sizes = [8 * n for n in peers]
    coarse_sizes = [4 * n for n in peers]

    before, after = in_order(*along_width(volume, peers[2]))
    own = jnp.concatenate([before[:, :, 4:], volume, after[:, :, :4]], axis=2)
    below, above = beside(own[:, 5:], own[:, :3], "gy", peers[1])
    sides = [
        jnp.concatenate([below[at], own[at], above[at]], axis=1)
        for at in (slice(5, 8), slice(0, 3))
    ]
    left, right = beside(sides[0], sides[1], "gx", peers[0])
    incoming = jnp.pad(cotangent.astype(F32), ((0, 0), (0, 0), (0, 4), (0, 0)))

    coarse, coarse_grad, slope, fine_sum, coarse_sum = call(
        lambda *refs: front_kernel(fine_sizes, coarse_sizes, *refs),
        [
            ((128, C), F32),
            ((128, C), BF16),
            ((12, 12, 16, C), F32),
            ((27 * C, C), BF16),
            ((27 * C, C), BF16),
        ],
        [
            place,
            own.reshape(8, 128, C),
            below.reshape(8, 48, C),
            above.reshape(8, 48, C),
            left.reshape(3, 224, C),
            right.reshape(3, 224, C),
            fine_weight.reshape(27 * C, C),
            coarse_weight,
            incoming.reshape(128, C),
        ],
        scratch=[
            ((14, 14, 24, C), F32),
            ((14, 192, 9 * C), BF16),
            ((12, 12, 16, C), F32),
            ((6, 16, C), F32),
            ((6, 6, 16, C), F32),
            ((8, 8, 16, C), F32),
            ((6, 6, 16, C), F32),
            ((12, 12, 16, C), F32),
        ],
        scalars=1,
        flops=2 * 5000 * 27 * C * C,
    )
    coarse_out = jax.nn.silu(coarse.reshape(4, 4, 8, C)[:, :, :4]).astype(BF16)

    first = lax.axis_index("core") == 0
    swap = [(0, 1), (1, 0)]
    cells_fine = fine_sizes[0] * fine_sizes[1] * fine_sizes[2]
    scale = jnp.where(first, 1.0 / math.sqrt(cells_fine), 1.0 / math.sqrt(cells_fine // 8))
    grads = coarse_grad.reshape(4, 4, 8, C)[:, :, :4]
    mine = jnp.where(first, fine_sum, coarse_sum).astype(F32)
    other = jnp.where(first, coarse_sum, fine_sum)
    mine = mine + lax.ppermute(other, "core", swap).astype(F32)

    halo = along_width(grads, peers[2])
    parts = spread_rows(mine, PLANE, plane)
    parts, halo = lax.optimization_barrier((parts, halo))
    part = summed(parts)
    length = part.shape[0]
    padded = -(-length // (16 * along)) * 16 * along
    part = jnp.pad(part, ((0, padded - length), (0, 0)))
    before, after = in_order(*halo)
    grads = jnp.concatenate([before[:, :, 2:], grads, after[:, :, :2]], axis=2)

    halo = beside(grads[:, 2:], grads[:, :2], "gy", peers[1])
    parts = spread_rows(part, LINE, along)
    parts, halo = lax.optimization_barrier((parts, halo))
    part = (summed(parts) * scale).astype(BF16)
    grads = jnp.concatenate([halo[0], grads, halo[1]], axis=1)

    halo = beside(grads[2:], grads[:2], "gx", peers[0])
    parts = gathered_rows(part, LINE, along)
    parts, halo = lax.optimization_barrier((parts, halo))
    part = joined(parts)[:length]
    around = jnp.concatenate([halo[0], grads, halo[1]], axis=0)
    (grad_volume,) = call(
        volume_kernel,
        [((512, C), BF16)],
        [around.reshape(512, C), coarse_weight, slope, fine_weight],
        scratch=[((8, 8, 16, C), F32), ((6, 6, 16, C), F32), ((10, 10, 16, C), F32)],
        flops=2 * 800 * 27 * C * C,
    )

    mine = joined(gathered_rows(part, PLANE, plane))
    other = lax.ppermute(mine, "core", swap)
    fine_done = jnp.where(first, mine, other)
    coarse_done = jnp.where(first, other, mine)
    return (
        coarse_out,
        grad_volume.reshape(8, 8, 8, C),
        fine_done.reshape(27, C, C),
        coarse_done.reshape(27, C, C),
    )


def solution(mesh):
    shape = mesh.devices.shape
    inner = Mesh(mesh.devices.reshape(shape[0], shape[1], shape[2] // 4, 2, 2), AXES)
    cells = P("gx", "gy", WIDTH, None)
    return jax.shard_map(
        local,
        mesh=inner,
        in_specs=(cells, P(), P(), cells),
        out_specs=(cells, cells, P(), P()),
        check_vma=False,
    )
```

time: 175 us -> 167 us (0.954)
  blocking collectives: 56.3 us -> 17.3 us
  starting transfers between devices: 69.8 us -> 95.6 us
  other arithmetic: 3.92 us -> 6.26 us
  waiting for transfers between devices: 27.4 us -> 29.6 us
    all_to_all x3 -> x1, blocking collectives: 56.3 us -> 17.3 us  [gathered_rows(): return lax.all_to_all(parts, axes, 0, 0, tiled=True)]
    ppermute x4 -> x6, starting transfers between devices: 28.1 us -> 43.6 us  [the longest x2 23.7 us: along_width(): lax.ppermute(x, WIDTH, [(i, i - 1 + 2 * (i % 2)) for i in range(1, count...]
    all_to_all x1 -> x3, starting transfers between devices: 13.8 us -> 27.4 us  [the longest x2 21.2 us: spread_rows(): return lax.all_to_all(parts, axes, 0, 0, tiled=True)]
    all_to_all x1 -> x3, waiting for transfers between devices: 12.1 us -> 7.71 us  [the longest x1 3.87 us: gathered_rows(): return lax.all_to_all(parts, axes, 0, 0, tiled=True)]
    ppermute x4 -> x6, waiting for transfers between devices: 4.22 us -> 8.25 us  [the longest x2 4.71 us: along_width(): lax.ppermute(x, WIDTH, [(i, i - 1 + 2 * (i % 2)) for i in range(1, count...]
    ppermute x4, starting transfers between devices: 22.7 us -> 19.5 us  [beside(): before = lax.ppermute(last, axis, line(count, 1))]
    ppermute x4, waiting for transfers between devices: 8.35 us -> 11.1 us  [beside(): after = lax.ppermute(leading, axis, line(count, -1))]
    pallas_call x4 -> x2, Pallas kernels: 15.1 us -> 14.7 us  [call(): pl.pallas_call(kernel, out_shape=[jax.ShapeDtypeStruct(s, t) for s, t in...]
  transfers between devices with their start and end apart: 13 -> 17, of which waited for: 7 -> 10; matrix products, arithmetic and copies ran while one was open for 0% -> 1% of each run, Pallas kernels for 2% -> 2%
where the time goes in v3:
time: 167 us
  starting transfers between devices  95.6 us (57%)
  waiting for transfers between devices  29.6 us (18%)
  blocking collectives  17.3 us (10%)
  Pallas kernels  14.7 us (9%)
  other arithmetic  6.26 us (4%)
  local copies, waits for them, and re-layouts  2.2 us (1%)
    ppermute x2, starting transfers between devices, along_width(): lax.ppermute(x, WIDTH, [(i, i - 1 + 2 * (i % 2)) for i in range(1, count...  23.7 us
    all_to_all x2, starting transfers between devices, spread_rows(): return lax.all_to_all(parts, axes, 0, 0, tiled=True)  21.2 us
    ppermute x4, starting transfers between devices, beside(): before = lax.ppermute(last, axis, line(count, 1))  19.5 us
    all_to_all x1, blocking collectives, gathered_rows(): return lax.all_to_all(parts, axes, 0, 0, tiled=True)  17.3 us
    pallas_call x2, Pallas kernels, call(): pl.pallas_call(kernel, out_shape=[jax.ShapeDtypeStruct(s, t) for s, t in...  14.7 us
    ppermute x4, waiting for transfers between devices, beside(): after = lax.ppermute(leading, axis, line(count, -1))  11.1 us
    ppermute x2, starting transfers between devices, along_width(): inner = lax.ppermute(x, WIDTH, [(i, i ^ 1) for i in range(count)])  10.7 us
    ppermute x1, starting transfers between devices, local(): other = lax.ppermute(mine, 'core', swap)  7.25 us
  transfers between devices with their start and end apart: 17, of which 10 were waited for; matrix products, arithmetic and copies ran while one was open for 1% of the time, Pallas kernels for 2%

profile of v3, /device:TPU:1, one launch (start us, length us, event | category | flops | bytes accessed | tf_op | source)
XLA Modules:
  0.0 166.6 jit_solution(5821609433463910409)
XLA Ops:
  0.6 8.8 %collective-permute-start.1 = (bf16[8,8,8,128]{3,2,1,0:T(8,128)(2,1)}, bf16[8,8,8,128]{3,2,1,0:T(8,128)(2,1)S(1)}, u32[]{:S(2)}, u32[]{:S(2)}) collective-permute-start(bf16[8,8,8,128]{3,2,1,0:T(8,128)(2,1)} %param.4), channel_id=1, source_target_pairs={{0,1},{1,0},{2,3},{3,2},{4,5},{5,4},{6,7},{7,6},{8,9},{9,8},{10,11... | collective-permute-start | bytes 393224 | tf_op jit(solution)/shard_map/ppermute | solution.py:196
  9.4 10.0 %collective-permute-start = (bf16[8,8,8,128]{3,2,1,0:T(8,128)(2,1)}, bf16[8,8,8,128]{3,2,1,0:T(8,128)(2,1)S(1)}, u32[]{:S(2)}, u32[]{:S(2)}) collective-permute-start(bf16[8,8,8,128]{3,2,1,0:T(8,128)(2,1)} %param.4), channel_id=1, source_target_pairs={{1,2},{2,1},{3,4},{4,3},{5,6},{6,5},{7,8},{8,7},{9,10},{10,9},{11,... | collective-permute-start | bytes 393224 | tf_op jit(solution)/shard_map/ppermute | solution.py:195
  20.2 4.7 %collective-permute-done = bf16[8,8,8,128]{3,2,1,0:T(8,128)(2,1)S(1)} collective-permute-done((bf16[8,8,8,128]{3,2,1,0:T(8,128)(2,1)}, bf16[8,8,8,128]{3,2,1,0:T(8,128)(2,1)S(1)}, u32[]{:S(2)}, u32[]{:S(2)}) %collective-permute-start) | collective-permute-done | bytes 131104 | tf_op jit(solution)/shard_map/ppermute | solution.py:195
  27.6 9.9 %collective-permute-start.2 = (bf16[8,3,16,128]{3,2,1,0:T(8,128)(2,1)S(1)}, bf16[8,3,16,128]{3,2,1,0:T(8,128)(2,1)S(1)}, u32[]{:S(2)}, u32[]{:S(2)}) collective-permute-start(bf16[8,3,16,128]{3,2,1,0:T(8,128)(2,1)S(1)} %get-tuple-element.37), channel_id=1, source_target_pairs={{0,16},{16,32},{32,48},{48,64},{64,80},{80,96},{96,112},{1,17},{17... | collective-permute-start | bytes 294920 | tf_op jit(solution)/shard_map/ppermute | solution.py:189
  37.6 1.6 collective-permute-done.2
  39.2 3.1 %collective-permute-start.4 = (bf16[3,14,16,128]{3,2,1,0:T(8,128)(2,1)S(1)}, bf16[3,14,16,128]{3,2,1,0:T(8,128)(2,1)S(1)}, u32[]{:S(2)}, u32[]{:S(2)}) collective-permute-start(bf16[3,14,16,128]{3,2,1,0:T(8,128)(2,1)S(1)} %pad_maximum_fusion.1), channel_id=1, source_target_pairs={{0,128},{128,256},{256,384},{1,129},{129,257},{257,385},{2,130},{1... | collective-permute-start | bytes 516104 | tf_op jit(solution)/shard_map/ppermute | solution.py:189
  44.6 3.9 %collective-permute-done.5 = bf16[3,14,16,128]{3,2,1,0:T(8,128)(2,1)S(1)} collective-permute-done((bf16[3,14,16,128]{3,2,1,0:T(8,128)(2,1)S(1)}, bf16[3,14,16,128]{3,2,1,0:T(8,128)(2,1)S(1)}, u32[]{:S(2)}, u32[]{:S(2)}) %collective-permute-start.5) | collective-permute-done | bytes 172064 | tf_op jit(solution)/shard_map/ppermute | solution.py:190
  48.5 11.5 %shard_map.75 = (f32[128,128]{1,0:T(8,128)S(1)}, bf16[128,128]{1,0:T(8,128)(2,1)S(1)}, f32[12,12,16,128]{3,2,1,0:T(8,128)S(1)}, bf16[3456,128]{1,0:T(8,128)(2,1)S(1)}, bf16[3456,128]{1,0:T(8,128)(2,1)S(1)}) custom-call(s32[3]{0:T(128)S(1)} %pad_add_fusion.refs_0_, bf16[8,128,128]{2,1,0:T(8,128)(2,1)S(1)} %bitcast.24, bf16[8,48,128]{2,1,0:T(8,128)(2,1)S(1)} %bitcast.28, ...), custom_call_target="tpu_custom_call" | custom-call | flops 4423680000 | bytes 5685260 | tf_op jit(solution)/shard_map/pallas_call | solution.py:173
  60.0 1.9 %collective-permute-start.6 = (bf16[3456,128]{1,0:T(8,128)(2,1)S(1)}, bf16[3456,128]{1,0:T(8,128)(2,1)S(1)}, u32[]{:S(2)}, u32[]{:S(2)}) collective-permute-start(bf16[3456,128]{1,0:T(8,128)(2,1)S(1)} %broadcast_select_fusion.2), channel_id=1, source_target_pairs={{0,1},{1,0},{2,3},{3,2},{4,5},{5,4},{6,7},{7,6},{8,9},{9,8},{10,11... | collective-permute-start | bytes 2654216 | tf_op jit(solution)/shard_map/ppermute | solution.py:286
  62.0 2.4 %collective-permute-done.6 = bf16[3456,128]{1,0:T(8,128)(2,1)S(1)} collective-permute-done((bf16[3456,128]{1,0:T(8,128)(2,1)S(1)}, bf16[3456,128]{1,0:T(8,128)(2,1)S(1)}, u32[]{:S(2)}, u32[]{:S(2)}) %collective-permute-start.6) | collective-permute-done | bytes 884768 | tf_op jit(solution)/shard_map/ppermute | solution.py:286
  65.6 9.2 %all-to-all-start = ((bf16[16,216,128]{2,1,0:T(8,128)(2,1)}), bf16[16,216,128]{2,1,0:T(8,128)(2,1)}, u32[]{:S(2)}, u32[]{:S(2)}) async-start(bf16[16,216,128]{2,1,0:T(8,128)(2,1)} %bitcast.34), calls=%async_computation | async-start | bytes 1769472 | tf_op jit(solution)/shard_map/all_to_all | solution.py:208
  74.8 13.7 %collective-permute-start.7 = (bf16[4,4,4,128]{3,2,1,0:T(4,128)(2,1)S(1)}, bf16[4,4,4,128]{3,2,1,0:T(4,128)(2,1)S(1)}, u32[]{:S(2)}, u32[]{:S(2)}) collective-permute-start(bf16[4,4,4,128]{3,2,1,0:T(4,128)(2,1)S(1)} %slice.89), channel_id=1, source_target_pairs={{1,2},{2,1},{3,4},{4,3},{5,6},{6,5},{7,8},{8,7},{9,10},{10,9},{11,... | collective-permute-start | bytes 49160 | tf_op jit(solution)/shard_map/ppermute | solution.py:195
  88.6 1.9 %collective-permute-start.8 = (bf16[4,4,4,128]{3,2,1,0:T(4,128)(2,1)S(1)}, bf16[4,4,4,128]{3,2,1,0:T(4,128)(2,1)S(1)}, u32[]{:S(2)}, u32[]{:S(2)}) collective-permute-start(bf16[4,4,4,128]{3,2,1,0:T(4,128)(2,1)S(1)} %slice.89), channel_id=1, source_target_pairs={{0,1},{1,0},{2,3},{3,2},{4,5},{5,4},{6,7},{7,6},{8,9},{9,8},{10,11... | collective-permute-start | bytes 49160 | tf_op jit(solution)/shard_map/ppermute | solution.py:196
  93.6 12.0 %all-to-all-start.1 = ((bf16[16,16,128]{2,1,0:T(8,128)(2,1)}), bf16[16,16,128]{2,1,0:T(8,128)(2,1)S(1)}, u32[]{:S(2)}, u32[]{:S(2)}) async-start(bf16[16,16,128]{2,1,0:T(8,128)(2,1)} %bitcast.13), calls=%async_computation.1 | async-start | bytes 131072 | tf_op jit(solution)/shard_map/all_to_all | solution.py:208
  105.7 3.3 %collective-permute-start.9 = (bf16[4,2,8,128]{3,2,1,0:T(8,128)(2,1)S(1)}, bf16[4,2,8,128]{3,2,1,0:T(8,128)(2,1)S(1)}, u32[]{:S(2)}, u32[]{:S(2)}) collective-permute-start(bf16[4,2,8,128]{3,2,1,0:T(8,128)(2,1)S(1)} %get-tuple-element.47), channel_id=1, source_target_pairs={{0,16},{16,32},{32,48},{48,64},{64,80},{80,96},{96,112},{1,17},{17... | collective-permute-start | bytes 49160 | tf_op jit(solution)/shard_map/ppermute | solution.py:189
  110.3 3.6 %collective-permute-done.10 = bf16[4,2,8,128]{3,2,1,0:T(8,128)(2,1)S(1)} collective-permute-done((bf16[4,2,8,128]{3,2,1,0:T(8,128)(2,1)S(1)}, bf16[4,2,8,128]{3,2,1,0:T(8,128)(2,1)S(1)}, u32[]{:S(2)}, u32[]{:S(2)}) %collective-permute-start.10) | collective-permute-done | bytes 16416 | tf_op jit(solution)/shard_map/ppermute | solution.py:190
  113.9 3.8 %all-to-all-done.1 = bf16[16,16,128]{2,1,0:T(8,128)(2,1)S(1)} async-done(((bf16[16,16,128]{2,1,0:T(8,128)(2,1)}), bf16[16,16,128]{2,1,0:T(8,128)(2,1)S(1)}, u32[]{:S(2)}, u32[]{:S(2)}) %all-to-all-start.1) | async-done | bytes 65568 | tf_op jit(solution)/shard_map/all_to_all | solution.py:208
  118.4 6.1 %all-to-all-start.2 = ((bf16[16,16,128]{2,1,0:T(8,128)(2,1)}), bf16[16,16,128]{2,1,0:T(8,128)(2,1)S(1)}, u32[]{:S(2)}, u32[]{:S(2)}) async-start(bf16[16,16,128]{2,1,0:T(8,128)(2,1)} %broadcast_in_dim.4), calls=%async_computation.2 | async-start | bytes 131072 | tf_op jit(solution)/shard_map/all_to_all | solution.py:214
  124.6 3.2 %collective-permute-start.11 = (bf16[2,8,8,128]{3,2,1,0:T(8,128)(2,1)S(1)}, bf16[2,8,8,128]{3,2,1,0:T(8,128)(2,1)S(1)}, u32[]{:S(2)}, u32[]{:S(2)}) collective-permute-start(bf16[2,8,8,128]{3,2,1,0:T(8,128)(2,1)S(1)} %get-tuple-element.45), channel_id=1, source_target_pairs={{0,128},{128,256},{256,384},{1,129},{129,257},{257,385},{2,130},{1... | collective-permute-start | bytes 98312 | tf_op jit(solution)/shard_map/ppermute | solution.py:189
  129.2 3.6 %collective-permute-done.12 = bf16[2,8,8,128]{3,2,1,0:T(8,128)(2,1)S(1)} collective-permute-done((bf16[2,8,8,128]{3,2,1,0:T(8,128)(2,1)S(1)}, bf16[2,8,8,128]{3,2,1,0:T(8,128)(2,1)S(1)}, u32[]{:S(2)}, u32[]{:S(2)}) %collective-permute-start.12) | collective-permute-done | bytes 32800 | tf_op jit(solution)/shard_map/ppermute | solution.py:190
  132.8 3.9 %all-to-all-done.2 = bf16[16,16,128]{2,1,0:T(8,128)(2,1)S(1)} async-done(((bf16[16,16,128]{2,1,0:T(8,128)(2,1)}), bf16[16,16,128]{2,1,0:T(8,128)(2,1)S(1)}, u32[]{:S(2)}, u32[]{:S(2)}) %all-to-all-start.2) | async-done | bytes 65568 | tf_op jit(solution)/shard_map/all_to_all | solution.py:214
  136.8 17.3 %all_to_all.20 = bf16[16,216,128]{2,1,0:T(8,128)(2,1)S(1)} all-to-all(bf16[16,216,128]{2,1,0:T(8,128)(2,1)S(1)} %broadcast_in_dim.5), channel_id=1, replica_groups=mesh['gx'=4,'gy'=8,'y'=4,'zh'=2,'core'=2] {'gx','y'}, dimensions={0} | all-to-all | bytes 1769472 | tf_op jit(solution)/shard_map/all_to_all | solution.py:214
  154.0 7.2 %collective-permute-start.13 = (bf16[3456,128]{1,0:T(8,128)(2,1)S(1)}, bf16[3456,128]{1,0:T(8,128)(2,1)S(1)}, u32[]{:S(2)}, u32[]{:S(2)}) collective-permute-start(bf16[3456,128]{1,0:T(8,128)(2,1)S(1)} %bitcast.33), channel_id=1, source_target_pairs={{0,1},{1,0},{2,3},{3,2},{4,5},{5,4},{6,7},{7,6},{8,9},{9,8},{10,11... | collective-permute-start | bytes 2654216 | tf_op jit(solution)/shard_map/ppermute | solution.py:318
  162.0 3.3 %shard_map.76 = bf16[512,128]{1,0:T(8,128)(2,1)} custom-call(bf16[512,128]{1,0:T(8,128)(2,1)S(1)} %bitcast.26, bf16[27,128,128]{2,1,0:T(8,128)(2,1)S(1)} %copy-done.1, f32[12,12,16,128]{3,2,1,0:T(8,128)S(1)} %get-tuple-element.30.slope, bf16[27,128,128]{2,1,0:T(8,128)(2,1)S(1)} %copy-done), custom_call_target="tpu_custom_call" | custom-call | flops 707788800 | bytes 3211264 | tf_op jit(solution)/shard_map/pallas_call | solution.py:173
  (46 shorter events, 15.8 us)
Async XLA Ops:
  0.6 19.6 %collective-permute-start.1 = (bf16[8,8,8,128]{3,2,1,0:T(8,128)(2,1)}, bf16[8,8,8,128]{3,2,1,0:T(8,128)(2,1)S(1)}, u32[]{:S(2)}, u32[]{:S(2)}) collective-permute-start(bf16[8,8,8,128]{3,2,1,0:T(8,128)(2,1)} %param.4), channel_id=1, source_target_pairs={{0,1},{1,0},{2,3},{3,2},{4,5},{5,4},{6,7},{7,6},{8,9},{9,8},{10,11... | collective-permute-start | bytes 393224 | tf_op jit(solution)/shard_map/ppermute | solution.py:196
  9.4 15.5 %collective-permute-start = (bf16[8,8,8,128]{3,2,1,0:T(8,128)(2,1)}, bf16[8,8,8,128]{3,2,1,0:T(8,128)(2,1)S(1)}, u32[]{:S(2)}, u32[]{:S(2)}) collective-permute-start(bf16[8,8,8,128]{3,2,1,0:T(8,128)(2,1)} %param.4), channel_id=1, source_target_pairs={{1,2},{2,1},{3,4},{4,3},{5,6},{6,5},{7,8},{8,7},{9,10},{10,9},{11,... | collective-permute-start | bytes 393224 | tf_op jit(solution)/shard_map/ppermute | solution.py:195
  25.1 23.4 %copy-start = (bf16[27,128,128]{2,1,0:T(8,128)(2,1)S(1)}, bf16[27,128,128]{2,1,0:T(8,128)(2,1)}, u32[]{:S(2)}) copy-start(bf16[27,128,128]{2,1,0:T(8,128)(2,1)} %weights.1) | copy-start | bytes 2654212
  25.1 23.4 %copy-start.1 = (bf16[27,128,128]{2,1,0:T(8,128)(2,1)S(1)}, bf16[27,128,128]{2,1,0:T(8,128)(2,1)}, u32[]{:S(2)}) copy-start(bf16[27,128,128]{2,1,0:T(8,128)(2,1)} %coarse_weights.1) | copy-start | bytes 2654212
  26.3 11.3 %collective-permute-start.3 = (bf16[8,3,16,128]{3,2,1,0:T(8,128)(2,1)S(1)}, bf16[8,3,16,128]{3,2,1,0:T(8,128)(2,1)S(1)}, u32[]{:S(2)}, u32[]{:S(2)}) collective-permute-start(bf16[8,3,16,128]{3,2,1,0:T(8,128)(2,1)S(1)} %get-tuple-element.36), channel_id=1, source_target_pairs={{16,0},{32,16},{48,32},{64,48},{80,64},{96,80},{112,96},{17,1},{33... | collective-permute-start | bytes 294920 | tf_op jit(solution)/shard_map/ppermute | solution.py:190
  27.6 11.5 %collective-permute-start.2 = (bf16[8,3,16,128]{3,2,1,0:T(8,128)(2,1)S(1)}, bf16[8,3,16,128]{3,2,1,0:T(8,128)(2,1)S(1)}, u32[]{:S(2)}, u32[]{:S(2)}) collective-permute-start(bf16[8,3,16,128]{3,2,1,0:T(8,128)(2,1)S(1)} %get-tuple-element.37), channel_id=1, source_target_pairs={{0,16},{16,32},{32,48},{48,64},{64,80},{80,96},{96,112},{1,17},{17... | collective-permute-start | bytes 294920 | tf_op jit(solution)/shard_map/ppermute | solution.py:189
  39.2 5.5 %collective-permute-start.4 = (bf16[3,14,16,128]{3,2,1,0:T(8,128)(2,1)S(1)}, bf16[3,14,16,128]{3,2,1,0:T(8,128)(2,1)S(1)}, u32[]{:S(2)}, u32[]{:S(2)}) collective-permute-start(bf16[3,14,16,128]{3,2,1,0:T(8,128)(2,1)S(1)} %pad_maximum_fusion.1), channel_id=1, source_target_pairs={{0,128},{128,256},{256,384},{1,129},{129,257},{257,385},{2,130},{1... | collective-permute-start | bytes 516104 | tf_op jit(solution)/shard_map/ppermute | solution.py:189
  42.3 6.2 %collective-permute-start.5 = (bf16[3,14,16,128]{3,2,1,0:T(8,128)(2,1)S(1)}, bf16[3,14,16,128]{3,2,1,0:T(8,128)(2,1)S(1)}, u32[]{:S(2)}, u32[]{:S(2)}) collective-permute-start(bf16[3,14,16,128]{3,2,1,0:T(8,128)(2,1)S(1)} %pad_maximum_fusion.2), channel_id=1, source_target_pairs={{128,0},{256,128},{384,256},{129,1},{257,129},{385,257},{130,2},{2... | collective-permute-start | bytes 516104 | tf_op jit(solution)/shard_map/ppermute | solution.py:190
  60.0 4.3 %collective-permute-start.6 = (bf16[3456,128]{1,0:T(8,128)(2,1)S(1)}, bf16[3456,128]{1,0:T(8,128)(2,1)S(1)}, u32[]{:S(2)}, u32[]{:S(2)}) collective-permute-start(bf16[3456,128]{1,0:T(8,128)(2,1)S(1)} %broadcast_select_fusion.2), channel_id=1, source_target_pairs={{0,1},{1,0},{2,3},{3,2},{4,5},{5,4},{6,7},{7,6},{8,9},{9,8},{10,11... | collective-permute-start | bytes 2654216 | tf_op jit(solution)/shard_map/ppermute | solution.py:286
  65.6 26.1 %all-to-all-start = ((bf16[16,216,128]{2,1,0:T(8,128)(2,1)}), bf16[16,216,128]{2,1,0:T(8,128)(2,1)}, u32[]{:S(2)}, u32[]{:S(2)}) async-start(bf16[16,216,128]{2,1,0:T(8,128)(2,1)} %bitcast.34), calls=%async_computation | async-start | bytes 1769472 | tf_op jit(solution)/shard_map/all_to_all | solution.py:208
  74.8 15.7 %collective-permute-start.7 = (bf16[4,4,4,128]{3,2,1,0:T(4,128)(2,1)S(1)}, bf16[4,4,4,128]{3,2,1,0:T(4,128)(2,1)S(1)}, u32[]{:S(2)}, u32[]{:S(2)}) collective-permute-start(bf16[4,4,4,128]{3,2,1,0:T(4,128)(2,1)S(1)} %slice.89), channel_id=1, source_target_pairs={{1,2},{2,1},{3,4},{4,3},{5,6},{6,5},{7,8},{8,7},{9,10},{10,9},{11,... | collective-permute-start | bytes 49160 | tf_op jit(solution)/shard_map/ppermute | solution.py:195
  88.6 3.1 %collective-permute-start.8 = (bf16[4,4,4,128]{3,2,1,0:T(4,128)(2,1)S(1)}, bf16[4,4,4,128]{3,2,1,0:T(4,128)(2,1)S(1)}, u32[]{:S(2)}, u32[]{:S(2)}) collective-permute-start(bf16[4,4,4,128]{3,2,1,0:T(4,128)(2,1)S(1)} %slice.89), channel_id=1, source_target_pairs={{0,1},{1,0},{2,3},{3,2},{4,5},{5,4},{6,7},{7,6},{8,9},{9,8},{10,11... | collective-permute-start | bytes 49160 | tf_op jit(solution)/shard_map/ppermute | solution.py:196
  93.6 24.1 %all-to-all-start.1 = ((bf16[16,16,128]{2,1,0:T(8,128)(2,1)}), bf16[16,16,128]{2,1,0:T(8,128)(2,1)S(1)}, u32[]{:S(2)}, u32[]{:S(2)}) async-start(bf16[16,16,128]{2,1,0:T(8,128)(2,1)} %bitcast.13), calls=%async_computation.1 | async-start | bytes 131072 | tf_op jit(solution)/shard_map/all_to_all | solution.py:208
  105.7 4.6 %collective-permute-start.9 = (bf16[4,2,8,128]{3,2,1,0:T(8,128)(2,1)S(1)}, bf16[4,2,8,128]{3,2,1,0:T(8,128)(2,1)S(1)}, u32[]{:S(2)}, u32[]{:S(2)}) collective-permute-start(bf16[4,2,8,128]{3,2,1,0:T(8,128)(2,1)S(1)} %get-tuple-element.47), channel_id=1, source_target_pairs={{0,16},{16,32},{32,48},{48,64},{64,80},{80,96},{96,112},{1,17},{17... | collective-permute-start | bytes 49160 | tf_op jit(solution)/shard_map/ppermute | solution.py:189
  109.0 4.9 %collective-permute-start.10 = (bf16[4,2,8,128]{3,2,1,0:T(8,128)(2,1)S(1)}, bf16[4,2,8,128]{3,2,1,0:T(8,128)(2,1)S(1)}, u32[]{:S(2)}, u32[]{:S(2)}) collective-permute-start(bf16[4,2,8,128]{3,2,1,0:T(8,128)(2,1)S(1)} %get-tuple-element.46), channel_id=1, source_target_pairs={{16,0},{32,16},{48,32},{64,48},{80,64},{96,80},{112,96},{17,1},{33... | collective-permute-start | bytes 49160 | tf_op jit(solution)/shard_map/ppermute | solution.py:190
  118.4 18.2 %all-to-all-start.2 = ((bf16[16,16,128]{2,1,0:T(8,128)(2,1)}), bf16[16,16,128]{2,1,0:T(8,128)(2,1)S(1)}, u32[]{:S(2)}, u32[]{:S(2)}) async-start(bf16[16,16,128]{2,1,0:T(8,128)(2,1)} %broadcast_in_dim.4), calls=%async_computation.2 | async-start | bytes 131072 | tf_op jit(solution)/shard_map/all_to_all | solution.py:214
  124.6 4.5 %collective-permute-start.11 = (bf16[2,8,8,128]{3,2,1,0:T(8,128)(2,1)S(1)}, bf16[2,8,8,128]{3,2,1,0:T(8,128)(2,1)S(1)}, u32[]{:S(2)}, u32[]{:S(2)}) collective-permute-start(bf16[2,8,8,128]{3,2,1,0:T(8,128)(2,1)S(1)} %get-tuple-element.45), channel_id=1, source_target_pairs={{0,128},{128,256},{256,384},{1,129},{129,257},{257,385},{2,130},{1... | collective-permute-start | bytes 98312 | tf_op jit(solution)/shard_map/ppermute | solution.py:189
  127.9 5.0 %collective-permute-start.12 = (bf16[2,8,8,128]{3,2,1,0:T(8,128)(2,1)S(1)}, bf16[2,8,8,128]{3,2,1,0:T(8,128)(2,1)S(1)}, u32[]{:S(2)}, u32[]{:S(2)}) collective-permute-start(bf16[2,8,8,128]{3,2,1,0:T(8,128)(2,1)S(1)} %get-tuple-element.44), channel_id=1, source_target_pairs={{128,0},{256,128},{384,256},{129,1},{257,129},{385,257},{130,2},{2... | collective-permute-start | bytes 98312 | tf_op jit(solution)/shard_map/ppermute | solution.py:190
  154.0 11.2 %collective-permute-start.13 = (bf16[3456,128]{1,0:T(8,128)(2,1)S(1)}, bf16[3456,128]{1,0:T(8,128)(2,1)S(1)}, u32[]{:S(2)}, u32[]{:S(2)}) collective-permute-start(bf16[3456,128]{1,0:T(8,128)(2,1)S(1)} %bitcast.33), channel_id=1, source_target_pairs={{0,1},{1,0},{2,3},{3,2},{4,5},{5,4},{6,7},{7,6},{8,9},{9,8},{10,11... | collective-permute-start | bytes 2654216 | tf_op jit(solution)/shard_map/ppermute | solution.py:318

commit v4 on v3

v4 whole, which is shorter than its diff:
```python
import math

import jax
import jax.numpy as jnp
from jax import lax
from jax.experimental import pallas as pl
from jax.experimental.pallas import tpu as pltpu
from jax.sharding import Mesh, PartitionSpec as P

AXES = ("gx", "gy", "y", "zh", "core")
WIDTH = ("y", "zh", "core")
PLANE = ("gx", "y")
LINE = ("gy", "zh")
C = 128
F32 = jnp.float32
BF16 = jnp.bfloat16


def silu_slope(values):
    sigma = 1.0 / (1.0 + jnp.exp(-values))
    return sigma * (1.0 + values * (1.0 - sigma))


def inside(shape, starts, sizes):
    keep = None
    for dim in range(3):
        at = starts[dim] + lax.broadcasted_iota(jnp.int32, shape, dim)
        ok = (at >= 0) & (at < sizes[dim])
        keep = ok if keep is None else keep & ok
    return keep


def taps():
    return [(i, j, k) for i in range(3) for j in range(3) for k in range(3)]


def flat(values):
    return values.reshape(-1, C).astype(BF16)


def weight_terms(turned, cells, sum_ref, at):
    terms = jnp.dot(turned, cells, preferred_element_type=F32)
    for t in range(9):
        row = (at + t) * C
        sum_ref[row : row + C] = terms[:, t * C : (t + 1) * C].T.astype(BF16)


def back_conv(grads, weights):
    cells = jnp.concatenate(
        [flat(grads[2 - i : 8 - i, 2 - j : 8 - j, 2 - k : 10 - k]) for i, j, k in taps()], axis=1
    )
    turned = jnp.concatenate([weights[t] for t in range(27)], axis=1)
    back = lax.dot_general(cells, turned, (((1,), (1,)), ((), ())), preferred_element_type=F32)
    return back.reshape(6, 6, 8, C)


def gather(wide, patches, planes, start, length):
    def plane(x, carry):
        for k in range(3):
            line = wide[x, :, start + k : start + k + length]
            for j in range(3):
                at = (3 * j + k) * C
                patches[x, :, at : at + C] = flat(line[j : j + 12])
        return carry

    lax.fori_loop(0, planes, plane, 0)


def fine_conv(patches, weights, at, planes):
    rows = planes * 288
    total = jnp.zeros((rows, C), F32)
    for i in range(3):
        cells = patches[pl.ds(at + i, planes)].reshape(rows, 9 * C)
        total = total + jnp.dot(
            cells, weights[9 * C * i : 9 * C * (i + 1)], preferred_element_type=F32
        )
    return total.reshape(planes, 12, 24, C)


def fill(wide, at, x, own, below, above):
    wide[at, 3:11, :24] = own[x].astype(F32).reshape(8, 24, C)
    wide[at, :3, :24] = below[x].astype(F32).reshape(3, 24, C)
    wide[at, 11:, :24] = above[x].astype(F32).reshape(3, 24, C)


def inner_kernel(own, below, above, weights, hidden_ref, wide, patches):
    for x in range(8):
        fill(wide, x, x, own, below, above)
    gather(wide, patches, 8, 1, 24)
    for part in range(2):
        hidden_ref[3 * part : 3 * part + 3] = fine_conv(patches, weights, 3 * part, 3)


def front_kernel(
    fine_sizes, coarse_sizes, place, own, below, above, left, right, weights, coarse_weights, incoming, inner,
    coarse_ref, grad_ref, slope_ref, pooled,
    wide, patches, outer, pairs,
):
    for x in range(3):
        wide[x, :, :24] = left[x].astype(F32).reshape(14, 24, C)
        wide[7 + x, :, :24] = right[x].astype(F32).reshape(14, 24, C)
    for x in range(2):
        fill(wide, 3 + x, x, own, below, above)
        fill(wide, 5 + x, 6 + x, own, below, above)
    gather(wide, patches, 10, 1, 24)
    for part in range(2):
        outer[3 * part : 3 * part + 3] = fine_conv(patches, weights, 5 * part, 3)

    for x in range(6):
        active = None
        for at in (2 * x, 2 * x + 1):
            value = inner[at - 3] if 3 <= at < 9 else outer[at if at < 3 else at - 6]
            sigma = 1.0 / (1.0 + jnp.exp(-value))
            slope = sigma * (1.0 + value * (1.0 - sigma)) * 0.125
            starts = [8 * place[0] - 2 + at, 8 * place[1] - 2, 8 * place[2] - 6]
            keep = inside((1, 12, 24, C), starts, fine_sizes)[0]
            slope_ref[at] = jnp.where(keep, slope, 0.0)
            value = value * sigma
            active = value if active is None else active + value
        active = active.reshape(6, 2, 24, C)
        pairs[...] = active[:, 0] + active[:, 1]
        mean = (pairs[:, pl.ds(0, 12, 2)] + pairs[:, pl.ds(1, 12, 2)]) * 0.125
        starts = [4 * place[0] - 1 + x, 4 * place[1] - 1, 4 * place[2] - 3]
        keep = inside((1, 6, 12, C), starts, coarse_sizes)[0]
        pooled[x, :, :12] = jnp.where(keep, mean, 0.0)
        pooled[x, :, 12:] = jnp.zeros((6, 4, C), F32)

    cells = [flat(pooled[i : i + 4, j : j + 4, k : k + 8]) for i, j, k in taps()]
    coarse = jnp.dot(
        jnp.concatenate(cells, axis=1), coarse_weights[...], preferred_element_type=F32
    )
    coarse_ref[...] = coarse
    grad_ref[...] = (incoming[...] * silu_slope(coarse)).astype(BF16)


def share_kernel(grad_in, pooled, coarse_weights, slope, turned_ref, sum_ref, grads, spread, shares):
    grad = grad_in[...].astype(F32)
    grads[...] = jnp.zeros((8, 8, 16, C), F32)
    grads[2:6, 2:6, :8] = grad.reshape(4, 4, 8, C)
    back = back_conv(grads, coarse_weights)
    spread[:, :, pl.ds(0, 8, 2)] = back
    spread[:, :, pl.ds(1, 8, 2)] = back
    for x in range(12):
        for y in range(12):
            shares[x, y] = spread[x // 2, y // 2, 2:10] * slope[x, y, 6:14]
    turned_ref[...] = shares[...].reshape(1152, C).T.astype(BF16)

    at = lax.broadcasted_iota(jnp.int32, (C, C), 0) % 8
    turned = jnp.where((at >= 2) & (at < 6), grad, 0.0).T.astype(BF16)
    for i in range(3):
        cells = [
            flat(pooled[i : i + 4, j : j + 4, k : k + 8]) for j in range(3) for k in range(3)
        ]
        weight_terms(turned, jnp.concatenate(cells, axis=1), sum_ref, 9 * i)


def fine_kernel(own, below, above, left, right, turned, sum_ref, wide, patches):
    for x in range(8):
        fill(wide, 3 + x, x, own, below, above)
    for x in range(3):
        wide[x, :, :24] = left[x].astype(F32).reshape(14, 24, C)
        wide[11 + x, :, :24] = right[x].astype(F32).reshape(14, 24, C)
    gather(wide, patches, 14, 7, 8)
    shares = turned[...]
    for i in range(3):
        weight_terms(shares, patches[i : i + 12].reshape(1152, 9 * C), sum_ref, 9 * i)


def volume_kernel(around, coarse_weights, slope, weights, out_ref, grads, spread, fine):
    for x in range(8):
        grads[x, :, :8] = around[64 * x : 64 * x + 64].astype(F32).reshape(8, 8, C)
    back = back_conv(grads, coarse_weights)
    spread[:, :, pl.ds(0, 8, 2)] = back
    spread[:, :, pl.ds(1, 8, 2)] = back
    for x in range(10):
        for y in range(10):
            fine[x, y] = spread[(x + 1) // 2, (y + 1) // 2] * slope[x + 1, y + 1, 4:20]
    total = jnp.zeros((512, C), F32)
    for i in range(3):
        cells = jnp.concatenate(
            [
                flat(fine[2 - i : 10 - i, 2 - j : 10 - j, 3 - k : 11 - k])
                for j in range(3)
                for k in range(3)
            ],
            axis=1,
        )
        turned = jnp.concatenate([weights[9 * i + t] for t in range(9)], axis=1)
        total = total + lax.dot_general(
            cells, turned, (((1,), (1,)), ((), ())), preferred_element_type=F32
        )
    out_ref[...] = total.astype(BF16)


def call(kernel, outs, inputs, scratch=(), scalars=0, flops=0):
    in_specs = [
        pl.BlockSpec(memory_space=pltpu.SMEM if n < scalars else pltpu.VMEM)
        for n in range(len(inputs))
    ]
    moved = sum(a.size * a.dtype.itemsize for a in inputs)
    moved += sum(math.prod(s) * jnp.dtype(t).itemsize for s, t in outs)
    return pl.pallas_call(
        kernel,
        out_shape=[jax.ShapeDtypeStruct(s, t) for s, t in outs],
        in_specs=in_specs,
        out_specs=[pl.BlockSpec(memory_space=pltpu.VMEM) for _ in outs],
        scratch_shapes=[pltpu.VMEM(s, t) for s, t in scratch],
        compiler_params=pltpu.CompilerParams(vmem_limit_bytes=40 * 1024 * 1024),
        cost_estimate=pl.CostEstimate(flops=flops, bytes_accessed=moved, transcendentals=0),
    )(*inputs)


def line(count, step):
    return [(i, i + step) for i in range(count) if 0 <= i + step < count]


def beside(last, leading, axis, count):
    before = lax.ppermute(last, axis, line(count, 1))
    after = lax.ppermute(leading, axis, line(count, -1))
    return before, after


def along_width(x, count):
    outer = lax.ppermute(x, WIDTH, [(i, i - 1 + 2 * (i % 2)) for i in range(1, count - 1)])
    inner = lax.ppermute(x, WIDTH, [(i, i ^ 1) for i in range(count)])
    return outer, inner


def in_order(outer, inner):
    first = lax.axis_index("core") == 0
    return jnp.where(first, outer, inner), jnp.where(first, inner, outer)


def spread_rows(terms, axes, peers):
    rows = terms.shape[0]
    parts = terms.astype(BF16).reshape(peers, rows // peers, C)
    return lax.all_to_all(parts, axes, 0, 0, tiled=True)


def gathered_rows(part, axes, peers):
    rows = part.shape[0]
    parts = jnp.broadcast_to(part[None], (peers, rows, C))
    return lax.all_to_all(parts, axes, 0, 0, tiled=True)


def summed(parts):
    return jnp.sum(parts.astype(F32), axis=0)


def joined(parts):
    return parts.reshape(-1, C)


def local(volume, fine_weight, coarse_weight, cotangent):
    sizes = {axis: lax.axis_size(axis) for axis in AXES}
    plane, along = (sizes["gx"] * sizes["y"], sizes["gy"] * sizes["zh"])
    peers = [sizes["gx"], sizes["gy"], sizes["y"] * sizes["zh"] * 2]
    place = [lax.axis_index("gx"), lax.axis_index("gy"), lax.axis_index(WIDTH)]
    place = jnp.stack([p.astype(jnp.int32) for p in place])
    fine_sizes = [8 * n for n in peers]
    coarse_sizes = [4 * n for n in peers]

    fine_rows = fine_weight.reshape(27 * C, C)
    coarse_rows = coarse_weight.reshape(27 * C, C)

    packed = jnp.concatenate([volume.reshape(512, C), cotangent.reshape(64, C)], axis=0)
    before, after = in_order(*along_width(packed, peers[2]))
    own = jnp.concatenate(
        [before[:512].reshape(8, 8, 8, C), volume, after[:512].reshape(8, 8, 8, C)], axis=2
    )
    incoming = jnp.concatenate(
        [
            before[512:].reshape(4, 4, 4, C)[:, :, 2:],
            cotangent,
            after[512:].reshape(4, 4, 4, C)[:, :, :2],
        ],
        axis=2,
    ).astype(F32)
    below, above = beside(own[:, 5:], own[:, :3], "gy", peers[1])
    sides = [
        jnp.concatenate([below[at], own[at], above[at]], axis=1)
        for at in (slice(5, 8), slice(0, 3))
    ]
    left, right = beside(sides[0], sides[1], "gx", peers[0])
    across = [own.reshape(8, 192, C), below.reshape(8, 72, C), above.reshape(8, 72, C)]
    (inner,) = call(
        inner_kernel,
        [((6, 12, 24, C), F32)],
        across + [fine_rows],
        scratch=[((8, 14, 32, C), F32), ((8, 288, 9 * C), BF16)],
        flops=2 * 1728 * 27 * C * C,
    )
    across = across + [left.reshape(3, 336, C), right.reshape(3, 336, C)]
    coarse, coarse_grad, slope, pooled = call(
        lambda *refs: front_kernel(fine_sizes, coarse_sizes, *refs),
        [((128, C), F32), ((128, C), BF16), ((12, 12, 24, C), F32), ((6, 6, 16, C), F32)],
        [place, *across, fine_rows, coarse_rows, incoming.reshape(128, C), inner],
        scratch=[
            ((10, 14, 32, C), F32),
            ((10, 288, 9 * C), BF16),
            ((6, 12, 24, C), F32),
            ((6, 24, C), F32),
        ],
        scalars=1,
        flops=2 * 1900 * 27 * C * C,
    )

    grads = coarse_grad.reshape(4, 4, 8, C)
    halo = beside(grads[:, 2:], grads[:, :2], "gy", peers[1])
    turned, coarse_sum = call(
        share_kernel,
        [((C, 1152), BF16), ((27 * C, C), BF16)],
        [coarse_grad, pooled, coarse_weight, slope],
        scratch=[((8, 8, 16, C), F32), ((6, 6, 16, C), F32), ((12, 12, 8, C), F32)],
        flops=2 * 1000 * 27 * C * C,
    )
    halo, turned = lax.optimization_barrier((halo, turned))
    grads = jnp.concatenate([halo[0], grads, halo[1]], axis=1)
    halo = beside(grads[2:], grads[:2], "gx", peers[0])
    (fine_sum,) = call(
        fine_kernel,
        [((27 * C, C), BF16)],
        [*across, turned],
        scratch=[((14, 14, 32, C), F32), ((14, 96, 9 * C), BF16)],
        flops=2 * 1152 * 27 * C * C,
    )
    halo, fine_sum = lax.optimization_barrier((halo, fine_sum))
    around = jnp.concatenate([halo[0], grads, halo[1]], axis=0)

    first = lax.axis_index("core") == 0
    swap = [(0, 1), (1, 0)]
    cells_fine = fine_sizes[0] * fine_sizes[1] * fine_sizes[2]
    scale = jnp.where(first, 1.0 / math.sqrt(cells_fine), 1.0 / math.sqrt(cells_fine // 8))
    mine = jnp.where(first, fine_sum, coarse_sum).astype(F32)
    other = jnp.where(first, coarse_sum, fine_sum)
    mine = mine + lax.ppermute(other, "core", swap).astype(F32)

    parts = spread_rows(mine, PLANE, plane)
    (grad_volume,) = call(
        volume_kernel,
        [((512, C), BF16)],
        [around.reshape(512, C), coarse_weight, slope, fine_weight],
        scratch=[((8, 8, 16, C), F32), ((6, 6, 16, C), F32), ((10, 10, 16, C), F32)],
        flops=2 * 800 * 27 * C * C,
    )
    coarse_out = jax.nn.silu(coarse.reshape(4, 4, 8, C)[:, :, 2:6]).astype(BF16)
    parts, grad_volume, coarse_out = lax.optimization_barrier((parts, grad_volume, coarse_out))
    part = summed(parts)
    length = part.shape[0]
    padded = -(-length // (16 * along)) * 16 * along
    part = jnp.pad(part, ((0, padded - length), (0, 0)))
    part = (summed(spread_rows(part, LINE, along)) * scale).astype(BF16)
    part = joined(gathered_rows(part, LINE, along))[:length]
    mine = joined(gathered_rows(part, PLANE, plane))
    other = lax.ppermute(mine, "core", swap)
    fine_done = jnp.where(first, mine, other)
    coarse_done = jnp.where(first, other, mine)
    return (
        coarse_out,
        grad_volume.reshape(8, 8, 8, C),
        fine_done.reshape(27, C, C),
        coarse_done.reshape(27, C, C),
    )


def solution(mesh):
    shape = mesh.devices.shape
    inner = Mesh(mesh.devices.reshape(shape[0], shape[1], shape[2] // 4, 2, 2), AXES)
    cells = P("gx", "gy", WIDTH, None)
    return jax.shard_map(
        local,
        mesh=inner,
        in_specs=(cells, P(), P(), cells),
        out_specs=(cells, cells, P(), P()),
        check_vma=False,
    )
```

time: 167 us -> 174 us (1.042)
  starting transfers between devices: 95.6 us -> 82.3 us
  blocking collectives: 17.3 us -> 29.2 us
  waiting for transfers between devices: 29.6 us -> 33.8 us
  other arithmetic: 6.26 us -> 8.58 us
  Pallas kernels: 14.7 us -> 16.9 us
    all_to_all x2, waiting for transfers between devices: 3.84 us -> 20.3 us  [spread_rows(): return lax.all_to_all(parts, axes, 0, 0, tiled=True)]
    ppermute x2 -> x1, starting transfers between devices: 23.7 us -> 9.97 us  [along_width(): lax.ppermute(x, WIDTH, [(i, i - 1 + 2 * (i % 2)) for i in range(1, count...]
    all_to_all x1 -> x2, blocking collectives: 17.3 us -> 29.2 us  [gathered_rows(): return lax.all_to_all(parts, axes, 0, 0, tiled=True)]
    ppermute x4, waiting for transfers between devices: 11.1 us -> 2.11 us  [beside(): after = lax.ppermute(leading, axis, line(count, -1))]
    all_to_all x1 -> x0, starting transfers between devices: 6.13 us -> none  [gathered_rows(): return lax.all_to_all(parts, axes, 0, 0, tiled=True)]
    all_to_all x2, starting transfers between devices: 21.2 us -> 26.4 us  [spread_rows(): return lax.all_to_all(parts, axes, 0, 0, tiled=True)]
    all_to_all x1 -> x0, waiting for transfers between devices: 3.87 us -> none  [gathered_rows(): return lax.all_to_all(parts, axes, 0, 0, tiled=True)]
    ppermute x4, starting transfers between devices: 19.5 us -> 22.1 us  [beside(): before = lax.ppermute(last, axis, line(count, 1))]
  transfers between devices with their start and end apart: 17 -> 14, of which waited for: 10 -> 8; matrix products, arithmetic and copies ran while one was open for 1% -> 1% of each run, Pallas kernels for 2% -> 6%
where the time goes in v4:
time: 174 us; the launch traced here: 173 us
  starting transfers between devices  82.3 us (47%)
  waiting for transfers between devices  33.8 us (19%)
  blocking collectives  29.2 us (17%)
  Pallas kernels  16.9 us (10%)
  other arithmetic  8.58 us (5%)
    all_to_all x2, blocking collectives, gathered_rows(): return lax.all_to_all(parts, axes, 0, 0, tiled=True)  29.2 us
    all_to_all x2, starting transfers between devices, spread_rows(): return lax.all_to_all(parts, axes, 0, 0, tiled=True)  26.4 us
    ppermute x4, starting transfers between devices, beside(): before = lax.ppermute(last, axis, line(count, 1))  22.1 us
    all_to_all x2, waiting for transfers between devices, spread_rows(): return lax.all_to_all(parts, axes, 0, 0, tiled=True)  20.3 us
    pallas_call x5, Pallas kernels, call(): pl.pallas_call(kernel, out_shape=[jax.ShapeDtypeStruct(s, t) for s, t in...  16.9 us
    ppermute x1, starting transfers between devices, along_width(): lax.ppermute(x, WIDTH, [(i, i - 1 + 2 * (i % 2)) for i in range(1, count...  9.97 us
    ppermute x1, starting transfers between devices, along_width(): inner = lax.ppermute(x, WIDTH, [(i, i ^ 1) for i in range(count)])  8.79 us
    ppermute x1, starting transfers between devices, local(): other = lax.ppermute(mine, 'core', swap)  7.98 us
  transfers between devices with their start and end apart: 14, of which 8 were waited for; matrix products, arithmetic and copies ran while one was open for 1% of the time, Pallas kernels for 6%

profile of v4, /device:TPU:1, one launch (start us, length us, event | category | flops | bytes accessed | tf_op | source)
XLA Modules:
  0.0 172.8 jit_solution(9756369436817653226)
XLA Ops:
  1.6 8.8 %collective-permute-start.1 = (bf16[576,128]{1,0:T(8,128)(2,1)S(1)}, bf16[576,128]{1,0:T(8,128)(2,1)S(1)}, u32[]{:S(2)}, u32[]{:S(2)}) collective-permute-start(bf16[576,128]{1,0:T(8,128)(2,1)S(1)} %pad_maximum_fusion.3), channel_id=1, source_target_pairs={{0,1},{1,0},{2,3},{3,2},{4,5},{5,4},{6,7},{7,6},{8,9},{9,8},{10,11... | collective-permute-start | bytes 442376 | tf_op jit(solution)/shard_map/ppermute | solution.py:225
  10.4 10.0 %collective-permute-start = (bf16[576,128]{1,0:T(8,128)(2,1)S(1)}, bf16[576,128]{1,0:T(8,128)(2,1)S(1)}, u32[]{:S(2)}, u32[]{:S(2)}) collective-permute-start(bf16[576,128]{1,0:T(8,128)(2,1)S(1)} %pad_maximum_fusion.3), channel_id=1, source_target_pairs={{1,2},{2,1},{3,4},{4,3},{5,6},{6,5},{7,8},{8,7},{9,10},{10,9},{11,... | collective-permute-start | bytes 442376 | tf_op jit(solution)/shard_map/ppermute | solution.py:224
  20.4 5.4 %collective-permute-done = bf16[576,128]{1,0:T(8,128)(2,1)S(1)} collective-permute-done((bf16[576,128]{1,0:T(8,128)(2,1)S(1)}, bf16[576,128]{1,0:T(8,128)(2,1)S(1)}, u32[]{:S(2)}, u32[]{:S(2)}) %collective-permute-start) | collective-permute-done | bytes 147488 | tf_op jit(solution)/shard_map/ppermute | solution.py:224
  28.4 10.5 %collective-permute-start.2 = (bf16[8,3,24,128]{3,2,1,0:T(8,128)(2,1)S(1)}, bf16[8,3,24,128]{3,2,1,0:T(8,128)(2,1)S(1)}, u32[]{:S(2)}, u32[]{:S(2)}) collective-permute-start(bf16[8,3,24,128]{3,2,1,0:T(8,128)(2,1)S(1)} %get-tuple-element.39), channel_id=1, source_target_pairs={{0,16},{16,32},{32,48},{48,64},{64,80},{80,96},{96,112},{1,17},{17... | collective-permute-start | bytes 442376 | tf_op jit(solution)/shard_map/ppermute | solution.py:218
  39.5 1.6 collective-permute-done.2
  41.1 3.1 %collective-permute-start.4 = (bf16[3,14,24,128]{3,2,1,0:T(8,128)(2,1)S(1)}, bf16[3,14,24,128]{3,2,1,0:T(8,128)(2,1)S(1)}, u32[]{:S(2)}, u32[]{:S(2)}) collective-permute-start(bf16[3,14,24,128]{3,2,1,0:T(8,128)(2,1)S(1)} %pad_maximum_fusion.1), channel_id=1, source_target_pairs={{0,128},{128,256},{256,384},{1,129},{129,257},{257,385},{2,130},{1... | collective-permute-start | bytes 774152 | tf_op jit(solution)/shard_map/ppermute | solution.py:218
  45.6 4.1 %shard_map.75.refs_9_ = f32[6,12,24,128]{3,2,1,0:T(8,128)S(1)} custom-call(bf16[8,192,128]{2,1,0:T(8,128)(2,1)S(1)} %bitcast.31, bf16[8,72,128]{2,1,0:T(8,128)(2,1)S(1)} %bitcast.44, bf16[8,72,128]{2,1,0:T(8,128)(2,1)S(1)} %bitcast.41, bf16[3456,128]{1,0:T(8,128)(2,1)S(1)} %bitcast.34), custom_call_target="tpu_custom_call" | custom-call | flops 1528823808 | bytes 2457600 | tf_op jit(solution)/shard_map/pallas_call | solution.py:202
  49.7 1.7 collective-permute-done.5
  51.4 5.8 %shard_map.76 = (f32[128,128]{1,0:T(8,128)S(1)}, bf16[128,128]{1,0:T(8,128)(2,1)S(1)}, f32[12,12,24,128]{3,2,1,0:T(8,128)S(1)}, f32[6,6,16,128]{3,2,1,0:T(8,128)S(1)}) custom-call(s32[3]{0:T(128)S(1)} %pad_add_fusion.refs_0_, bf16[8,192,128]{2,1,0:T(8,128)(2,1)S(1)} %bitcast.32, bf16[8,72,128]{2,1,0:T(8,128)(2,1)S(1)} %bitcast.45, ...), custom_call_target="tpu_custom_call" | custom-call | flops 1680998400 | bytes 6086668 | tf_op jit(solution)/shard_map/pallas_call | solution.py:202
  58.4 4.4 %collective-permute-start.6 = (bf16[4,2,8,128]{3,2,1,0:T(8,128)(2,1)S(1)}, bf16[4,2,8,128]{3,2,1,0:T(8,128)(2,1)S(1)}, u32[]{:S(2)}, u32[]{:S(2)}) collective-permute-start(bf16[4,2,8,128]{3,2,1,0:T(8,128)(2,1)S(1)} %get-tuple-element.49), channel_id=1, source_target_pairs={{0,16},{16,32},{32,48},{48,64},{64,80},{80,96},{96,112},{1,17},{17... | collective-permute-start | bytes 49160 | tf_op jit(solution)/shard_map/ppermute | solution.py:218
  62.9 1.6 shard_map.77
  65.9 4.0 %collective-permute-start.8 = (bf16[2,8,8,128]{3,2,1,0:T(8,128)(2,1)S(1)}, bf16[2,8,8,128]{3,2,1,0:T(8,128)(2,1)S(1)}, u32[]{:S(2)}, u32[]{:S(2)}) collective-permute-start(bf16[2,8,8,128]{3,2,1,0:T(8,128)(2,1)S(1)} %get-tuple-element.47), channel_id=1, source_target_pairs={{0,128},{128,256},{256,384},{1,129},{129,257},{257,385},{2,130},{1... | collective-permute-start | bytes 98312 | tf_op jit(solution)/shard_map/ppermute | solution.py:218
  69.9 2.2 %shard_map.78 = bf16[3456,128]{1,0:T(8,128)(2,1)S(1)} custom-call(bf16[8,192,128]{2,1,0:T(8,128)(2,1)S(1)} %bitcast.33, bf16[8,72,128]{2,1,0:T(8,128)(2,1)S(1)} %bitcast.46, bf16[8,72,128]{2,1,0:T(8,128)(2,1)S(1)} %bitcast.43, bf16[3,336,128]{2,1,0:T(8,128)(2,1)S(1)} %bitcast.49, bf16[3,336,128]{2,1,0:T(8,128)(2,1)S(1)} %bitcast.51, ...), custom_call_target="tpu_custom_call" | custom-call | flops 1019215872 | bytes 2383872 | tf_op jit(solution)/shard_map/pallas_call | solution.py:202
  72.2 1.9 %collective-permute-start.10 = (bf16[3456,128]{1,0:T(8,128)(2,1)S(1)}, bf16[3456,128]{1,0:T(8,128)(2,1)S(1)}, u32[]{:S(2)}, u32[]{:S(2)}) collective-permute-start(bf16[3456,128]{1,0:T(8,128)(2,1)S(1)} %broadcast_select_fusion.2), channel_id=1, source_target_pairs={{0,1},{1,0},{2,3},{3,2},{4,5},{5,4},{6,7},{7,6},{8,9},{9,8},{10,11... | collective-permute-start | bytes 2654216 | tf_op jit(solution)/shard_map/ppermute | solution.py:336
  74.2 2.4 %collective-permute-done.10 = bf16[3456,128]{1,0:T(8,128)(2,1)S(1)} collective-permute-done((bf16[3456,128]{1,0:T(8,128)(2,1)S(1)}, bf16[3456,128]{1,0:T(8,128)(2,1)S(1)}, u32[]{:S(2)}, u32[]{:S(2)}) %collective-permute-start.10) | collective-permute-done | bytes 884768 | tf_op jit(solution)/shard_map/ppermute | solution.py:336
  77.8 12.4 %all-to-all-start = ((bf16[16,216,128]{2,1,0:T(8,128)(2,1)}), bf16[16,216,128]{2,1,0:T(8,128)(2,1)}, u32[]{:S(2)}, u32[]{:S(2)}) async-start(bf16[16,216,128]{2,1,0:T(8,128)(2,1)} %bitcast.52), calls=%async_computation | async-start | bytes 1769472 | tf_op jit(solution)/shard_map/all_to_all | solution.py:237
  92.5 3.3 %shard_map.79 = bf16[512,128]{1,0:T(8,128)(2,1)} custom-call(bf16[512,128]{1,0:T(8,128)(2,1)S(1)} %bitcast.37, bf16[27,128,128]{2,1,0:T(8,128)(2,1)S(1)} %copy-done.1, f32[12,12,24,128]{3,2,1,0:T(8,128)S(1)} %get-tuple-element.21.slope, bf16[27,128,128]{2,1,0:T(8,128)(2,1)S(1)} %copy-done), custom_call_target="tpu_custom_call" | custom-call | flops 707788800 | bytes 3801088 | tf_op jit(solution)/shard_map/pallas_call | solution.py:202
  95.8 8.2 %all-to-all-done = bf16[16,216,128]{2,1,0:T(8,128)(2,1)} async-done(((bf16[16,216,128]{2,1,0:T(8,128)(2,1)}), bf16[16,216,128]{2,1,0:T(8,128)(2,1)}, u32[]{:S(2)}, u32[]{:S(2)}) %all-to-all-start) | async-done | bytes 884768 | tf_op jit(solution)/shard_map/all_to_all | solution.py:237
  105.9 14.0 %all-to-all-start.1 = ((bf16[16,16,128]{2,1,0:T(8,128)(2,1)}), bf16[16,16,128]{2,1,0:T(8,128)(2,1)S(1)}, u32[]{:S(2)}, u32[]{:S(2)}) async-start(bf16[16,16,128]{2,1,0:T(8,128)(2,1)} %bitcast.22), calls=%async_computation.1 | async-start | bytes 131072 | tf_op jit(solution)/shard_map/all_to_all | solution.py:237
  119.9 12.1 %all-to-all-done.1 = bf16[16,16,128]{2,1,0:T(8,128)(2,1)S(1)} async-done(((bf16[16,16,128]{2,1,0:T(8,128)(2,1)}), bf16[16,16,128]{2,1,0:T(8,128)(2,1)S(1)}, u32[]{:S(2)}, u32[]{:S(2)}) %all-to-all-start.1) | async-done | bytes 65568 | tf_op jit(solution)/shard_map/all_to_all | solution.py:237
  132.1 14.2 %all_to_all.20 = bf16[16,16,128]{2,1,0:T(8,128)(2,1)S(1)} all-to-all(bf16[16,16,128]{2,1,0:T(8,128)(2,1)S(1)} %broadcast_in_dim.4), channel_id=1, replica_groups=mesh['gx'=4,'gy'=8,'y'=4,'zh'=2,'core'=2] {'gy','zh'}, dimensions={0} | all-to-all | bytes 131072 | tf_op jit(solution)/shard_map/all_to_all | solution.py:243
  146.4 15.0 %all_to_all.21 = bf16[16,216,128]{2,1,0:T(8,128)(2,1)S(1)} all-to-all(bf16[16,216,128]{2,1,0:T(8,128)(2,1)S(1)} %broadcast_in_dim.5), channel_id=1, replica_groups=mesh['gx'=4,'gy'=8,'y'=4,'zh'=2,'core'=2] {'gx','y'}, dimensions={0} | all-to-all | bytes 1769472 | tf_op jit(solution)/shard_map/all_to_all | solution.py:243
  161.4 8.0 %collective-permute-start.11 = (bf16[3456,128]{1,0:T(8,128)(2,1)S(1)}, bf16[3456,128]{1,0:T(8,128)(2,1)S(1)}, u32[]{:S(2)}, u32[]{:S(2)}) collective-permute-start(bf16[3456,128]{1,0:T(8,128)(2,1)S(1)} %bitcast.53), channel_id=1, source_target_pairs={{0,1},{1,0},{2,3},{3,2},{4,5},{5,4},{6,7},{7,6},{8,9},{9,8},{10,11... | collective-permute-start | bytes 2654216 | tf_op jit(solution)/shard_map/ppermute | solution.py:355
  169.3 2.0 %collective-permute-done.11 = bf16[3456,128]{1,0:T(8,128)(2,1)S(1)} collective-permute-done((bf16[3456,128]{1,0:T(8,128)(2,1)S(1)}, bf16[3456,128]{1,0:T(8,128)(2,1)S(1)}, u32[]{:S(2)}, u32[]{:S(2)}) %collective-permute-start.11) | collective-permute-done | bytes 884768 | tf_op jit(solution)/shard_map/ppermute | solution.py:355
  (60 shorter events, 15.2 us)
Async XLA Ops:
  0.6 38.3 %copy-start.4 = (bf16[4,4,4,128]{3,2,1,0:T(4,128)(2,1)S(1)}, bf16[4,4,4,128]{3,2,1,0:T(4,128)(2,1)}, u32[]{:S(2)}) copy-start(bf16[4,4,4,128]{3,2,1,0:T(4,128)(2,1)} %param.7) | copy-start | bytes 49156
  1.6 18.9 %collective-permute-start.1 = (bf16[576,128]{1,0:T(8,128)(2,1)S(1)}, bf16[576,128]{1,0:T(8,128)(2,1)S(1)}, u32[]{:S(2)}, u32[]{:S(2)}) collective-permute-start(bf16[576,128]{1,0:T(8,128)(2,1)S(1)} %pad_maximum_fusion.3), channel_id=1, source_target_pairs={{0,1},{1,0},{2,3},{3,2},{4,5},{5,4},{6,7},{7,6},{8,9},{9,8},{10,11... | collective-permute-start | bytes 442376 | tf_op jit(solution)/shard_map/ppermute | solution.py:225
  10.4 15.5 %collective-permute-start = (bf16[576,128]{1,0:T(8,128)(2,1)S(1)}, bf16[576,128]{1,0:T(8,128)(2,1)S(1)}, u32[]{:S(2)}, u32[]{:S(2)}) collective-permute-start(bf16[576,128]{1,0:T(8,128)(2,1)S(1)} %pad_maximum_fusion.3), channel_id=1, source_target_pairs={{1,2},{2,1},{3,4},{4,3},{5,6},{6,5},{7,8},{8,7},{9,10},{10,9},{11,... | collective-permute-start | bytes 442376 | tf_op jit(solution)/shard_map/ppermute | solution.py:224
  25.9 19.7 %copy-start = (bf16[27,128,128]{2,1,0:T(8,128)(2,1)S(1)}, bf16[27,128,128]{2,1,0:T(8,128)(2,1)}, u32[]{:S(2)}) copy-start(bf16[27,128,128]{2,1,0:T(8,128)(2,1)} %weights.1) | copy-start | bytes 2654212
  27.0 12.4 %collective-permute-start.3 = (bf16[8,3,24,128]{3,2,1,0:T(8,128)(2,1)S(1)}, bf16[8,3,24,128]{3,2,1,0:T(8,128)(2,1)S(1)}, u32[]{:S(2)}, u32[]{:S(2)}) collective-permute-start(bf16[8,3,24,128]{3,2,1,0:T(8,128)(2,1)S(1)} %get-tuple-element.38), channel_id=1, source_target_pairs={{16,0},{32,16},{48,32},{64,48},{80,64},{96,80},{112,96},{17,1},{33... | collective-permute-start | bytes 442376 | tf_op jit(solution)/shard_map/ppermute | solution.py:219
  28.4 12.6 %collective-permute-start.2 = (bf16[8,3,24,128]{3,2,1,0:T(8,128)(2,1)S(1)}, bf16[8,3,24,128]{3,2,1,0:T(8,128)(2,1)S(1)}, u32[]{:S(2)}, u32[]{:S(2)}) collective-permute-start(bf16[8,3,24,128]{3,2,1,0:T(8,128)(2,1)S(1)} %get-tuple-element.39), channel_id=1, source_target_pairs={{0,16},{16,32},{32,48},{48,64},{64,80},{80,96},{96,112},{1,17},{17... | collective-permute-start | bytes 442376 | tf_op jit(solution)/shard_map/ppermute | solution.py:218
  41.1 8.6 %collective-permute-start.4 = (bf16[3,14,24,128]{3,2,1,0:T(8,128)(2,1)S(1)}, bf16[3,14,24,128]{3,2,1,0:T(8,128)(2,1)S(1)}, u32[]{:S(2)}, u32[]{:S(2)}) collective-permute-start(bf16[3,14,24,128]{3,2,1,0:T(8,128)(2,1)S(1)} %pad_maximum_fusion.1), channel_id=1, source_target_pairs={{0,128},{128,256},{256,384},{1,129},{129,257},{257,385},{2,130},{1... | collective-permute-start | bytes 774152 | tf_op jit(solution)/shard_map/ppermute | solution.py:218
  44.3 7.1 %collective-permute-start.5 = (bf16[3,14,24,128]{3,2,1,0:T(8,128)(2,1)S(1)}, bf16[3,14,24,128]{3,2,1,0:T(8,128)(2,1)S(1)}, u32[]{:S(2)}, u32[]{:S(2)}) collective-permute-start(bf16[3,14,24,128]{3,2,1,0:T(8,128)(2,1)S(1)} %pad_maximum_fusion.2), channel_id=1, source_target_pairs={{128,0},{256,128},{384,256},{129,1},{257,129},{385,257},{130,2},{2... | collective-permute-start | bytes 774152 | tf_op jit(solution)/shard_map/ppermute | solution.py:219
  45.6 5.7 %copy-start.1 = (bf16[27,128,128]{2,1,0:T(8,128)(2,1)S(1)}, bf16[27,128,128]{2,1,0:T(8,128)(2,1)}, u32[]{:S(2)}) copy-start(bf16[27,128,128]{2,1,0:T(8,128)(2,1)} %coarse_weights.3) | copy-start | bytes 2654212
  57.1 7.5 %copy-start.2 = (bf16[128,128]{1,0:T(8,128)(2,1)}, bf16[128,128]{1,0:T(8,128)(2,1)S(1)}, u32[]{:S(2)}) copy-start(bf16[128,128]{1,0:T(8,128)(2,1)S(1)} %get-tuple-element.19.grad_in) | copy-start | bytes 98308
  57.1 7.5 %copy-start.3 = (f32[128,128]{1,0:T(8,128)}, f32[128,128]{1,0:T(8,128)S(1)}, u32[]{:S(2)}) copy-start(f32[128,128]{1,0:T(8,128)S(1)} %get-tuple-element.30) | copy-start | bytes 196612
  57.1 7.4 %collective-permute-start.7 = (bf16[4,2,8,128]{3,2,1,0:T(8,128)(2,1)S(1)}, bf16[4,2,8,128]{3,2,1,0:T(8,128)(2,1)S(1)}, u32[]{:S(2)}, u32[]{:S(2)}) collective-permute-start(bf16[4,2,8,128]{3,2,1,0:T(8,128)(2,1)S(1)} %get-tuple-element.48), channel_id=1, source_target_pairs={{16,0},{32,16},{48,32},{64,48},{80,64},{96,80},{112,96},{17,1},{33... | collective-permute-start | bytes 49160 | tf_op jit(solution)/shard_map/ppermute | solution.py:219
  58.4 6.1 %collective-permute-start.6 = (bf16[4,2,8,128]{3,2,1,0:T(8,128)(2,1)S(1)}, bf16[4,2,8,128]{3,2,1,0:T(8,128)(2,1)S(1)}, u32[]{:S(2)}, u32[]{:S(2)}) collective-permute-start(bf16[4,2,8,128]{3,2,1,0:T(8,128)(2,1)S(1)} %get-tuple-element.49), channel_id=1, source_target_pairs={{0,16},{16,32},{32,48},{48,64},{64,80},{80,96},{96,112},{1,17},{17... | collective-permute-start | bytes 49160 | tf_op jit(solution)/shard_map/ppermute | solution.py:218
  64.5 1.4 copy-start.5
  64.6 7.5 %collective-permute-start.9 = (bf16[2,8,8,128]{3,2,1,0:T(8,128)(2,1)S(1)}, bf16[2,8,8,128]{3,2,1,0:T(8,128)(2,1)S(1)}, u32[]{:S(2)}, u32[]{:S(2)}) collective-permute-start(bf16[2,8,8,128]{3,2,1,0:T(8,128)(2,1)S(1)} %get-tuple-element.46), channel_id=1, source_target_pairs={{128,0},{256,128},{384,256},{129,1},{257,129},{385,257},{130,2},{2... | collective-permute-start | bytes 98312 | tf_op jit(solution)/shard_map/ppermute | solution.py:219
  65.9 6.2 %collective-permute-start.8 = (bf16[2,8,8,128]{3,2,1,0:T(8,128)(2,1)S(1)}, bf16[2,8,8,128]{3,2,1,0:T(8,128)(2,1)S(1)}, u32[]{:S(2)}, u32[]{:S(2)}) collective-permute-start(bf16[2,8,8,128]{3,2,1,0:T(8,128)(2,1)S(1)} %get-tuple-element.47), channel_id=1, source_target_pairs={{0,128},{128,256},{256,384},{1,129},{129,257},{257,385},{2,130},{1... | collective-permute-start | bytes 98312 | tf_op jit(solution)/shard_map/ppermute | solution.py:218
  72.1 5.7 %copy-start.6 = (bf16[2,8,8,128]{3,2,1,0:T(8,128)(2,1)}, bf16[2,8,8,128]{3,2,1,0:T(8,128)(2,1)S(1)}, u32[]{:S(2)}) copy-start(bf16[2,8,8,128]{3,2,1,0:T(8,128)(2,1)S(1)} %collective-permute-done.9) | copy-start | bytes 98308
  72.1 5.7 %copy-start.7 = (bf16[2,8,8,128]{3,2,1,0:T(8,128)(2,1)}, bf16[2,8,8,128]{3,2,1,0:T(8,128)(2,1)S(1)}, u32[]{:S(2)}) copy-start(bf16[2,8,8,128]{3,2,1,0:T(8,128)(2,1)S(1)} %collective-permute-done.8) | copy-start | bytes 98308
  72.2 4.3 %collective-permute-start.10 = (bf16[3456,128]{1,0:T(8,128)(2,1)S(1)}, bf16[3456,128]{1,0:T(8,128)(2,1)S(1)}, u32[]{:S(2)}, u32[]{:S(2)}) collective-permute-start(bf16[3456,128]{1,0:T(8,128)(2,1)S(1)} %broadcast_select_fusion.2), channel_id=1, source_target_pairs={{0,1},{1,0},{2,3},{3,2},{4,5},{5,4},{6,7},{7,6},{8,9},{9,8},{10,11... | collective-permute-start | bytes 2654216 | tf_op jit(solution)/shard_map/ppermute | solution.py:336
  77.8 26.1 %all-to-all-start = ((bf16[16,216,128]{2,1,0:T(8,128)(2,1)}), bf16[16,216,128]{2,1,0:T(8,128)(2,1)}, u32[]{:S(2)}, u32[]{:S(2)}) async-start(bf16[16,216,128]{2,1,0:T(8,128)(2,1)} %bitcast.52), calls=%async_computation | async-start | bytes 1769472 | tf_op jit(solution)/shard_map/all_to_all | solution.py:237
  105.9 26.1 %all-to-all-start.1 = ((bf16[16,16,128]{2,1,0:T(8,128)(2,1)}), bf16[16,16,128]{2,1,0:T(8,128)(2,1)S(1)}, u32[]{:S(2)}, u32[]{:S(2)}) async-start(bf16[16,16,128]{2,1,0:T(8,128)(2,1)} %bitcast.22), calls=%async_computation.1 | async-start | bytes 131072 | tf_op jit(solution)/shard_map/all_to_all | solution.py:237
  161.4 10.0 %collective-permute-start.11 = (bf16[3456,128]{1,0:T(8,128)(2,1)S(1)}, bf16[3456,128]{1,0:T(8,128)(2,1)S(1)}, u32[]{:S(2)}, u32[]{:S(2)}) collective-permute-start(bf16[3456,128]{1,0:T(8,128)(2,1)S(1)} %bitcast.53), channel_id=1, source_target_pairs={{0,1},{1,0},{2,3},{3,2},{4,5},{5,4},{6,7},{7,6},{8,9},{9,8},{10,11... | collective-permute-start | bytes 2654216 | tf_op jit(solution)/shard_map/ppermute | solution.py:355

commit v5 on v4

--- a/solution.py
+++ b/solution.py
@@ -93,15 +93,15 @@
 
 def front_kernel(
     fine_sizes, coarse_sizes, place, own, below, above, left, right, weights, coarse_weights, incoming, inner,
-    coarse_ref, grad_ref, slope_ref, pooled,
-    wide, patches, outer, pairs,
+    coarse_ref, grad_ref, slope_ref, fine_ref, coarse_sum_ref,
+    wide, patches, outer, pairs, pooled, grads, spread, shares, near,
 ):
+    order = [0, 1, 2, 3, 4, 10, 11, 12, 13, 5, 6, 7, 8, 9]
     for x in range(3):
         wide[x, :, :24] = left[x].astype(F32).reshape(14, 24, C)
-        wide[7 + x, :, :24] = right[x].astype(F32).reshape(14, 24, C)
-    for x in range(2):
-        fill(wide, 3 + x, x, own, below, above)
-        fill(wide, 5 + x, 6 + x, own, below, above)
+        wide[order[11 + x], :, :24] = right[x].astype(F32).reshape(14, 24, C)
+    for x in range(8):
+        fill(wide, order[3 + x], x, own, below, above)
     gather(wide, patches, 10, 1, 24)
     for part in range(2):
         outer[3 * part : 3 * part + 3] = fine_conv(patches, weights, 5 * part, 3)
@@ -127,14 +127,15 @@
 
     cells = [flat(pooled[i : i + 4, j : j + 4, k : k + 8]) for i, j, k in taps()]
     coarse = jnp.dot(
-        jnp.concatenate(cells, axis=1), coarse_weights[...], preferred_element_type=F32
+        jnp.concatenate(cells, axis=1),
+        coarse_weights[...].reshape(27 * C, C),
+        preferred_element_type=F32,
     )
     coarse_ref[...] = coarse
-    grad_ref[...] = (incoming[...] * silu_slope(coarse)).astype(BF16)
-
-
-def share_kernel(grad_in, pooled, coarse_weights, slope, turned_ref, sum_ref, grads, spread, shares):
-    grad = grad_in[...].astype(F32)
+    grad = (incoming[...] * silu_slope(coarse)).astype(BF16)
+    grad_ref[...] = grad
+    grad = grad.astype(F32)
+
     grads[...] = jnp.zeros((8, 8, 16, C), F32)
     grads[2:6, 2:6, :8] = grad.reshape(4, 4, 8, C)
     back = back_conv(grads, coarse_weights)
@@ -142,28 +143,23 @@
     spread[:, :, pl.ds(1, 8, 2)] = back
     for x in range(12):
         for y in range(12):
-            shares[x, y] = spread[x // 2, y // 2, 2:10] * slope[x, y, 6:14]
-    turned_ref[...] = shares[...].reshape(1152, C).T.astype(BF16)
+            shares[x, y] = spread[x // 2, y // 2, 2:10] * slope_ref[x, y, 6:14]
+    turned = shares[...].reshape(1152, C).T.astype(BF16)
+    for x in range(14):
+        for k in range(3):
+            line = wide[order[x], :, 7 + k : 15 + k]
+            for j in range(3):
+                at = (3 * j + k) * C
+                near[x, :, at : at + C] = flat(line[j : j + 12])
+    for i in range(3):
+        weight_terms(turned, near[i : i + 12].reshape(1152, 9 * C), fine_ref, 9 * i)
 
     at = lax.broadcasted_iota(jnp.int32, (C, C), 0) % 8
     turned = jnp.where((at >= 2) & (at < 6), grad, 0.0).T.astype(BF16)
     for i in range(3):
-        cells = [
-            flat(pooled[i : i + 4, j : j + 4, k : k + 8]) for j in range(3) for k in range(3)
-        ]
-        weight_terms(turned, jnp.concatenate(cells, axis=1), sum_ref, 9 * i)
-
-
-def fine_kernel(own, below, above, left, right, turned, sum_ref, wide, patches):
-    for x in range(8):
-        fill(wide, 3 + x, x, own, below, above)
-    for x in range(3):
-        wide[x, :, :24] = left[x].astype(F32).reshape(14, 24, C)
-        wide[11 + x, :, :24] = right[x].astype(F32).reshape(14, 24, C)
-    gather(wide, patches, 14, 7, 8)
-    shares = turned[...]
-    for i in range(3):
-        weight_terms(shares, patches[i : i + 12].reshape(1152, 9 * C), sum_ref, 9 * i)
+        weight_terms(
+            turned, jnp.concatenate(cells[9 * i : 9 * i + 9], axis=1), coarse_sum_ref, 9 * i
+        )
 
 
 def volume_kernel(around, coarse_weights, slope, weights, out_ref, grads, spread, fine):
@@ -261,7 +257,6 @@
     coarse_sizes = [4 * n for n in peers]
 
     fine_rows = fine_weight.reshape(27 * C, C)
-    coarse_rows = coarse_weight.reshape(27 * C, C)
 
     packed = jnp.concatenate([volume.reshape(512, C), cotangent.reshape(64, C)], axis=0)
     before, after = in_order(*along_width(packed, peers[2]))
@@ -291,41 +286,30 @@
         flops=2 * 1728 * 27 * C * C,
     )
     across = across + [left.reshape(3, 336, C), right.reshape(3, 336, C)]
-    coarse, coarse_grad, slope, pooled = call(
+    coarse, coarse_grad, slope, fine_sum, coarse_sum = call(
         lambda *refs: front_kernel(fine_sizes, coarse_sizes, *refs),
-        [((128, C), F32), ((128, C), BF16), ((12, 12, 24, C), F32), ((6, 6, 16, C), F32)],
-        [place, *across, fine_rows, coarse_rows, incoming.reshape(128, C), inner],
+        [
+            ((128, C), F32),
+            ((128, C), BF16),
+            ((12, 12, 24, C), F32),
+            ((27 * C, C), BF16),
+            ((27 * C, C), BF16),
+        ],
+        [place, *across, fine_rows, coarse_weight, incoming.reshape(128, C), inner],
         scratch=[
-            ((10, 14, 32, C), F32),
+            ((14, 14, 32, C), F32),
             ((10, 288, 9 * C), BF16),
             ((6, 12, 24, C), F32),
             ((6, 24, C), F32),
+            ((6, 6, 16, C), F32),
+            ((8, 8, 16, C), F32),
+            ((6, 6, 16, C), F32),
+            ((12, 12, 8, C), F32),
+            ((14, 96, 9 * C), BF16),
         ],
         scalars=1,
-        flops=2 * 1900 * 27 * C * C,
-    )
-
-    grads = coarse_grad.reshape(4, 4, 8, C)
-    halo = beside(grads[:, 2:], grads[:, :2], "gy", peers[1])
-    turned, coarse_sum = call(
-        share_kernel,
-        [((C, 1152), BF16), ((27 * C, C), BF16)],
-        [coarse_grad, pooled, coarse_weight, slope],
-        scratch=[((8, 8, 16, C), F32), ((6, 6, 16, C), F32), ((12, 12, 8, C), F32)],
-        flops=2 * 1000 * 27 * C * C,
-    )
-    halo, turned = lax.optimization_barrier((halo, turned))
-    grads = jnp.concatenate([halo[0], grads, halo[1]], axis=1)
-    halo = beside(grads[2:], grads[:2], "gx", peers[0])
-    (fine_sum,) = call(
-        fine_kernel,
-        [((27 * C, C), BF16)],
-        [*across, turned],
-        scratch=[((14, 14, 32, C), F32), ((14, 96, 9 * C), BF16)],
-        flops=2 * 1152 * 27 * C * C,
-    )
-    halo, fine_sum = lax.optimization_barrier((halo, fine_sum))
-    around = jnp.concatenate([halo[0], grads, halo[1]], axis=0)
+        flops=2 * 4000 * 27 * C * C,
+    )
 
     first = lax.axis_index("core") == 0
     swap = [(0, 1), (1, 0)]
@@ -335,7 +319,22 @@
     other = jnp.where(first, coarse_sum, fine_sum)
     mine = mine + lax.ppermute(other, "core", swap).astype(F32)
 
+    grads = coarse_grad.reshape(4, 4, 8, C)
+    halo = beside(grads[:, 2:], grads[:, :2], "gy", peers[1])
+    coarse_out = jax.nn.silu(coarse.reshape(4, 4, 8, C)[:, :, 2:6]).astype(BF16)
     parts = spread_rows(mine, PLANE, plane)
+    parts, halo, coarse_out = lax.optimization_barrier((parts, halo, coarse_out))
+    part = summed(parts)
+    length = part.shape[0]
+    padded = -(-length // (16 * along)) * 16 * along
+    part = jnp.pad(part, ((0, padded - length), (0, 0)))
+    part = (summed(spread_rows(part, LINE, along)) * scale).astype(BF16)
+    parts = gathered_rows(part, LINE, along)
+    parts, halo = lax.optimization_barrier((parts, halo))
+    part = joined(parts)[:length]
+    grads = jnp.concatenate([halo[0], grads, halo[1]], axis=1)
+    halo = beside(grads[2:], grads[:2], "gx", peers[0])
+    around = jnp.concatenate([halo[0], grads, halo[1]], axis=0)
     (grad_volume,) = call(
         volume_kernel,
         [((512, C), BF16)],
@@ -343,15 +342,9 @@
         scratch=[((8, 8, 16, C), F32), ((6, 6, 16, C), F32), ((10, 10, 16, C), F32)],
         flops=2 * 800 * 27 * C * C,
     )
-    coarse_out = jax.nn.silu(coarse.reshape(4, 4, 8, C)[:, :, 2:6]).astype(BF16)
-    parts, grad_volume, coarse_out = lax.optimization_barrier((parts, grad_volume, coarse_out))
-    part = summed(parts)
-    length = part.shape[0]
-    padded = -(-length // (16 * along)) * 16 * along
-    part = jnp.pad(part, ((0, padded - length), (0, 0)))
-    part = (summed(spread_rows(part, LINE, along)) * scale).astype(BF16)
-    part = joined(gathered_rows(part, LINE, along))[:length]
-    mine = joined(gathered_rows(part, PLANE, plane))
+    parts = gathered_rows(part, PLANE, plane)
+    parts, grad_volume = lax.optimization_barrier((parts, grad_volume))
+    mine = joined(parts)
     other = lax.ppermute(mine, "core", swap)
     fine_done = jnp.where(first, mine, other)
     coarse_done = jnp.where(first, other, mine)

time: 174 us -> 166 us (0.954)
  blocking collectives: 29.2 us -> 14.2 us
  other arithmetic: 8.58 us -> 11.9 us
  starting transfers between devices: 82.3 us -> 85.1 us
  local copies, waits for them, and re-layouts: 0.96 us -> 3.41 us
    all_to_all x2 -> x1, blocking collectives: 29.2 us -> 14.2 us  [gathered_rows(): return lax.all_to_all(parts, axes, 0, 0, tiled=True)]
    ppermute x1, starting transfers between devices: 8.79 us -> 1.92 us  [along_width(): inner = lax.ppermute(x, WIDTH, [(i, i ^ 1) for i in range(count)])]
    ppermute x1, starting transfers between devices: 9.97 us -> 16.8 us  [along_width(): lax.ppermute(x, WIDTH, [(i, i - 1 + 2 * (i % 2)) for i in range(1, count...]
    ppermute x4, waiting for transfers between devices: 2.11 us -> 7.29 us  [beside(): after = lax.ppermute(leading, axis, line(count, -1))]
    all_to_all x0 -> x1, starting transfers between devices: none -> 4.52 us  [gathered_rows(): return lax.all_to_all(parts, axes, 0, 0, tiled=True)]
    ppermute x1, waiting for transfers between devices: 5.41 us -> 1.82 us  [along_width(): lax.ppermute(x, WIDTH, [(i, i - 1 + 2 * (i % 2)) for i in range(1, count...]
    all_to_all x2, starting transfers between devices: 26.4 us -> 24.1 us  [spread_rows(): return lax.all_to_all(parts, axes, 0, 0, tiled=True)]
    all_to_all x2, waiting for transfers between devices: 20.3 us -> 18.1 us  [spread_rows(): return lax.all_to_all(parts, axes, 0, 0, tiled=True)]
  transfers between devices with their start and end apart: 14 -> 15, of which waited for: 8 -> 9; matrix products, arithmetic and copies ran while one was open for 1% -> 2% of each run, Pallas kernels for 6% -> 4%
where the time goes in v5:
time: 166 us; the launch traced here: 165 us
  starting transfers between devices  85.1 us (51%)
  waiting for transfers between devices  32.4 us (20%)
  Pallas kernels  17 us (10%)
  blocking collectives  14.2 us (9%)
  other arithmetic  11.9 us (7%)
  local copies, waits for them, and re-layouts  3.41 us (2%)
    all_to_all x2, starting transfers between devices, spread_rows(): return lax.all_to_all(parts, axes, 0, 0, tiled=True)  24.1 us
    ppermute x4, starting transfers between devices, beside(): before = lax.ppermute(last, axis, line(count, 1))  21.8 us
    all_to_all x2, waiting for transfers between devices, spread_rows(): return lax.all_to_all(parts, axes, 0, 0, tiled=True)  18.1 us
    pallas_call x3, Pallas kernels, call(): pl.pallas_call(kernel, out_shape=[jax.ShapeDtypeStruct(s, t) for s, t in...  17 us
    ppermute x1, starting transfers between devices, along_width(): lax.ppermute(x, WIDTH, [(i, i - 1 + 2 * (i % 2)) for i in range(1, count...  16.8 us
    all_to_all x1, blocking collectives, gathered_rows(): return lax.all_to_all(parts, axes, 0, 0, tiled=True)  14.2 us
    ppermute x1, starting transfers between devices, local(): other = lax.ppermute(mine, 'core', swap)  8.64 us
    ppermute x4, waiting for transfers between devices, beside(): after = lax.ppermute(leading, axis, line(count, -1))  7.29 us
  transfers between devices with their start and end apart: 15, of which 9 were waited for; matrix products, arithmetic and copies ran while one was open for 2% of the time, Pallas kernels for 4%

profile of v5, /device:TPU:1, one launch (start us, length us, event | category | flops | bytes accessed | tf_op | source)
XLA Modules:
  0.0 165.0 jit_solution(18053575397087664144)
XLA Ops:
  1.6 16.8 %collective-permute-start = (bf16[576,128]{1,0:T(8,128)(2,1)S(1)}, bf16[576,128]{1,0:T(8,128)(2,1)S(1)}, u32[]{:S(2)}, u32[]{:S(2)}) collective-permute-start(bf16[576,128]{1,0:T(8,128)(2,1)S(1)} %pad_maximum_fusion.3), channel_id=1, source_target_pairs={{1,2},{2,1},{3,4},{4,3},{5,6},{6,5},{7,8},{8,7},{9,10},{10,9},{11,... | collective-permute-start | bytes 442376 | tf_op jit(solution)/shard_map/ppermute | solution.py:220
  18.4 1.9 %collective-permute-start.1 = (bf16[576,128]{1,0:T(8,128)(2,1)S(1)}, bf16[576,128]{1,0:T(8,128)(2,1)S(1)}, u32[]{:S(2)}, u32[]{:S(2)}) collective-permute-start(bf16[576,128]{1,0:T(8,128)(2,1)S(1)} %pad_maximum_fusion.3), channel_id=1, source_target_pairs={{0,1},{1,0},{2,3},{3,2},{4,5},{5,4},{6,7},{7,6},{8,9},{9,8},{10,11... | collective-permute-start | bytes 442376 | tf_op jit(solution)/shard_map/ppermute | solution.py:221
  20.4 1.8 %collective-permute-done = bf16[576,128]{1,0:T(8,128)(2,1)S(1)} collective-permute-done((bf16[576,128]{1,0:T(8,128)(2,1)S(1)}, bf16[576,128]{1,0:T(8,128)(2,1)S(1)}, u32[]{:S(2)}, u32[]{:S(2)}) %collective-permute-start) | collective-permute-done | bytes 147488 | tf_op jit(solution)/shard_map/ppermute | solution.py:220
  23.4 11.6 %collective-permute-start.2 = (bf16[8,3,24,128]{3,2,1,0:T(8,128)(2,1)S(1)}, bf16[8,3,24,128]{3,2,1,0:T(8,128)(2,1)S(1)}, u32[]{:S(2)}, u32[]{:S(2)}) collective-permute-start(bf16[8,3,24,128]{3,2,1,0:T(8,128)(2,1)S(1)} %get-tuple-element.37), channel_id=1, source_target_pairs={{0,16},{16,32},{32,48},{48,64},{64,80},{80,96},{96,112},{1,17},{17... | collective-permute-start | bytes 442376 | tf_op jit(solution)/shard_map/ppermute | solution.py:214
  37.1 3.9 %collective-permute-done.3 = bf16[8,3,24,128]{3,2,1,0:T(8,128)(2,1)S(1)} collective-permute-done((bf16[8,3,24,128]{3,2,1,0:T(8,128)(2,1)S(1)}, bf16[8,3,24,128]{3,2,1,0:T(8,128)(2,1)S(1)}, u32[]{:S(2)}, u32[]{:S(2)}) %collective-permute-start.3) | collective-permute-done | bytes 147488 | tf_op jit(solution)/shard_map/ppermute | solution.py:215
  42.4 4.1 %collective-permute-start.4 = (bf16[3,14,24,128]{3,2,1,0:T(8,128)(2,1)S(1)}, bf16[3,14,24,128]{3,2,1,0:T(8,128)(2,1)S(1)}, u32[]{:S(2)}, u32[]{:S(2)}) collective-permute-start(bf16[3,14,24,128]{3,2,1,0:T(8,128)(2,1)S(1)} %pad_maximum_fusion.1), channel_id=1, source_target_pairs={{0,128},{128,256},{256,384},{1,129},{129,257},{257,385},{2,130},{1... | collective-permute-start | bytes 774152 | tf_op jit(solution)/shard_map/ppermute | solution.py:214
  46.5 4.1 %shard_map.75.refs_9_ = f32[6,12,24,128]{3,2,1,0:T(8,128)S(1)} custom-call(bf16[8,192,128]{2,1,0:T(8,128)(2,1)S(1)} %bitcast.30, bf16[8,72,128]{2,1,0:T(8,128)(2,1)S(1)} %bitcast.38, bf16[8,72,128]{2,1,0:T(8,128)(2,1)S(1)} %bitcast.40, bf16[3456,128]{1,0:T(8,128)(2,1)S(1)} %bitcast.32), custom_call_target="tpu_custom_call" | custom-call | flops 1528823808 | bytes 2457600 | tf_op jit(solution)/shard_map/pallas_call | solution.py:198
  50.6 9.7 %shard_map.76 = (f32[128,128]{1,0:T(8,128)S(1)}, bf16[128,128]{1,0:T(8,128)(2,1)S(1)}, f32[12,12,24,128]{3,2,1,0:T(8,128)S(1)}, bf16[3456,128]{1,0:T(8,128)(2,1)S(1)}, bf16[3456,128]{1,0:T(8,128)(2,1)S(1)}) custom-call(s32[3]{0:T(128)S(1)} %pad_add_fusion.refs_0_, bf16[8,192,128]{2,1,0:T(8,128)(2,1)S(1)} %bitcast.31, bf16[8,72,128]{2,1,0:T(8,128)(2,1)S(1)} %bitcast.39, ...), custom_call_target="tpu_custom_call" | custom-call | flops 3538944000 | bytes 7561228 | tf_op jit(solution)/shard_map/pallas_call | solution.py:198
  60.4 1.9 %collective-permute-start.6 = (bf16[3456,128]{1,0:T(8,128)(2,1)S(1)}, bf16[3456,128]{1,0:T(8,128)(2,1)S(1)}, u32[]{:S(2)}, u32[]{:S(2)}) collective-permute-start(bf16[3456,128]{1,0:T(8,128)(2,1)S(1)} %broadcast_select_fusion.2), channel_id=1, source_target_pairs={{0,1},{1,0},{2,3},{3,2},{4,5},{5,4},{6,7},{7,6},{8,9},{9,8},{10,11... | collective-permute-start | bytes 2654216 | tf_op jit(solution)/shard_map/ppermute | solution.py:320
  62.3 2.4 %collective-permute-done.6 = bf16[3456,128]{1,0:T(8,128)(2,1)S(1)} collective-permute-done((bf16[3456,128]{1,0:T(8,128)(2,1)S(1)}, bf16[3456,128]{1,0:T(8,128)(2,1)S(1)}, u32[]{:S(2)}, u32[]{:S(2)}) %collective-permute-start.6) | collective-permute-done | bytes 884768 | tf_op jit(solution)/shard_map/ppermute | solution.py:320
  65.9 11.1 %all-to-all-start = ((bf16[16,216,128]{2,1,0:T(8,128)(2,1)}), bf16[16,216,128]{2,1,0:T(8,128)(2,1)}, u32[]{:S(2)}, u32[]{:S(2)}) async-start(bf16[16,216,128]{2,1,0:T(8,128)(2,1)} %bitcast.45), calls=%async_computation | async-start | bytes 1769472 | tf_op jit(solution)/shard_map/all_to_all | solution.py:233
  77.8 2.2 %collective-permute-start.7 = (bf16[4,2,8,128]{3,2,1,0:T(8,128)(2,1)S(1)}, bf16[4,2,8,128]{3,2,1,0:T(8,128)(2,1)S(1)}, u32[]{:S(2)}, u32[]{:S(2)}) collective-permute-start(bf16[4,2,8,128]{3,2,1,0:T(8,128)(2,1)S(1)} %get-tuple-element.47), channel_id=1, source_target_pairs={{0,16},{16,32},{32,48},{48,64},{64,80},{80,96},{96,112},{1,17},{17... | collective-permute-start | bytes 49160 | tf_op jit(solution)/shard_map/ppermute | solution.py:214
  83.0 1.9 %collective-permute-done.8 = bf16[4,2,8,128]{3,2,1,0:T(8,128)(2,1)} collective-permute-done((bf16[4,2,8,128]{3,2,1,0:T(8,128)(2,1)S(1)}, bf16[4,2,8,128]{3,2,1,0:T(8,128)(2,1)}, u32[]{:S(2)}, u32[]{:S(2)}) %collective-permute-start.8) | collective-permute-done | bytes 16416 | tf_op jit(solution)/shard_map/ppermute | solution.py:215
  84.9 5.9 %all-to-all-done = bf16[16,216,128]{2,1,0:T(8,128)(2,1)} async-done(((bf16[16,216,128]{2,1,0:T(8,128)(2,1)}), bf16[16,216,128]{2,1,0:T(8,128)(2,1)}, u32[]{:S(2)}, u32[]{:S(2)}) %all-to-all-start) | async-done | bytes 884768 | tf_op jit(solution)/shard_map/all_to_all | solution.py:233
  90.8 1.9 %reduce = bf16[216,128]{1,0:T(8,128)(2,1)} reduce(bf16[16,216,128]{2,1,0:T(8,128)(2,1)} %all-to-all-done, bf16[]{:T(256)} %constant.35.clone.1), dimensions={0}, to_apply=%region_0.1.clone | reduce | flops 414720 | bytes 940034 | tf_op jit(solution)/shard_map/reduce_sum | solution.py:243
  94.2 13.0 %all-to-all-start.1 = ((bf16[16,16,128]{2,1,0:T(8,128)(2,1)}), bf16[16,16,128]{2,1,0:T(8,128)(2,1)}, u32[]{:S(2)}, u32[]{:S(2)}) async-start(bf16[16,16,128]{2,1,0:T(8,128)(2,1)} %bitcast.51), calls=%async_computation.1 | async-start | bytes 131072 | tf_op jit(solution)/shard_map/all_to_all | solution.py:233
  107.2 12.2 %all-to-all-done.1 = bf16[16,16,128]{2,1,0:T(8,128)(2,1)} async-done(((bf16[16,16,128]{2,1,0:T(8,128)(2,1)}), bf16[16,16,128]{2,1,0:T(8,128)(2,1)}, u32[]{:S(2)}, u32[]{:S(2)}) %all-to-all-start.1) | async-done | bytes 65568 | tf_op jit(solution)/shard_map/all_to_all | solution.py:233
  120.2 14.2 %all_to_all.20 = bf16[16,16,128]{2,1,0:T(8,128)(2,1)S(1)} all-to-all(bf16[16,16,128]{2,1,0:T(8,128)(2,1)S(1)} %broadcast_in_dim.4), channel_id=1, replica_groups=mesh['gx'=4,'gy'=8,'y'=4,'zh'=2,'core'=2] {'gy','zh'}, dimensions={0} | all-to-all | bytes 131072 | tf_op jit(solution)/shard_map/all_to_all | solution.py:239
  135.4 4.5 %all-to-all-start.3 = ((bf16[16,216,128]{2,1,0:T(8,128)(2,1)}), bf16[16,216,128]{2,1,0:T(8,128)(2,1)}, u32[]{:S(2)}, u32[]{:S(2)}) async-start(bf16[16,216,128]{2,1,0:T(8,128)(2,1)} %broadcast_in_dim.5), calls=%async_computation.3 | async-start | bytes 1769472 | tf_op jit(solution)/shard_map/all_to_all | solution.py:239
  142.1 4.0 %collective-permute-start.9 = (bf16[2,8,8,128]{3,2,1,0:T(8,128)(2,1)S(1)}, bf16[2,8,8,128]{3,2,1,0:T(8,128)(2,1)S(1)}, u32[]{:S(2)}, u32[]{:S(2)}) collective-permute-start(bf16[2,8,8,128]{3,2,1,0:T(8,128)(2,1)S(1)} %get-tuple-element.44), channel_id=1, source_target_pairs={{0,128},{128,256},{256,384},{1,129},{129,257},{257,385},{2,130},{1... | collective-permute-start | bytes 98312 | tf_op jit(solution)/shard_map/ppermute | solution.py:214
  148.4 3.3 %shard_map.77 = bf16[512,128]{1,0:T(8,128)(2,1)} custom-call(bf16[512,128]{1,0:T(8,128)(2,1)S(1)} %bitcast.34, bf16[27,128,128]{2,1,0:T(8,128)(2,1)S(1)} %copy-done.1, f32[12,12,24,128]{3,2,1,0:T(8,128)S(1)} %get-tuple-element.29.slope, bf16[27,128,128]{2,1,0:T(8,128)(2,1)S(1)} %copy-done), custom_call_target="tpu_custom_call" | custom-call | flops 707788800 | bytes 3801088 | tf_op jit(solution)/shard_map/pallas_call | solution.py:198
  151.6 8.6 %collective-permute-start.11 = (bf16[3456,128]{1,0:T(8,128)(2,1)}, bf16[3456,128]{1,0:T(8,128)(2,1)S(1)}, u32[]{:S(2)}, u32[]{:S(2)}) collective-permute-start(bf16[3456,128]{1,0:T(8,128)(2,1)} %bitcast.23), channel_id=1, source_target_pairs={{0,1},{1,0},{2,3},{3,2},{4,5},{5,4},{6,7},{7,6},{8,9},{9,8},{10,11... | collective-permute-start | bytes 2654216 | tf_op jit(solution)/shard_map/ppermute | solution.py:348
  160.3 2.2 %collective-permute-done.11 = bf16[3456,128]{1,0:T(8,128)(2,1)S(1)} collective-permute-done((bf16[3456,128]{1,0:T(8,128)(2,1)}, bf16[3456,128]{1,0:T(8,128)(2,1)S(1)}, u32[]{:S(2)}, u32[]{:S(2)}) %collective-permute-start.11) | collective-permute-done | bytes 884768 | tf_op jit(solution)/shard_map/ppermute | solution.py:348
  162.5 2.5 %broadcast_select_fusion = (bf16[3456,128]{1,0:T(8,128)(2,1)}, bf16[3456,128]{1,0:T(8,128)(2,1)}) fusion(bf16[3456,128]{1,0:T(8,128)(2,1)S(1)} %collective-permute-done.11, pred[]{:T(512)S(6)} %eq.4, bf16[16,216,128]{2,1,0:T(8,128)(2,1)} %all-to-all-done.3), kind=kLoop, calls=%fused_computation.1 | loop fusion | flops 884736 | bytes 3538945 | tf_op jit(solution)/shard_map/jit(_where)/select_n | solution.py:350
  (53 shorter events, 18.4 us)
Async XLA Ops:
  0.6 35.8 %copy-start.4 = (bf16[4,4,4,128]{3,2,1,0:T(4,128)(2,1)S(1)}, bf16[4,4,4,128]{3,2,1,0:T(4,128)(2,1)}, u32[]{:S(2)}) copy-start(bf16[4,4,4,128]{3,2,1,0:T(4,128)(2,1)} %param.7) | copy-start | bytes 49156
  1.6 20.7 %collective-permute-start = (bf16[576,128]{1,0:T(8,128)(2,1)S(1)}, bf16[576,128]{1,0:T(8,128)(2,1)S(1)}, u32[]{:S(2)}, u32[]{:S(2)}) collective-permute-start(bf16[576,128]{1,0:T(8,128)(2,1)S(1)} %pad_maximum_fusion.3), channel_id=1, source_target_pairs={{1,2},{2,1},{3,4},{4,3},{5,6},{6,5},{7,8},{8,7},{9,10},{10,9},{11,... | collective-permute-start | bytes 442376 | tf_op jit(solution)/shard_map/ppermute | solution.py:220
  18.4 3.8 %collective-permute-start.1 = (bf16[576,128]{1,0:T(8,128)(2,1)S(1)}, bf16[576,128]{1,0:T(8,128)(2,1)S(1)}, u32[]{:S(2)}, u32[]{:S(2)}) collective-permute-start(bf16[576,128]{1,0:T(8,128)(2,1)S(1)} %pad_maximum_fusion.3), channel_id=1, source_target_pairs={{0,1},{1,0},{2,3},{3,2},{4,5},{5,4},{6,7},{7,6},{8,9},{9,8},{10,11... | collective-permute-start | bytes 442376 | tf_op jit(solution)/shard_map/ppermute | solution.py:221
  22.3 24.1 %copy-start = (bf16[27,128,128]{2,1,0:T(8,128)(2,1)S(1)}, bf16[27,128,128]{2,1,0:T(8,128)(2,1)}, u32[]{:S(2)}) copy-start(bf16[27,128,128]{2,1,0:T(8,128)(2,1)} %weights.1) | copy-start | bytes 2654212
  23.4 13.7 %collective-permute-start.2 = (bf16[8,3,24,128]{3,2,1,0:T(8,128)(2,1)S(1)}, bf16[8,3,24,128]{3,2,1,0:T(8,128)(2,1)S(1)}, u32[]{:S(2)}, u32[]{:S(2)}) collective-permute-start(bf16[8,3,24,128]{3,2,1,0:T(8,128)(2,1)S(1)} %get-tuple-element.37), channel_id=1, source_target_pairs={{0,16},{16,32},{32,48},{48,64},{64,80},{80,96},{96,112},{1,17},{17... | collective-permute-start | bytes 442376 | tf_op jit(solution)/shard_map/ppermute | solution.py:214
  35.1 5.9 %collective-permute-start.3 = (bf16[8,3,24,128]{3,2,1,0:T(8,128)(2,1)S(1)}, bf16[8,3,24,128]{3,2,1,0:T(8,128)(2,1)S(1)}, u32[]{:S(2)}, u32[]{:S(2)}) collective-permute-start(bf16[8,3,24,128]{3,2,1,0:T(8,128)(2,1)S(1)} %get-tuple-element.36), channel_id=1, source_target_pairs={{16,0},{32,16},{48,32},{64,48},{80,64},{96,80},{112,96},{17,1},{33... | collective-permute-start | bytes 442376 | tf_op jit(solution)/shard_map/ppermute | solution.py:215
  41.0 9.5 %collective-permute-start.5 = (bf16[3,14,24,128]{3,2,1,0:T(8,128)(2,1)S(1)}, bf16[3,14,24,128]{3,2,1,0:T(8,128)(2,1)S(1)}, u32[]{:S(2)}, u32[]{:S(2)}) collective-permute-start(bf16[3,14,24,128]{3,2,1,0:T(8,128)(2,1)S(1)} %pad_maximum_fusion.2), channel_id=1, source_target_pairs={{128,0},{256,128},{384,256},{129,1},{257,129},{385,257},{130,2},{2... | collective-permute-start | bytes 774152 | tf_op jit(solution)/shard_map/ppermute | solution.py:215
  42.4 8.2 %collective-permute-start.4 = (bf16[3,14,24,128]{3,2,1,0:T(8,128)(2,1)S(1)}, bf16[3,14,24,128]{3,2,1,0:T(8,128)(2,1)S(1)}, u32[]{:S(2)}, u32[]{:S(2)}) collective-permute-start(bf16[3,14,24,128]{3,2,1,0:T(8,128)(2,1)S(1)} %pad_maximum_fusion.1), channel_id=1, source_target_pairs={{0,128},{128,256},{256,384},{1,129},{129,257},{257,385},{2,130},{1... | collective-permute-start | bytes 774152 | tf_op jit(solution)/shard_map/ppermute | solution.py:214
  46.5 4.1 %copy-start.1 = (bf16[27,128,128]{2,1,0:T(8,128)(2,1)S(1)}, bf16[27,128,128]{2,1,0:T(8,128)(2,1)}, u32[]{:S(2)}) copy-start(bf16[27,128,128]{2,1,0:T(8,128)(2,1)} %coarse_weights.1) | copy-start | bytes 2654212
  60.2 5.7 %copy-start.2 = (bf16[128,128]{1,0:T(8,128)(2,1)}, bf16[128,128]{1,0:T(8,128)(2,1)S(1)}, u32[]{:S(2)}) copy-start(bf16[128,128]{1,0:T(8,128)(2,1)S(1)} %get-tuple-element.20) | copy-start | bytes 98308
  60.2 5.7 %copy-start.3 = (f32[128,128]{1,0:T(8,128)}, f32[128,128]{1,0:T(8,128)S(1)}, u32[]{:S(2)}) copy-start(f32[128,128]{1,0:T(8,128)S(1)} %get-tuple-element.21) | copy-start | bytes 196612
  60.4 4.3 %collective-permute-start.6 = (bf16[3456,128]{1,0:T(8,128)(2,1)S(1)}, bf16[3456,128]{1,0:T(8,128)(2,1)S(1)}, u32[]{:S(2)}, u32[]{:S(2)}) collective-permute-start(bf16[3456,128]{1,0:T(8,128)(2,1)S(1)} %broadcast_select_fusion.2), channel_id=1, source_target_pairs={{0,1},{1,0},{2,3},{3,2},{4,5},{5,4},{6,7},{7,6},{8,9},{9,8},{10,11... | collective-permute-start | bytes 2654216 | tf_op jit(solution)/shard_map/ppermute | solution.py:320
  65.9 24.8 %all-to-all-start = ((bf16[16,216,128]{2,1,0:T(8,128)(2,1)}), bf16[16,216,128]{2,1,0:T(8,128)(2,1)}, u32[]{:S(2)}, u32[]{:S(2)}) async-start(bf16[16,216,128]{2,1,0:T(8,128)(2,1)} %bitcast.45), calls=%async_computation | async-start | bytes 1769472 | tf_op jit(solution)/shard_map/all_to_all | solution.py:233
  77.8 5.2 %collective-permute-start.7 = (bf16[4,2,8,128]{3,2,1,0:T(8,128)(2,1)S(1)}, bf16[4,2,8,128]{3,2,1,0:T(8,128)(2,1)S(1)}, u32[]{:S(2)}, u32[]{:S(2)}) collective-permute-start(bf16[4,2,8,128]{3,2,1,0:T(8,128)(2,1)S(1)} %get-tuple-element.47), channel_id=1, source_target_pairs={{0,16},{16,32},{32,48},{48,64},{64,80},{80,96},{96,112},{1,17},{17... | collective-permute-start | bytes 49160 | tf_op jit(solution)/shard_map/ppermute | solution.py:214
  80.0 4.9 %collective-permute-start.8 = (bf16[4,2,8,128]{3,2,1,0:T(8,128)(2,1)S(1)}, bf16[4,2,8,128]{3,2,1,0:T(8,128)(2,1)}, u32[]{:S(2)}, u32[]{:S(2)}) collective-permute-start(bf16[4,2,8,128]{3,2,1,0:T(8,128)(2,1)S(1)} %get-tuple-element.46), channel_id=1, source_target_pairs={{16,0},{32,16},{48,32},{64,48},{80,64},{96,80},{112,96},{17,1},{33... | collective-permute-start | bytes 49160 | tf_op jit(solution)/shard_map/ppermute | solution.py:215
  94.2 25.2 %all-to-all-start.1 = ((bf16[16,16,128]{2,1,0:T(8,128)(2,1)}), bf16[16,16,128]{2,1,0:T(8,128)(2,1)}, u32[]{:S(2)}, u32[]{:S(2)}) async-start(bf16[16,16,128]{2,1,0:T(8,128)(2,1)} %bitcast.51), calls=%async_computation.1 | async-start | bytes 131072 | tf_op jit(solution)/shard_map/all_to_all | solution.py:233
  135.4 16.2 %all-to-all-start.3 = ((bf16[16,216,128]{2,1,0:T(8,128)(2,1)}), bf16[16,216,128]{2,1,0:T(8,128)(2,1)}, u32[]{:S(2)}, u32[]{:S(2)}) async-start(bf16[16,216,128]{2,1,0:T(8,128)(2,1)} %broadcast_in_dim.5), calls=%async_computation.3 | async-start | bytes 1769472 | tf_op jit(solution)/shard_map/all_to_all | solution.py:239
  140.8 6.8 %collective-permute-start.10 = (bf16[2,8,8,128]{3,2,1,0:T(8,128)(2,1)S(1)}, bf16[2,8,8,128]{3,2,1,0:T(8,128)(2,1)S(1)}, u32[]{:S(2)}, u32[]{:S(2)}) collective-permute-start(bf16[2,8,8,128]{3,2,1,0:T(8,128)(2,1)S(1)} %get-tuple-element.45), channel_id=1, source_target_pairs={{128,0},{256,128},{384,256},{129,1},{257,129},{385,257},{130,2},{2... | collective-permute-start | bytes 98312 | tf_op jit(solution)/shard_map/ppermute | solution.py:215
  142.1 5.5 %collective-permute-start.9 = (bf16[2,8,8,128]{3,2,1,0:T(8,128)(2,1)S(1)}, bf16[2,8,8,128]{3,2,1,0:T(8,128)(2,1)S(1)}, u32[]{:S(2)}, u32[]{:S(2)}) collective-permute-start(bf16[2,8,8,128]{3,2,1,0:T(8,128)(2,1)S(1)} %get-tuple-element.44), channel_id=1, source_target_pairs={{0,128},{128,256},{256,384},{1,129},{129,257},{257,385},{2,130},{1... | collective-permute-start | bytes 98312 | tf_op jit(solution)/shard_map/ppermute | solution.py:214
  151.6 10.9 %collective-permute-start.11 = (bf16[3456,128]{1,0:T(8,128)(2,1)}, bf16[3456,128]{1,0:T(8,128)(2,1)S(1)}, u32[]{:S(2)}, u32[]{:S(2)}) collective-permute-start(bf16[3456,128]{1,0:T(8,128)(2,1)} %bitcast.23), channel_id=1, source_target_pairs={{0,1},{1,0},{2,3},{3,2},{4,5},{5,4},{6,7},{7,6},{8,9},{9,8},{10,11... | collective-permute-start | bytes 2654216 | tf_op jit(solution)/shard_map/ppermute | solution.py:348

commit v6 on v5

--- a/solution.py
+++ b/solution.py
@@ -54,27 +54,27 @@
     return back.reshape(6, 6, 8, C)
 
 
-def gather(wide, patches, planes, start, length):
+def gather(wide, patches, planes, columns=12):
     def plane(x, carry):
         for k in range(3):
-            line = wide[x, :, start + k : start + k + length]
+            line = wide[x, :, 1 + k : 25 + k]
             for j in range(3):
                 at = (3 * j + k) * C
-                patches[x, :, at : at + C] = flat(line[j : j + 12])
+                patches[x, :, at : at + C] = flat(line[j : j + columns])
         return carry
 
     lax.fori_loop(0, planes, plane, 0)
 
 
-def fine_conv(patches, weights, at, planes):
-    rows = planes * 288
+def fine_conv(patches, weights, at, planes, columns=12):
+    rows = planes * columns * 24
     total = jnp.zeros((rows, C), F32)
     for i in range(3):
         cells = patches[pl.ds(at + i, planes)].reshape(rows, 9 * C)
         total = total + jnp.dot(
             cells, weights[9 * C * i : 9 * C * (i + 1)], preferred_element_type=F32
         )
-    return total.reshape(planes, 12, 24, C)
+    return total.reshape(planes, columns, 24, C)
 
 
 def fill(wide, at, x, own, below, above):
@@ -83,16 +83,37 @@
     wide[at, 11:, :24] = above[x].astype(F32).reshape(3, 24, C)
 
 
-def inner_kernel(own, below, above, weights, hidden_ref, wide, patches):
+def middle_kernel(own, weights, hidden_ref, wide, patches):
     for x in range(8):
-        fill(wide, x, x, own, below, above)
-    gather(wide, patches, 8, 1, 24)
-    for part in range(2):
-        hidden_ref[3 * part : 3 * part + 3] = fine_conv(patches, weights, 3 * part, 3)
+        wide[x, :, :24] = own[x].astype(F32).reshape(8, 24, C)
+    gather(wide, patches, 8, 6)
+    hidden_ref[...] = fine_conv(patches, weights, 0, 6, 6)
+
+
+def sides_kernel(own, below, above, weights, hidden_ref, wide, patches):
+    for x in range(8):
+        rows = own[x].astype(F32).reshape(8, 24, C)
+        wide[x, :3, :24] = below[x].astype(F32).reshape(3, 24, C)
+        wide[x, 3:5, :24] = rows[:2]
+        wide[x, 5:7, :24] = rows[6:]
+        wide[x, 7:, :24] = above[x].astype(F32).reshape(3, 24, C)
+
+    def plane(x, carry):
+        for k in range(3):
+            line = wide[x, :, 1 + k : 25 + k]
+            for j in range(3):
+                at = (3 * j + k) * C
+                cells = jnp.concatenate([line[j : j + 3], line[5 + j : 8 + j]], axis=0)
+                patches[x, :, at : at + C] = flat(cells)
+        return carry
+
+    lax.fori_loop(0, 8, plane, 0)
+    hidden_ref[...] = fine_conv(patches, weights, 0, 6, 6)
 
 
 def front_kernel(
-    fine_sizes, coarse_sizes, place, own, below, above, left, right, weights, coarse_weights, incoming, inner,
+    fine_sizes, coarse_sizes, place, own, below, above, left, right, weights, coarse_weights, incoming,
+    middle, sides,
     coarse_ref, grad_ref, slope_ref, fine_ref, coarse_sum_ref,
     wide, patches, outer, pairs, pooled, grads, spread, shares, near,
 ):
@@ -102,14 +123,18 @@
         wide[order[11 + x], :, :24] = right[x].astype(F32).reshape(14, 24, C)
     for x in range(8):
         fill(wide, order[3 + x], x, own, below, above)
-    gather(wide, patches, 10, 1, 24)
+    gather(wide, patches, 10)
     for part in range(2):
         outer[3 * part : 3 * part + 3] = fine_conv(patches, weights, 5 * part, 3)
 
     for x in range(6):
         active = None
         for at in (2 * x, 2 * x + 1):
-            value = inner[at - 3] if 3 <= at < 9 else outer[at if at < 3 else at - 6]
+            if 3 <= at < 9:
+                edges = sides[at - 3]
+                value = jnp.concatenate([edges[:3], middle[at - 3], edges[3:]], axis=0)
+            else:
+                value = outer[at if at < 3 else at - 6]
             sigma = 1.0 / (1.0 + jnp.exp(-value))
             slope = sigma * (1.0 + value * (1.0 - sigma)) * 0.125
             starts = [8 * place[0] - 2 + at, 8 * place[1] - 2, 8 * place[2] - 6]
@@ -188,6 +213,57 @@
     out_ref[...] = total.astype(BF16)
 
 
+def plane_sum_kernel(parts, out_ref):
+    total = parts[0].astype(F32)
+    for at in range(1, parts.shape[0]):
+        total = total + parts[at].astype(F32)
+    rows = out_ref.shape[0] - total.shape[0]
+    out_ref[...] = jnp.concatenate([total, jnp.zeros((rows, C), F32)], axis=0).astype(BF16)
+
+
+def line_sum_kernel(scale, parts, out_ref):
+    total = parts[0].astype(F32)
+    for at in range(1, parts.shape[0]):
+        total = total + parts[at].astype(F32)
+    total = (total * scale[0]).astype(BF16)
+    for at in range(out_ref.shape[0]):
+        out_ref[at] = total
+
+
+def keep_kernel(core, mine, fine_ref, coarse_ref, done):
+    for at, ref in ((0, fine_ref), (1, coarse_ref)):
+
+        @pl.when(core[0] == at)
+        def _(ref=ref):
+            copy = pltpu.make_async_copy(mine, ref, done)
+            copy.start()
+            copy.wait()
+
+
+def take_kernel(core, other, fine_in, coarse_in, fine_ref, coarse_ref, done):
+    for at, ref in ((1, fine_ref), (0, coarse_ref)):
+
+        @pl.when(core[0] == at)
+        def _(ref=ref):
+            copy = pltpu.make_async_copy(other, ref, done)
+            copy.start()
+            copy.wait()
+
+
+def copies(kernel, inputs, aliases):
+    shape = jax.ShapeDtypeStruct((27 * C, C), BF16)
+    return pl.pallas_call(
+        kernel,
+        out_shape=[shape, shape],
+        in_specs=[pl.BlockSpec(memory_space=pltpu.SMEM)]
+        + [pl.BlockSpec(memory_space=pl.ANY) for _ in inputs[1:]],
+        out_specs=[pl.BlockSpec(memory_space=pl.ANY) for _ in range(2)],
+        scratch_shapes=[pltpu.SemaphoreType.DMA],
+        input_output_aliases=aliases,
+        cost_estimate=pl.CostEstimate(flops=0, bytes_accessed=2 * 27 * C * C * 2, transcendentals=0),
+    )(*inputs)
+
+
 def call(kernel, outs, inputs, scratch=(), scalars=0, flops=0):
     in_specs = [
         pl.BlockSpec(memory_space=pltpu.SMEM if n < scalars else pltpu.VMEM)
@@ -227,20 +303,8 @@
     return jnp.where(first, outer, inner), jnp.where(first, inner, outer)
 
 
-def spread_rows(terms, axes, peers):
-    rows = terms.shape[0]
-    parts = terms.astype(BF16).reshape(peers, rows // peers, C)
+def exchanged(parts, axes):
     return lax.all_to_all(parts, axes, 0, 0, tiled=True)
-
-
-def gathered_rows(part, axes, peers):
-    rows = part.shape[0]
-    parts = jnp.broadcast_to(part[None], (peers, rows, C))
-    return lax.all_to_all(parts, axes, 0, 0, tiled=True)
-
-
-def summed(parts):
-    return jnp.sum(parts.astype(F32), axis=0)
 
 
 def joined(parts):
@@ -251,7 +315,7 @@
     sizes = {axis: lax.axis_size(axis) for axis in AXES}
     plane, along = (sizes["gx"] * sizes["y"], sizes["gy"] * sizes["zh"])
     peers = [sizes["gx"], sizes["gy"], sizes["y"] * sizes["zh"] * 2]
-    place = [lax.axis_index("gx"), lax.axis_index("gy"), lax.axis_index(WIDTH)]
+    place = [lax.axis_index(axis) for axis in ("gx", "gy", WIDTH, "core")]
     place = jnp.stack([p.astype(jnp.int32) for p in place])
     fine_sizes = [8 * n for n in peers]
     coarse_sizes = [4 * n for n in peers]
@@ -260,9 +324,13 @@
 
     packed = jnp.concatenate([volume.reshape(512, C), cotangent.reshape(64, C)], axis=0)
     before, after = in_order(*along_width(packed, peers[2]))
-    own = jnp.concatenate(
-        [before[:512].reshape(8, 8, 8, C), volume, after[:512].reshape(8, 8, 8, C)], axis=2
-    )
+    before_cells, after_cells = (b[:512].reshape(8, 8, 8, C) for b in (before, after))
+    slabs = [
+        jnp.concatenate([before_cells[:, at], volume[:, at], after_cells[:, at]], axis=2)
+        for at in (slice(5, 8), slice(0, 3))
+    ]
+    below, above = beside(slabs[0], slabs[1], "gy", peers[1])
+    own = jnp.concatenate([before_cells, volume, after_cells], axis=2)
     incoming = jnp.concatenate(
         [
             before[512:].reshape(4, 4, 4, C)[:, :, 2:],
@@ -271,19 +339,25 @@
         ],
         axis=2,
     ).astype(F32)
-    below, above = beside(own[:, 5:], own[:, :3], "gy", peers[1])
     sides = [
         jnp.concatenate([below[at], own[at], above[at]], axis=1)
         for at in (slice(5, 8), slice(0, 3))
     ]
     left, right = beside(sides[0], sides[1], "gx", peers[0])
+    (middle,) = call(
+        middle_kernel,
+        [((6, 6, 24, C), F32)],
+        [own.reshape(8, 192, C), fine_rows],
+        scratch=[((8, 8, 32, C), F32), ((8, 144, 9 * C), BF16)],
+        flops=2 * 864 * 27 * C * C,
+    )
     across = [own.reshape(8, 192, C), below.reshape(8, 72, C), above.reshape(8, 72, C)]
-    (inner,) = call(
-        inner_kernel,
-        [((6, 12, 24, C), F32)],
+    (edges,) = call(
+        sides_kernel,
+        [((6, 6, 24, C), F32)],
         across + [fine_rows],
-        scratch=[((8, 14, 32, C), F32), ((8, 288, 9 * C), BF16)],
-        flops=2 * 1728 * 27 * C * C,
+        scratch=[((8, 10, 32, C), F32), ((8, 144, 9 * C), BF16)],
+        flops=2 * 864 * 27 * C * C,
     )
     across = across + [left.reshape(3, 336, C), right.reshape(3, 336, C)]
     coarse, coarse_grad, slope, fine_sum, coarse_sum = call(
@@ -295,7 +369,7 @@
             ((27 * C, C), BF16),
             ((27 * C, C), BF16),
         ],
-        [place, *across, fine_rows, coarse_weight, incoming.reshape(128, C), inner],
+        [place, *across, fine_rows, coarse_weight, incoming.reshape(128, C), middle, edges],
         scratch=[
             ((14, 14, 32, C), F32),
             ((10, 288, 9 * C), BF16),
@@ -315,6 +389,7 @@
     swap = [(0, 1), (1, 0)]
     cells_fine = fine_sizes[0] * fine_sizes[1] * fine_sizes[2]
     scale = jnp.where(first, 1.0 / math.sqrt(cells_fine), 1.0 / math.sqrt(cells_fine // 8))
+    scale = scale.astype(F32).reshape(1)
     mine = jnp.where(first, fine_sum, coarse_sum).astype(F32)
     other = jnp.where(first, coarse_sum, fine_sum)
     mine = mine + lax.ppermute(other, "core", swap).astype(F32)
@@ -322,14 +397,14 @@
     grads = coarse_grad.reshape(4, 4, 8, C)
     halo = beside(grads[:, 2:], grads[:, :2], "gy", peers[1])
     coarse_out = jax.nn.silu(coarse.reshape(4, 4, 8, C)[:, :, 2:6]).astype(BF16)
-    parts = spread_rows(mine, PLANE, plane)
+    parts = exchanged(mine.astype(BF16).reshape(plane, -1, C), PLANE)
     parts, halo, coarse_out = lax.optimization_barrier((parts, halo, coarse_out))
-    part = summed(parts)
-    length = part.shape[0]
+    length = parts.shape[1]
     padded = -(-length // (16 * along)) * 16 * along
-    part = jnp.pad(part, ((0, padded - length), (0, 0)))
-    part = (summed(spread_rows(part, LINE, along)) * scale).astype(BF16)
-    parts = gathered_rows(part, LINE, along)
+    (part,) = call(plane_sum_kernel, [((padded, C), BF16)], [parts])
+    parts = exchanged(part.reshape(along, padded // along, C), LINE)
+    (parts,) = call(line_sum_kernel, [(parts.shape, BF16)], [scale, parts], scalars=1)
+    parts = exchanged(parts, LINE)
     parts, halo = lax.optimization_barrier((parts, halo))
     part = joined(parts)[:length]
     grads = jnp.concatenate([halo[0], grads, halo[1]], axis=1)
@@ -342,12 +417,15 @@
         scratch=[((8, 8, 16, C), F32), ((6, 6, 16, C), F32), ((10, 10, 16, C), F32)],
         flops=2 * 800 * 27 * C * C,
     )
-    parts = gathered_rows(part, PLANE, plane)
+    parts = exchanged(jnp.broadcast_to(part[None], (plane, length, C)), PLANE)
     parts, grad_volume = lax.optimization_barrier((parts, grad_volume))
     mine = joined(parts)
     other = lax.ppermute(mine, "core", swap)
-    fine_done = jnp.where(first, mine, other)
-    coarse_done = jnp.where(first, other, mine)
+    core = place[3:]
+    fine_done, coarse_done = copies(keep_kernel, [core, mine], {})
+    fine_done, coarse_done = copies(
+        take_kernel, [core, other, fine_done, coarse_done], {2: 0, 3: 1}
+    )
     return (
         coarse_out,
         grad_volume.reshape(8, 8, 8, C),

time: 166 us -> 213 us (1.28)
  Pallas kernels: 17 us -> 73.1 us
  waiting for transfers between devices: 32.4 us -> 24 us
  other arithmetic: 11.9 us -> 5.75 us
  starting transfers between devices: 85.1 us -> 89.3 us
    pallas_call x0 -> x2, Pallas kernels: none -> 55.8 us  [copies(): pl.pallas_call(kernel, out_shape=[shape, shape], in_specs=[pl.BlockSpec(m...]
    ppermute x4, waiting for transfers between devices: 7.29 us -> 3.51 us  [beside(): after = lax.ppermute(leading, axis, line(count, -1))]
    reduce_sum x2 -> x0, other arithmetic: 2.78 us -> none  [summed(): return jnp.sum(parts.astype(F32), axis=0)]
    ppermute x4, starting transfers between devices: 21.8 us -> 24.6 us  [beside(): before = lax.ppermute(last, axis, line(count, 1))]
    select_n x1 -> x0, other arithmetic: 2.49 us -> none  [local(): coarse_done = jnp.where(first, other, mine)]
    ppermute x1, waiting for transfers between devices: 2.24 us -> 0.01 us  [local(): other = lax.ppermute(mine, 'core', swap)]
    pallas_call x3 -> x6, Pallas kernels: 17 us -> 17.3 us  [call(): pl.pallas_call(kernel, out_shape=[jax.ShapeDtypeStruct(s, t) for s, t in...]
  transfers between devices with their start and end apart: 15 -> 15, of which waited for: 9 -> 7; matrix products, arithmetic and copies ran while one was open for 2% -> 2% of each run, Pallas kernels for 4% -> 17%
where the time goes in v6:
time: 213 us; the launch traced here: 212 us
  starting transfers between devices  89.3 us (42%)
  Pallas kernels  73.1 us (34%)
  waiting for transfers between devices  24 us (11%)
  blocking collectives  14.3 us (7%)
  other arithmetic  5.75 us (3%)
  local copies, waits for them, and re-layouts  4.34 us (2%)
    pallas_call x2, Pallas kernels, copies(): pl.pallas_call(kernel, out_shape=[shape, shape], in_specs=[pl.BlockSpec(m...  55.8 us
    all_to_all x3, starting transfers between devices, exchanged(): return lax.all_to_all(parts, axes, 0, 0, tiled=True)  30.1 us
    ppermute x4, starting transfers between devices, beside(): before = lax.ppermute(last, axis, line(count, 1))  24.6 us
    pallas_call x6, Pallas kernels, call(): pl.pallas_call(kernel, out_shape=[jax.ShapeDtypeStruct(s, t) for s, t in...  17.3 us
    ppermute x1, starting transfers between devices, along_width(): lax.ppermute(x, WIDTH, [(i, i - 1 + 2 * (i % 2)) for i in range(1, count...  16.8 us
    all_to_all x3, waiting for transfers between devices, exchanged(): return lax.all_to_all(parts, axes, 0, 0, tiled=True)  16 us
    all_to_all x1, blocking collectives, exchanged(): return lax.all_to_all(parts, axes, 0, 0, tiled=True)  14.3 us
    ppermute x1, starting transfers between devices, local(): other = lax.ppermute(mine, 'core', swap)  8.64 us
  transfers between devices with their start and end apart: 15, of which 7 were waited for; matrix products, arithmetic and copies ran while one was open for 2% of the time, Pallas kernels for 17%

profile of v6, /device:TPU:1, one launch (start us, length us, event | category | flops | bytes accessed | tf_op | source)
XLA Modules:
  0.0 212.1 jit_solution(18054964861487705728)
XLA Ops:
  1.6 16.8 %collective-permute-start = (bf16[576,128]{1,0:T(8,128)(2,1)S(1)}, bf16[576,128]{1,0:T(8,128)(2,1)S(1)}, u32[]{:S(2)}, u32[]{:S(2)}) collective-permute-start(bf16[576,128]{1,0:T(8,128)(2,1)S(1)} %pad_maximum_fusion.3), channel_id=1, source_target_pairs={{1,2},{2,1},{3,4},{4,3},{5,6},{6,5},{7,8},{8,7},{9,10},{10,9},{11,... | collective-permute-start | bytes 442376 | tf_op jit(solution)/shard_map/ppermute | solution.py:296
  18.5 1.9 collective-permute-start.1
  23.9 12.3 %collective-permute-start.2 = (bf16[8,3,24,128]{3,2,1,0:T(8,128)(2,1)S(1)}, bf16[8,3,24,128]{3,2,1,0:T(8,128)(2,1)S(1)}, u32[]{:S(2)}, u32[]{:S(2)}) collective-permute-start(bf16[8,3,24,128]{3,2,1,0:T(8,128)(2,1)S(1)} %pad_maximum_fusion.4), channel_id=1, source_target_pairs={{0,16},{16,32},{32,48},{48,64},{64,80},{80,96},{96,112},{1,17},{17... | collective-permute-start | bytes 442376 | tf_op jit(solution)/shard_map/ppermute | solution.py:290
  36.2 2.1 shard_map.75.refs_9_
  40.1 4.0 %collective-permute-start.4 = (bf16[3,14,24,128]{3,2,1,0:T(8,128)(2,1)S(1)}, bf16[3,14,24,128]{3,2,1,0:T(8,128)(2,1)S(1)}, u32[]{:S(2)}, u32[]{:S(2)}) collective-permute-start(bf16[3,14,24,128]{3,2,1,0:T(8,128)(2,1)S(1)} %pad_maximum_fusion.1), channel_id=1, source_target_pairs={{0,128},{128,256},{256,384},{1,129},{129,257},{257,385},{2,130},{1... | collective-permute-start | bytes 774152 | tf_op jit(solution)/shard_map/ppermute | solution.py:290
  44.1 2.1 %shard_map.76.refs_10_ = f32[6,6,24,128]{3,2,1,0:T(8,128)S(1)} custom-call(bf16[8,192,128]{2,1,0:T(8,128)(2,1)S(1)} %bitcast.31, bf16[8,72,128]{2,1,0:T(8,128)(2,1)S(1)} %bitcast.43, bf16[8,72,128]{2,1,0:T(8,128)(2,1)S(1)} %bitcast.41, bf16[3456,128]{1,0:T(8,128)(2,1)S(1)} %bitcast.34), custom_call_target="tpu_custom_call" | custom-call | flops 764411904 | bytes 2015232 | tf_op jit(solution)/shard_map/pallas_call | solution.py:274
  47.3 9.7 %shard_map.77 = (f32[128,128]{1,0:T(8,128)S(1)}, bf16[128,128]{1,0:T(8,128)(2,1)S(1)}, f32[12,12,24,128]{3,2,1,0:T(8,128)S(1)}, bf16[3456,128]{1,0:T(8,128)(2,1)S(1)}, bf16[3456,128]{1,0:T(8,128)(2,1)S(1)}) custom-call(s32[4]{0:T(128)S(1)} %pad_add_fusion.refs_0_, bf16[8,192,128]{2,1,0:T(8,128)(2,1)S(1)} %bitcast.32, bf16[8,72,128]{2,1,0:T(8,128)(2,1)S(1)} %bitcast.44, ...), custom_call_target="tpu_custom_call" | custom-call | flops 3538944000 | bytes 7561232 | tf_op jit(solution)/shard_map/pallas_call | solution.py:274
  57.1 1.9 collective-permute-start.6
  59.0 2.4 %collective-permute-done.6 = bf16[3456,128]{1,0:T(8,128)(2,1)S(1)} collective-permute-done((bf16[3456,128]{1,0:T(8,128)(2,1)S(1)}, bf16[3456,128]{1,0:T(8,128)(2,1)S(1)}, u32[]{:S(2)}, u32[]{:S(2)}) %collective-permute-start.6) | collective-permute-done | bytes 884768 | tf_op jit(solution)/shard_map/ppermute | solution.py:395
  62.7 11.6 %all-to-all-start = ((bf16[16,216,128]{2,1,0:T(8,128)(2,1)}), bf16[16,216,128]{2,1,0:T(8,128)(2,1)S(1)}, u32[]{:S(2)}, u32[]{:S(2)}) async-start(bf16[16,216,128]{2,1,0:T(8,128)(2,1)} %bitcast.48), calls=%async_computation | async-start | bytes 1769472 | tf_op jit(solution)/shard_map/all_to_all | solution.py:307
  75.1 4.3 %collective-permute-start.7 = (bf16[4,2,8,128]{3,2,1,0:T(8,128)(2,1)S(1)}, bf16[4,2,8,128]{3,2,1,0:T(8,128)(2,1)S(1)}, u32[]{:S(2)}, u32[]{:S(2)}) collective-permute-start(bf16[4,2,8,128]{3,2,1,0:T(8,128)(2,1)S(1)} %get-tuple-element.57), channel_id=1, source_target_pairs={{0,16},{16,32},{32,48},{48,64},{64,80},{80,96},{96,112},{1,17},{17... | collective-permute-start | bytes 49160 | tf_op jit(solution)/shard_map/ppermute | solution.py:290
  80.7 1.5 fusion
  82.2 2.0 collective-permute-done.8
  84.2 3.9 %all-to-all-done.parts = bf16[16,216,128]{2,1,0:T(8,128)(2,1)S(1)} async-done(((bf16[16,216,128]{2,1,0:T(8,128)(2,1)}), bf16[16,216,128]{2,1,0:T(8,128)(2,1)S(1)}, u32[]{:S(2)}, u32[]{:S(2)}) %all-to-all-start) | async-done | bytes 884768 | tf_op jit(solution)/shard_map/all_to_all | solution.py:307
  88.8 14.0 %all-to-all-start.1 = ((bf16[16,16,128]{2,1,0:T(8,128)(2,1)}), bf16[16,16,128]{2,1,0:T(8,128)(2,1)S(1)}, u32[]{:S(2)}, u32[]{:S(2)}) async-start(bf16[16,16,128]{2,1,0:T(8,128)(2,1)} %bitcast.40), calls=%async_computation.1 | async-start | bytes 131072 | tf_op jit(solution)/shard_map/all_to_all | solution.py:307
  102.8 12.1 %all-to-all-done.1.parts = bf16[16,16,128]{2,1,0:T(8,128)(2,1)S(1)} async-done(((bf16[16,16,128]{2,1,0:T(8,128)(2,1)}), bf16[16,16,128]{2,1,0:T(8,128)(2,1)S(1)}, u32[]{:S(2)}, u32[]{:S(2)}) %all-to-all-start.1) | async-done | bytes 65568 | tf_op jit(solution)/shard_map/all_to_all | solution.py:307
  114.9 14.3 %all_to_all.20 = bf16[16,16,128]{2,1,0:T(8,128)(2,1)S(1)} all-to-all(bf16[16,16,128]{2,1,0:T(8,128)(2,1)S(1)} %shard_map.79), channel_id=1, replica_groups=mesh['gx'=4,'gy'=8,'y'=4,'zh'=2,'core'=2] {'gy','zh'}, dimensions={0} | all-to-all | bytes 131072 | tf_op jit(solution)/shard_map/all_to_all | solution.py:307
  130.3 4.5 %all-to-all-start.3 = ((bf16[16,216,128]{2,1,0:T(8,128)(2,1)}), bf16[16,216,128]{2,1,0:T(8,128)(2,1)}, u32[]{:S(2)}, u32[]{:S(2)}) async-start(bf16[16,216,128]{2,1,0:T(8,128)(2,1)} %broadcast_in_dim.2), calls=%async_computation.3 | async-start | bytes 1769472 | tf_op jit(solution)/shard_map/all_to_all | solution.py:307
  136.9 4.0 %collective-permute-start.9 = (bf16[2,8,8,128]{3,2,1,0:T(8,128)(2,1)S(1)}, bf16[2,8,8,128]{3,2,1,0:T(8,128)(2,1)S(1)}, u32[]{:S(2)}, u32[]{:S(2)}) collective-permute-start(bf16[2,8,8,128]{3,2,1,0:T(8,128)(2,1)S(1)} %get-tuple-element.54), channel_id=1, source_target_pairs={{0,128},{128,256},{256,384},{1,129},{129,257},{257,385},{2,130},{1... | collective-permute-start | bytes 98312 | tf_op jit(solution)/shard_map/ppermute | solution.py:290
  140.9 1.5 collective-permute-done.10
  143.2 3.3 %shard_map.80 = bf16[512,128]{1,0:T(8,128)(2,1)} custom-call(bf16[512,128]{1,0:T(8,128)(2,1)S(1)} %bitcast.36, bf16[27,128,128]{2,1,0:T(8,128)(2,1)S(1)} %copy-done.2, f32[12,12,24,128]{3,2,1,0:T(8,128)S(1)} %get-tuple-element.33.slope, bf16[27,128,128]{2,1,0:T(8,128)(2,1)S(1)} %copy-done), custom_call_target="tpu_custom_call" | custom-call | flops 707788800 | bytes 3801088 | tf_op jit(solution)/shard_map/pallas_call | solution.py:274
  146.5 8.6 %collective-permute-start.11 = (bf16[3456,128]{1,0:T(8,128)(2,1)}, bf16[3456,128]{1,0:T(8,128)(2,1)S(1)}, u32[]{:S(2)}, u32[]{:S(2)}) collective-permute-start(bf16[3456,128]{1,0:T(8,128)(2,1)} %bitcast.25.mine), channel_id=1, source_target_pairs={{0,1},{1,0},{2,3},{3,2},{4,5},{5,4},{6,7},{7,6},{8,9},{9,8},{10,11... | collective-permute-start | bytes 2654216 | tf_op jit(solution)/shard_map/ppermute | solution.py:423
  155.1 27.9 %shard_map.81 = (bf16[3456,128]{1,0:T(8,128)(2,1)}, bf16[3456,128]{1,0:T(8,128)(2,1)}) custom-call(s32[1]{0:T(128)} %bitcast.3.core, bf16[3456,128]{1,0:T(8,128)(2,1)} %bitcast.25.mine), custom_call_target="tpu_custom_call" | custom-call | bytes 1769472 | tf_op jit(solution)/shard_map/pallas_call | solution.py:255
  184.0 27.9 %shard_map.82 = (bf16[3456,128]{1,0:T(8,128)(2,1)}, bf16[3456,128]{1,0:T(8,128)(2,1)}) custom-call(s32[1]{0:T(128)} %bitcast.3.core, bf16[3456,128]{1,0:T(8,128)(2,1)} %copy-done.7, bf16[3456,128]{1,0:T(8,128)(2,1)} %get-tuple-element.36.fine_in, bf16[3456,128]{1,0:T(8,128)(2,1)} %get-tuple-element.37.coarse_in), custom_call_target="tpu_custom_call", output_to_operand_aliasing={{0}: (2, {}), {1}: (3, {})} | custom-call | bytes 1769472 | tf_op jit(solution)/shard_map/pallas_call | solution.py:255
  (63 shorter events, 16.1 us)
Async XLA Ops:
  0.6 21.8 %copy-start.6 = (bf16[8,8,8,128]{3,2,1,0:T(8,128)(2,1)S(1)}, bf16[8,8,8,128]{3,2,1,0:T(8,128)(2,1)}, u32[]{:S(2)}) copy-start(bf16[8,8,8,128]{3,2,1,0:T(8,128)(2,1)} %param.4) | copy-start | bytes 393220
  1.6 20.7 %collective-permute-start = (bf16[576,128]{1,0:T(8,128)(2,1)S(1)}, bf16[576,128]{1,0:T(8,128)(2,1)S(1)}, u32[]{:S(2)}, u32[]{:S(2)}) collective-permute-start(bf16[576,128]{1,0:T(8,128)(2,1)S(1)} %pad_maximum_fusion.3), channel_id=1, source_target_pairs={{1,2},{2,1},{3,4},{4,3},{5,6},{6,5},{7,8},{8,7},{9,10},{10,9},{11,... | collective-permute-start | bytes 442376 | tf_op jit(solution)/shard_map/ppermute | solution.py:296
  18.5 3.8 %collective-permute-start.1 = (bf16[576,128]{1,0:T(8,128)(2,1)S(1)}, bf16[576,128]{1,0:T(8,128)(2,1)S(1)}, u32[]{:S(2)}, u32[]{:S(2)}) collective-permute-start(bf16[576,128]{1,0:T(8,128)(2,1)S(1)} %pad_maximum_fusion.3), channel_id=1, source_target_pairs={{0,1},{1,0},{2,3},{3,2},{4,5},{5,4},{6,7},{7,6},{8,9},{9,8},{10,11... | collective-permute-start | bytes 442376 | tf_op jit(solution)/shard_map/ppermute | solution.py:297
  21.2 15.0 %copy-start = (bf16[27,128,128]{2,1,0:T(8,128)(2,1)S(1)}, bf16[27,128,128]{2,1,0:T(8,128)(2,1)}, u32[]{:S(2)}) copy-start(bf16[27,128,128]{2,1,0:T(8,128)(2,1)} %weights.1) | copy-start | bytes 2654212
  22.5 15.9 %collective-permute-start.3 = (bf16[8,3,24,128]{3,2,1,0:T(8,128)(2,1)S(1)}, bf16[8,3,24,128]{3,2,1,0:T(8,128)(2,1)S(1)}, u32[]{:S(2)}, u32[]{:S(2)}) collective-permute-start(bf16[8,3,24,128]{3,2,1,0:T(8,128)(2,1)S(1)} %pad_maximum_fusion.5), channel_id=1, source_target_pairs={{16,0},{32,16},{48,32},{64,48},{80,64},{96,80},{112,96},{17,1},{33... | collective-permute-start | bytes 442376 | tf_op jit(solution)/shard_map/ppermute | solution.py:291
  23.9 14.6 %copy-start.8 = (bf16[4,4,4,128]{3,2,1,0:T(4,128)(2,1)S(1)}, bf16[4,4,4,128]{3,2,1,0:T(4,128)(2,1)}, u32[]{:S(2)}) copy-start(bf16[4,4,4,128]{3,2,1,0:T(4,128)(2,1)} %param.7) | copy-start | bytes 49156
  23.9 14.6 %collective-permute-start.2 = (bf16[8,3,24,128]{3,2,1,0:T(8,128)(2,1)S(1)}, bf16[8,3,24,128]{3,2,1,0:T(8,128)(2,1)S(1)}, u32[]{:S(2)}, u32[]{:S(2)}) collective-permute-start(bf16[8,3,24,128]{3,2,1,0:T(8,128)(2,1)S(1)} %pad_maximum_fusion.4), channel_id=1, source_target_pairs={{0,16},{16,32},{32,48},{48,64},{64,80},{80,96},{96,112},{1,17},{17... | collective-permute-start | bytes 442376 | tf_op jit(solution)/shard_map/ppermute | solution.py:290
  38.6 8.7 %copy-start.1 = (bf16[27,128,128]{2,1,0:T(8,128)(2,1)S(1)}, bf16[27,128,128]{2,1,0:T(8,128)(2,1)}, u32[]{:S(2)}) copy-start(bf16[27,128,128]{2,1,0:T(8,128)(2,1)} %coarse_weights.1) | copy-start | bytes 2654212
  38.6 7.6 %collective-permute-start.5 = (bf16[3,14,24,128]{3,2,1,0:T(8,128)(2,1)S(1)}, bf16[3,14,24,128]{3,2,1,0:T(8,128)(2,1)S(1)}, u32[]{:S(2)}, u32[]{:S(2)}) collective-permute-start(bf16[3,14,24,128]{3,2,1,0:T(8,128)(2,1)S(1)} %pad_maximum_fusion.2), channel_id=1, source_target_pairs={{128,0},{256,128},{384,256},{129,1},{257,129},{385,257},{130,2},{2... | collective-permute-start | bytes 774152 | tf_op jit(solution)/shard_map/ppermute | solution.py:291
  40.1 7.2 %collective-permute-start.4 = (bf16[3,14,24,128]{3,2,1,0:T(8,128)(2,1)S(1)}, bf16[3,14,24,128]{3,2,1,0:T(8,128)(2,1)S(1)}, u32[]{:S(2)}, u32[]{:S(2)}) collective-permute-start(bf16[3,14,24,128]{3,2,1,0:T(8,128)(2,1)S(1)} %pad_maximum_fusion.1), channel_id=1, source_target_pairs={{0,128},{128,256},{256,384},{1,129},{129,257},{257,385},{2,130},{1... | collective-permute-start | bytes 774152 | tf_op jit(solution)/shard_map/ppermute | solution.py:290
  57.0 5.7 %copy-start.3 = (bf16[128,128]{1,0:T(8,128)(2,1)}, bf16[128,128]{1,0:T(8,128)(2,1)S(1)}, u32[]{:S(2)}) copy-start(bf16[128,128]{1,0:T(8,128)(2,1)S(1)} %get-tuple-element.24) | copy-start | bytes 98308
  57.0 5.7 %copy-start.5 = (f32[128,128]{1,0:T(8,128)}, f32[128,128]{1,0:T(8,128)S(1)}, u32[]{:S(2)}) copy-start(f32[128,128]{1,0:T(8,128)S(1)} %get-tuple-element.25) | copy-start | bytes 196612
  57.1 4.3 %collective-permute-start.6 = (bf16[3456,128]{1,0:T(8,128)(2,1)S(1)}, bf16[3456,128]{1,0:T(8,128)(2,1)S(1)}, u32[]{:S(2)}, u32[]{:S(2)}) collective-permute-start(bf16[3456,128]{1,0:T(8,128)(2,1)S(1)} %broadcast_select_fusion), channel_id=1, source_target_pairs={{0,1},{1,0},{2,3},{3,2},{4,5},{5,4},{6,7},{7,6},{8,9},{9,8},{10,11... | collective-permute-start | bytes 2654216 | tf_op jit(solution)/shard_map/ppermute | solution.py:395
  62.7 25.3 %all-to-all-start = ((bf16[16,216,128]{2,1,0:T(8,128)(2,1)}), bf16[16,216,128]{2,1,0:T(8,128)(2,1)S(1)}, u32[]{:S(2)}, u32[]{:S(2)}) async-start(bf16[16,216,128]{2,1,0:T(8,128)(2,1)} %bitcast.48), calls=%async_computation | async-start | bytes 1769472 | tf_op jit(solution)/shard_map/all_to_all | solution.py:307
  75.1 7.1 %collective-permute-start.7 = (bf16[4,2,8,128]{3,2,1,0:T(8,128)(2,1)S(1)}, bf16[4,2,8,128]{3,2,1,0:T(8,128)(2,1)S(1)}, u32[]{:S(2)}, u32[]{:S(2)}) collective-permute-start(bf16[4,2,8,128]{3,2,1,0:T(8,128)(2,1)S(1)} %get-tuple-element.57), channel_id=1, source_target_pairs={{0,16},{16,32},{32,48},{48,64},{64,80},{80,96},{96,112},{1,17},{17... | collective-permute-start | bytes 49160 | tf_op jit(solution)/shard_map/ppermute | solution.py:290
  79.4 4.8 %collective-permute-start.8 = (bf16[4,2,8,128]{3,2,1,0:T(8,128)(2,1)S(1)}, bf16[4,2,8,128]{3,2,1,0:T(8,128)(2,1)}, u32[]{:S(2)}, u32[]{:S(2)}) collective-permute-start(bf16[4,2,8,128]{3,2,1,0:T(8,128)(2,1)S(1)} %get-tuple-element.56), channel_id=1, source_target_pairs={{16,0},{32,16},{48,32},{64,48},{80,64},{96,80},{112,96},{17,1},{33... | collective-permute-start | bytes 49160 | tf_op jit(solution)/shard_map/ppermute | solution.py:291
  88.2 0.6 copy-start.4
  88.8 26.1 %all-to-all-start.1 = ((bf16[16,16,128]{2,1,0:T(8,128)(2,1)}), bf16[16,16,128]{2,1,0:T(8,128)(2,1)S(1)}, u32[]{:S(2)}, u32[]{:S(2)}) async-start(bf16[16,16,128]{2,1,0:T(8,128)(2,1)} %bitcast.40), calls=%async_computation.1 | async-start | bytes 131072 | tf_op jit(solution)/shard_map/all_to_all | solution.py:307
  114.9 28.3 %copy-start.2 = (bf16[27,128,128]{2,1,0:T(8,128)(2,1)S(1)}, bf16[27,128,128]{2,1,0:T(8,128)(2,1)}, u32[]{:S(2)}) copy-start(bf16[27,128,128]{2,1,0:T(8,128)(2,1)} %coarse_weights.1) | copy-start | bytes 2654212
  130.3 16.2 %all-to-all-start.3 = ((bf16[16,216,128]{2,1,0:T(8,128)(2,1)}), bf16[16,216,128]{2,1,0:T(8,128)(2,1)}, u32[]{:S(2)}, u32[]{:S(2)}) async-start(bf16[16,216,128]{2,1,0:T(8,128)(2,1)} %broadcast_in_dim.2), calls=%async_computation.3 | async-start | bytes 1769472 | tf_op jit(solution)/shard_map/all_to_all | solution.py:307
  135.6 6.8 %collective-permute-start.10 = (bf16[2,8,8,128]{3,2,1,0:T(8,128)(2,1)S(1)}, bf16[2,8,8,128]{3,2,1,0:T(8,128)(2,1)S(1)}, u32[]{:S(2)}, u32[]{:S(2)}) collective-permute-start(bf16[2,8,8,128]{3,2,1,0:T(8,128)(2,1)S(1)} %get-tuple-element.55), channel_id=1, source_target_pairs={{128,0},{256,128},{384,256},{129,1},{257,129},{385,257},{130,2},{2... | collective-permute-start | bytes 98312 | tf_op jit(solution)/shard_map/ppermute | solution.py:291
  136.9 5.5 %collective-permute-start.9 = (bf16[2,8,8,128]{3,2,1,0:T(8,128)(2,1)S(1)}, bf16[2,8,8,128]{3,2,1,0:T(8,128)(2,1)S(1)}, u32[]{:S(2)}, u32[]{:S(2)}) collective-permute-start(bf16[2,8,8,128]{3,2,1,0:T(8,128)(2,1)S(1)} %get-tuple-element.54), channel_id=1, source_target_pairs={{0,128},{128,256},{256,384},{1,129},{129,257},{257,385},{2,130},{1... | collective-permute-start | bytes 98312 | tf_op jit(solution)/shard_map/ppermute | solution.py:290
  146.5 36.6 %collective-permute-start.11 = (bf16[3456,128]{1,0:T(8,128)(2,1)}, bf16[3456,128]{1,0:T(8,128)(2,1)S(1)}, u32[]{:S(2)}, u32[]{:S(2)}) collective-permute-start(bf16[3456,128]{1,0:T(8,128)(2,1)} %bitcast.25.mine), channel_id=1, source_target_pairs={{0,1},{1,0},{2,3},{3,2},{4,5},{5,4},{6,7},{7,6},{8,9},{9,8},{10,11... | collective-permute-start | bytes 2654216 | tf_op jit(solution)/shard_map/ppermute | solution.py:423
  183.1 0.9 copy-start.7

commit v7 on v6

--- a/solution.py
+++ b/solution.py
@@ -230,38 +230,35 @@
         out_ref[at] = total
 
 
-def keep_kernel(core, mine, fine_ref, coarse_ref, done):
-    for at, ref in ((0, fine_ref), (1, coarse_ref)):
+def place_kernel(core, mine, other, fine_ref, coarse_ref, done):
+    for at, first, second in ((0, fine_ref, coarse_ref), (1, coarse_ref, fine_ref)):
 
         @pl.when(core[0] == at)
-        def _(ref=ref):
-            copy = pltpu.make_async_copy(mine, ref, done)
-            copy.start()
-            copy.wait()
-
-
-def take_kernel(core, other, fine_in, coarse_in, fine_ref, coarse_ref, done):
-    for at, ref in ((1, fine_ref), (0, coarse_ref)):
-
-        @pl.when(core[0] == at)
-        def _(ref=ref):
-            copy = pltpu.make_async_copy(other, ref, done)
-            copy.start()
-            copy.wait()
-
-
-def copies(kernel, inputs, aliases):
+        def _(first=first, second=second):
+            moves = [
+                pltpu.make_async_copy(mine, first, done.at[0]),
+                pltpu.make_async_copy(other, second, done.at[1]),
+            ]
+            for move in moves:
+                move.start()
+            for move in moves:
+                move.wait()
+
+
+def placed(core, mine, other):
     shape = jax.ShapeDtypeStruct((27 * C, C), BF16)
     return pl.pallas_call(
-        kernel,
+        place_kernel,
         out_shape=[shape, shape],
-        in_specs=[pl.BlockSpec(memory_space=pltpu.SMEM)]
-        + [pl.BlockSpec(memory_space=pl.ANY) for _ in inputs[1:]],
+        in_specs=[
+            pl.BlockSpec(memory_space=pltpu.SMEM),
+            pl.BlockSpec(memory_space=pltpu.VMEM),
+            pl.BlockSpec(memory_space=pltpu.VMEM),
+        ],
         out_specs=[pl.BlockSpec(memory_space=pl.ANY) for _ in range(2)],
-        scratch_shapes=[pltpu.SemaphoreType.DMA],
-        input_output_aliases=aliases,
-        cost_estimate=pl.CostEstimate(flops=0, bytes_accessed=2 * 27 * C * C * 2, transcendentals=0),
-    )(*inputs)
+        scratch_shapes=[pltpu.SemaphoreType.DMA((2,))],
+        cost_estimate=pl.CostEstimate(flops=0, bytes_accessed=4 * 27 * C * C * 2, transcendentals=0),
+    )(core, mine, other)
 
 
 def call(kernel, outs, inputs, scratch=(), scalars=0, flops=0):
@@ -421,11 +418,7 @@
     parts, grad_volume = lax.optimization_barrier((parts, grad_volume))
     mine = joined(parts)
     other = lax.ppermute(mine, "core", swap)
-    core = place[3:]
-    fine_done, coarse_done = copies(keep_kernel, [core, mine], {})
-    fine_done, coarse_done = copies(
-        take_kernel, [core, other, fine_done, coarse_done], {2: 0, 3: 1}
-    )
+    fine_done, coarse_done = placed(place[3:], mine, other)
     return (
         coarse_out,
         grad_volume.reshape(8, 8, 8, C),

time: 213 us -> 162 us (0.76)
  Pallas kernels: 73.1 us -> 20 us
  waiting for transfers between devices: 24 us -> 26.2 us
    pallas_call x2 -> x1, Pallas kernels: 55.8 us -> 2.65 us  [placed(): pl.pallas_call(place_kernel, out_shape=[shape, shape], in_specs=[pl.Block...]
    ppermute x1, waiting for transfers between devices: 0.01 us -> 2.24 us  [local(): other = lax.ppermute(mine, 'core', swap)]
  transfers between devices with their start and end apart: 15 -> 15, of which waited for: 7 -> 8; matrix products, arithmetic and copies ran while one was open for 2% -> 3% of each run, Pallas kernels for 17% -> 5%
where the time goes in v7:
time: 162 us; the launch traced here: 161 us
  starting transfers between devices  89.3 us (55%)
  waiting for transfers between devices  26.2 us (16%)
  Pallas kernels  20 us (12%)
  blocking collectives  14.3 us (9%)
  other arithmetic  5.75 us (4%)
  local copies, waits for them, and re-layouts  4.35 us (3%)
    all_to_all x3, starting transfers between devices, exchanged(): return lax.all_to_all(parts, axes, 0, 0, tiled=True)  30.1 us
    ppermute x4, starting transfers between devices, beside(): before = lax.ppermute(last, axis, line(count, 1))  24.6 us
    pallas_call x6, Pallas kernels, call(): pl.pallas_call(kernel, out_shape=[jax.ShapeDtypeStruct(s, t) for s, t in...  17.3 us
    ppermute x1, starting transfers between devices, along_width(): lax.ppermute(x, WIDTH, [(i, i - 1 + 2 * (i % 2)) for i in range(1, count...  16.8 us
    all_to_all x3, waiting for transfers between devices, exchanged(): return lax.all_to_all(parts, axes, 0, 0, tiled=True)  16 us
    all_to_all x1, blocking collectives, exchanged(): return lax.all_to_all(parts, axes, 0, 0, tiled=True)  14.3 us
    ppermute x1, starting transfers between devices, local(): other = lax.ppermute(mine, 'core', swap)  8.64 us
    ppermute x4, starting transfers between devices, beside(): after = lax.ppermute(leading, axis, line(count, -1))  5.3 us
  transfers between devices with their start and end apart: 15, of which 8 were waited for; matrix products, arithmetic and copies ran while one was open for 3% of the time, Pallas kernels for 5%

profile of v7, /device:TPU:1, one launch (start us, length us, event | category | flops | bytes accessed | tf_op | source)
XLA Modules:
  0.0 161.1 jit_solution(1356700116679947143)
XLA Ops:
  1.6 16.8 %collective-permute-start = (bf16[576,128]{1,0:T(8,128)(2,1)S(1)}, bf16[576,128]{1,0:T(8,128)(2,1)S(1)}, u32[]{:S(2)}, u32[]{:S(2)}) collective-permute-start(bf16[576,128]{1,0:T(8,128)(2,1)S(1)} %pad_maximum_fusion.3), channel_id=1, source_target_pairs={{1,2},{2,1},{3,4},{4,3},{5,6},{6,5},{7,8},{8,7},{9,10},{10,9},{11,... | collective-permute-start | bytes 442376 | tf_op jit(solution)/shard_map/ppermute | solution.py:293
  18.5 1.9 %collective-permute-start.1 = (bf16[576,128]{1,0:T(8,128)(2,1)S(1)}, bf16[576,128]{1,0:T(8,128)(2,1)S(1)}, u32[]{:S(2)}, u32[]{:S(2)}) collective-permute-start(bf16[576,128]{1,0:T(8,128)(2,1)S(1)} %pad_maximum_fusion.3), channel_id=1, source_target_pairs={{0,1},{1,0},{2,3},{3,2},{4,5},{5,4},{6,7},{7,6},{8,9},{9,8},{10,11... | collective-permute-start | bytes 442376 | tf_op jit(solution)/shard_map/ppermute | solution.py:294
  23.9 12.3 %collective-permute-start.2 = (bf16[8,3,24,128]{3,2,1,0:T(8,128)(2,1)S(1)}, bf16[8,3,24,128]{3,2,1,0:T(8,128)(2,1)S(1)}, u32[]{:S(2)}, u32[]{:S(2)}) collective-permute-start(bf16[8,3,24,128]{3,2,1,0:T(8,128)(2,1)S(1)} %pad_maximum_fusion.4), channel_id=1, source_target_pairs={{0,16},{16,32},{32,48},{48,64},{64,80},{80,96},{96,112},{1,17},{17... | collective-permute-start | bytes 442376 | tf_op jit(solution)/shard_map/ppermute | solution.py:287
  36.2 2.1 %shard_map.75.refs_9_ = f32[6,6,24,128]{3,2,1,0:T(8,128)S(1)} custom-call(bf16[8,192,128]{2,1,0:T(8,128)(2,1)S(1)} %bitcast.30, bf16[3456,128]{1,0:T(8,128)(2,1)S(1)} %bitcast.33), custom_call_target="tpu_custom_call" | custom-call | flops 764411904 | bytes 1720320 | tf_op jit(solution)/shard_map/pallas_call | solution.py:271
  40.1 4.0 %collective-permute-start.4 = (bf16[3,14,24,128]{3,2,1,0:T(8,128)(2,1)S(1)}, bf16[3,14,24,128]{3,2,1,0:T(8,128)(2,1)S(1)}, u32[]{:S(2)}, u32[]{:S(2)}) collective-permute-start(bf16[3,14,24,128]{3,2,1,0:T(8,128)(2,1)S(1)} %pad_maximum_fusion.1), channel_id=1, source_target_pairs={{0,128},{128,256},{256,384},{1,129},{129,257},{257,385},{2,130},{1... | collective-permute-start | bytes 774152 | tf_op jit(solution)/shard_map/ppermute | solution.py:287
  44.1 2.1 %shard_map.76.refs_10_ = f32[6,6,24,128]{3,2,1,0:T(8,128)S(1)} custom-call(bf16[8,192,128]{2,1,0:T(8,128)(2,1)S(1)} %bitcast.31, bf16[8,72,128]{2,1,0:T(8,128)(2,1)S(1)} %bitcast.43, bf16[8,72,128]{2,1,0:T(8,128)(2,1)S(1)} %bitcast.41, bf16[3456,128]{1,0:T(8,128)(2,1)S(1)} %bitcast.34), custom_call_target="tpu_custom_call" | custom-call | flops 764411904 | bytes 2015232 | tf_op jit(solution)/shard_map/pallas_call | solution.py:271
  47.3 9.7 %shard_map.77 = (f32[128,128]{1,0:T(8,128)S(1)}, bf16[128,128]{1,0:T(8,128)(2,1)S(1)}, f32[12,12,24,128]{3,2,1,0:T(8,128)S(1)}, bf16[3456,128]{1,0:T(8,128)(2,1)S(1)}, bf16[3456,128]{1,0:T(8,128)(2,1)S(1)}) custom-call(s32[4]{0:T(128)S(1)} %pad_add_fusion.refs_0_, bf16[8,192,128]{2,1,0:T(8,128)(2,1)S(1)} %bitcast.32, bf16[8,72,128]{2,1,0:T(8,128)(2,1)S(1)} %bitcast.44, ...), custom_call_target="tpu_custom_call" | custom-call | flops 3538944000 | bytes 7561232 | tf_op jit(solution)/shard_map/pallas_call | solution.py:271
  57.1 1.9 %collective-permute-start.6 = (bf16[3456,128]{1,0:T(8,128)(2,1)S(1)}, bf16[3456,128]{1,0:T(8,128)(2,1)S(1)}, u32[]{:S(2)}, u32[]{:S(2)}) collective-permute-start(bf16[3456,128]{1,0:T(8,128)(2,1)S(1)} %broadcast_select_fusion), channel_id=1, source_target_pairs={{0,1},{1,0},{2,3},{3,2},{4,5},{5,4},{6,7},{7,6},{8,9},{9,8},{10,11... | collective-permute-start | bytes 2654216 | tf_op jit(solution)/shard_map/ppermute | solution.py:392
  59.0 2.4 %collective-permute-done.6 = bf16[3456,128]{1,0:T(8,128)(2,1)S(1)} collective-permute-done((bf16[3456,128]{1,0:T(8,128)(2,1)S(1)}, bf16[3456,128]{1,0:T(8,128)(2,1)S(1)}, u32[]{:S(2)}, u32[]{:S(2)}) %collective-permute-start.6) | collective-permute-done | bytes 884768 | tf_op jit(solution)/shard_map/ppermute | solution.py:392
  62.7 11.6 %all-to-all-start = ((bf16[16,216,128]{2,1,0:T(8,128)(2,1)}), bf16[16,216,128]{2,1,0:T(8,128)(2,1)S(1)}, u32[]{:S(2)}, u32[]{:S(2)}) async-start(bf16[16,216,128]{2,1,0:T(8,128)(2,1)} %bitcast.48), calls=%async_computation | async-start | bytes 1769472 | tf_op jit(solution)/shard_map/all_to_all | solution.py:304
  75.1 4.3 %collective-permute-start.7 = (bf16[4,2,8,128]{3,2,1,0:T(8,128)(2,1)S(1)}, bf16[4,2,8,128]{3,2,1,0:T(8,128)(2,1)S(1)}, u32[]{:S(2)}, u32[]{:S(2)}) collective-permute-start(bf16[4,2,8,128]{3,2,1,0:T(8,128)(2,1)S(1)} %get-tuple-element.53), channel_id=1, source_target_pairs={{0,16},{16,32},{32,48},{48,64},{64,80},{80,96},{96,112},{1,17},{17... | collective-permute-start | bytes 49160 | tf_op jit(solution)/shard_map/ppermute | solution.py:287
  80.7 1.5 fusion
  82.2 2.0 %collective-permute-done.8 = bf16[4,2,8,128]{3,2,1,0:T(8,128)(2,1)} collective-permute-done((bf16[4,2,8,128]{3,2,1,0:T(8,128)(2,1)S(1)}, bf16[4,2,8,128]{3,2,1,0:T(8,128)(2,1)}, u32[]{:S(2)}, u32[]{:S(2)}) %collective-permute-start.8) | collective-permute-done | bytes 16416 | tf_op jit(solution)/shard_map/ppermute | solution.py:288
  84.2 3.9 %all-to-all-done.parts = bf16[16,216,128]{2,1,0:T(8,128)(2,1)S(1)} async-done(((bf16[16,216,128]{2,1,0:T(8,128)(2,1)}), bf16[16,216,128]{2,1,0:T(8,128)(2,1)S(1)}, u32[]{:S(2)}, u32[]{:S(2)}) %all-to-all-start) | async-done | bytes 884768 | tf_op jit(solution)/shard_map/all_to_all | solution.py:304
  88.8 14.0 %all-to-all-start.1 = ((bf16[16,16,128]{2,1,0:T(8,128)(2,1)}), bf16[16,16,128]{2,1,0:T(8,128)(2,1)S(1)}, u32[]{:S(2)}, u32[]{:S(2)}) async-start(bf16[16,16,128]{2,1,0:T(8,128)(2,1)} %bitcast.40), calls=%async_computation.1 | async-start | bytes 131072 | tf_op jit(solution)/shard_map/all_to_all | solution.py:304
  102.8 12.1 %all-to-all-done.1.parts = bf16[16,16,128]{2,1,0:T(8,128)(2,1)S(1)} async-done(((bf16[16,16,128]{2,1,0:T(8,128)(2,1)}), bf16[16,16,128]{2,1,0:T(8,128)(2,1)S(1)}, u32[]{:S(2)}, u32[]{:S(2)}) %all-to-all-start.1) | async-done | bytes 65568 | tf_op jit(solution)/shard_map/all_to_all | solution.py:304
  114.9 14.3 %all_to_all.20 = bf16[16,16,128]{2,1,0:T(8,128)(2,1)S(1)} all-to-all(bf16[16,16,128]{2,1,0:T(8,128)(2,1)S(1)} %shard_map.79), channel_id=1, replica_groups=mesh['gx'=4,'gy'=8,'y'=4,'zh'=2,'core'=2] {'gy','zh'}, dimensions={0} | all-to-all | bytes 131072 | tf_op jit(solution)/shard_map/all_to_all | solution.py:304
  130.3 4.5 %all-to-all-start.3 = ((bf16[16,216,128]{2,1,0:T(8,128)(2,1)}), bf16[16,216,128]{2,1,0:T(8,128)(2,1)}, u32[]{:S(2)}, u32[]{:S(2)}) async-start(bf16[16,216,128]{2,1,0:T(8,128)(2,1)} %broadcast_in_dim.2), calls=%async_computation.3 | async-start | bytes 1769472 | tf_op jit(solution)/shard_map/all_to_all | solution.py:304
  136.9 4.0 %collective-permute-start.9 = (bf16[2,8,8,128]{3,2,1,0:T(8,128)(2,1)S(1)}, bf16[2,8,8,128]{3,2,1,0:T(8,128)(2,1)S(1)}, u32[]{:S(2)}, u32[]{:S(2)}) collective-permute-start(bf16[2,8,8,128]{3,2,1,0:T(8,128)(2,1)S(1)} %get-tuple-element.50), channel_id=1, source_target_pairs={{0,128},{128,256},{256,384},{1,129},{129,257},{257,385},{2,130},{1... | collective-permute-start | bytes 98312 | tf_op jit(solution)/shard_map/ppermute | solution.py:287
  140.9 1.5 collective-permute-done.10
  143.2 3.3 %shard_map.80 = bf16[512,128]{1,0:T(8,128)(2,1)} custom-call(bf16[512,128]{1,0:T(8,128)(2,1)S(1)} %bitcast.36, bf16[27,128,128]{2,1,0:T(8,128)(2,1)S(1)} %copy-done.2, f32[12,12,24,128]{3,2,1,0:T(8,128)S(1)} %get-tuple-element.31.slope, bf16[27,128,128]{2,1,0:T(8,128)(2,1)S(1)} %copy-done), custom_call_target="tpu_custom_call" | custom-call | flops 707788800 | bytes 3801088 | tf_op jit(solution)/shard_map/pallas_call | solution.py:271
  146.5 8.6 %collective-permute-start.11 = (bf16[3456,128]{1,0:T(8,128)(2,1)}, bf16[3456,128]{1,0:T(8,128)(2,1)S(1)}, u32[]{:S(2)}, u32[]{:S(2)}) collective-permute-start(bf16[3456,128]{1,0:T(8,128)(2,1)} %bitcast.25.mine), channel_id=1, source_target_pairs={{0,1},{1,0},{2,3},{3,2},{4,5},{5,4},{6,7},{7,6},{8,9},{9,8},{10,11... | collective-permute-start | bytes 2654216 | tf_op jit(solution)/shard_map/ppermute | solution.py:420
  155.1 2.2 %collective-permute-done.11.other = bf16[3456,128]{1,0:T(8,128)(2,1)S(1)} collective-permute-done((bf16[3456,128]{1,0:T(8,128)(2,1)}, bf16[3456,128]{1,0:T(8,128)(2,1)S(1)}, u32[]{:S(2)}, u32[]{:S(2)}) %collective-permute-start.11) | collective-permute-done | bytes 884768 | tf_op jit(solution)/shard_map/ppermute | solution.py:420
  158.3 2.7 %shard_map.81 = (bf16[3456,128]{1,0:T(8,128)(2,1)}, bf16[3456,128]{1,0:T(8,128)(2,1)}) custom-call(s32[1]{0:T(128)} %bitcast.3.core, bf16[3456,128]{1,0:T(8,128)(2,1)} %bitcast.25.mine, bf16[3456,128]{1,0:T(8,128)(2,1)} %copy-done.7), custom_call_target="tpu_custom_call" | custom-call | bytes 3538944 | tf_op jit(solution)/shard_map/pallas_call | solution.py:250
  (62 shorter events, 16.1 us)
Async XLA Ops:
  0.6 21.8 %copy-start.6 = (bf16[8,8,8,128]{3,2,1,0:T(8,128)(2,1)S(1)}, bf16[8,8,8,128]{3,2,1,0:T(8,128)(2,1)}, u32[]{:S(2)}) copy-start(bf16[8,8,8,128]{3,2,1,0:T(8,128)(2,1)} %param.4) | copy-start | bytes 393220
  1.6 20.7 %collective-permute-start = (bf16[576,128]{1,0:T(8,128)(2,1)S(1)}, bf16[576,128]{1,0:T(8,128)(2,1)S(1)}, u32[]{:S(2)}, u32[]{:S(2)}) collective-permute-start(bf16[576,128]{1,0:T(8,128)(2,1)S(1)} %pad_maximum_fusion.3), channel_id=1, source_target_pairs={{1,2},{2,1},{3,4},{4,3},{5,6},{6,5},{7,8},{8,7},{9,10},{10,9},{11,... | collective-permute-start | bytes 442376 | tf_op jit(solution)/shard_map/ppermute | solution.py:293
  18.5 3.8 %collective-permute-start.1 = (bf16[576,128]{1,0:T(8,128)(2,1)S(1)}, bf16[576,128]{1,0:T(8,128)(2,1)S(1)}, u32[]{:S(2)}, u32[]{:S(2)}) collective-permute-start(bf16[576,128]{1,0:T(8,128)(2,1)S(1)} %pad_maximum_fusion.3), channel_id=1, source_target_pairs={{0,1},{1,0},{2,3},{3,2},{4,5},{5,4},{6,7},{7,6},{8,9},{9,8},{10,11... | collective-permute-start | bytes 442376 | tf_op jit(solution)/shard_map/ppermute | solution.py:294
  21.2 15.0 %copy-start = (bf16[27,128,128]{2,1,0:T(8,128)(2,1)S(1)}, bf16[27,128,128]{2,1,0:T(8,128)(2,1)}, u32[]{:S(2)}) copy-start(bf16[27,128,128]{2,1,0:T(8,128)(2,1)} %weights.1) | copy-start | bytes 2654212
  22.5 15.9 %collective-permute-start.3 = (bf16[8,3,24,128]{3,2,1,0:T(8,128)(2,1)S(1)}, bf16[8,3,24,128]{3,2,1,0:T(8,128)(2,1)S(1)}, u32[]{:S(2)}, u32[]{:S(2)}) collective-permute-start(bf16[8,3,24,128]{3,2,1,0:T(8,128)(2,1)S(1)} %pad_maximum_fusion.5), channel_id=1, source_target_pairs={{16,0},{32,16},{48,32},{64,48},{80,64},{96,80},{112,96},{17,1},{33... | collective-permute-start | bytes 442376 | tf_op jit(solution)/shard_map/ppermute | solution.py:288
  23.9 14.6 %copy-start.8 = (bf16[4,4,4,128]{3,2,1,0:T(4,128)(2,1)S(1)}, bf16[4,4,4,128]{3,2,1,0:T(4,128)(2,1)}, u32[]{:S(2)}) copy-start(bf16[4,4,4,128]{3,2,1,0:T(4,128)(2,1)} %param.7) | copy-start | bytes 49156
  23.9 14.6 %collective-permute-start.2 = (bf16[8,3,24,128]{3,2,1,0:T(8,128)(2,1)S(1)}, bf16[8,3,24,128]{3,2,1,0:T(8,128)(2,1)S(1)}, u32[]{:S(2)}, u32[]{:S(2)}) collective-permute-start(bf16[8,3,24,128]{3,2,1,0:T(8,128)(2,1)S(1)} %pad_maximum_fusion.4), channel_id=1, source_target_pairs={{0,16},{16,32},{32,48},{48,64},{64,80},{80,96},{96,112},{1,17},{17... | collective-permute-start | bytes 442376 | tf_op jit(solution)/shard_map/ppermute | solution.py:287
  38.6 8.7 %copy-start.1 = (bf16[27,128,128]{2,1,0:T(8,128)(2,1)S(1)}, bf16[27,128,128]{2,1,0:T(8,128)(2,1)}, u32[]{:S(2)}) copy-start(bf16[27,128,128]{2,1,0:T(8,128)(2,1)} %coarse_weights.1) | copy-start | bytes 2654212
  38.6 7.6 %collective-permute-start.5 = (bf16[3,14,24,128]{3,2,1,0:T(8,128)(2,1)S(1)}, bf16[3,14,24,128]{3,2,1,0:T(8,128)(2,1)S(1)}, u32[]{:S(2)}, u32[]{:S(2)}) collective-permute-start(bf16[3,14,24,128]{3,2,1,0:T(8,128)(2,1)S(1)} %pad_maximum_fusion.2), channel_id=1, source_target_pairs={{128,0},{256,128},{384,256},{129,1},{257,129},{385,257},{130,2},{2... | collective-permute-start | bytes 774152 | tf_op jit(solution)/shard_map/ppermute | solution.py:288
  40.1 7.2 %collective-permute-start.4 = (bf16[3,14,24,128]{3,2,1,0:T(8,128)(2,1)S(1)}, bf16[3,14,24,128]{3,2,1,0:T(8,128)(2,1)S(1)}, u32[]{:S(2)}, u32[]{:S(2)}) collective-permute-start(bf16[3,14,24,128]{3,2,1,0:T(8,128)(2,1)S(1)} %pad_maximum_fusion.1), channel_id=1, source_target_pairs={{0,128},{128,256},{256,384},{1,129},{129,257},{257,385},{2,130},{1... | collective-permute-start | bytes 774152 | tf_op jit(solution)/shard_map/ppermute | solution.py:287
  57.0 5.7 %copy-start.3 = (bf16[128,128]{1,0:T(8,128)(2,1)}, bf16[128,128]{1,0:T(8,128)(2,1)S(1)}, u32[]{:S(2)}) copy-start(bf16[128,128]{1,0:T(8,128)(2,1)S(1)} %get-tuple-element.22) | copy-start | bytes 98308
  57.0 5.7 %copy-start.5 = (f32[128,128]{1,0:T(8,128)}, f32[128,128]{1,0:T(8,128)S(1)}, u32[]{:S(2)}) copy-start(f32[128,128]{1,0:T(8,128)S(1)} %get-tuple-element.23) | copy-start | bytes 196612
  57.1 4.3 %collective-permute-start.6 = (bf16[3456,128]{1,0:T(8,128)(2,1)S(1)}, bf16[3456,128]{1,0:T(8,128)(2,1)S(1)}, u32[]{:S(2)}, u32[]{:S(2)}) collective-permute-start(bf16[3456,128]{1,0:T(8,128)(2,1)S(1)} %broadcast_select_fusion), channel_id=1, source_target_pairs={{0,1},{1,0},{2,3},{3,2},{4,5},{5,4},{6,7},{7,6},{8,9},{9,8},{10,11... | collective-permute-start | bytes 2654216 | tf_op jit(solution)/shard_map/ppermute | solution.py:392
  62.7 25.3 %all-to-all-start = ((bf16[16,216,128]{2,1,0:T(8,128)(2,1)}), bf16[16,216,128]{2,1,0:T(8,128)(2,1)S(1)}, u32[]{:S(2)}, u32[]{:S(2)}) async-start(bf16[16,216,128]{2,1,0:T(8,128)(2,1)} %bitcast.48), calls=%async_computation | async-start | bytes 1769472 | tf_op jit(solution)/shard_map/all_to_all | solution.py:304
  75.1 7.1 %collective-permute-start.7 = (bf16[4,2,8,128]{3,2,1,0:T(8,128)(2,1)S(1)}, bf16[4,2,8,128]{3,2,1,0:T(8,128)(2,1)S(1)}, u32[]{:S(2)}, u32[]{:S(2)}) collective-permute-start(bf16[4,2,8,128]{3,2,1,0:T(8,128)(2,1)S(1)} %get-tuple-element.53), channel_id=1, source_target_pairs={{0,16},{16,32},{32,48},{48,64},{64,80},{80,96},{96,112},{1,17},{17... | collective-permute-start | bytes 49160 | tf_op jit(solution)/shard_map/ppermute | solution.py:287
  79.4 4.8 %collective-permute-start.8 = (bf16[4,2,8,128]{3,2,1,0:T(8,128)(2,1)S(1)}, bf16[4,2,8,128]{3,2,1,0:T(8,128)(2,1)}, u32[]{:S(2)}, u32[]{:S(2)}) collective-permute-start(bf16[4,2,8,128]{3,2,1,0:T(8,128)(2,1)S(1)} %get-tuple-element.52), channel_id=1, source_target_pairs={{16,0},{32,16},{48,32},{64,48},{80,64},{96,80},{112,96},{17,1},{33... | collective-permute-start | bytes 49160 | tf_op jit(solution)/shard_map/ppermute | solution.py:288
  88.2 0.6 copy-start.4
  88.8 26.1 %all-to-all-start.1 = ((bf16[16,16,128]{2,1,0:T(8,128)(2,1)}), bf16[16,16,128]{2,1,0:T(8,128)(2,1)S(1)}, u32[]{:S(2)}, u32[]{:S(2)}) async-start(bf16[16,16,128]{2,1,0:T(8,128)(2,1)} %bitcast.40), calls=%async_computation.1 | async-start | bytes 131072 | tf_op jit(solution)/shard_map/all_to_all | solution.py:304
  114.9 28.3 %copy-start.2 = (bf16[27,128,128]{2,1,0:T(8,128)(2,1)S(1)}, bf16[27,128,128]{2,1,0:T(8,128)(2,1)}, u32[]{:S(2)}) copy-start(bf16[27,128,128]{2,1,0:T(8,128)(2,1)} %coarse_weights.1) | copy-start | bytes 2654212
  130.3 16.2 %all-to-all-start.3 = ((bf16[16,216,128]{2,1,0:T(8,128)(2,1)}), bf16[16,216,128]{2,1,0:T(8,128)(2,1)}, u32[]{:S(2)}, u32[]{:S(2)}) async-start(bf16[16,216,128]{2,1,0:T(8,128)(2,1)} %broadcast_in_dim.2), calls=%async_computation.3 | async-start | bytes 1769472 | tf_op jit(solution)/shard_map/all_to_all | solution.py:304
  135.6 6.8 %collective-permute-start.10 = (bf16[2,8,8,128]{3,2,1,0:T(8,128)(2,1)S(1)}, bf16[2,8,8,128]{3,2,1,0:T(8,128)(2,1)S(1)}, u32[]{:S(2)}, u32[]{:S(2)}) collective-permute-start(bf16[2,8,8,128]{3,2,1,0:T(8,128)(2,1)S(1)} %get-tuple-element.51), channel_id=1, source_target_pairs={{128,0},{256,128},{384,256},{129,1},{257,129},{385,257},{130,2},{2... | collective-permute-start | bytes 98312 | tf_op jit(solution)/shard_map/ppermute | solution.py:288
  136.9 5.5 %collective-permute-start.9 = (bf16[2,8,8,128]{3,2,1,0:T(8,128)(2,1)S(1)}, bf16[2,8,8,128]{3,2,1,0:T(8,128)(2,1)S(1)}, u32[]{:S(2)}, u32[]{:S(2)}) collective-permute-start(bf16[2,8,8,128]{3,2,1,0:T(8,128)(2,1)S(1)} %get-tuple-element.50), channel_id=1, source_target_pairs={{0,128},{128,256},{256,384},{1,129},{129,257},{257,385},{2,130},{1... | collective-permute-start | bytes 98312 | tf_op jit(solution)/shard_map/ppermute | solution.py:287
  146.5 10.9 %collective-permute-start.11 = (bf16[3456,128]{1,0:T(8,128)(2,1)}, bf16[3456,128]{1,0:T(8,128)(2,1)S(1)}, u32[]{:S(2)}, u32[]{:S(2)}) collective-permute-start(bf16[3456,128]{1,0:T(8,128)(2,1)} %bitcast.25.mine), channel_id=1, source_target_pairs={{0,1},{1,0},{2,3},{3,2},{4,5},{5,4},{6,7},{7,6},{8,9},{9,8},{10,11... | collective-permute-start | bytes 2654216 | tf_op jit(solution)/shard_map/ppermute | solution.py:420
  157.4 0.9 copy-start.7

commit v8 on v7

--- a/solution.py
+++ b/solution.py
@@ -230,37 +230,6 @@
         out_ref[at] = total
 
 
-def place_kernel(core, mine, other, fine_ref, coarse_ref, done):
-    for at, first, second in ((0, fine_ref, coarse_ref), (1, coarse_ref, fine_ref)):
-
-        @pl.when(core[0] == at)
-        def _(first=first, second=second):
-            moves = [
-                pltpu.make_async_copy(mine, first, done.at[0]),
-                pltpu.make_async_copy(other, second, done.at[1]),
-            ]
-            for move in moves:
-                move.start()
-            for move in moves:
-                move.wait()
-
-
-def placed(core, mine, other):
-    shape = jax.ShapeDtypeStruct((27 * C, C), BF16)
-    return pl.pallas_call(
-        place_kernel,
-        out_shape=[shape, shape],
-        in_specs=[
-            pl.BlockSpec(memory_space=pltpu.SMEM),
-            pl.BlockSpec(memory_space=pltpu.VMEM),
-            pl.BlockSpec(memory_space=pltpu.VMEM),
-        ],
-        out_specs=[pl.BlockSpec(memory_space=pl.ANY) for _ in range(2)],
-        scratch_shapes=[pltpu.SemaphoreType.DMA((2,))],
-        cost_estimate=pl.CostEstimate(flops=0, bytes_accessed=4 * 27 * C * C * 2, transcendentals=0),
-    )(core, mine, other)
-
-
 def call(kernel, outs, inputs, scratch=(), scalars=0, flops=0):
     in_specs = [
         pl.BlockSpec(memory_space=pltpu.SMEM if n < scalars else pltpu.VMEM)
@@ -312,7 +281,7 @@
     sizes = {axis: lax.axis_size(axis) for axis in AXES}
     plane, along = (sizes["gx"] * sizes["y"], sizes["gy"] * sizes["zh"])
     peers = [sizes["gx"], sizes["gy"], sizes["y"] * sizes["zh"] * 2]
-    place = [lax.axis_index(axis) for axis in ("gx", "gy", WIDTH, "core")]
+    place = [lax.axis_index(axis) for axis in ("gx", "gy", WIDTH)]
     place = jnp.stack([p.astype(jnp.int32) for p in place])
     fine_sizes = [8 * n for n in peers]
     coarse_sizes = [4 * n for n in peers]
@@ -407,6 +376,8 @@
     grads = jnp.concatenate([halo[0], grads, halo[1]], axis=1)
     halo = beside(grads[2:], grads[:2], "gx", peers[0])
     around = jnp.concatenate([halo[0], grads, halo[1]], axis=0)
+    parts = exchanged(jnp.broadcast_to(part[None], (plane, length, C)), PLANE)
+    parts, around = lax.optimization_barrier((parts, around))
     (grad_volume,) = call(
         volume_kernel,
         [((512, C), BF16)],
@@ -414,11 +385,10 @@
         scratch=[((8, 8, 16, C), F32), ((6, 6, 16, C), F32), ((10, 10, 16, C), F32)],
         flops=2 * 800 * 27 * C * C,
     )
-    parts = exchanged(jnp.broadcast_to(part[None], (plane, length, C)), PLANE)
-    parts, grad_volume = lax.optimization_barrier((parts, grad_volume))
     mine = joined(parts)
     other = lax.ppermute(mine, "core", swap)
-    fine_done, coarse_done = placed(place[3:], mine, other)
+    fine_done = jnp.where(first, mine, other)
+    coarse_done = jnp.where(first, other, mine)
     return (
         coarse_out,
         grad_volume.reshape(8, 8, 8, C),

time: 162 us -> 162 us (level)
  other arithmetic: 5.75 us -> 8.89 us
  Pallas kernels: 20 us -> 17.3 us
    pallas_call x1 -> x0, Pallas kernels: 2.65 us -> none  [placed(): pl.pallas_call(place_kernel, out_shape=[shape, shape], in_specs=[pl.Block...]
    select_n x0 -> x1, other arithmetic: none -> 2.49 us  [local(): coarse_done = jnp.where(first, other, mine)]
    ppermute x1, waiting for transfers between devices: 2.24 us -> 0.01 us  [local(): other = lax.ppermute(mine, 'core', swap)]
    all_to_all x3, waiting for transfers between devices: 16 us -> 18 us  [exchanged(): return lax.all_to_all(parts, axes, 0, 0, tiled=True)]
where the time goes in v8:
time: 162 us; the launch traced here: 161 us
  starting transfers between devices  89.3 us (55%)
  waiting for transfers between devices  25.9 us (16%)
  Pallas kernels  17.3 us (11%)
  blocking collectives  14.3 us (9%)
  other arithmetic  8.89 us (5%)
  local copies, waits for them, and re-layouts  4.32 us (3%)
    all_to_all x3, starting transfers between devices, exchanged(): return lax.all_to_all(parts, axes, 0, 0, tiled=True)  30.1 us
    ppermute x4, starting transfers between devices, beside(): before = lax.ppermute(last, axis, line(count, 1))  24.6 us
    all_to_all x3, waiting for transfers between devices, exchanged(): return lax.all_to_all(parts, axes, 0, 0, tiled=True)  18 us
    pallas_call x6, Pallas kernels, call(): pl.pallas_call(kernel, out_shape=[jax.ShapeDtypeStruct(s, t) for s, t in...  17.3 us
    ppermute x1, starting transfers between devices, along_width(): lax.ppermute(x, WIDTH, [(i, i - 1 + 2 * (i % 2)) for i in range(1, count...  16.8 us
    all_to_all x1, blocking collectives, exchanged(): return lax.all_to_all(parts, axes, 0, 0, tiled=True)  14.3 us
    ppermute x1, starting transfers between devices, local(): other = lax.ppermute(mine, 'core', swap)  8.6 us
    ppermute x4, starting transfers between devices, beside(): after = lax.ppermute(leading, axis, line(count, -1))  5.3 us
  transfers between devices with their start and end apart: 15, of which 8 were waited for; matrix products, arithmetic and copies ran while one was open for 3% of the time, Pallas kernels for 5%

profile of v8, /device:TPU:1, one launch (start us, length us, event | category | flops | bytes accessed | tf_op | source)
XLA Modules:
  0.0 161.1 jit_solution(2523811407106329309)
XLA Ops:
  1.6 16.8 %collective-permute-start = (bf16[576,128]{1,0:T(8,128)(2,1)S(1)}, bf16[576,128]{1,0:T(8,128)(2,1)S(1)}, u32[]{:S(2)}, u32[]{:S(2)}) collective-permute-start(bf16[576,128]{1,0:T(8,128)(2,1)S(1)} %pad_maximum_fusion.3), channel_id=1, source_target_pairs={{1,2},{2,1},{3,4},{4,3},{5,6},{6,5},{7,8},{8,7},{9,10},{10,9},{11,... | collective-permute-start | bytes 442376 | tf_op jit(solution)/shard_map/ppermute | solution.py:262
  18.5 1.9 %collective-permute-start.1 = (bf16[576,128]{1,0:T(8,128)(2,1)S(1)}, bf16[576,128]{1,0:T(8,128)(2,1)S(1)}, u32[]{:S(2)}, u32[]{:S(2)}) collective-permute-start(bf16[576,128]{1,0:T(8,128)(2,1)S(1)} %pad_maximum_fusion.3), channel_id=1, source_target_pairs={{0,1},{1,0},{2,3},{3,2},{4,5},{5,4},{6,7},{7,6},{8,9},{9,8},{10,11... | collective-permute-start | bytes 442376 | tf_op jit(solution)/shard_map/ppermute | solution.py:263
  23.9 12.3 %collective-permute-start.2 = (bf16[8,3,24,128]{3,2,1,0:T(8,128)(2,1)S(1)}, bf16[8,3,24,128]{3,2,1,0:T(8,128)(2,1)S(1)}, u32[]{:S(2)}, u32[]{:S(2)}) collective-permute-start(bf16[8,3,24,128]{3,2,1,0:T(8,128)(2,1)S(1)} %pad_maximum_fusion.4), channel_id=1, source_target_pairs={{0,16},{16,32},{32,48},{48,64},{64,80},{80,96},{96,112},{1,17},{17... | collective-permute-start | bytes 442376 | tf_op jit(solution)/shard_map/ppermute | solution.py:256
  36.2 2.1 %shard_map.75.refs_9_ = f32[6,6,24,128]{3,2,1,0:T(8,128)S(1)} custom-call(bf16[8,192,128]{2,1,0:T(8,128)(2,1)S(1)} %bitcast.31, bf16[3456,128]{1,0:T(8,128)(2,1)S(1)} %bitcast.34), custom_call_target="tpu_custom_call" | custom-call | flops 764411904 | bytes 1720320 | tf_op jit(solution)/shard_map/pallas_call | solution.py:240
  40.1 4.0 %collective-permute-start.4 = (bf16[3,14,24,128]{3,2,1,0:T(8,128)(2,1)S(1)}, bf16[3,14,24,128]{3,2,1,0:T(8,128)(2,1)S(1)}, u32[]{:S(2)}, u32[]{:S(2)}) collective-permute-start(bf16[3,14,24,128]{3,2,1,0:T(8,128)(2,1)S(1)} %pad_maximum_fusion.1), channel_id=1, source_target_pairs={{0,128},{128,256},{256,384},{1,129},{129,257},{257,385},{2,130},{1... | collective-permute-start | bytes 774152 | tf_op jit(solution)/shard_map/ppermute | solution.py:256
  44.1 2.1 %shard_map.76.refs_10_ = f32[6,6,24,128]{3,2,1,0:T(8,128)S(1)} custom-call(bf16[8,192,128]{2,1,0:T(8,128)(2,1)S(1)} %bitcast.32, bf16[8,72,128]{2,1,0:T(8,128)(2,1)S(1)} %bitcast.44, bf16[8,72,128]{2,1,0:T(8,128)(2,1)S(1)} %bitcast.42, bf16[3456,128]{1,0:T(8,128)(2,1)S(1)} %bitcast.35), custom_call_target="tpu_custom_call" | custom-call | flops 764411904 | bytes 2015232 | tf_op jit(solution)/shard_map/pallas_call | solution.py:240
  47.3 9.7 %shard_map.77 = (f32[128,128]{1,0:T(8,128)S(1)}, bf16[128,128]{1,0:T(8,128)(2,1)S(1)}, f32[12,12,24,128]{3,2,1,0:T(8,128)S(1)}, bf16[3456,128]{1,0:T(8,128)(2,1)S(1)}, bf16[3456,128]{1,0:T(8,128)(2,1)S(1)}) custom-call(s32[3]{0:T(128)S(1)} %pad_add_fusion.refs_0_, bf16[8,192,128]{2,1,0:T(8,128)(2,1)S(1)} %bitcast.33, bf16[8,72,128]{2,1,0:T(8,128)(2,1)S(1)} %bitcast.45, ...), custom_call_target="tpu_custom_call" | custom-call | flops 3538944000 | bytes 7561228 | tf_op jit(solution)/shard_map/pallas_call | solution.py:240
  57.1 1.9 %collective-permute-start.6 = (bf16[3456,128]{1,0:T(8,128)(2,1)S(1)}, bf16[3456,128]{1,0:T(8,128)(2,1)S(1)}, u32[]{:S(2)}, u32[]{:S(2)}) collective-permute-start(bf16[3456,128]{1,0:T(8,128)(2,1)S(1)} %broadcast_select_fusion.2), channel_id=1, source_target_pairs={{0,1},{1,0},{2,3},{3,2},{4,5},{5,4},{6,7},{7,6},{8,9},{9,8},{10,11... | collective-permute-start | bytes 2654216 | tf_op jit(solution)/shard_map/ppermute | solution.py:361
  59.0 2.4 %collective-permute-done.6 = bf16[3456,128]{1,0:T(8,128)(2,1)S(1)} collective-permute-done((bf16[3456,128]{1,0:T(8,128)(2,1)S(1)}, bf16[3456,128]{1,0:T(8,128)(2,1)S(1)}, u32[]{:S(2)}, u32[]{:S(2)}) %collective-permute-start.6) | collective-permute-done | bytes 884768 | tf_op jit(solution)/shard_map/ppermute | solution.py:361
  62.7 11.6 %all-to-all-start = ((bf16[16,216,128]{2,1,0:T(8,128)(2,1)}), bf16[16,216,128]{2,1,0:T(8,128)(2,1)S(1)}, u32[]{:S(2)}, u32[]{:S(2)}) async-start(bf16[16,216,128]{2,1,0:T(8,128)(2,1)} %bitcast.49), calls=%async_computation | async-start | bytes 1769472 | tf_op jit(solution)/shard_map/all_to_all | solution.py:273
  75.1 4.3 %collective-permute-start.7 = (bf16[4,2,8,128]{3,2,1,0:T(8,128)(2,1)S(1)}, bf16[4,2,8,128]{3,2,1,0:T(8,128)(2,1)S(1)}, u32[]{:S(2)}, u32[]{:S(2)}) collective-permute-start(bf16[4,2,8,128]{3,2,1,0:T(8,128)(2,1)S(1)} %get-tuple-element.51), channel_id=1, source_target_pairs={{0,16},{16,32},{32,48},{48,64},{64,80},{80,96},{96,112},{1,17},{17... | collective-permute-start | bytes 49160 | tf_op jit(solution)/shard_map/ppermute | solution.py:256
  80.7 1.5 fusion
  82.2 2.0 %collective-permute-done.8 = bf16[4,2,8,128]{3,2,1,0:T(8,128)(2,1)} collective-permute-done((bf16[4,2,8,128]{3,2,1,0:T(8,128)(2,1)S(1)}, bf16[4,2,8,128]{3,2,1,0:T(8,128)(2,1)}, u32[]{:S(2)}, u32[]{:S(2)}) %collective-permute-start.8) | collective-permute-done | bytes 16416 | tf_op jit(solution)/shard_map/ppermute | solution.py:257
  84.2 3.9 %all-to-all-done.parts = bf16[16,216,128]{2,1,0:T(8,128)(2,1)S(1)} async-done(((bf16[16,216,128]{2,1,0:T(8,128)(2,1)}), bf16[16,216,128]{2,1,0:T(8,128)(2,1)S(1)}, u32[]{:S(2)}, u32[]{:S(2)}) %all-to-all-start) | async-done | bytes 884768 | tf_op jit(solution)/shard_map/all_to_all | solution.py:273
  88.8 14.0 %all-to-all-start.1 = ((bf16[16,16,128]{2,1,0:T(8,128)(2,1)}), bf16[16,16,128]{2,1,0:T(8,128)(2,1)S(1)}, u32[]{:S(2)}, u32[]{:S(2)}) async-start(bf16[16,16,128]{2,1,0:T(8,128)(2,1)} %bitcast.41), calls=%async_computation.1 | async-start | bytes 131072 | tf_op jit(solution)/shard_map/all_to_all | solution.py:273
  102.8 12.1 %all-to-all-done.1.parts = bf16[16,16,128]{2,1,0:T(8,128)(2,1)S(1)} async-done(((bf16[16,16,128]{2,1,0:T(8,128)(2,1)}), bf16[16,16,128]{2,1,0:T(8,128)(2,1)S(1)}, u32[]{:S(2)}, u32[]{:S(2)}) %all-to-all-start.1) | async-done | bytes 65568 | tf_op jit(solution)/shard_map/all_to_all | solution.py:273
  114.9 14.3 %all_to_all.20 = bf16[16,16,128]{2,1,0:T(8,128)(2,1)S(1)} all-to-all(bf16[16,16,128]{2,1,0:T(8,128)(2,1)S(1)} %shard_map.79), channel_id=1, replica_groups=mesh['gx'=4,'gy'=8,'y'=4,'zh'=2,'core'=2] {'gy','zh'}, dimensions={0} | all-to-all | bytes 131072 | tf_op jit(solution)/shard_map/all_to_all | solution.py:273
  130.3 4.5 %all-to-all-start.3 = ((bf16[16,216,128]{2,1,0:T(8,128)(2,1)}), bf16[16,216,128]{2,1,0:T(8,128)(2,1)}, u32[]{:S(2)}, u32[]{:S(2)}) async-start(bf16[16,216,128]{2,1,0:T(8,128)(2,1)} %broadcast_in_dim.2), calls=%async_computation.3 | async-start | bytes 1769472 | tf_op jit(solution)/shard_map/all_to_all | solution.py:273
  136.9 4.0 %collective-permute-start.9 = (bf16[2,8,8,128]{3,2,1,0:T(8,128)(2,1)S(1)}, bf16[2,8,8,128]{3,2,1,0:T(8,128)(2,1)S(1)}, u32[]{:S(2)}, u32[]{:S(2)}) collective-permute-start(bf16[2,8,8,128]{3,2,1,0:T(8,128)(2,1)S(1)} %get-tuple-element.48), channel_id=1, source_target_pairs={{0,128},{128,256},{256,384},{1,129},{129,257},{257,385},{2,130},{1... | collective-permute-start | bytes 98312 | tf_op jit(solution)/shard_map/ppermute | solution.py:256
  140.9 1.5 collective-permute-done.10
  143.9 2.0 %all-to-all-done.3 = bf16[16,216,128]{2,1,0:T(8,128)(2,1)} async-done(((bf16[16,216,128]{2,1,0:T(8,128)(2,1)}), bf16[16,216,128]{2,1,0:T(8,128)(2,1)}, u32[]{:S(2)}, u32[]{:S(2)}) %all-to-all-start.3) | async-done | bytes 884768 | tf_op jit(solution)/shard_map/all_to_all | solution.py:273
  145.8 8.6 %collective-permute-start.11 = (bf16[3456,128]{1,0:T(8,128)(2,1)}, bf16[3456,128]{1,0:T(8,128)(2,1)S(1)}, u32[]{:S(2)}, u32[]{:S(2)}) collective-permute-start(bf16[3456,128]{1,0:T(8,128)(2,1)} %bitcast.24), channel_id=1, source_target_pairs={{0,1},{1,0},{2,3},{3,2},{4,5},{5,4},{6,7},{7,6},{8,9},{9,8},{10,11... | collective-permute-start | bytes 2654216 | tf_op jit(solution)/shard_map/ppermute | solution.py:389
  155.4 3.3 %shard_map.80 = bf16[512,128]{1,0:T(8,128)(2,1)} custom-call(bf16[512,128]{1,0:T(8,128)(2,1)S(1)} %bitcast.37, bf16[27,128,128]{2,1,0:T(8,128)(2,1)S(1)} %copy-done.2, f32[12,12,24,128]{3,2,1,0:T(8,128)S(1)} %get-tuple-element.30.slope, bf16[27,128,128]{2,1,0:T(8,128)(2,1)S(1)} %copy-done), custom_call_target="tpu_custom_call" | custom-call | flops 707788800 | bytes 3801088 | tf_op jit(solution)/shard_map/pallas_call | solution.py:240
  158.6 2.5 %broadcast_select_fusion = (bf16[3456,128]{1,0:T(8,128)(2,1)}, bf16[3456,128]{1,0:T(8,128)(2,1)}) fusion(bf16[3456,128]{1,0:T(8,128)(2,1)S(1)} %collective-permute-done.11, pred[]{:T(512)S(6)} %eq.4, bf16[16,216,128]{2,1,0:T(8,128)(2,1)} %all-to-all-done.3), kind=kLoop, calls=%fused_computation.1 | loop fusion | flops 884736 | bytes 3538945 | tf_op jit(solution)/shard_map/jit(_where)/select_n | solution.py:391
  (62 shorter events, 16.8 us)
Async XLA Ops:
  0.6 21.8 %copy-start.7 = (bf16[8,8,8,128]{3,2,1,0:T(8,128)(2,1)S(1)}, bf16[8,8,8,128]{3,2,1,0:T(8,128)(2,1)}, u32[]{:S(2)}) copy-start(bf16[8,8,8,128]{3,2,1,0:T(8,128)(2,1)} %param.4) | copy-start | bytes 393220
  1.6 20.7 %collective-permute-start = (bf16[576,128]{1,0:T(8,128)(2,1)S(1)}, bf16[576,128]{1,0:T(8,128)(2,1)S(1)}, u32[]{:S(2)}, u32[]{:S(2)}) collective-permute-start(bf16[576,128]{1,0:T(8,128)(2,1)S(1)} %pad_maximum_fusion.3), channel_id=1, source_target_pairs={{1,2},{2,1},{3,4},{4,3},{5,6},{6,5},{7,8},{8,7},{9,10},{10,9},{11,... | collective-permute-start | bytes 442376 | tf_op jit(solution)/shard_map/ppermute | solution.py:262
  18.5 3.8 %collective-permute-start.1 = (bf16[576,128]{1,0:T(8,128)(2,1)S(1)}, bf16[576,128]{1,0:T(8,128)(2,1)S(1)}, u32[]{:S(2)}, u32[]{:S(2)}) collective-permute-start(bf16[576,128]{1,0:T(8,128)(2,1)S(1)} %pad_maximum_fusion.3), channel_id=1, source_target_pairs={{0,1},{1,0},{2,3},{3,2},{4,5},{5,4},{6,7},{7,6},{8,9},{9,8},{10,11... | collective-permute-start | bytes 442376 | tf_op jit(solution)/shard_map/ppermute | solution.py:263
  21.2 15.0 %copy-start = (bf16[27,128,128]{2,1,0:T(8,128)(2,1)S(1)}, bf16[27,128,128]{2,1,0:T(8,128)(2,1)}, u32[]{:S(2)}) copy-start(bf16[27,128,128]{2,1,0:T(8,128)(2,1)} %weights.1) | copy-start | bytes 2654212
  22.5 15.9 %collective-permute-start.3 = (bf16[8,3,24,128]{3,2,1,0:T(8,128)(2,1)S(1)}, bf16[8,3,24,128]{3,2,1,0:T(8,128)(2,1)S(1)}, u32[]{:S(2)}, u32[]{:S(2)}) collective-permute-start(bf16[8,3,24,128]{3,2,1,0:T(8,128)(2,1)S(1)} %pad_maximum_fusion.5), channel_id=1, source_target_pairs={{16,0},{32,16},{48,32},{64,48},{80,64},{96,80},{112,96},{17,1},{33... | collective-permute-start | bytes 442376 | tf_op jit(solution)/shard_map/ppermute | solution.py:257
  23.9 14.6 %copy-start.8 = (bf16[4,4,4,128]{3,2,1,0:T(4,128)(2,1)S(1)}, bf16[4,4,4,128]{3,2,1,0:T(4,128)(2,1)}, u32[]{:S(2)}) copy-start(bf16[4,4,4,128]{3,2,1,0:T(4,128)(2,1)} %param.7) | copy-start | bytes 49156
  23.9 14.6 %collective-permute-start.2 = (bf16[8,3,24,128]{3,2,1,0:T(8,128)(2,1)S(1)}, bf16[8,3,24,128]{3,2,1,0:T(8,128)(2,1)S(1)}, u32[]{:S(2)}, u32[]{:S(2)}) collective-permute-start(bf16[8,3,24,128]{3,2,1,0:T(8,128)(2,1)S(1)} %pad_maximum_fusion.4), channel_id=1, source_target_pairs={{0,16},{16,32},{32,48},{48,64},{64,80},{80,96},{96,112},{1,17},{17... | collective-permute-start | bytes 442376 | tf_op jit(solution)/shard_map/ppermute | solution.py:256
  38.6 8.7 %copy-start.1 = (bf16[27,128,128]{2,1,0:T(8,128)(2,1)S(1)}, bf16[27,128,128]{2,1,0:T(8,128)(2,1)}, u32[]{:S(2)}) copy-start(bf16[27,128,128]{2,1,0:T(8,128)(2,1)} %coarse_weights.1) | copy-start | bytes 2654212
  38.6 7.6 %collective-permute-start.5 = (bf16[3,14,24,128]{3,2,1,0:T(8,128)(2,1)S(1)}, bf16[3,14,24,128]{3,2,1,0:T(8,128)(2,1)S(1)}, u32[]{:S(2)}, u32[]{:S(2)}) collective-permute-start(bf16[3,14,24,128]{3,2,1,0:T(8,128)(2,1)S(1)} %pad_maximum_fusion.2), channel_id=1, source_target_pairs={{128,0},{256,128},{384,256},{129,1},{257,129},{385,257},{130,2},{2... | collective-permute-start | bytes 774152 | tf_op jit(solution)/shard_map/ppermute | solution.py:257
  40.1 7.2 %collective-permute-start.4 = (bf16[3,14,24,128]{3,2,1,0:T(8,128)(2,1)S(1)}, bf16[3,14,24,128]{3,2,1,0:T(8,128)(2,1)S(1)}, u32[]{:S(2)}, u32[]{:S(2)}) collective-permute-start(bf16[3,14,24,128]{3,2,1,0:T(8,128)(2,1)S(1)} %pad_maximum_fusion.1), channel_id=1, source_target_pairs={{0,128},{128,256},{256,384},{1,129},{129,257},{257,385},{2,130},{1... | collective-permute-start | bytes 774152 | tf_op jit(solution)/shard_map/ppermute | solution.py:256
  57.0 5.7 %copy-start.4 = (bf16[128,128]{1,0:T(8,128)(2,1)}, bf16[128,128]{1,0:T(8,128)(2,1)S(1)}, u32[]{:S(2)}) copy-start(bf16[128,128]{1,0:T(8,128)(2,1)S(1)} %get-tuple-element.20) | copy-start | bytes 98308
  57.0 5.7 %copy-start.6 = (f32[128,128]{1,0:T(8,128)}, f32[128,128]{1,0:T(8,128)S(1)}, u32[]{:S(2)}) copy-start(f32[128,128]{1,0:T(8,128)S(1)} %get-tuple-element.21) | copy-start | bytes 196612
  57.1 4.3 %collective-permute-start.6 = (bf16[3456,128]{1,0:T(8,128)(2,1)S(1)}, bf16[3456,128]{1,0:T(8,128)(2,1)S(1)}, u32[]{:S(2)}, u32[]{:S(2)}) collective-permute-start(bf16[3456,128]{1,0:T(8,128)(2,1)S(1)} %broadcast_select_fusion.2), channel_id=1, source_target_pairs={{0,1},{1,0},{2,3},{3,2},{4,5},{5,4},{6,7},{7,6},{8,9},{9,8},{10,11... | collective-permute-start | bytes 2654216 | tf_op jit(solution)/shard_map/ppermute | solution.py:361
  62.7 25.3 %all-to-all-start = ((bf16[16,216,128]{2,1,0:T(8,128)(2,1)}), bf16[16,216,128]{2,1,0:T(8,128)(2,1)S(1)}, u32[]{:S(2)}, u32[]{:S(2)}) async-start(bf16[16,216,128]{2,1,0:T(8,128)(2,1)} %bitcast.49), calls=%async_computation | async-start | bytes 1769472 | tf_op jit(solution)/shard_map/all_to_all | solution.py:273
  75.1 7.1 %collective-permute-start.7 = (bf16[4,2,8,128]{3,2,1,0:T(8,128)(2,1)S(1)}, bf16[4,2,8,128]{3,2,1,0:T(8,128)(2,1)S(1)}, u32[]{:S(2)}, u32[]{:S(2)}) collective-permute-start(bf16[4,2,8,128]{3,2,1,0:T(8,128)(2,1)S(1)} %get-tuple-element.51), channel_id=1, source_target_pairs={{0,16},{16,32},{32,48},{48,64},{64,80},{80,96},{96,112},{1,17},{17... | collective-permute-start | bytes 49160 | tf_op jit(solution)/shard_map/ppermute | solution.py:256
  79.4 4.8 %collective-permute-start.8 = (bf16[4,2,8,128]{3,2,1,0:T(8,128)(2,1)S(1)}, bf16[4,2,8,128]{3,2,1,0:T(8,128)(2,1)}, u32[]{:S(2)}, u32[]{:S(2)}) collective-permute-start(bf16[4,2,8,128]{3,2,1,0:T(8,128)(2,1)S(1)} %get-tuple-element.50), channel_id=1, source_target_pairs={{16,0},{32,16},{48,32},{64,48},{80,64},{96,80},{112,96},{17,1},{33... | collective-permute-start | bytes 49160 | tf_op jit(solution)/shard_map/ppermute | solution.py:257
  88.2 0.6 copy-start.5
  88.8 26.1 %all-to-all-start.1 = ((bf16[16,16,128]{2,1,0:T(8,128)(2,1)}), bf16[16,16,128]{2,1,0:T(8,128)(2,1)S(1)}, u32[]{:S(2)}, u32[]{:S(2)}) async-start(bf16[16,16,128]{2,1,0:T(8,128)(2,1)} %bitcast.41), calls=%async_computation.1 | async-start | bytes 131072 | tf_op jit(solution)/shard_map/all_to_all | solution.py:273
  114.9 39.6 %copy-start.2 = (bf16[27,128,128]{2,1,0:T(8,128)(2,1)S(1)}, bf16[27,128,128]{2,1,0:T(8,128)(2,1)}, u32[]{:S(2)}) copy-start(bf16[27,128,128]{2,1,0:T(8,128)(2,1)} %coarse_weights.1) | copy-start | bytes 2654212
  130.3 15.6 %all-to-all-start.3 = ((bf16[16,216,128]{2,1,0:T(8,128)(2,1)}), bf16[16,216,128]{2,1,0:T(8,128)(2,1)}, u32[]{:S(2)}, u32[]{:S(2)}) async-start(bf16[16,216,128]{2,1,0:T(8,128)(2,1)} %broadcast_in_dim.2), calls=%async_computation.3 | async-start | bytes 1769472 | tf_op jit(solution)/shard_map/all_to_all | solution.py:273
  135.6 6.8 %collective-permute-start.10 = (bf16[2,8,8,128]{3,2,1,0:T(8,128)(2,1)S(1)}, bf16[2,8,8,128]{3,2,1,0:T(8,128)(2,1)S(1)}, u32[]{:S(2)}, u32[]{:S(2)}) collective-permute-start(bf16[2,8,8,128]{3,2,1,0:T(8,128)(2,1)S(1)} %get-tuple-element.49), channel_id=1, source_target_pairs={{128,0},{256,128},{384,256},{129,1},{257,129},{385,257},{130,2},{2... | collective-permute-start | bytes 98312 | tf_op jit(solution)/shard_map/ppermute | solution.py:257
  136.9 5.5 %collective-permute-start.9 = (bf16[2,8,8,128]{3,2,1,0:T(8,128)(2,1)S(1)}, bf16[2,8,8,128]{3,2,1,0:T(8,128)(2,1)S(1)}, u32[]{:S(2)}, u32[]{:S(2)}) collective-permute-start(bf16[2,8,8,128]{3,2,1,0:T(8,128)(2,1)S(1)} %get-tuple-element.48), channel_id=1, source_target_pairs={{0,128},{128,256},{256,384},{1,129},{129,257},{257,385},{2,130},{1... | collective-permute-start | bytes 98312 | tf_op jit(solution)/shard_map/ppermute | solution.py:256
  145.8 12.8 %collective-permute-start.11 = (bf16[3456,128]{1,0:T(8,128)(2,1)}, bf16[3456,128]{1,0:T(8,128)(2,1)S(1)}, u32[]{:S(2)}, u32[]{:S(2)}) collective-permute-start(bf16[3456,128]{1,0:T(8,128)(2,1)} %bitcast.24), channel_id=1, source_target_pairs={{0,1},{1,0},{2,3},{3,2},{4,5},{5,4},{6,7},{7,6},{8,9},{9,8},{10,11... | collective-permute-start | bytes 2654216 | tf_op jit(solution)/shard_map/ppermute | solution.py:389
  154.5 0.9 copy-start.3

commit v9 on v8

--- a/solution.py
+++ b/solution.py
@@ -187,15 +187,21 @@
         )
 
 
-def volume_kernel(around, coarse_weights, slope, weights, out_ref, grads, spread, fine):
-    for x in range(8):
-        grads[x, :, :8] = around[64 * x : 64 * x + 64].astype(F32).reshape(8, 8, C)
+def fine_grad_kernel(left, middle, right, coarse_weights, slope, fine_ref, grads, spread):
+    for x in range(2):
+        for at, part in ((x, left), (6 + x, right)):
+            grads[at, :, :8] = part[64 * x : 64 * x + 64].astype(F32).reshape(8, 8, C)
+    for x in range(4):
+        grads[2 + x, :, :8] = middle[64 * x : 64 * x + 64].astype(F32).reshape(8, 8, C)
     back = back_conv(grads, coarse_weights)
     spread[:, :, pl.ds(0, 8, 2)] = back
     spread[:, :, pl.ds(1, 8, 2)] = back
     for x in range(10):
         for y in range(10):
-            fine[x, y] = spread[(x + 1) // 2, (y + 1) // 2] * slope[x + 1, y + 1, 4:20]
+            fine_ref[x, y] = spread[(x + 1) // 2, (y + 1) // 2] * slope[x + 1, y + 1, 4:20]
+
+
+def volume_kernel(fine, weights, out_ref):
     total = jnp.zeros((512, C), F32)
     for i in range(3):
         cells = jnp.concatenate(
@@ -375,15 +381,26 @@
     part = joined(parts)[:length]
     grads = jnp.concatenate([halo[0], grads, halo[1]], axis=1)
     halo = beside(grads[2:], grads[:2], "gx", peers[0])
-    around = jnp.concatenate([halo[0], grads, halo[1]], axis=0)
+    (fine_grad,) = call(
+        fine_grad_kernel,
+        [((10, 10, 16, C), F32)],
+        [
+            halo[0].reshape(128, C),
+            grads.reshape(256, C),
+            halo[1].reshape(128, C),
+            coarse_weight,
+            slope,
+        ],
+        scratch=[((8, 8, 16, C), F32), ((6, 6, 16, C), F32)],
+        flops=2 * 288 * 27 * C * C,
+    )
     parts = exchanged(jnp.broadcast_to(part[None], (plane, length, C)), PLANE)
-    parts, around = lax.optimization_barrier((parts, around))
+    parts, fine_grad = lax.optimization_barrier((parts, fine_grad))
     (grad_volume,) = call(
         volume_kernel,
         [((512, C), BF16)],
-        [around.reshape(512, C), coarse_weight, slope, fine_weight],
-        scratch=[((8, 8, 16, C), F32), ((6, 6, 16, C), F32), ((10, 10, 16, C), F32)],
-        flops=2 * 800 * 27 * C * C,
+        [fine_grad, fine_weight],
+        flops=2 * 512 * 27 * C * C,
     )
     mine = joined(parts)
     other = lax.ppermute(mine, "core", swap)

time: 162 us -> 161 us (level)
    ppermute x4, waiting for transfers between devices: 3.51 us -> 5.41 us  [beside(): after = lax.ppermute(leading, axis, line(count, -1))]
    pallas_call x6 -> x7, Pallas kernels: 17.3 us -> 16.5 us  [call(): pl.pallas_call(kernel, out_shape=[jax.ShapeDtypeStruct(s, t) for s, t in...]
  transfers between devices with their start and end apart: 15 -> 15, of which waited for: 8 -> 9; matrix products, arithmetic and copies ran while one was open for 3% -> 3% of each run, Pallas kernels for 5% -> 4%
where the time goes in v9:
time: 161 us; the launch traced here: 160 us
  starting transfers between devices  88.6 us (55%)
  waiting for transfers between devices  27.5 us (17%)
  Pallas kernels  16.5 us (10%)
  blocking collectives  14.2 us (9%)
  other arithmetic  7.38 us (5%)
  local copies, waits for them, and re-layouts  4.58 us (3%)
    all_to_all x3, starting transfers between devices, exchanged(): return lax.all_to_all(parts, axes, 0, 0, tiled=True)  30.2 us
    ppermute x4, starting transfers between devices, beside(): before = lax.ppermute(last, axis, line(count, 1))  23.8 us
    all_to_all x3, waiting for transfers between devices, exchanged(): return lax.all_to_all(parts, axes, 0, 0, tiled=True)  17.1 us
    ppermute x1, starting transfers between devices, along_width(): lax.ppermute(x, WIDTH, [(i, i - 1 + 2 * (i % 2)) for i in range(1, count...  16.8 us
    pallas_call x7, Pallas kernels, call(): pl.pallas_call(kernel, out_shape=[jax.ShapeDtypeStruct(s, t) for s, t in...  16.5 us
    all_to_all x1, blocking collectives, exchanged(): return lax.all_to_all(parts, axes, 0, 0, tiled=True)  14.2 us
    ppermute x1, starting transfers between devices, local(): other = lax.ppermute(mine, 'core', swap)  8.6 us
    ppermute x4, waiting for transfers between devices, beside(): after = lax.ppermute(leading, axis, line(count, -1))  5.41 us
  transfers between devices with their start and end apart: 15, of which 9 were waited for; matrix products, arithmetic and copies ran while one was open for 3% of the time, Pallas kernels for 4%

profile of v9, /device:TPU:1, one launch (start us, length us, event | category | flops | bytes accessed | tf_op | source)
XLA Modules:
  0.0 159.8 jit_solution(11644175958167658838)
XLA Ops:
  1.6 16.8 %collective-permute-start = (bf16[576,128]{1,0:T(8,128)(2,1)S(1)}, bf16[576,128]{1,0:T(8,128)(2,1)S(1)}, u32[]{:S(2)}, u32[]{:S(2)}) collective-permute-start(bf16[576,128]{1,0:T(8,128)(2,1)S(1)} %pad_maximum_fusion.3), channel_id=1, source_target_pairs={{1,2},{2,1},{3,4},{4,3},{5,6},{6,5},{7,8},{8,7},{9,10},{10,9},{11,... | collective-permute-start | bytes 442376 | tf_op jit(solution)/shard_map/ppermute | solution.py:268
  18.5 1.9 %collective-permute-start.1 = (bf16[576,128]{1,0:T(8,128)(2,1)S(1)}, bf16[576,128]{1,0:T(8,128)(2,1)S(1)}, u32[]{:S(2)}, u32[]{:S(2)}) collective-permute-start(bf16[576,128]{1,0:T(8,128)(2,1)S(1)} %pad_maximum_fusion.3), channel_id=1, source_target_pairs={{0,1},{1,0},{2,3},{3,2},{4,5},{5,4},{6,7},{7,6},{8,9},{9,8},{10,11... | collective-permute-start | bytes 442376 | tf_op jit(solution)/shard_map/ppermute | solution.py:269
  23.9 12.3 %collective-permute-start.2 = (bf16[8,3,24,128]{3,2,1,0:T(8,128)(2,1)S(1)}, bf16[8,3,24,128]{3,2,1,0:T(8,128)(2,1)S(1)}, u32[]{:S(2)}, u32[]{:S(2)}) collective-permute-start(bf16[8,3,24,128]{3,2,1,0:T(8,128)(2,1)S(1)} %pad_maximum_fusion.4), channel_id=1, source_target_pairs={{0,16},{16,32},{32,48},{48,64},{64,80},{80,96},{96,112},{1,17},{17... | collective-permute-start | bytes 442376 | tf_op jit(solution)/shard_map/ppermute | solution.py:262
  36.2 2.1 %shard_map.75.refs_9_ = f32[6,6,24,128]{3,2,1,0:T(8,128)S(1)} custom-call(bf16[8,192,128]{2,1,0:T(8,128)(2,1)S(1)} %bitcast.33, bf16[3456,128]{1,0:T(8,128)(2,1)S(1)} %bitcast.36), custom_call_target="tpu_custom_call" | custom-call | flops 764411904 | bytes 1720320 | tf_op jit(solution)/shard_map/pallas_call | solution.py:246
  38.6 1.4 collective-permute-start.5
  40.1 4.0 %collective-permute-start.4 = (bf16[3,14,24,128]{3,2,1,0:T(8,128)(2,1)S(1)}, bf16[3,14,24,128]{3,2,1,0:T(8,128)(2,1)S(1)}, u32[]{:S(2)}, u32[]{:S(2)}) collective-permute-start(bf16[3,14,24,128]{3,2,1,0:T(8,128)(2,1)S(1)} %pad_maximum_fusion.1), channel_id=1, source_target_pairs={{0,128},{128,256},{256,384},{1,129},{129,257},{257,385},{2,130},{1... | collective-permute-start | bytes 774152 | tf_op jit(solution)/shard_map/ppermute | solution.py:262
  44.1 2.1 %shard_map.76.refs_10_ = f32[6,6,24,128]{3,2,1,0:T(8,128)S(1)} custom-call(bf16[8,192,128]{2,1,0:T(8,128)(2,1)S(1)} %bitcast.34, bf16[8,72,128]{2,1,0:T(8,128)(2,1)S(1)} %bitcast.45, bf16[8,72,128]{2,1,0:T(8,128)(2,1)S(1)} %bitcast.43, bf16[3456,128]{1,0:T(8,128)(2,1)S(1)} %bitcast.37), custom_call_target="tpu_custom_call" | custom-call | flops 764411904 | bytes 2015232 | tf_op jit(solution)/shard_map/pallas_call | solution.py:246
  47.3 9.7 %shard_map.77 = (f32[128,128]{1,0:T(8,128)S(1)}, bf16[128,128]{1,0:T(8,128)(2,1)S(1)}, f32[12,12,24,128]{3,2,1,0:T(8,128)S(1)}, bf16[3456,128]{1,0:T(8,128)(2,1)S(1)}, bf16[3456,128]{1,0:T(8,128)(2,1)S(1)}) custom-call(s32[3]{0:T(128)S(1)} %pad_add_fusion.refs_0_, bf16[8,192,128]{2,1,0:T(8,128)(2,1)S(1)} %bitcast.35, bf16[8,72,128]{2,1,0:T(8,128)(2,1)S(1)} %bitcast.46, ...), custom_call_target="tpu_custom_call" | custom-call | flops 3538944000 | bytes 7561228 | tf_op jit(solution)/shard_map/pallas_call | solution.py:246
  57.1 1.9 %collective-permute-start.6 = (bf16[3456,128]{1,0:T(8,128)(2,1)S(1)}, bf16[3456,128]{1,0:T(8,128)(2,1)S(1)}, u32[]{:S(2)}, u32[]{:S(2)}) collective-permute-start(bf16[3456,128]{1,0:T(8,128)(2,1)S(1)} %broadcast_select_fusion.2), channel_id=1, source_target_pairs={{0,1},{1,0},{2,3},{3,2},{4,5},{5,4},{6,7},{7,6},{8,9},{9,8},{10,11... | collective-permute-start | bytes 2654216 | tf_op jit(solution)/shard_map/ppermute | solution.py:367
  59.0 2.4 %collective-permute-done.6 = bf16[3456,128]{1,0:T(8,128)(2,1)S(1)} collective-permute-done((bf16[3456,128]{1,0:T(8,128)(2,1)S(1)}, bf16[3456,128]{1,0:T(8,128)(2,1)S(1)}, u32[]{:S(2)}, u32[]{:S(2)}) %collective-permute-start.6) | collective-permute-done | bytes 884768 | tf_op jit(solution)/shard_map/ppermute | solution.py:367
  62.7 11.6 %all-to-all-start = ((bf16[16,216,128]{2,1,0:T(8,128)(2,1)}), bf16[16,216,128]{2,1,0:T(8,128)(2,1)S(1)}, u32[]{:S(2)}, u32[]{:S(2)}) async-start(bf16[16,216,128]{2,1,0:T(8,128)(2,1)} %bitcast.52), calls=%async_computation | async-start | bytes 1769472 | tf_op jit(solution)/shard_map/all_to_all | solution.py:279
  75.1 4.3 %collective-permute-start.7 = (bf16[4,2,8,128]{3,2,1,0:T(8,128)(2,1)S(1)}, bf16[4,2,8,128]{3,2,1,0:T(8,128)(2,1)S(1)}, u32[]{:S(2)}, u32[]{:S(2)}) collective-permute-start(bf16[4,2,8,128]{3,2,1,0:T(8,128)(2,1)S(1)} %get-tuple-element.51), channel_id=1, source_target_pairs={{0,16},{16,32},{32,48},{48,64},{64,80},{80,96},{96,112},{1,17},{17... | collective-permute-start | bytes 49160 | tf_op jit(solution)/shard_map/ppermute | solution.py:262
  80.6 1.5 fusion
  82.1 2.0 %collective-permute-done.8 = bf16[4,2,8,128]{3,2,1,0:T(8,128)(2,1)} collective-permute-done((bf16[4,2,8,128]{3,2,1,0:T(8,128)(2,1)S(1)}, bf16[4,2,8,128]{3,2,1,0:T(8,128)(2,1)}, u32[]{:S(2)}, u32[]{:S(2)}) %collective-permute-start.8) | collective-permute-done | bytes 16416 | tf_op jit(solution)/shard_map/ppermute | solution.py:263
  84.1 3.9 %all-to-all-done.parts = bf16[16,216,128]{2,1,0:T(8,128)(2,1)S(1)} async-done(((bf16[16,216,128]{2,1,0:T(8,128)(2,1)}), bf16[16,216,128]{2,1,0:T(8,128)(2,1)S(1)}, u32[]{:S(2)}, u32[]{:S(2)}) %all-to-all-start) | async-done | bytes 884768 | tf_op jit(solution)/shard_map/all_to_all | solution.py:279
  88.8 14.1 %all-to-all-start.1 = ((bf16[16,16,128]{2,1,0:T(8,128)(2,1)}), bf16[16,16,128]{2,1,0:T(8,128)(2,1)S(1)}, u32[]{:S(2)}, u32[]{:S(2)}) async-start(bf16[16,16,128]{2,1,0:T(8,128)(2,1)} %bitcast.40), calls=%async_computation.1 | async-start | bytes 131072 | tf_op jit(solution)/shard_map/all_to_all | solution.py:279
  102.9 12.1 %all-to-all-done.1.parts = bf16[16,16,128]{2,1,0:T(8,128)(2,1)S(1)} async-done(((bf16[16,16,128]{2,1,0:T(8,128)(2,1)}), bf16[16,16,128]{2,1,0:T(8,128)(2,1)S(1)}, u32[]{:S(2)}, u32[]{:S(2)}) %all-to-all-start.1) | async-done | bytes 65568 | tf_op jit(solution)/shard_map/all_to_all | solution.py:279
  115.0 14.2 %all_to_all.20 = bf16[16,16,128]{2,1,0:T(8,128)(2,1)S(1)} all-to-all(bf16[16,16,128]{2,1,0:T(8,128)(2,1)S(1)} %shard_map.79), channel_id=1, replica_groups=mesh['gx'=4,'gy'=8,'y'=4,'zh'=2,'core'=2] {'gy','zh'}, dimensions={0} | all-to-all | bytes 131072 | tf_op jit(solution)/shard_map/all_to_all | solution.py:279
  130.2 4.5 %all-to-all-start.3 = ((bf16[16,216,128]{2,1,0:T(8,128)(2,1)}), bf16[16,216,128]{2,1,0:T(8,128)(2,1)}, u32[]{:S(2)}, u32[]{:S(2)}) async-start(bf16[16,216,128]{2,1,0:T(8,128)(2,1)} %broadcast_in_dim.2), calls=%async_computation.3 | async-start | bytes 1769472 | tf_op jit(solution)/shard_map/all_to_all | solution.py:279
  135.5 3.2 %collective-permute-start.9 = (bf16[2,8,8,128]{3,2,1,0:T(8,128)(2,1)S(1)}, bf16[2,8,8,128]{3,2,1,0:T(8,128)(2,1)S(1)}, u32[]{:S(2)}, u32[]{:S(2)}) collective-permute-start(bf16[2,8,8,128]{3,2,1,0:T(8,128)(2,1)S(1)} %get-tuple-element.49), channel_id=1, source_target_pairs={{0,128},{128,256},{256,384},{1,129},{129,257},{257,385},{2,130},{1... | collective-permute-start | bytes 98312 | tf_op jit(solution)/shard_map/ppermute | solution.py:262
  140.5 3.4 %collective-permute-done.10 = bf16[2,8,8,128]{3,2,1,0:T(8,128)(2,1)S(1)} collective-permute-done((bf16[2,8,8,128]{3,2,1,0:T(8,128)(2,1)S(1)}, bf16[2,8,8,128]{3,2,1,0:T(8,128)(2,1)S(1)}, u32[]{:S(2)}, u32[]{:S(2)}) %collective-permute-start.10) | collective-permute-done | bytes 32800 | tf_op jit(solution)/shard_map/ppermute | solution.py:263
  145.8 8.6 %collective-permute-start.11 = (bf16[3456,128]{1,0:T(8,128)(2,1)}, bf16[3456,128]{1,0:T(8,128)(2,1)S(1)}, u32[]{:S(2)}, u32[]{:S(2)}) collective-permute-start(bf16[3456,128]{1,0:T(8,128)(2,1)} %bitcast.26), channel_id=1, source_target_pairs={{0,1},{1,0},{2,3},{3,2},{4,5},{5,4},{6,7},{7,6},{8,9},{9,8},{10,11... | collective-permute-start | bytes 2654216 | tf_op jit(solution)/shard_map/ppermute | solution.py:406
  155.6 1.7 %shard_map.81 = bf16[512,128]{1,0:T(8,128)(2,1)} custom-call(f32[10,10,16,128]{3,2,1,0:T(8,128)S(1)} %shard_map.80.fine, bf16[27,128,128]{2,1,0:T(8,128)(2,1)S(1)} %copy-done.2), custom_call_target="tpu_custom_call" | custom-call | flops 452984832 | bytes 1835008 | tf_op jit(solution)/shard_map/pallas_call | solution.py:246
  157.3 2.5 %broadcast_select_fusion = (bf16[3456,128]{1,0:T(8,128)(2,1)}, bf16[3456,128]{1,0:T(8,128)(2,1)}) fusion(bf16[3456,128]{1,0:T(8,128)(2,1)S(1)} %collective-permute-done.11, pred[]{:T(512)S(6)} %eq.4, bf16[16,216,128]{2,1,0:T(8,128)(2,1)} %all-to-all-done.3), kind=kLoop, calls=%fused_computation.1 | loop fusion | flops 884736 | bytes 3538945 | tf_op jit(solution)/shard_map/jit(_where)/select_n | solution.py:408
  (62 shorter events, 16.4 us)
Async XLA Ops:
  0.6 21.8 %copy-start.7 = (bf16[8,8,8,128]{3,2,1,0:T(8,128)(2,1)S(1)}, bf16[8,8,8,128]{3,2,1,0:T(8,128)(2,1)}, u32[]{:S(2)}) copy-start(bf16[8,8,8,128]{3,2,1,0:T(8,128)(2,1)} %param.4) | copy-start | bytes 393220
  1.6 20.7 %collective-permute-start = (bf16[576,128]{1,0:T(8,128)(2,1)S(1)}, bf16[576,128]{1,0:T(8,128)(2,1)S(1)}, u32[]{:S(2)}, u32[]{:S(2)}) collective-permute-start(bf16[576,128]{1,0:T(8,128)(2,1)S(1)} %pad_maximum_fusion.3), channel_id=1, source_target_pairs={{1,2},{2,1},{3,4},{4,3},{5,6},{6,5},{7,8},{8,7},{9,10},{10,9},{11,... | collective-permute-start | bytes 442376 | tf_op jit(solution)/shard_map/ppermute | solution.py:268
  18.5 3.8 %collective-permute-start.1 = (bf16[576,128]{1,0:T(8,128)(2,1)S(1)}, bf16[576,128]{1,0:T(8,128)(2,1)S(1)}, u32[]{:S(2)}, u32[]{:S(2)}) collective-permute-start(bf16[576,128]{1,0:T(8,128)(2,1)S(1)} %pad_maximum_fusion.3), channel_id=1, source_target_pairs={{0,1},{1,0},{2,3},{3,2},{4,5},{5,4},{6,7},{7,6},{8,9},{9,8},{10,11... | collective-permute-start | bytes 442376 | tf_op jit(solution)/shard_map/ppermute | solution.py:269
  21.2 15.0 %copy-start.1 = (bf16[27,128,128]{2,1,0:T(8,128)(2,1)S(1)}, bf16[27,128,128]{2,1,0:T(8,128)(2,1)}, u32[]{:S(2)}) copy-start(bf16[27,128,128]{2,1,0:T(8,128)(2,1)} %weights.1) | copy-start | bytes 2654212
  22.5 15.9 %collective-permute-start.3 = (bf16[8,3,24,128]{3,2,1,0:T(8,128)(2,1)S(1)}, bf16[8,3,24,128]{3,2,1,0:T(8,128)(2,1)S(1)}, u32[]{:S(2)}, u32[]{:S(2)}) collective-permute-start(bf16[8,3,24,128]{3,2,1,0:T(8,128)(2,1)S(1)} %pad_maximum_fusion.5), channel_id=1, source_target_pairs={{16,0},{32,16},{48,32},{64,48},{80,64},{96,80},{112,96},{17,1},{33... | collective-permute-start | bytes 442376 | tf_op jit(solution)/shard_map/ppermute | solution.py:263
  23.9 14.6 %copy-start.8 = (bf16[4,4,4,128]{3,2,1,0:T(4,128)(2,1)S(1)}, bf16[4,4,4,128]{3,2,1,0:T(4,128)(2,1)}, u32[]{:S(2)}) copy-start(bf16[4,4,4,128]{3,2,1,0:T(4,128)(2,1)} %param.7) | copy-start | bytes 49156
  23.9 14.6 %collective-permute-start.2 = (bf16[8,3,24,128]{3,2,1,0:T(8,128)(2,1)S(1)}, bf16[8,3,24,128]{3,2,1,0:T(8,128)(2,1)S(1)}, u32[]{:S(2)}, u32[]{:S(2)}) collective-permute-start(bf16[8,3,24,128]{3,2,1,0:T(8,128)(2,1)S(1)} %pad_maximum_fusion.4), channel_id=1, source_target_pairs={{0,16},{16,32},{32,48},{48,64},{64,80},{80,96},{96,112},{1,17},{17... | collective-permute-start | bytes 442376 | tf_op jit(solution)/shard_map/ppermute | solution.py:262
  38.6 8.7 %copy-start = (bf16[27,128,128]{2,1,0:T(8,128)(2,1)S(1)}, bf16[27,128,128]{2,1,0:T(8,128)(2,1)}, u32[]{:S(2)}) copy-start(bf16[27,128,128]{2,1,0:T(8,128)(2,1)} %coarse_weights.1) | copy-start | bytes 2654212
  38.6 7.6 %collective-permute-start.5 = (bf16[3,14,24,128]{3,2,1,0:T(8,128)(2,1)S(1)}, bf16[3,14,24,128]{3,2,1,0:T(8,128)(2,1)S(1)}, u32[]{:S(2)}, u32[]{:S(2)}) collective-permute-start(bf16[3,14,24,128]{3,2,1,0:T(8,128)(2,1)S(1)} %pad_maximum_fusion.2), channel_id=1, source_target_pairs={{128,0},{256,128},{384,256},{129,1},{257,129},{385,257},{130,2},{2... | collective-permute-start | bytes 774152 | tf_op jit(solution)/shard_map/ppermute | solution.py:263
  40.1 7.2 %collective-permute-start.4 = (bf16[3,14,24,128]{3,2,1,0:T(8,128)(2,1)S(1)}, bf16[3,14,24,128]{3,2,1,0:T(8,128)(2,1)S(1)}, u32[]{:S(2)}, u32[]{:S(2)}) collective-permute-start(bf16[3,14,24,128]{3,2,1,0:T(8,128)(2,1)S(1)} %pad_maximum_fusion.1), channel_id=1, source_target_pairs={{0,128},{128,256},{256,384},{1,129},{129,257},{257,385},{2,130},{1... | collective-permute-start | bytes 774152 | tf_op jit(solution)/shard_map/ppermute | solution.py:262
  57.0 5.7 %copy-start.4 = (bf16[128,128]{1,0:T(8,128)(2,1)}, bf16[128,128]{1,0:T(8,128)(2,1)S(1)}, u32[]{:S(2)}) copy-start(bf16[128,128]{1,0:T(8,128)(2,1)S(1)} %get-tuple-element.20) | copy-start | bytes 98308
  57.0 5.7 %copy-start.6 = (f32[128,128]{1,0:T(8,128)}, f32[128,128]{1,0:T(8,128)S(1)}, u32[]{:S(2)}) copy-start(f32[128,128]{1,0:T(8,128)S(1)} %get-tuple-element.21) | copy-start | bytes 196612
  57.1 4.3 %collective-permute-start.6 = (bf16[3456,128]{1,0:T(8,128)(2,1)S(1)}, bf16[3456,128]{1,0:T(8,128)(2,1)S(1)}, u32[]{:S(2)}, u32[]{:S(2)}) collective-permute-start(bf16[3456,128]{1,0:T(8,128)(2,1)S(1)} %broadcast_select_fusion.2), channel_id=1, source_target_pairs={{0,1},{1,0},{2,3},{3,2},{4,5},{5,4},{6,7},{7,6},{8,9},{9,8},{10,11... | collective-permute-start | bytes 2654216 | tf_op jit(solution)/shard_map/ppermute | solution.py:367
  62.7 25.3 %all-to-all-start = ((bf16[16,216,128]{2,1,0:T(8,128)(2,1)}), bf16[16,216,128]{2,1,0:T(8,128)(2,1)S(1)}, u32[]{:S(2)}, u32[]{:S(2)}) async-start(bf16[16,216,128]{2,1,0:T(8,128)(2,1)} %bitcast.52), calls=%async_computation | async-start | bytes 1769472 | tf_op jit(solution)/shard_map/all_to_all | solution.py:279
  75.1 7.1 %collective-permute-start.7 = (bf16[4,2,8,128]{3,2,1,0:T(8,128)(2,1)S(1)}, bf16[4,2,8,128]{3,2,1,0:T(8,128)(2,1)S(1)}, u32[]{:S(2)}, u32[]{:S(2)}) collective-permute-start(bf16[4,2,8,128]{3,2,1,0:T(8,128)(2,1)S(1)} %get-tuple-element.51), channel_id=1, source_target_pairs={{0,16},{16,32},{32,48},{48,64},{64,80},{80,96},{96,112},{1,17},{17... | collective-permute-start | bytes 49160 | tf_op jit(solution)/shard_map/ppermute | solution.py:262
  79.3 4.8 %collective-permute-start.8 = (bf16[4,2,8,128]{3,2,1,0:T(8,128)(2,1)S(1)}, bf16[4,2,8,128]{3,2,1,0:T(8,128)(2,1)}, u32[]{:S(2)}, u32[]{:S(2)}) collective-permute-start(bf16[4,2,8,128]{3,2,1,0:T(8,128)(2,1)S(1)} %get-tuple-element.50), channel_id=1, source_target_pairs={{16,0},{32,16},{48,32},{64,48},{80,64},{96,80},{112,96},{17,1},{33... | collective-permute-start | bytes 49160 | tf_op jit(solution)/shard_map/ppermute | solution.py:263
  88.1 0.6 copy-start.3
  88.8 46.0 %copy-start.5 = (bf16[128,128]{1,0:T(8,128)(2,1)S(1)}, bf16[128,128]{1,0:T(8,128)(2,1)}, u32[]{:S(2)}) copy-start(bf16[128,128]{1,0:T(8,128)(2,1)} %copy-done.4) | copy-start | bytes 98308
  88.8 26.2 %all-to-all-start.1 = ((bf16[16,16,128]{2,1,0:T(8,128)(2,1)}), bf16[16,16,128]{2,1,0:T(8,128)(2,1)S(1)}, u32[]{:S(2)}, u32[]{:S(2)}) async-start(bf16[16,16,128]{2,1,0:T(8,128)(2,1)} %bitcast.40), calls=%async_computation.1 | async-start | bytes 131072 | tf_op jit(solution)/shard_map/all_to_all | solution.py:279
  130.2 15.6 %all-to-all-start.3 = ((bf16[16,216,128]{2,1,0:T(8,128)(2,1)}), bf16[16,216,128]{2,1,0:T(8,128)(2,1)}, u32[]{:S(2)}, u32[]{:S(2)}) async-start(bf16[16,216,128]{2,1,0:T(8,128)(2,1)} %broadcast_in_dim.2), calls=%async_computation.3 | async-start | bytes 1769472 | tf_op jit(solution)/shard_map/all_to_all | solution.py:279
  135.5 5.0 %collective-permute-start.9 = (bf16[2,8,8,128]{3,2,1,0:T(8,128)(2,1)S(1)}, bf16[2,8,8,128]{3,2,1,0:T(8,128)(2,1)S(1)}, u32[]{:S(2)}, u32[]{:S(2)}) collective-permute-start(bf16[2,8,8,128]{3,2,1,0:T(8,128)(2,1)S(1)} %get-tuple-element.49), channel_id=1, source_target_pairs={{0,128},{128,256},{256,384},{1,129},{129,257},{257,385},{2,130},{1... | collective-permute-start | bytes 98312 | tf_op jit(solution)/shard_map/ppermute | solution.py:262
  138.8 5.2 %collective-permute-start.10 = (bf16[2,8,8,128]{3,2,1,0:T(8,128)(2,1)S(1)}, bf16[2,8,8,128]{3,2,1,0:T(8,128)(2,1)S(1)}, u32[]{:S(2)}, u32[]{:S(2)}) collective-permute-start(bf16[2,8,8,128]{3,2,1,0:T(8,128)(2,1)S(1)} %get-tuple-element.48), channel_id=1, source_target_pairs={{128,0},{256,128},{384,256},{129,1},{257,129},{385,257},{130,2},{2... | collective-permute-start | bytes 98312 | tf_op jit(solution)/shard_map/ppermute | solution.py:263
  145.8 11.5 %collective-permute-start.11 = (bf16[3456,128]{1,0:T(8,128)(2,1)}, bf16[3456,128]{1,0:T(8,128)(2,1)S(1)}, u32[]{:S(2)}, u32[]{:S(2)}) collective-permute-start(bf16[3456,128]{1,0:T(8,128)(2,1)} %bitcast.26), channel_id=1, source_target_pairs={{0,1},{1,0},{2,3},{3,2},{4,5},{5,4},{6,7},{7,6},{8,9},{9,8},{10,11... | collective-permute-start | bytes 2654216 | tf_op jit(solution)/shard_map/ppermute | solution.py:406
  154.4 1.2 copy-start.2

commit v10 on v9

--- a/solution.py
+++ b/solution.py
@@ -212,7 +212,9 @@
             ],
             axis=1,
         )
-        turned = jnp.concatenate([weights[9 * i + t] for t in range(9)], axis=1)
+        turned = jnp.concatenate(
+            [weights[(9 * i + t) * C : (9 * i + t + 1) * C] for t in range(9)], axis=1
+        )
         total = total + lax.dot_general(
             cells, turned, (((1,), (1,)), ((), ())), preferred_element_type=F32
         )
@@ -249,7 +251,7 @@
         in_specs=in_specs,
         out_specs=[pl.BlockSpec(memory_space=pltpu.VMEM) for _ in outs],
         scratch_shapes=[pltpu.VMEM(s, t) for s, t in scratch],
-        compiler_params=pltpu.CompilerParams(vmem_limit_bytes=40 * 1024 * 1024),
+        compiler_params=pltpu.CompilerParams(vmem_limit_bytes=28 * 1024 * 1024),
         cost_estimate=pl.CostEstimate(flops=flops, bytes_accessed=moved, transcendentals=0),
     )(*inputs)
 
@@ -294,23 +296,18 @@
 
     fine_rows = fine_weight.reshape(27 * C, C)
 
-    packed = jnp.concatenate([volume.reshape(512, C), cotangent.reshape(64, C)], axis=0)
-    before, after = in_order(*along_width(packed, peers[2]))
-    before_cells, after_cells = (b[:512].reshape(8, 8, 8, C) for b in (before, after))
+    halo = along_width(volume, peers[2])
+    cots = along_width(cotangent, peers[2])
+    halo, cots = lax.optimization_barrier((halo, cots))
+    before_cells, after_cells = in_order(*halo)
     slabs = [
         jnp.concatenate([before_cells[:, at], volume[:, at], after_cells[:, at]], axis=2)
         for at in (slice(5, 8), slice(0, 3))
     ]
     below, above = beside(slabs[0], slabs[1], "gy", peers[1])
     own = jnp.concatenate([before_cells, volume, after_cells], axis=2)
-    incoming = jnp.concatenate(
-        [
-            before[512:].reshape(4, 4, 4, C)[:, :, 2:],
-            cotangent,
-            after[512:].reshape(4, 4, 4, C)[:, :, :2],
-        ],
-        axis=2,
-    ).astype(F32)
+    before, after = in_order(*cots)
+    incoming = jnp.concatenate([before[:, :, 2:], cotangent, after[:, :, :2]], axis=2).astype(F32)
     sides = [
         jnp.concatenate([below[at], own[at], above[at]], axis=1)
         for at in (slice(5, 8), slice(0, 3))
@@ -399,7 +396,7 @@
     (grad_volume,) = call(
         volume_kernel,
         [((512, C), BF16)],
-        [fine_grad, fine_weight],
+        [fine_grad, fine_rows],
         flops=2 * 512 * 27 * C * C,
     )
     mine = joined(parts)

time: 161 us -> 161 us (level)
  waiting for transfers between devices: 27.5 us -> 34.8 us
  starting transfers between devices: 88.6 us -> 81.8 us
    ppermute x1 -> x2, waiting for transfers between devices: 0.97 us -> 9.39 us  [along_width(): lax.ppermute(x, WIDTH, [(i, i - 1 + 2 * (i % 2)) for i in range(1, count...]
    ppermute x4, starting transfers between devices: 23.8 us -> 16.6 us  [beside(): before = lax.ppermute(last, axis, line(count, 1))]
    all_to_all x3, starting transfers between devices: 30.2 us -> 26.7 us  [exchanged(): return lax.all_to_all(parts, axes, 0, 0, tiled=True)]
    ppermute x1 -> x2, starting transfers between devices: 16.8 us -> 18.9 us  [along_width(): lax.ppermute(x, WIDTH, [(i, i - 1 + 2 * (i % 2)) for i in range(1, count...]
    ppermute x4, waiting for transfers between devices: 5.41 us -> 3.42 us  [beside(): after = lax.ppermute(leading, axis, line(count, -1))]
    ppermute x1 -> x2, starting transfers between devices: 1.92 us -> 3.85 us  [along_width(): inner = lax.ppermute(x, WIDTH, [(i, i ^ 1) for i in range(count)])]
  transfers between devices with their start and end apart: 15 -> 17, of which waited for: 9 -> 8; matrix products, arithmetic and copies ran while one was open for 3% -> 3% of each run, Pallas kernels for 4% -> 4%
where the time goes in v10:
time: 161 us; the launch traced here: 160 us
  starting transfers between devices  81.8 us (51%)
  waiting for transfers between devices  34.8 us (22%)
  Pallas kernels  16.5 us (10%)
  blocking collectives  14.2 us (9%)
  other arithmetic  7.33 us (5%)
  local copies, waits for them, and re-layouts  4.53 us (3%)
    all_to_all x3, starting transfers between devices, exchanged(): return lax.all_to_all(parts, axes, 0, 0, tiled=True)  26.7 us
    ppermute x2, starting transfers between devices, along_width(): lax.ppermute(x, WIDTH, [(i, i - 1 + 2 * (i % 2)) for i in range(1, count...  18.9 us
    all_to_all x3, waiting for transfers between devices, exchanged(): return lax.all_to_all(parts, axes, 0, 0, tiled=True)  18.1 us
    ppermute x4, starting transfers between devices, beside(): before = lax.ppermute(last, axis, line(count, 1))  16.6 us
    pallas_call x7, Pallas kernels, call(): pl.pallas_call(kernel, out_shape=[jax.ShapeDtypeStruct(s, t) for s, t in...  16.5 us
    all_to_all x1, blocking collectives, exchanged(): return lax.all_to_all(parts, axes, 0, 0, tiled=True)  14.2 us
    ppermute x2, waiting for transfers between devices, along_width(): lax.ppermute(x, WIDTH, [(i, i - 1 + 2 * (i % 2)) for i in range(1, count...  9.39 us
    ppermute x1, starting transfers between devices, local(): other = lax.ppermute(mine, 'core', swap)  8.59 us
  transfers between devices with their start and end apart: 17, of which 8 were waited for; matrix products, arithmetic and copies ran while one was open for 3% of the time, Pallas kernels for 4%

profile of v10, /device:TPU:1, one launch (start us, length us, event | category | flops | bytes accessed | tf_op | source)
XLA Modules:
  0.0 160.2 jit_solution(9713595088017269178)
XLA Ops:
  0.6 17.0 %collective-permute-start = (bf16[8,8,8,128]{3,2,1,0:T(8,128)(2,1)}, bf16[8,8,8,128]{3,2,1,0:T(8,128)(2,1)S(1)}, u32[]{:S(2)}, u32[]{:S(2)}) collective-permute-start(bf16[8,8,8,128]{3,2,1,0:T(8,128)(2,1)} %param.4), channel_id=1, source_target_pairs={{1,2},{2,1},{3,4},{4,3},{5,6},{6,5},{7,8},{8,7},{9,10},{10,9},{11,... | collective-permute-start | bytes 393224 | tf_op jit(solution)/shard_map/ppermute | solution.py:270
  17.6 1.9 %collective-permute-start.1 = (bf16[8,8,8,128]{3,2,1,0:T(8,128)(2,1)}, bf16[8,8,8,128]{3,2,1,0:T(8,128)(2,1)S(1)}, u32[]{:S(2)}, u32[]{:S(2)}) collective-permute-start(bf16[8,8,8,128]{3,2,1,0:T(8,128)(2,1)} %param.4), channel_id=1, source_target_pairs={{0,1},{1,0},{2,3},{3,2},{4,5},{5,4},{6,7},{7,6},{8,9},{9,8},{10,11... | collective-permute-start | bytes 393224 | tf_op jit(solution)/shard_map/ppermute | solution.py:271
  19.5 1.9 %collective-permute-start.2 = (bf16[4,4,4,128]{3,2,1,0:T(4,128)(2,1)}, bf16[4,4,4,128]{3,2,1,0:T(4,128)(2,1)S(1)}, u32[]{:S(2)}, u32[]{:S(2)}) collective-permute-start(bf16[4,4,4,128]{3,2,1,0:T(4,128)(2,1)} %param.7), channel_id=1, source_target_pairs={{1,2},{2,1},{3,4},{4,3},{5,6},{6,5},{7,8},{8,7},{9,10},{10,9},{11,... | collective-permute-start | bytes 49160 | tf_op jit(solution)/shard_map/ppermute | solution.py:270
  21.5 1.9 %collective-permute-start.3 = (bf16[4,4,4,128]{3,2,1,0:T(4,128)(2,1)}, bf16[4,4,4,128]{3,2,1,0:T(4,128)(2,1)S(1)}, u32[]{:S(2)}, u32[]{:S(2)}) collective-permute-start(bf16[4,4,4,128]{3,2,1,0:T(4,128)(2,1)} %param.7), channel_id=1, source_target_pairs={{0,1},{1,0},{2,3},{3,2},{4,5},{5,4},{6,7},{7,6},{8,9},{9,8},{10,11... | collective-permute-start | bytes 49160 | tf_op jit(solution)/shard_map/ppermute | solution.py:271
  24.3 9.4 %collective-permute-done.2 = bf16[4,4,4,128]{3,2,1,0:T(4,128)(2,1)S(1)} collective-permute-done((bf16[4,4,4,128]{3,2,1,0:T(4,128)(2,1)}, bf16[4,4,4,128]{3,2,1,0:T(4,128)(2,1)S(1)}, u32[]{:S(2)}, u32[]{:S(2)}) %collective-permute-start.2) | collective-permute-done | bytes 16416 | tf_op jit(solution)/shard_map/ppermute | solution.py:270
  36.2 4.0 %collective-permute-start.4 = (bf16[8,3,24,128]{3,2,1,0:T(8,128)(2,1)S(1)}, bf16[8,3,24,128]{3,2,1,0:T(8,128)(2,1)S(1)}, u32[]{:S(2)}, u32[]{:S(2)}) collective-permute-start(bf16[8,3,24,128]{3,2,1,0:T(8,128)(2,1)S(1)} %pad_maximum_fusion.3), channel_id=1, source_target_pairs={{0,16},{16,32},{32,48},{48,64},{64,80},{80,96},{96,112},{1,17},{17... | collective-permute-start | bytes 442376 | tf_op jit(solution)/shard_map/ppermute | solution.py:264
  40.3 2.1 %shard_map.75.refs_9_ = f32[6,6,24,128]{3,2,1,0:T(8,128)S(1)} custom-call(bf16[8,192,128]{2,1,0:T(8,128)(2,1)S(1)} %bitcast.27, bf16[3456,128]{1,0:T(8,128)(2,1)S(1)} %bitcast.30), custom_call_target="tpu_custom_call" | custom-call | flops 764411904 | bytes 1720320 | tf_op jit(solution)/shard_map/pallas_call | solution.py:248
  44.0 4.0 %collective-permute-start.6 = (bf16[3,14,24,128]{3,2,1,0:T(8,128)(2,1)S(1)}, bf16[3,14,24,128]{3,2,1,0:T(8,128)(2,1)S(1)}, u32[]{:S(2)}, u32[]{:S(2)}) collective-permute-start(bf16[3,14,24,128]{3,2,1,0:T(8,128)(2,1)S(1)} %pad_maximum_fusion.1), channel_id=1, source_target_pairs={{0,128},{128,256},{256,384},{1,129},{129,257},{257,385},{2,130},{1... | collective-permute-start | bytes 774152 | tf_op jit(solution)/shard_map/ppermute | solution.py:264
  48.0 2.1 %shard_map.76.refs_10_ = f32[6,6,24,128]{3,2,1,0:T(8,128)S(1)} custom-call(bf16[8,192,128]{2,1,0:T(8,128)(2,1)S(1)} %bitcast.28, bf16[8,72,128]{2,1,0:T(8,128)(2,1)S(1)} %bitcast.40, bf16[8,72,128]{2,1,0:T(8,128)(2,1)S(1)} %bitcast.38, bf16[3456,128]{1,0:T(8,128)(2,1)S(1)} %bitcast.31), custom_call_target="tpu_custom_call" | custom-call | flops 764411904 | bytes 2015232 | tf_op jit(solution)/shard_map/pallas_call | solution.py:248
  51.3 9.6 %shard_map.77 = (f32[128,128]{1,0:T(8,128)S(1)}, bf16[128,128]{1,0:T(8,128)(2,1)S(1)}, f32[12,12,24,128]{3,2,1,0:T(8,128)S(1)}, bf16[3456,128]{1,0:T(8,128)(2,1)S(1)}, bf16[3456,128]{1,0:T(8,128)(2,1)S(1)}) custom-call(s32[3]{0:T(128)S(1)} %pad_add_fusion.refs_0_, bf16[8,192,128]{2,1,0:T(8,128)(2,1)S(1)} %bitcast.29, bf16[8,72,128]{2,1,0:T(8,128)(2,1)S(1)} %bitcast.41, ...), custom_call_target="tpu_custom_call" | custom-call | flops 3538944000 | bytes 7561228 | tf_op jit(solution)/shard_map/pallas_call | solution.py:248
  61.0 1.9 %collective-permute-start.8 = (bf16[3456,128]{1,0:T(8,128)(2,1)S(1)}, bf16[3456,128]{1,0:T(8,128)(2,1)S(1)}, u32[]{:S(2)}, u32[]{:S(2)}) collective-permute-start(bf16[3456,128]{1,0:T(8,128)(2,1)S(1)} %broadcast_select_fusion.2), channel_id=1, source_target_pairs={{0,1},{1,0},{2,3},{3,2},{4,5},{5,4},{6,7},{7,6},{8,9},{9,8},{10,11... | collective-permute-start | bytes 2654216 | tf_op jit(solution)/shard_map/ppermute | solution.py:364
  63.0 2.4 %collective-permute-done.8 = bf16[3456,128]{1,0:T(8,128)(2,1)S(1)} collective-permute-done((bf16[3456,128]{1,0:T(8,128)(2,1)S(1)}, bf16[3456,128]{1,0:T(8,128)(2,1)S(1)}, u32[]{:S(2)}, u32[]{:S(2)}) %collective-permute-start.8) | collective-permute-done | bytes 884768 | tf_op jit(solution)/shard_map/ppermute | solution.py:364
  66.6 13.7 %all-to-all-start = ((bf16[16,216,128]{2,1,0:T(8,128)(2,1)}), bf16[16,216,128]{2,1,0:T(8,128)(2,1)S(1)}, u32[]{:S(2)}, u32[]{:S(2)}) async-start(bf16[16,216,128]{2,1,0:T(8,128)(2,1)} %bitcast.47), calls=%async_computation | async-start | bytes 1769472 | tf_op jit(solution)/shard_map/all_to_all | solution.py:281
  82.3 5.3 %collective-permute-start.9 = (bf16[4,2,8,128]{3,2,1,0:T(8,128)(2,1)S(1)}, bf16[4,2,8,128]{3,2,1,0:T(8,128)(2,1)}, u32[]{:S(2)}, u32[]{:S(2)}) collective-permute-start(bf16[4,2,8,128]{3,2,1,0:T(8,128)(2,1)S(1)} %get-tuple-element.59), channel_id=1, source_target_pairs={{0,16},{16,32},{32,48},{48,64},{64,80},{80,96},{96,112},{1,17},{17... | collective-permute-start | bytes 49160 | tf_op jit(solution)/shard_map/ppermute | solution.py:264
  89.2 4.9 %all-to-all-done.parts = bf16[16,216,128]{2,1,0:T(8,128)(2,1)S(1)} async-done(((bf16[16,216,128]{2,1,0:T(8,128)(2,1)}), bf16[16,216,128]{2,1,0:T(8,128)(2,1)S(1)}, u32[]{:S(2)}, u32[]{:S(2)}) %all-to-all-start) | async-done | bytes 884768 | tf_op jit(solution)/shard_map/all_to_all | solution.py:281
  94.8 8.5 %all-to-all-start.1 = ((bf16[16,16,128]{2,1,0:T(8,128)(2,1)}), bf16[16,16,128]{2,1,0:T(8,128)(2,1)S(1)}, u32[]{:S(2)}, u32[]{:S(2)}) async-start(bf16[16,16,128]{2,1,0:T(8,128)(2,1)} %bitcast.35), calls=%async_computation.1 | async-start | bytes 131072 | tf_op jit(solution)/shard_map/all_to_all | solution.py:281
  103.2 12.1 %all-to-all-done.1.parts = bf16[16,16,128]{2,1,0:T(8,128)(2,1)S(1)} async-done(((bf16[16,16,128]{2,1,0:T(8,128)(2,1)}), bf16[16,16,128]{2,1,0:T(8,128)(2,1)S(1)}, u32[]{:S(2)}, u32[]{:S(2)}) %all-to-all-start.1) | async-done | bytes 65568 | tf_op jit(solution)/shard_map/all_to_all | solution.py:281
  115.4 14.2 %all_to_all.20 = bf16[16,16,128]{2,1,0:T(8,128)(2,1)S(1)} all-to-all(bf16[16,16,128]{2,1,0:T(8,128)(2,1)S(1)} %shard_map.79), channel_id=1, replica_groups=mesh['gx'=4,'gy'=8,'y'=4,'zh'=2,'core'=2] {'gy','zh'}, dimensions={0} | all-to-all | bytes 131072 | tf_op jit(solution)/shard_map/all_to_all | solution.py:281
  130.6 4.5 %all-to-all-start.3 = ((bf16[16,216,128]{2,1,0:T(8,128)(2,1)}), bf16[16,216,128]{2,1,0:T(8,128)(2,1)}, u32[]{:S(2)}, u32[]{:S(2)}) async-start(bf16[16,216,128]{2,1,0:T(8,128)(2,1)} %broadcast_in_dim.2), calls=%async_computation.3 | async-start | bytes 1769472 | tf_op jit(solution)/shard_map/all_to_all | solution.py:281
  135.9 3.2 %collective-permute-start.11 = (bf16[2,8,8,128]{3,2,1,0:T(8,128)(2,1)S(1)}, bf16[2,8,8,128]{3,2,1,0:T(8,128)(2,1)S(1)}, u32[]{:S(2)}, u32[]{:S(2)}) collective-permute-start(bf16[2,8,8,128]{3,2,1,0:T(8,128)(2,1)S(1)} %get-tuple-element.57), channel_id=1, source_target_pairs={{0,128},{128,256},{256,384},{1,129},{129,257},{257,385},{2,130},{1... | collective-permute-start | bytes 98312 | tf_op jit(solution)/shard_map/ppermute | solution.py:264
  140.9 3.4 %collective-permute-done.12 = bf16[2,8,8,128]{3,2,1,0:T(8,128)(2,1)S(1)} collective-permute-done((bf16[2,8,8,128]{3,2,1,0:T(8,128)(2,1)S(1)}, bf16[2,8,8,128]{3,2,1,0:T(8,128)(2,1)S(1)}, u32[]{:S(2)}, u32[]{:S(2)}) %collective-permute-start.12) | collective-permute-done | bytes 32800 | tf_op jit(solution)/shard_map/ppermute | solution.py:265
  146.2 8.6 %collective-permute-start.13 = (bf16[3456,128]{1,0:T(8,128)(2,1)}, bf16[3456,128]{1,0:T(8,128)(2,1)S(1)}, u32[]{:S(2)}, u32[]{:S(2)}) collective-permute-start(bf16[3456,128]{1,0:T(8,128)(2,1)} %bitcast.20), channel_id=1, source_target_pairs={{0,1},{1,0},{2,3},{3,2},{4,5},{5,4},{6,7},{7,6},{8,9},{9,8},{10,11... | collective-permute-start | bytes 2654216 | tf_op jit(solution)/shard_map/ppermute | solution.py:403
  156.0 1.7 %shard_map.81 = bf16[512,128]{1,0:T(8,128)(2,1)} custom-call(f32[10,10,16,128]{3,2,1,0:T(8,128)S(1)} %shard_map.80.fine, bf16[3456,128]{1,0:T(8,128)(2,1)S(1)} %bitcast.33), custom_call_target="tpu_custom_call" | custom-call | flops 452984832 | bytes 1835008 | tf_op jit(solution)/shard_map/pallas_call | solution.py:248
  157.7 2.5 %broadcast_select_fusion = (bf16[3456,128]{1,0:T(8,128)(2,1)}, bf16[3456,128]{1,0:T(8,128)(2,1)}) fusion(bf16[3456,128]{1,0:T(8,128)(2,1)S(1)} %collective-permute-done.13, pred[]{:T(512)S(6)} %eq.2, bf16[16,216,128]{2,1,0:T(8,128)(2,1)} %all-to-all-done.3), kind=kLoop, calls=%fused_computation.1 | loop fusion | flops 884736 | bytes 3538945 | tf_op jit(solution)/shard_map/jit(_where)/select_n | solution.py:405
  (58 shorter events, 18.2 us)
Async XLA Ops:
  0.6 39.6 %copy-start.1 = (bf16[27,128,128]{2,1,0:T(8,128)(2,1)S(1)}, bf16[27,128,128]{2,1,0:T(8,128)(2,1)}, u32[]{:S(2)}) copy-start(bf16[27,128,128]{2,1,0:T(8,128)(2,1)} %param.5) | copy-start | bytes 2654212
  0.6 33.1 %collective-permute-start = (bf16[8,8,8,128]{3,2,1,0:T(8,128)(2,1)}, bf16[8,8,8,128]{3,2,1,0:T(8,128)(2,1)S(1)}, u32[]{:S(2)}, u32[]{:S(2)}) collective-permute-start(bf16[8,8,8,128]{3,2,1,0:T(8,128)(2,1)} %param.4), channel_id=1, source_target_pairs={{1,2},{2,1},{3,4},{4,3},{5,6},{6,5},{7,8},{8,7},{9,10},{10,9},{11,... | collective-permute-start | bytes 393224 | tf_op jit(solution)/shard_map/ppermute | solution.py:270
  17.6 16.1 %collective-permute-start.1 = (bf16[8,8,8,128]{3,2,1,0:T(8,128)(2,1)}, bf16[8,8,8,128]{3,2,1,0:T(8,128)(2,1)S(1)}, u32[]{:S(2)}, u32[]{:S(2)}) collective-permute-start(bf16[8,8,8,128]{3,2,1,0:T(8,128)(2,1)} %param.4), channel_id=1, source_target_pairs={{0,1},{1,0},{2,3},{3,2},{4,5},{5,4},{6,7},{7,6},{8,9},{9,8},{10,11... | collective-permute-start | bytes 393224 | tf_op jit(solution)/shard_map/ppermute | solution.py:271
  19.5 14.2 %collective-permute-start.2 = (bf16[4,4,4,128]{3,2,1,0:T(4,128)(2,1)}, bf16[4,4,4,128]{3,2,1,0:T(4,128)(2,1)S(1)}, u32[]{:S(2)}, u32[]{:S(2)}) collective-permute-start(bf16[4,4,4,128]{3,2,1,0:T(4,128)(2,1)} %param.7), channel_id=1, source_target_pairs={{1,2},{2,1},{3,4},{4,3},{5,6},{6,5},{7,8},{8,7},{9,10},{10,9},{11,... | collective-permute-start | bytes 49160 | tf_op jit(solution)/shard_map/ppermute | solution.py:270
  21.5 12.3 %collective-permute-start.3 = (bf16[4,4,4,128]{3,2,1,0:T(4,128)(2,1)}, bf16[4,4,4,128]{3,2,1,0:T(4,128)(2,1)S(1)}, u32[]{:S(2)}, u32[]{:S(2)}) collective-permute-start(bf16[4,4,4,128]{3,2,1,0:T(4,128)(2,1)} %param.7), channel_id=1, source_target_pairs={{0,1},{1,0},{2,3},{3,2},{4,5},{5,4},{6,7},{7,6},{8,9},{9,8},{10,11... | collective-permute-start | bytes 49160 | tf_op jit(solution)/shard_map/ppermute | solution.py:271
  34.8 7.6 %collective-permute-start.5 = (bf16[8,3,24,128]{3,2,1,0:T(8,128)(2,1)S(1)}, bf16[8,3,24,128]{3,2,1,0:T(8,128)(2,1)S(1)}, u32[]{:S(2)}, u32[]{:S(2)}) collective-permute-start(bf16[8,3,24,128]{3,2,1,0:T(8,128)(2,1)S(1)} %pad_maximum_fusion.4), channel_id=1, source_target_pairs={{16,0},{32,16},{48,32},{64,48},{80,64},{96,80},{112,96},{17,1},{33... | collective-permute-start | bytes 442376 | tf_op jit(solution)/shard_map/ppermute | solution.py:265
  36.2 6.2 %copy-start.7 = (bf16[4,4,4,128]{3,2,1,0:T(4,128)(2,1)S(1)}, bf16[4,4,4,128]{3,2,1,0:T(4,128)(2,1)}, u32[]{:S(2)}) copy-start(bf16[4,4,4,128]{3,2,1,0:T(4,128)(2,1)} %param.7) | copy-start | bytes 49156
  36.2 6.3 %collective-permute-start.4 = (bf16[8,3,24,128]{3,2,1,0:T(8,128)(2,1)S(1)}, bf16[8,3,24,128]{3,2,1,0:T(8,128)(2,1)S(1)}, u32[]{:S(2)}, u32[]{:S(2)}) collective-permute-start(bf16[8,3,24,128]{3,2,1,0:T(8,128)(2,1)S(1)} %pad_maximum_fusion.3), channel_id=1, source_target_pairs={{0,16},{16,32},{32,48},{48,64},{64,80},{80,96},{96,112},{1,17},{17... | collective-permute-start | bytes 442376 | tf_op jit(solution)/shard_map/ppermute | solution.py:264
  42.5 8.7 %copy-start = (bf16[27,128,128]{2,1,0:T(8,128)(2,1)S(1)}, bf16[27,128,128]{2,1,0:T(8,128)(2,1)}, u32[]{:S(2)}) copy-start(bf16[27,128,128]{2,1,0:T(8,128)(2,1)} %coarse_weights.1) | copy-start | bytes 2654212
  42.5 7.6 %collective-permute-start.7 = (bf16[3,14,24,128]{3,2,1,0:T(8,128)(2,1)S(1)}, bf16[3,14,24,128]{3,2,1,0:T(8,128)(2,1)S(1)}, u32[]{:S(2)}, u32[]{:S(2)}) collective-permute-start(bf16[3,14,24,128]{3,2,1,0:T(8,128)(2,1)S(1)} %pad_maximum_fusion.2), channel_id=1, source_target_pairs={{128,0},{256,128},{384,256},{129,1},{257,129},{385,257},{130,2},{2... | collective-permute-start | bytes 774152 | tf_op jit(solution)/shard_map/ppermute | solution.py:265
  44.0 7.2 %collective-permute-start.6 = (bf16[3,14,24,128]{3,2,1,0:T(8,128)(2,1)S(1)}, bf16[3,14,24,128]{3,2,1,0:T(8,128)(2,1)S(1)}, u32[]{:S(2)}, u32[]{:S(2)}) collective-permute-start(bf16[3,14,24,128]{3,2,1,0:T(8,128)(2,1)S(1)} %pad_maximum_fusion.1), channel_id=1, source_target_pairs={{0,128},{128,256},{256,384},{1,129},{129,257},{257,385},{2,130},{1... | collective-permute-start | bytes 774152 | tf_op jit(solution)/shard_map/ppermute | solution.py:264
  60.9 5.7 %copy-start.4 = (bf16[128,128]{1,0:T(8,128)(2,1)}, bf16[128,128]{1,0:T(8,128)(2,1)S(1)}, u32[]{:S(2)}) copy-start(bf16[128,128]{1,0:T(8,128)(2,1)S(1)} %get-tuple-element.28) | copy-start | bytes 98308
  60.9 5.7 %copy-start.6 = (f32[128,128]{1,0:T(8,128)}, f32[128,128]{1,0:T(8,128)S(1)}, u32[]{:S(2)}) copy-start(f32[128,128]{1,0:T(8,128)S(1)} %get-tuple-element.29) | copy-start | bytes 196612
  61.0 4.3 %collective-permute-start.8 = (bf16[3456,128]{1,0:T(8,128)(2,1)S(1)}, bf16[3456,128]{1,0:T(8,128)(2,1)S(1)}, u32[]{:S(2)}, u32[]{:S(2)}) collective-permute-start(bf16[3456,128]{1,0:T(8,128)(2,1)S(1)} %broadcast_select_fusion.2), channel_id=1, source_target_pairs={{0,1},{1,0},{2,3},{3,2},{4,5},{5,4},{6,7},{7,6},{8,9},{9,8},{10,11... | collective-permute-start | bytes 2654216 | tf_op jit(solution)/shard_map/ppermute | solution.py:364
  66.6 27.4 %all-to-all-start = ((bf16[16,216,128]{2,1,0:T(8,128)(2,1)}), bf16[16,216,128]{2,1,0:T(8,128)(2,1)S(1)}, u32[]{:S(2)}, u32[]{:S(2)}) async-start(bf16[16,216,128]{2,1,0:T(8,128)(2,1)} %bitcast.47), calls=%async_computation | async-start | bytes 1769472 | tf_op jit(solution)/shard_map/all_to_all | solution.py:281
  81.1 8.1 %collective-permute-start.10 = (bf16[4,2,8,128]{3,2,1,0:T(8,128)(2,1)S(1)}, bf16[4,2,8,128]{3,2,1,0:T(8,128)(2,1)S(1)}, u32[]{:S(2)}, u32[]{:S(2)}) collective-permute-start(bf16[4,2,8,128]{3,2,1,0:T(8,128)(2,1)S(1)} %get-tuple-element.58), channel_id=1, source_target_pairs={{16,0},{32,16},{48,32},{64,48},{80,64},{96,80},{112,96},{17,1},{33... | collective-permute-start | bytes 49160 | tf_op jit(solution)/shard_map/ppermute | solution.py:265
  82.3 6.8 %collective-permute-start.9 = (bf16[4,2,8,128]{3,2,1,0:T(8,128)(2,1)S(1)}, bf16[4,2,8,128]{3,2,1,0:T(8,128)(2,1)}, u32[]{:S(2)}, u32[]{:S(2)}) collective-permute-start(bf16[4,2,8,128]{3,2,1,0:T(8,128)(2,1)S(1)} %get-tuple-element.59), channel_id=1, source_target_pairs={{0,16},{16,32},{32,48},{48,64},{64,80},{80,96},{96,112},{1,17},{17... | collective-permute-start | bytes 49160 | tf_op jit(solution)/shard_map/ppermute | solution.py:264
  94.8 40.4 %copy-start.5 = (bf16[128,128]{1,0:T(8,128)(2,1)S(1)}, bf16[128,128]{1,0:T(8,128)(2,1)}, u32[]{:S(2)}) copy-start(bf16[128,128]{1,0:T(8,128)(2,1)} %copy-done.4) | copy-start | bytes 98308
  94.8 20.6 %all-to-all-start.1 = ((bf16[16,16,128]{2,1,0:T(8,128)(2,1)}), bf16[16,16,128]{2,1,0:T(8,128)(2,1)S(1)}, u32[]{:S(2)}, u32[]{:S(2)}) async-start(bf16[16,16,128]{2,1,0:T(8,128)(2,1)} %bitcast.35), calls=%async_computation.1 | async-start | bytes 131072 | tf_op jit(solution)/shard_map/all_to_all | solution.py:281
  130.6 15.6 %all-to-all-start.3 = ((bf16[16,216,128]{2,1,0:T(8,128)(2,1)}), bf16[16,216,128]{2,1,0:T(8,128)(2,1)}, u32[]{:S(2)}, u32[]{:S(2)}) async-start(bf16[16,216,128]{2,1,0:T(8,128)(2,1)} %broadcast_in_dim.2), calls=%async_computation.3 | async-start | bytes 1769472 | tf_op jit(solution)/shard_map/all_to_all | solution.py:281
  135.9 5.0 %collective-permute-start.11 = (bf16[2,8,8,128]{3,2,1,0:T(8,128)(2,1)S(1)}, bf16[2,8,8,128]{3,2,1,0:T(8,128)(2,1)S(1)}, u32[]{:S(2)}, u32[]{:S(2)}) collective-permute-start(bf16[2,8,8,128]{3,2,1,0:T(8,128)(2,1)S(1)} %get-tuple-element.57), channel_id=1, source_target_pairs={{0,128},{128,256},{256,384},{1,129},{129,257},{257,385},{2,130},{1... | collective-permute-start | bytes 98312 | tf_op jit(solution)/shard_map/ppermute | solution.py:264
  139.1 5.2 %collective-permute-start.12 = (bf16[2,8,8,128]{3,2,1,0:T(8,128)(2,1)S(1)}, bf16[2,8,8,128]{3,2,1,0:T(8,128)(2,1)S(1)}, u32[]{:S(2)}, u32[]{:S(2)}) collective-permute-start(bf16[2,8,8,128]{3,2,1,0:T(8,128)(2,1)S(1)} %get-tuple-element.56), channel_id=1, source_target_pairs={{128,0},{256,128},{384,256},{129,1},{257,129},{385,257},{130,2},{2... | collective-permute-start | bytes 98312 | tf_op jit(solution)/shard_map/ppermute | solution.py:265
  146.2 11.5 %collective-permute-start.13 = (bf16[3456,128]{1,0:T(8,128)(2,1)}, bf16[3456,128]{1,0:T(8,128)(2,1)S(1)}, u32[]{:S(2)}, u32[]{:S(2)}) collective-permute-start(bf16[3456,128]{1,0:T(8,128)(2,1)} %bitcast.20), channel_id=1, source_target_pairs={{0,1},{1,0},{2,3},{3,2},{4,5},{5,4},{6,7},{7,6},{8,9},{9,8},{10,11... | collective-permute-start | bytes 2654216 | tf_op jit(solution)/shard_map/ppermute | solution.py:403
  154.8 1.2 copy-start.2
  (1 other events, 0.6 us)

commit v11 on v10

--- a/solution.py
+++ b/solution.py
@@ -298,13 +298,13 @@
 
     halo = along_width(volume, peers[2])
     cots = along_width(cotangent, peers[2])
-    halo, cots = lax.optimization_barrier((halo, cots))
     before_cells, after_cells = in_order(*halo)
     slabs = [
         jnp.concatenate([before_cells[:, at], volume[:, at], after_cells[:, at]], axis=2)
         for at in (slice(5, 8), slice(0, 3))
     ]
     below, above = beside(slabs[0], slabs[1], "gy", peers[1])
+    (below, above), cots = lax.optimization_barrier(((below, above), cots))
     own = jnp.concatenate([before_cells, volume, after_cells], axis=2)
     before, after = in_order(*cots)
     incoming = jnp.concatenate([before[:, :, 2:], cotangent, after[:, :, :2]], axis=2).astype(F32)

time: 161 us -> 161 us (level)
  starting transfers between devices: 81.8 us -> 90.5 us
  waiting for transfers between devices: 34.8 us -> 26.1 us
    ppermute x2, waiting for transfers between devices: 9.39 us -> 0.01 us  [along_width(): lax.ppermute(x, WIDTH, [(i, i - 1 + 2 * (i % 2)) for i in range(1, count...]
    ppermute x4, starting transfers between devices: 16.6 us -> 21.1 us  [beside(): before = lax.ppermute(last, axis, line(count, 1))]
    all_to_all x3, starting transfers between devices: 26.7 us -> 30.9 us  [exchanged(): return lax.all_to_all(parts, axes, 0, 0, tiled=True)]
  transfers between devices with their start and end apart: 17 -> 17, of which waited for: 8 -> 7; matrix products, arithmetic and copies ran while one was open for 3% -> 3% of each run, Pallas kernels for 4% -> 4%
where the time goes in v11:
time: 161 us; the launch traced here: 160 us
  starting transfers between devices  90.5 us (56%)
  waiting for transfers between devices  26.1 us (16%)
  Pallas kernels  16.5 us (10%)
  blocking collectives  14.2 us (9%)
  other arithmetic  7.33 us (5%)
  local copies, waits for them, and re-layouts  4.53 us (3%)
    all_to_all x3, starting transfers between devices, exchanged(): return lax.all_to_all(parts, axes, 0, 0, tiled=True)  30.9 us
    ppermute x4, starting transfers between devices, beside(): before = lax.ppermute(last, axis, line(count, 1))  21.1 us
    ppermute x2, starting transfers between devices, along_width(): lax.ppermute(x, WIDTH, [(i, i - 1 + 2 * (i % 2)) for i in range(1, count...  18.9 us
    all_to_all x3, waiting for transfers between devices, exchanged(): return lax.all_to_all(parts, axes, 0, 0, tiled=True)  18.1 us
    pallas_call x7, Pallas kernels, call(): pl.pallas_call(kernel, out_shape=[jax.ShapeDtypeStruct(s, t) for s, t in...  16.5 us
    all_to_all x1, blocking collectives, exchanged(): return lax.all_to_all(parts, axes, 0, 0, tiled=True)  14.2 us
    ppermute x1, starting transfers between devices, local(): other = lax.ppermute(mine, 'core', swap)  8.59 us
    ppermute x4, starting transfers between devices, beside(): after = lax.ppermute(leading, axis, line(count, -1))  5.16 us
  transfers between devices with their start and end apart: 17, of which 7 were waited for; matrix products, arithmetic and copies ran while one was open for 3% of the time, Pallas kernels for 4%

profile of v11, /device:TPU:1, one launch (start us, length us, event | category | flops | bytes accessed | tf_op | source)
XLA Modules:
  0.0 160.1 jit_solution(12373733274232572798)
XLA Ops:
  0.6 17.0 %collective-permute-start = (bf16[8,8,8,128]{3,2,1,0:T(8,128)(2,1)}, bf16[8,8,8,128]{3,2,1,0:T(8,128)(2,1)S(1)}, u32[]{:S(2)}, u32[]{:S(2)}) collective-permute-start(bf16[8,8,8,128]{3,2,1,0:T(8,128)(2,1)} %param.4), channel_id=1, source_target_pairs={{1,2},{2,1},{3,4},{4,3},{5,6},{6,5},{7,8},{8,7},{9,10},{10,9},{11,... | collective-permute-start | bytes 393224 | tf_op jit(solution)/shard_map/ppermute | solution.py:270
  17.6 1.9 %collective-permute-start.1 = (bf16[8,8,8,128]{3,2,1,0:T(8,128)(2,1)}, bf16[8,8,8,128]{3,2,1,0:T(8,128)(2,1)S(1)}, u32[]{:S(2)}, u32[]{:S(2)}) collective-permute-start(bf16[8,8,8,128]{3,2,1,0:T(8,128)(2,1)} %param.4), channel_id=1, source_target_pairs={{0,1},{1,0},{2,3},{3,2},{4,5},{5,4},{6,7},{7,6},{8,9},{9,8},{10,11... | collective-permute-start | bytes 393224 | tf_op jit(solution)/shard_map/ppermute | solution.py:271
  19.5 1.9 %collective-permute-start.4 = (bf16[4,4,4,128]{3,2,1,0:T(4,128)(2,1)}, bf16[4,4,4,128]{3,2,1,0:T(4,128)(2,1)S(1)}, u32[]{:S(2)}, u32[]{:S(2)}) collective-permute-start(bf16[4,4,4,128]{3,2,1,0:T(4,128)(2,1)} %param.7), channel_id=1, source_target_pairs={{1,2},{2,1},{3,4},{4,3},{5,6},{6,5},{7,8},{8,7},{9,10},{10,9},{11,... | collective-permute-start | bytes 49160 | tf_op jit(solution)/shard_map/ppermute | solution.py:270
  21.5 1.9 %collective-permute-start.5 = (bf16[4,4,4,128]{3,2,1,0:T(4,128)(2,1)}, bf16[4,4,4,128]{3,2,1,0:T(4,128)(2,1)S(1)}, u32[]{:S(2)}, u32[]{:S(2)}) collective-permute-start(bf16[4,4,4,128]{3,2,1,0:T(4,128)(2,1)} %param.7), channel_id=1, source_target_pairs={{0,1},{1,0},{2,3},{3,2},{4,5},{5,4},{6,7},{7,6},{8,9},{9,8},{10,11... | collective-permute-start | bytes 49160 | tf_op jit(solution)/shard_map/ppermute | solution.py:271
  26.8 8.4 %collective-permute-start.2 = (bf16[8,3,24,128]{3,2,1,0:T(8,128)(2,1)S(1)}, bf16[8,3,24,128]{3,2,1,0:T(8,128)(2,1)S(1)}, u32[]{:S(2)}, u32[]{:S(2)}) collective-permute-start(bf16[8,3,24,128]{3,2,1,0:T(8,128)(2,1)S(1)} %pad_maximum_fusion.3), channel_id=1, source_target_pairs={{0,16},{16,32},{32,48},{48,64},{64,80},{80,96},{96,112},{1,17},{17... | collective-permute-start | bytes 442376 | tf_op jit(solution)/shard_map/ppermute | solution.py:264
  35.3 2.1 %shard_map.75.refs_9_ = f32[6,6,24,128]{3,2,1,0:T(8,128)S(1)} custom-call(bf16[8,192,128]{2,1,0:T(8,128)(2,1)S(1)} %bitcast.27, bf16[3456,128]{1,0:T(8,128)(2,1)S(1)} %bitcast.30), custom_call_target="tpu_custom_call" | custom-call | flops 764411904 | bytes 1720320 | tf_op jit(solution)/shard_map/pallas_call | solution.py:248
  38.9 4.1 %collective-permute-start.6 = (bf16[3,14,24,128]{3,2,1,0:T(8,128)(2,1)S(1)}, bf16[3,14,24,128]{3,2,1,0:T(8,128)(2,1)S(1)}, u32[]{:S(2)}, u32[]{:S(2)}) collective-permute-start(bf16[3,14,24,128]{3,2,1,0:T(8,128)(2,1)S(1)} %pad_maximum_fusion.1), channel_id=1, source_target_pairs={{0,128},{128,256},{256,384},{1,129},{129,257},{257,385},{2,130},{1... | collective-permute-start | bytes 774152 | tf_op jit(solution)/shard_map/ppermute | solution.py:264
  43.1 2.1 %shard_map.76.refs_10_ = f32[6,6,24,128]{3,2,1,0:T(8,128)S(1)} custom-call(bf16[8,192,128]{2,1,0:T(8,128)(2,1)S(1)} %bitcast.28, bf16[8,72,128]{2,1,0:T(8,128)(2,1)S(1)} %bitcast.40, bf16[8,72,128]{2,1,0:T(8,128)(2,1)S(1)} %bitcast.38, bf16[3456,128]{1,0:T(8,128)(2,1)S(1)} %bitcast.31), custom_call_target="tpu_custom_call" | custom-call | flops 764411904 | bytes 2015232 | tf_op jit(solution)/shard_map/pallas_call | solution.py:248
  45.3 1.7 %collective-permute-done.6 = bf16[3,14,24,128]{3,2,1,0:T(8,128)(2,1)S(1)} collective-permute-done((bf16[3,14,24,128]{3,2,1,0:T(8,128)(2,1)S(1)}, bf16[3,14,24,128]{3,2,1,0:T(8,128)(2,1)S(1)}, u32[]{:S(2)}, u32[]{:S(2)}) %collective-permute-start.6) | collective-permute-done | bytes 258080 | tf_op jit(solution)/shard_map/ppermute | solution.py:264
  47.0 9.6 %shard_map.77 = (f32[128,128]{1,0:T(8,128)S(1)}, bf16[128,128]{1,0:T(8,128)(2,1)S(1)}, f32[12,12,24,128]{3,2,1,0:T(8,128)S(1)}, bf16[3456,128]{1,0:T(8,128)(2,1)S(1)}, bf16[3456,128]{1,0:T(8,128)(2,1)S(1)}) custom-call(s32[3]{0:T(128)S(1)} %pad_add_fusion.refs_0_, bf16[8,192,128]{2,1,0:T(8,128)(2,1)S(1)} %bitcast.29, bf16[8,72,128]{2,1,0:T(8,128)(2,1)S(1)} %bitcast.41, ...), custom_call_target="tpu_custom_call" | custom-call | flops 3538944000 | bytes 7561228 | tf_op jit(solution)/shard_map/pallas_call | solution.py:248
  56.7 1.9 %collective-permute-start.8 = (bf16[3456,128]{1,0:T(8,128)(2,1)S(1)}, bf16[3456,128]{1,0:T(8,128)(2,1)S(1)}, u32[]{:S(2)}, u32[]{:S(2)}) collective-permute-start(bf16[3456,128]{1,0:T(8,128)(2,1)S(1)} %broadcast_select_fusion.2), channel_id=1, source_target_pairs={{0,1},{1,0},{2,3},{3,2},{4,5},{5,4},{6,7},{7,6},{8,9},{9,8},{10,11... | collective-permute-start | bytes 2654216 | tf_op jit(solution)/shard_map/ppermute | solution.py:364
  58.7 2.4 %collective-permute-done.8 = bf16[3456,128]{1,0:T(8,128)(2,1)S(1)} collective-permute-done((bf16[3456,128]{1,0:T(8,128)(2,1)S(1)}, bf16[3456,128]{1,0:T(8,128)(2,1)S(1)}, u32[]{:S(2)}, u32[]{:S(2)}) %collective-permute-start.8) | collective-permute-done | bytes 884768 | tf_op jit(solution)/shard_map/ppermute | solution.py:364
  62.3 11.7 %all-to-all-start = ((bf16[16,216,128]{2,1,0:T(8,128)(2,1)}), bf16[16,216,128]{2,1,0:T(8,128)(2,1)S(1)}, u32[]{:S(2)}, u32[]{:S(2)}) async-start(bf16[16,216,128]{2,1,0:T(8,128)(2,1)} %bitcast.47), calls=%async_computation | async-start | bytes 1769472 | tf_op jit(solution)/shard_map/all_to_all | solution.py:281
  76.0 5.3 %collective-permute-start.9 = (bf16[4,2,8,128]{3,2,1,0:T(8,128)(2,1)S(1)}, bf16[4,2,8,128]{3,2,1,0:T(8,128)(2,1)}, u32[]{:S(2)}, u32[]{:S(2)}) collective-permute-start(bf16[4,2,8,128]{3,2,1,0:T(8,128)(2,1)S(1)} %get-tuple-element.59), channel_id=1, source_target_pairs={{0,16},{16,32},{32,48},{48,64},{64,80},{80,96},{96,112},{1,17},{17... | collective-permute-start | bytes 49160 | tf_op jit(solution)/shard_map/ppermute | solution.py:264
  82.9 4.8 %all-to-all-done.parts = bf16[16,216,128]{2,1,0:T(8,128)(2,1)S(1)} async-done(((bf16[16,216,128]{2,1,0:T(8,128)(2,1)}), bf16[16,216,128]{2,1,0:T(8,128)(2,1)S(1)}, u32[]{:S(2)}, u32[]{:S(2)}) %all-to-all-start) | async-done | bytes 884768 | tf_op jit(solution)/shard_map/all_to_all | solution.py:281
  88.5 14.7 %all-to-all-start.1 = ((bf16[16,16,128]{2,1,0:T(8,128)(2,1)}), bf16[16,16,128]{2,1,0:T(8,128)(2,1)S(1)}, u32[]{:S(2)}, u32[]{:S(2)}) async-start(bf16[16,16,128]{2,1,0:T(8,128)(2,1)} %bitcast.35), calls=%async_computation.1 | async-start | bytes 131072 | tf_op jit(solution)/shard_map/all_to_all | solution.py:281
  103.2 12.1 %all-to-all-done.1.parts = bf16[16,16,128]{2,1,0:T(8,128)(2,1)S(1)} async-done(((bf16[16,16,128]{2,1,0:T(8,128)(2,1)}), bf16[16,16,128]{2,1,0:T(8,128)(2,1)S(1)}, u32[]{:S(2)}, u32[]{:S(2)}) %all-to-all-start.1) | async-done | bytes 65568 | tf_op jit(solution)/shard_map/all_to_all | solution.py:281
  115.3 14.2 %all_to_all.20 = bf16[16,16,128]{2,1,0:T(8,128)(2,1)S(1)} all-to-all(bf16[16,16,128]{2,1,0:T(8,128)(2,1)S(1)} %shard_map.79), channel_id=1, replica_groups=mesh['gx'=4,'gy'=8,'y'=4,'zh'=2,'core'=2] {'gy','zh'}, dimensions={0} | all-to-all | bytes 131072 | tf_op jit(solution)/shard_map/all_to_all | solution.py:281
  130.6 4.5 %all-to-all-start.3 = ((bf16[16,216,128]{2,1,0:T(8,128)(2,1)}), bf16[16,216,128]{2,1,0:T(8,128)(2,1)}, u32[]{:S(2)}, u32[]{:S(2)}) async-start(bf16[16,216,128]{2,1,0:T(8,128)(2,1)} %broadcast_in_dim.2), calls=%async_computation.3 | async-start | bytes 1769472 | tf_op jit(solution)/shard_map/all_to_all | solution.py:281
  135.8 3.2 %collective-permute-start.11 = (bf16[2,8,8,128]{3,2,1,0:T(8,128)(2,1)S(1)}, bf16[2,8,8,128]{3,2,1,0:T(8,128)(2,1)S(1)}, u32[]{:S(2)}, u32[]{:S(2)}) collective-permute-start(bf16[2,8,8,128]{3,2,1,0:T(8,128)(2,1)S(1)} %get-tuple-element.57), channel_id=1, source_target_pairs={{0,128},{128,256},{256,384},{1,129},{129,257},{257,385},{2,130},{1... | collective-permute-start | bytes 98312 | tf_op jit(solution)/shard_map/ppermute | solution.py:264
  140.8 3.4 %collective-permute-done.12 = bf16[2,8,8,128]{3,2,1,0:T(8,128)(2,1)S(1)} collective-permute-done((bf16[2,8,8,128]{3,2,1,0:T(8,128)(2,1)S(1)}, bf16[2,8,8,128]{3,2,1,0:T(8,128)(2,1)S(1)}, u32[]{:S(2)}, u32[]{:S(2)}) %collective-permute-start.12) | collective-permute-done | bytes 32800 | tf_op jit(solution)/shard_map/ppermute | solution.py:265
  146.1 8.6 %collective-permute-start.13 = (bf16[3456,128]{1,0:T(8,128)(2,1)}, bf16[3456,128]{1,0:T(8,128)(2,1)S(1)}, u32[]{:S(2)}, u32[]{:S(2)}) collective-permute-start(bf16[3456,128]{1,0:T(8,128)(2,1)} %bitcast.20), channel_id=1, source_target_pairs={{0,1},{1,0},{2,3},{3,2},{4,5},{5,4},{6,7},{7,6},{8,9},{9,8},{10,11... | collective-permute-start | bytes 2654216 | tf_op jit(solution)/shard_map/ppermute | solution.py:403
  155.9 1.7 %shard_map.81 = bf16[512,128]{1,0:T(8,128)(2,1)} custom-call(f32[10,10,16,128]{3,2,1,0:T(8,128)S(1)} %shard_map.80.fine, bf16[3456,128]{1,0:T(8,128)(2,1)S(1)} %bitcast.33), custom_call_target="tpu_custom_call" | custom-call | flops 452984832 | bytes 1835008 | tf_op jit(solution)/shard_map/pallas_call | solution.py:248
  157.6 2.5 %broadcast_select_fusion = (bf16[3456,128]{1,0:T(8,128)(2,1)}, bf16[3456,128]{1,0:T(8,128)(2,1)}) fusion(bf16[3456,128]{1,0:T(8,128)(2,1)S(1)} %collective-permute-done.13, pred[]{:T(512)S(6)} %eq.2, bf16[16,216,128]{2,1,0:T(8,128)(2,1)} %all-to-all-done.3), kind=kLoop, calls=%fused_computation.1 | loop fusion | flops 884736 | bytes 3538945 | tf_op jit(solution)/shard_map/jit(_where)/select_n | solution.py:405
  (58 shorter events, 17.0 us)
Async XLA Ops:
  0.6 34.6 %copy-start.1 = (bf16[27,128,128]{2,1,0:T(8,128)(2,1)S(1)}, bf16[27,128,128]{2,1,0:T(8,128)(2,1)}, u32[]{:S(2)}) copy-start(bf16[27,128,128]{2,1,0:T(8,128)(2,1)} %param.5) | copy-start | bytes 2654212
  0.6 23.7 %collective-permute-start = (bf16[8,8,8,128]{3,2,1,0:T(8,128)(2,1)}, bf16[8,8,8,128]{3,2,1,0:T(8,128)(2,1)S(1)}, u32[]{:S(2)}, u32[]{:S(2)}) collective-permute-start(bf16[8,8,8,128]{3,2,1,0:T(8,128)(2,1)} %param.4), channel_id=1, source_target_pairs={{1,2},{2,1},{3,4},{4,3},{5,6},{6,5},{7,8},{8,7},{9,10},{10,9},{11,... | collective-permute-start | bytes 393224 | tf_op jit(solution)/shard_map/ppermute | solution.py:270
  17.6 6.7 %collective-permute-start.1 = (bf16[8,8,8,128]{3,2,1,0:T(8,128)(2,1)}, bf16[8,8,8,128]{3,2,1,0:T(8,128)(2,1)S(1)}, u32[]{:S(2)}, u32[]{:S(2)}) collective-permute-start(bf16[8,8,8,128]{3,2,1,0:T(8,128)(2,1)} %param.4), channel_id=1, source_target_pairs={{0,1},{1,0},{2,3},{3,2},{4,5},{5,4},{6,7},{7,6},{8,9},{9,8},{10,11... | collective-permute-start | bytes 393224 | tf_op jit(solution)/shard_map/ppermute | solution.py:271
  19.5 17.8 %collective-permute-start.4 = (bf16[4,4,4,128]{3,2,1,0:T(4,128)(2,1)}, bf16[4,4,4,128]{3,2,1,0:T(4,128)(2,1)S(1)}, u32[]{:S(2)}, u32[]{:S(2)}) collective-permute-start(bf16[4,4,4,128]{3,2,1,0:T(4,128)(2,1)} %param.7), channel_id=1, source_target_pairs={{1,2},{2,1},{3,4},{4,3},{5,6},{6,5},{7,8},{8,7},{9,10},{10,9},{11,... | collective-permute-start | bytes 49160 | tf_op jit(solution)/shard_map/ppermute | solution.py:270
  21.5 15.9 %collective-permute-start.5 = (bf16[4,4,4,128]{3,2,1,0:T(4,128)(2,1)}, bf16[4,4,4,128]{3,2,1,0:T(4,128)(2,1)S(1)}, u32[]{:S(2)}, u32[]{:S(2)}) collective-permute-start(bf16[4,4,4,128]{3,2,1,0:T(4,128)(2,1)} %param.7), channel_id=1, source_target_pairs={{0,1},{1,0},{2,3},{3,2},{4,5},{5,4},{6,7},{7,6},{8,9},{9,8},{10,11... | collective-permute-start | bytes 49160 | tf_op jit(solution)/shard_map/ppermute | solution.py:271
  25.4 12.0 %collective-permute-start.3 = (bf16[8,3,24,128]{3,2,1,0:T(8,128)(2,1)S(1)}, bf16[8,3,24,128]{3,2,1,0:T(8,128)(2,1)S(1)}, u32[]{:S(2)}, u32[]{:S(2)}) collective-permute-start(bf16[8,3,24,128]{3,2,1,0:T(8,128)(2,1)S(1)} %pad_maximum_fusion.4), channel_id=1, source_target_pairs={{16,0},{32,16},{48,32},{64,48},{80,64},{96,80},{112,96},{17,1},{33... | collective-permute-start | bytes 442376 | tf_op jit(solution)/shard_map/ppermute | solution.py:265
  26.8 10.7 %collective-permute-start.2 = (bf16[8,3,24,128]{3,2,1,0:T(8,128)(2,1)S(1)}, bf16[8,3,24,128]{3,2,1,0:T(8,128)(2,1)S(1)}, u32[]{:S(2)}, u32[]{:S(2)}) collective-permute-start(bf16[8,3,24,128]{3,2,1,0:T(8,128)(2,1)S(1)} %pad_maximum_fusion.3), channel_id=1, source_target_pairs={{0,16},{16,32},{32,48},{48,64},{64,80},{80,96},{96,112},{1,17},{17... | collective-permute-start | bytes 442376 | tf_op jit(solution)/shard_map/ppermute | solution.py:264
  35.3 7.8 %copy-start.7 = (bf16[4,4,4,128]{3,2,1,0:T(4,128)(2,1)S(1)}, bf16[4,4,4,128]{3,2,1,0:T(4,128)(2,1)}, u32[]{:S(2)}) copy-start(bf16[4,4,4,128]{3,2,1,0:T(4,128)(2,1)} %param.7) | copy-start | bytes 49156
  37.5 7.7 %collective-permute-start.7 = (bf16[3,14,24,128]{3,2,1,0:T(8,128)(2,1)S(1)}, bf16[3,14,24,128]{3,2,1,0:T(8,128)(2,1)S(1)}, u32[]{:S(2)}, u32[]{:S(2)}) collective-permute-start(bf16[3,14,24,128]{3,2,1,0:T(8,128)(2,1)S(1)} %pad_maximum_fusion.2), channel_id=1, source_target_pairs={{128,0},{256,128},{384,256},{129,1},{257,129},{385,257},{130,2},{2... | collective-permute-start | bytes 774152 | tf_op jit(solution)/shard_map/ppermute | solution.py:265
  38.8 8.1 %copy-start = (bf16[27,128,128]{2,1,0:T(8,128)(2,1)S(1)}, bf16[27,128,128]{2,1,0:T(8,128)(2,1)}, u32[]{:S(2)}) copy-start(bf16[27,128,128]{2,1,0:T(8,128)(2,1)} %coarse_weights.1) | copy-start | bytes 2654212
  38.9 8.1 %collective-permute-start.6 = (bf16[3,14,24,128]{3,2,1,0:T(8,128)(2,1)S(1)}, bf16[3,14,24,128]{3,2,1,0:T(8,128)(2,1)S(1)}, u32[]{:S(2)}, u32[]{:S(2)}) collective-permute-start(bf16[3,14,24,128]{3,2,1,0:T(8,128)(2,1)S(1)} %pad_maximum_fusion.1), channel_id=1, source_target_pairs={{0,128},{128,256},{256,384},{1,129},{129,257},{257,385},{2,130},{1... | collective-permute-start | bytes 774152 | tf_op jit(solution)/shard_map/ppermute | solution.py:264
  56.6 5.7 %copy-start.4 = (bf16[128,128]{1,0:T(8,128)(2,1)}, bf16[128,128]{1,0:T(8,128)(2,1)S(1)}, u32[]{:S(2)}) copy-start(bf16[128,128]{1,0:T(8,128)(2,1)S(1)} %get-tuple-element.28) | copy-start | bytes 98308
  56.6 5.7 %copy-start.6 = (f32[128,128]{1,0:T(8,128)}, f32[128,128]{1,0:T(8,128)S(1)}, u32[]{:S(2)}) copy-start(f32[128,128]{1,0:T(8,128)S(1)} %get-tuple-element.29) | copy-start | bytes 196612
  56.7 4.3 %collective-permute-start.8 = (bf16[3456,128]{1,0:T(8,128)(2,1)S(1)}, bf16[3456,128]{1,0:T(8,128)(2,1)S(1)}, u32[]{:S(2)}, u32[]{:S(2)}) collective-permute-start(bf16[3456,128]{1,0:T(8,128)(2,1)S(1)} %broadcast_select_fusion.2), channel_id=1, source_target_pairs={{0,1},{1,0},{2,3},{3,2},{4,5},{5,4},{6,7},{7,6},{8,9},{9,8},{10,11... | collective-permute-start | bytes 2654216 | tf_op jit(solution)/shard_map/ppermute | solution.py:364
  62.3 25.4 %all-to-all-start = ((bf16[16,216,128]{2,1,0:T(8,128)(2,1)}), bf16[16,216,128]{2,1,0:T(8,128)(2,1)S(1)}, u32[]{:S(2)}, u32[]{:S(2)}) async-start(bf16[16,216,128]{2,1,0:T(8,128)(2,1)} %bitcast.47), calls=%async_computation | async-start | bytes 1769472 | tf_op jit(solution)/shard_map/all_to_all | solution.py:281
  74.8 8.1 %collective-permute-start.10 = (bf16[4,2,8,128]{3,2,1,0:T(8,128)(2,1)S(1)}, bf16[4,2,8,128]{3,2,1,0:T(8,128)(2,1)S(1)}, u32[]{:S(2)}, u32[]{:S(2)}) collective-permute-start(bf16[4,2,8,128]{3,2,1,0:T(8,128)(2,1)S(1)} %get-tuple-element.58), channel_id=1, source_target_pairs={{16,0},{32,16},{48,32},{64,48},{80,64},{96,80},{112,96},{17,1},{33... | collective-permute-start | bytes 49160 | tf_op jit(solution)/shard_map/ppermute | solution.py:265
  76.0 6.8 %collective-permute-start.9 = (bf16[4,2,8,128]{3,2,1,0:T(8,128)(2,1)S(1)}, bf16[4,2,8,128]{3,2,1,0:T(8,128)(2,1)}, u32[]{:S(2)}, u32[]{:S(2)}) collective-permute-start(bf16[4,2,8,128]{3,2,1,0:T(8,128)(2,1)S(1)} %get-tuple-element.59), channel_id=1, source_target_pairs={{0,16},{16,32},{32,48},{48,64},{64,80},{80,96},{96,112},{1,17},{17... | collective-permute-start | bytes 49160 | tf_op jit(solution)/shard_map/ppermute | solution.py:264
  88.5 46.6 %copy-start.5 = (bf16[128,128]{1,0:T(8,128)(2,1)S(1)}, bf16[128,128]{1,0:T(8,128)(2,1)}, u32[]{:S(2)}) copy-start(bf16[128,128]{1,0:T(8,128)(2,1)} %copy-done.4) | copy-start | bytes 98308
  88.5 26.8 %all-to-all-start.1 = ((bf16[16,16,128]{2,1,0:T(8,128)(2,1)}), bf16[16,16,128]{2,1,0:T(8,128)(2,1)S(1)}, u32[]{:S(2)}, u32[]{:S(2)}) async-start(bf16[16,16,128]{2,1,0:T(8,128)(2,1)} %bitcast.35), calls=%async_computation.1 | async-start | bytes 131072 | tf_op jit(solution)/shard_map/all_to_all | solution.py:281
  130.6 15.6 %all-to-all-start.3 = ((bf16[16,216,128]{2,1,0:T(8,128)(2,1)}), bf16[16,216,128]{2,1,0:T(8,128)(2,1)}, u32[]{:S(2)}, u32[]{:S(2)}) async-start(bf16[16,216,128]{2,1,0:T(8,128)(2,1)} %broadcast_in_dim.2), calls=%async_computation.3 | async-start | bytes 1769472 | tf_op jit(solution)/shard_map/all_to_all | solution.py:281
  135.8 5.0 %collective-permute-start.11 = (bf16[2,8,8,128]{3,2,1,0:T(8,128)(2,1)S(1)}, bf16[2,8,8,128]{3,2,1,0:T(8,128)(2,1)S(1)}, u32[]{:S(2)}, u32[]{:S(2)}) collective-permute-start(bf16[2,8,8,128]{3,2,1,0:T(8,128)(2,1)S(1)} %get-tuple-element.57), channel_id=1, source_target_pairs={{0,128},{128,256},{256,384},{1,129},{129,257},{257,385},{2,130},{1... | collective-permute-start | bytes 98312 | tf_op jit(solution)/shard_map/ppermute | solution.py:264
  139.1 5.2 %collective-permute-start.12 = (bf16[2,8,8,128]{3,2,1,0:T(8,128)(2,1)S(1)}, bf16[2,8,8,128]{3,2,1,0:T(8,128)(2,1)S(1)}, u32[]{:S(2)}, u32[]{:S(2)}) collective-permute-start(bf16[2,8,8,128]{3,2,1,0:T(8,128)(2,1)S(1)} %get-tuple-element.56), channel_id=1, source_target_pairs={{128,0},{256,128},{384,256},{129,1},{257,129},{385,257},{130,2},{2... | collective-permute-start | bytes 98312 | tf_op jit(solution)/shard_map/ppermute | solution.py:265
  146.1 11.5 %collective-permute-start.13 = (bf16[3456,128]{1,0:T(8,128)(2,1)}, bf16[3456,128]{1,0:T(8,128)(2,1)S(1)}, u32[]{:S(2)}, u32[]{:S(2)}) collective-permute-start(bf16[3456,128]{1,0:T(8,128)(2,1)} %bitcast.20), channel_id=1, source_target_pairs={{0,1},{1,0},{2,3},{3,2},{4,5},{5,4},{6,7},{7,6},{8,9},{9,8},{10,11... | collective-permute-start | bytes 2654216 | tf_op jit(solution)/shard_map/ppermute | solution.py:403
  154.7 1.2 copy-start.2
  (1 other events, 0.6 us)

commit v12 on v9

--- a/solution.py
+++ b/solution.py
@@ -187,7 +187,7 @@
         )
 
 
-def fine_grad_kernel(left, middle, right, coarse_weights, slope, fine_ref, grads, spread):
+def fine_grad_kernel(left, middle, right, coarse_weights, slope, weights, fine_ref, begun_ref, grads, spread):
     for x in range(2):
         for at, part in ((x, left), (6 + x, right)):
             grads[at, :, :8] = part[64 * x : 64 * x + 64].astype(F32).reshape(8, 8, C)
@@ -199,23 +199,24 @@
     for x in range(10):
         for y in range(10):
             fine_ref[x, y] = spread[(x + 1) // 2, (y + 1) // 2] * slope[x + 1, y + 1, 4:20]
-
-
-def volume_kernel(fine, weights, out_ref):
-    total = jnp.zeros((512, C), F32)
-    for i in range(3):
-        cells = jnp.concatenate(
-            [
-                flat(fine[2 - i : 10 - i, 2 - j : 10 - j, 3 - k : 11 - k])
-                for j in range(3)
-                for k in range(3)
-            ],
-            axis=1,
-        )
-        turned = jnp.concatenate([weights[9 * i + t] for t in range(9)], axis=1)
-        total = total + lax.dot_general(
-            cells, turned, (((1,), (1,)), ((), ())), preferred_element_type=F32
-        )
+    begun_ref[...] = volume_terms(fine_ref, weights, 0)
+
+
+def volume_terms(fine, weights, i):
+    cells = jnp.concatenate(
+        [
+            flat(fine[2 - i : 10 - i, 2 - j : 10 - j, 3 - k : 11 - k])
+            for j in range(3)
+            for k in range(3)
+        ],
+        axis=1,
+    )
+    turned = jnp.concatenate([weights[9 * i + t] for t in range(9)], axis=1)
+    return lax.dot_general(cells, turned, (((1,), (1,)), ((), ())), preferred_element_type=F32)
+
+
+def volume_kernel(fine, begun, weights, out_ref):
+    total = begun[...] + volume_terms(fine, weights, 1) + volume_terms(fine, weights, 2)
     out_ref[...] = total.astype(BF16)
 
 
@@ -381,26 +382,27 @@
     part = joined(parts)[:length]
     grads = jnp.concatenate([halo[0], grads, halo[1]], axis=1)
     halo = beside(grads[2:], grads[:2], "gx", peers[0])
-    (fine_grad,) = call(
+    fine_grad, begun = call(
         fine_grad_kernel,
-        [((10, 10, 16, C), F32)],
+        [((10, 10, 16, C), F32), ((512, C), F32)],
         [
             halo[0].reshape(128, C),
             grads.reshape(256, C),
             halo[1].reshape(128, C),
             coarse_weight,
             slope,
+            fine_weight,
         ],
         scratch=[((8, 8, 16, C), F32), ((6, 6, 16, C), F32)],
-        flops=2 * 288 * 27 * C * C,
+        flops=2 * 460 * 27 * C * C,
     )
     parts = exchanged(jnp.broadcast_to(part[None], (plane, length, C)), PLANE)
-    parts, fine_grad = lax.optimization_barrier((parts, fine_grad))
+    parts, fine_grad, begun = lax.optimization_barrier((parts, fine_grad, begun))
     (grad_volume,) = call(
         volume_kernel,
         [((512, C), BF16)],
-        [fine_grad, fine_weight],
-        flops=2 * 512 * 27 * C * C,
+        [fine_grad, begun, fine_weight],
+        flops=2 * 342 * 27 * C * C,
     )
     mine = joined(parts)
     other = lax.ppermute(mine, "core", swap)

time: 161 us -> 164 us (1.019)
  local copies, waits for them, and re-layouts: 4.58 us -> 7.1 us
    unnamed x18 -> x24, local copies, waits for them, and re-layouts: 1.83 us -> 4.35 us
  transfers between devices with their start and end apart: 15 -> 15, of which waited for: 9 -> 8; matrix products, arithmetic and copies ran while one was open for 3% -> 3% of each run, Pallas kernels for 4% -> 5%
where the time goes in v12:
time: 164 us; the launch traced here: 163 us
  starting transfers between devices  88.7 us (54%)
  waiting for transfers between devices  26.4 us (16%)
  Pallas kernels  18 us (11%)
  blocking collectives  14.2 us (9%)
  other arithmetic  7.46 us (5%)
  local copies, waits for them, and re-layouts  7.1 us (4%)
    all_to_all x3, starting transfers between devices, exchanged(): return lax.all_to_all(parts, axes, 0, 0, tiled=True)  30.3 us
    ppermute x4, starting transfers between devices, beside(): before = lax.ppermute(last, axis, line(count, 1))  23.8 us
    pallas_call x7, Pallas kernels, call(): pl.pallas_call(kernel, out_shape=[jax.ShapeDtypeStruct(s, t) for s, t in...  18 us
    ppermute x1, starting transfers between devices, along_width(): lax.ppermute(x, WIDTH, [(i, i - 1 + 2 * (i % 2)) for i in range(1, count...  16.8 us
    all_to_all x3, waiting for transfers between devices, exchanged(): return lax.all_to_all(parts, axes, 0, 0, tiled=True)  16.1 us
    all_to_all x1, blocking collectives, exchanged(): return lax.all_to_all(parts, axes, 0, 0, tiled=True)  14.2 us
    ppermute x1, starting transfers between devices, local(): other = lax.ppermute(mine, 'core', swap)  8.67 us
    ppermute x4, waiting for transfers between devices, beside(): after = lax.ppermute(leading, axis, line(count, -1))  5.5 us
  transfers between devices with their start and end apart: 15, of which 8 were waited for; matrix products, arithmetic and copies ran while one was open for 3% of the time, Pallas kernels for 5%

profile of v12, /device:TPU:1, one launch (start us, length us, event | category | flops | bytes accessed | tf_op | source)
XLA Modules:
  0.0 163.0 jit_solution(13634645577598271048)
XLA Ops:
  1.6 16.8 %collective-permute-start = (bf16[576,128]{1,0:T(8,128)(2,1)S(1)}, bf16[576,128]{1,0:T(8,128)(2,1)S(1)}, u32[]{:S(2)}, u32[]{:S(2)}) collective-permute-start(bf16[576,128]{1,0:T(8,128)(2,1)S(1)} %pad_maximum_fusion.3), channel_id=1, source_target_pairs={{1,2},{2,1},{3,4},{4,3},{5,6},{6,5},{7,8},{8,7},{9,10},{10,9},{11,... | collective-permute-start | bytes 442376 | tf_op jit(solution)/shard_map/ppermute | solution.py:269
  18.5 1.9 %collective-permute-start.1 = (bf16[576,128]{1,0:T(8,128)(2,1)S(1)}, bf16[576,128]{1,0:T(8,128)(2,1)S(1)}, u32[]{:S(2)}, u32[]{:S(2)}) collective-permute-start(bf16[576,128]{1,0:T(8,128)(2,1)S(1)} %pad_maximum_fusion.3), channel_id=1, source_target_pairs={{0,1},{1,0},{2,3},{3,2},{4,5},{5,4},{6,7},{7,6},{8,9},{9,8},{10,11... | collective-permute-start | bytes 442376 | tf_op jit(solution)/shard_map/ppermute | solution.py:270
  23.9 12.3 %collective-permute-start.2 = (bf16[8,3,24,128]{3,2,1,0:T(8,128)(2,1)S(1)}, bf16[8,3,24,128]{3,2,1,0:T(8,128)(2,1)S(1)}, u32[]{:S(2)}, u32[]{:S(2)}) collective-permute-start(bf16[8,3,24,128]{3,2,1,0:T(8,128)(2,1)S(1)} %pad_maximum_fusion.4), channel_id=1, source_target_pairs={{0,16},{16,32},{32,48},{48,64},{64,80},{80,96},{96,112},{1,17},{17... | collective-permute-start | bytes 442376 | tf_op jit(solution)/shard_map/ppermute | solution.py:263
  36.2 2.1 %shard_map.75.refs_9_ = f32[6,6,24,128]{3,2,1,0:T(8,128)S(1)} custom-call(bf16[8,192,128]{2,1,0:T(8,128)(2,1)S(1)} %bitcast.36, bf16[3456,128]{1,0:T(8,128)(2,1)S(1)} %bitcast.33), custom_call_target="tpu_custom_call" | custom-call | flops 764411904 | bytes 1720320 | tf_op jit(solution)/shard_map/pallas_call | solution.py:247
  40.1 4.0 %collective-permute-start.4 = (bf16[3,14,24,128]{3,2,1,0:T(8,128)(2,1)S(1)}, bf16[3,14,24,128]{3,2,1,0:T(8,128)(2,1)S(1)}, u32[]{:S(2)}, u32[]{:S(2)}) collective-permute-start(bf16[3,14,24,128]{3,2,1,0:T(8,128)(2,1)S(1)} %pad_maximum_fusion.1), channel_id=1, source_target_pairs={{0,128},{128,256},{256,384},{1,129},{129,257},{257,385},{2,130},{1... | collective-permute-start | bytes 774152 | tf_op jit(solution)/shard_map/ppermute | solution.py:263
  44.1 2.1 %shard_map.76.refs_10_ = f32[6,6,24,128]{3,2,1,0:T(8,128)S(1)} custom-call(bf16[8,192,128]{2,1,0:T(8,128)(2,1)S(1)} %bitcast.37, bf16[8,72,128]{2,1,0:T(8,128)(2,1)S(1)} %bitcast.45, bf16[8,72,128]{2,1,0:T(8,128)(2,1)S(1)} %bitcast.43, bf16[3456,128]{1,0:T(8,128)(2,1)S(1)} %bitcast.34), custom_call_target="tpu_custom_call" | custom-call | flops 764411904 | bytes 2015232 | tf_op jit(solution)/shard_map/pallas_call | solution.py:247
  47.3 9.6 %shard_map.77 = (f32[128,128]{1,0:T(8,128)S(1)}, bf16[128,128]{1,0:T(8,128)(2,1)S(1)}, f32[12,12,24,128]{3,2,1,0:T(8,128)S(1)}, bf16[3456,128]{1,0:T(8,128)(2,1)S(1)}, bf16[3456,128]{1,0:T(8,128)(2,1)S(1)}) custom-call(s32[3]{0:T(128)S(1)} %pad_add_fusion.refs_0_, bf16[8,192,128]{2,1,0:T(8,128)(2,1)S(1)} %bitcast.38, bf16[8,72,128]{2,1,0:T(8,128)(2,1)S(1)} %bitcast.46, ...), custom_call_target="tpu_custom_call" | custom-call | flops 3538944000 | bytes 7561228 | tf_op jit(solution)/shard_map/pallas_call | solution.py:247
  57.1 1.9 %collective-permute-start.6 = (bf16[3456,128]{1,0:T(8,128)(2,1)S(1)}, bf16[3456,128]{1,0:T(8,128)(2,1)S(1)}, u32[]{:S(2)}, u32[]{:S(2)}) collective-permute-start(bf16[3456,128]{1,0:T(8,128)(2,1)S(1)} %broadcast_select_fusion.2), channel_id=1, source_target_pairs={{0,1},{1,0},{2,3},{3,2},{4,5},{5,4},{6,7},{7,6},{8,9},{9,8},{10,11... | collective-permute-start | bytes 2654216 | tf_op jit(solution)/shard_map/ppermute | solution.py:368
  59.0 2.4 %collective-permute-done.6 = bf16[3456,128]{1,0:T(8,128)(2,1)S(1)} collective-permute-done((bf16[3456,128]{1,0:T(8,128)(2,1)S(1)}, bf16[3456,128]{1,0:T(8,128)(2,1)S(1)}, u32[]{:S(2)}, u32[]{:S(2)}) %collective-permute-start.6) | collective-permute-done | bytes 884768 | tf_op jit(solution)/shard_map/ppermute | solution.py:368
  62.7 11.6 %all-to-all-start = ((bf16[16,216,128]{2,1,0:T(8,128)(2,1)}), bf16[16,216,128]{2,1,0:T(8,128)(2,1)S(1)}, u32[]{:S(2)}, u32[]{:S(2)}) async-start(bf16[16,216,128]{2,1,0:T(8,128)(2,1)} %bitcast.52), calls=%async_computation | async-start | bytes 1769472 | tf_op jit(solution)/shard_map/all_to_all | solution.py:280
  75.1 4.3 %collective-permute-start.7 = (bf16[4,2,8,128]{3,2,1,0:T(8,128)(2,1)S(1)}, bf16[4,2,8,128]{3,2,1,0:T(8,128)(2,1)S(1)}, u32[]{:S(2)}, u32[]{:S(2)}) collective-permute-start(bf16[4,2,8,128]{3,2,1,0:T(8,128)(2,1)S(1)} %get-tuple-element.57), channel_id=1, source_target_pairs={{0,16},{16,32},{32,48},{48,64},{64,80},{80,96},{96,112},{1,17},{17... | collective-permute-start | bytes 49160 | tf_op jit(solution)/shard_map/ppermute | solution.py:263
  80.7 1.5 fusion
  82.1 2.0 %collective-permute-done.8 = bf16[4,2,8,128]{3,2,1,0:T(8,128)(2,1)} collective-permute-done((bf16[4,2,8,128]{3,2,1,0:T(8,128)(2,1)S(1)}, bf16[4,2,8,128]{3,2,1,0:T(8,128)(2,1)}, u32[]{:S(2)}, u32[]{:S(2)}) %collective-permute-start.8) | collective-permute-done | bytes 16416 | tf_op jit(solution)/shard_map/ppermute | solution.py:264
  84.1 3.9 %all-to-all-done.parts = bf16[16,216,128]{2,1,0:T(8,128)(2,1)S(1)} async-done(((bf16[16,216,128]{2,1,0:T(8,128)(2,1)}), bf16[16,216,128]{2,1,0:T(8,128)(2,1)S(1)}, u32[]{:S(2)}, u32[]{:S(2)}) %all-to-all-start) | async-done | bytes 884768 | tf_op jit(solution)/shard_map/all_to_all | solution.py:280
  88.8 14.1 %all-to-all-start.1 = ((bf16[16,16,128]{2,1,0:T(8,128)(2,1)}), bf16[16,16,128]{2,1,0:T(8,128)(2,1)}, u32[]{:S(2)}, u32[]{:S(2)}) async-start(bf16[16,16,128]{2,1,0:T(8,128)(2,1)} %bitcast.40), calls=%async_computation.1 | async-start | bytes 131072 | tf_op jit(solution)/shard_map/all_to_all | solution.py:280
  102.9 12.2 %all-to-all-done.1.parts = bf16[16,16,128]{2,1,0:T(8,128)(2,1)} async-done(((bf16[16,16,128]{2,1,0:T(8,128)(2,1)}), bf16[16,16,128]{2,1,0:T(8,128)(2,1)}, u32[]{:S(2)}, u32[]{:S(2)}) %all-to-all-start.1) | async-done | bytes 65568 | tf_op jit(solution)/shard_map/all_to_all | solution.py:280
  116.0 14.2 %all_to_all.20 = bf16[16,16,128]{2,1,0:T(8,128)(2,1)S(1)} all-to-all(bf16[16,16,128]{2,1,0:T(8,128)(2,1)S(1)} %shard_map.79), channel_id=1, replica_groups=mesh['gx'=4,'gy'=8,'y'=4,'zh'=2,'core'=2] {'gy','zh'}, dimensions={0} | all-to-all | bytes 131072 | tf_op jit(solution)/shard_map/all_to_all | solution.py:280
  131.2 4.5 %all-to-all-start.3 = ((bf16[16,216,128]{2,1,0:T(8,128)(2,1)}), bf16[16,216,128]{2,1,0:T(8,128)(2,1)}, u32[]{:S(2)}, u32[]{:S(2)}) async-start(bf16[16,216,128]{2,1,0:T(8,128)(2,1)} %broadcast_in_dim.2), calls=%async_computation.3 | async-start | bytes 1769472 | tf_op jit(solution)/shard_map/all_to_all | solution.py:280
  136.5 3.2 %collective-permute-start.9 = (bf16[2,8,8,128]{3,2,1,0:T(8,128)(2,1)S(1)}, bf16[2,8,8,128]{3,2,1,0:T(8,128)(2,1)S(1)}, u32[]{:S(2)}, u32[]{:S(2)}) collective-permute-start(bf16[2,8,8,128]{3,2,1,0:T(8,128)(2,1)S(1)} %get-tuple-element.55), channel_id=1, source_target_pairs={{0,128},{128,256},{256,384},{1,129},{129,257},{257,385},{2,130},{1... | collective-permute-start | bytes 98312 | tf_op jit(solution)/shard_map/ppermute | solution.py:263
  141.5 3.5 %collective-permute-done.10 = bf16[2,8,8,128]{3,2,1,0:T(8,128)(2,1)S(1)} collective-permute-done((bf16[2,8,8,128]{3,2,1,0:T(8,128)(2,1)S(1)}, bf16[2,8,8,128]{3,2,1,0:T(8,128)(2,1)S(1)}, u32[]{:S(2)}, u32[]{:S(2)}) %collective-permute-start.10) | collective-permute-done | bytes 32800 | tf_op jit(solution)/shard_map/ppermute | solution.py:264
  145.0 1.7 %shard_map.80 = (f32[10,10,16,128]{3,2,1,0:T(8,128)S(1)}, f32[512,128]{1,0:T(8,128)S(1)}) custom-call(bf16[128,128]{1,0:T(8,128)(2,1)S(1)} %bitcast.47, bf16[256,128]{1,0:T(8,128)(2,1)S(1)} %bitcast.39, bf16[128,128]{1,0:T(8,128)(2,1)S(1)} %bitcast.48, bf16[27,128,128]{2,1,0:T(8,128)(2,1)S(1)} %copy-done.2, f32[12,12,24,128]{3,2,1,0:T(8,128)S(1)} %get-tuple-element.32.slope, ...), custom_call_target="tpu_custom_call" | custom-call | flops 406978560 | bytes 4751360 | tf_op jit(solution)/shard_map/pallas_call | solution.py:247
  148.3 8.7 %collective-permute-start.11 = (bf16[3456,128]{1,0:T(8,128)(2,1)}, bf16[3456,128]{1,0:T(8,128)(2,1)S(1)}, u32[]{:S(2)}, u32[]{:S(2)}) collective-permute-start(bf16[3456,128]{1,0:T(8,128)(2,1)} %bitcast.26), channel_id=1, source_target_pairs={{0,1},{1,0},{2,3},{3,2},{4,5},{5,4},{6,7},{7,6},{8,9},{9,8},{10,11... | collective-permute-start | bytes 2654216 | tf_op jit(solution)/shard_map/ppermute | solution.py:408
  159.1 1.4 shard_map.81
  160.5 2.5 %broadcast_select_fusion = (bf16[3456,128]{1,0:T(8,128)(2,1)}, bf16[3456,128]{1,0:T(8,128)(2,1)}) fusion(bf16[3456,128]{1,0:T(8,128)(2,1)S(1)} %collective-permute-done.11, pred[]{:T(512)S(6)} %eq.4, bf16[16,216,128]{2,1,0:T(8,128)(2,1)} %all-to-all-done.3), kind=kLoop, calls=%fused_computation.1 | loop fusion | flops 884736 | bytes 3538945 | tf_op jit(solution)/shard_map/jit(_where)/select_n | solution.py:410
  (68 shorter events, 19.4 us)
Async XLA Ops:
  0.6 21.8 %copy-start.10 = (bf16[8,8,8,128]{3,2,1,0:T(8,128)(2,1)S(1)}, bf16[8,8,8,128]{3,2,1,0:T(8,128)(2,1)}, u32[]{:S(2)}) copy-start(bf16[8,8,8,128]{3,2,1,0:T(8,128)(2,1)} %param.4) | copy-start | bytes 393220
  1.6 20.7 %collective-permute-start = (bf16[576,128]{1,0:T(8,128)(2,1)S(1)}, bf16[576,128]{1,0:T(8,128)(2,1)S(1)}, u32[]{:S(2)}, u32[]{:S(2)}) collective-permute-start(bf16[576,128]{1,0:T(8,128)(2,1)S(1)} %pad_maximum_fusion.3), channel_id=1, source_target_pairs={{1,2},{2,1},{3,4},{4,3},{5,6},{6,5},{7,8},{8,7},{9,10},{10,9},{11,... | collective-permute-start | bytes 442376 | tf_op jit(solution)/shard_map/ppermute | solution.py:269
  18.5 3.8 %collective-permute-start.1 = (bf16[576,128]{1,0:T(8,128)(2,1)S(1)}, bf16[576,128]{1,0:T(8,128)(2,1)S(1)}, u32[]{:S(2)}, u32[]{:S(2)}) collective-permute-start(bf16[576,128]{1,0:T(8,128)(2,1)S(1)} %pad_maximum_fusion.3), channel_id=1, source_target_pairs={{0,1},{1,0},{2,3},{3,2},{4,5},{5,4},{6,7},{7,6},{8,9},{9,8},{10,11... | collective-permute-start | bytes 442376 | tf_op jit(solution)/shard_map/ppermute | solution.py:270
  21.2 15.0 %copy-start = (bf16[27,128,128]{2,1,0:T(8,128)(2,1)S(1)}, bf16[27,128,128]{2,1,0:T(8,128)(2,1)}, u32[]{:S(2)}) copy-start(bf16[27,128,128]{2,1,0:T(8,128)(2,1)} %weights.3) | copy-start | bytes 2654212
  22.5 15.9 %collective-permute-start.3 = (bf16[8,3,24,128]{3,2,1,0:T(8,128)(2,1)S(1)}, bf16[8,3,24,128]{3,2,1,0:T(8,128)(2,1)S(1)}, u32[]{:S(2)}, u32[]{:S(2)}) collective-permute-start(bf16[8,3,24,128]{3,2,1,0:T(8,128)(2,1)S(1)} %pad_maximum_fusion.5), channel_id=1, source_target_pairs={{16,0},{32,16},{48,32},{64,48},{80,64},{96,80},{112,96},{17,1},{33... | collective-permute-start | bytes 442376 | tf_op jit(solution)/shard_map/ppermute | solution.py:264
  23.9 14.6 %copy-start.11 = (bf16[4,4,4,128]{3,2,1,0:T(4,128)(2,1)S(1)}, bf16[4,4,4,128]{3,2,1,0:T(4,128)(2,1)}, u32[]{:S(2)}) copy-start(bf16[4,4,4,128]{3,2,1,0:T(4,128)(2,1)} %param.7) | copy-start | bytes 49156
  23.9 14.6 %collective-permute-start.2 = (bf16[8,3,24,128]{3,2,1,0:T(8,128)(2,1)S(1)}, bf16[8,3,24,128]{3,2,1,0:T(8,128)(2,1)S(1)}, u32[]{:S(2)}, u32[]{:S(2)}) collective-permute-start(bf16[8,3,24,128]{3,2,1,0:T(8,128)(2,1)S(1)} %pad_maximum_fusion.4), channel_id=1, source_target_pairs={{0,16},{16,32},{32,48},{48,64},{64,80},{80,96},{96,112},{1,17},{17... | collective-permute-start | bytes 442376 | tf_op jit(solution)/shard_map/ppermute | solution.py:263
  38.6 8.7 %copy-start.1 = (bf16[27,128,128]{2,1,0:T(8,128)(2,1)S(1)}, bf16[27,128,128]{2,1,0:T(8,128)(2,1)}, u32[]{:S(2)}) copy-start(bf16[27,128,128]{2,1,0:T(8,128)(2,1)} %coarse_weights.1) | copy-start | bytes 2654212
  38.6 7.6 %collective-permute-start.5 = (bf16[3,14,24,128]{3,2,1,0:T(8,128)(2,1)S(1)}, bf16[3,14,24,128]{3,2,1,0:T(8,128)(2,1)S(1)}, u32[]{:S(2)}, u32[]{:S(2)}) collective-permute-start(bf16[3,14,24,128]{3,2,1,0:T(8,128)(2,1)S(1)} %pad_maximum_fusion.2), channel_id=1, source_target_pairs={{128,0},{256,128},{384,256},{129,1},{257,129},{385,257},{130,2},{2... | collective-permute-start | bytes 774152 | tf_op jit(solution)/shard_map/ppermute | solution.py:264
  40.1 7.2 %collective-permute-start.4 = (bf16[3,14,24,128]{3,2,1,0:T(8,128)(2,1)S(1)}, bf16[3,14,24,128]{3,2,1,0:T(8,128)(2,1)S(1)}, u32[]{:S(2)}, u32[]{:S(2)}) collective-permute-start(bf16[3,14,24,128]{3,2,1,0:T(8,128)(2,1)S(1)} %pad_maximum_fusion.1), channel_id=1, source_target_pairs={{0,128},{128,256},{256,384},{1,129},{129,257},{257,385},{2,130},{1... | collective-permute-start | bytes 774152 | tf_op jit(solution)/shard_map/ppermute | solution.py:263
  57.0 5.7 %copy-start.8 = (bf16[128,128]{1,0:T(8,128)(2,1)}, bf16[128,128]{1,0:T(8,128)(2,1)S(1)}, u32[]{:S(2)}) copy-start(bf16[128,128]{1,0:T(8,128)(2,1)S(1)} %get-tuple-element.23) | copy-start | bytes 98308
  57.0 5.7 %copy-start.9 = (f32[128,128]{1,0:T(8,128)}, f32[128,128]{1,0:T(8,128)S(1)}, u32[]{:S(2)}) copy-start(f32[128,128]{1,0:T(8,128)S(1)} %get-tuple-element.24) | copy-start | bytes 196612
  57.1 4.3 %collective-permute-start.6 = (bf16[3456,128]{1,0:T(8,128)(2,1)S(1)}, bf16[3456,128]{1,0:T(8,128)(2,1)S(1)}, u32[]{:S(2)}, u32[]{:S(2)}) collective-permute-start(bf16[3456,128]{1,0:T(8,128)(2,1)S(1)} %broadcast_select_fusion.2), channel_id=1, source_target_pairs={{0,1},{1,0},{2,3},{3,2},{4,5},{5,4},{6,7},{7,6},{8,9},{9,8},{10,11... | collective-permute-start | bytes 2654216 | tf_op jit(solution)/shard_map/ppermute | solution.py:368
  62.7 25.3 %all-to-all-start = ((bf16[16,216,128]{2,1,0:T(8,128)(2,1)}), bf16[16,216,128]{2,1,0:T(8,128)(2,1)S(1)}, u32[]{:S(2)}, u32[]{:S(2)}) async-start(bf16[16,216,128]{2,1,0:T(8,128)(2,1)} %bitcast.52), calls=%async_computation | async-start | bytes 1769472 | tf_op jit(solution)/shard_map/all_to_all | solution.py:280
  75.1 7.1 %collective-permute-start.7 = (bf16[4,2,8,128]{3,2,1,0:T(8,128)(2,1)S(1)}, bf16[4,2,8,128]{3,2,1,0:T(8,128)(2,1)S(1)}, u32[]{:S(2)}, u32[]{:S(2)}) collective-permute-start(bf16[4,2,8,128]{3,2,1,0:T(8,128)(2,1)S(1)} %get-tuple-element.57), channel_id=1, source_target_pairs={{0,16},{16,32},{32,48},{48,64},{64,80},{80,96},{96,112},{1,17},{17... | collective-permute-start | bytes 49160 | tf_op jit(solution)/shard_map/ppermute | solution.py:263
  79.4 4.8 %collective-permute-start.8 = (bf16[4,2,8,128]{3,2,1,0:T(8,128)(2,1)S(1)}, bf16[4,2,8,128]{3,2,1,0:T(8,128)(2,1)}, u32[]{:S(2)}, u32[]{:S(2)}) collective-permute-start(bf16[4,2,8,128]{3,2,1,0:T(8,128)(2,1)S(1)} %get-tuple-element.56), channel_id=1, source_target_pairs={{16,0},{32,16},{48,32},{64,48},{80,64},{96,80},{112,96},{17,1},{33... | collective-permute-start | bytes 49160 | tf_op jit(solution)/shard_map/ppermute | solution.py:264
  88.8 56.2 %copy-start.2 = (bf16[27,128,128]{2,1,0:T(8,128)(2,1)S(1)}, bf16[27,128,128]{2,1,0:T(8,128)(2,1)}, u32[]{:S(2)}) copy-start(bf16[27,128,128]{2,1,0:T(8,128)(2,1)} %coarse_weights.1) | copy-start | bytes 2654212
  88.8 26.3 %all-to-all-start.1 = ((bf16[16,16,128]{2,1,0:T(8,128)(2,1)}), bf16[16,16,128]{2,1,0:T(8,128)(2,1)}, u32[]{:S(2)}, u32[]{:S(2)}) async-start(bf16[16,16,128]{2,1,0:T(8,128)(2,1)} %bitcast.40), calls=%async_computation.1 | async-start | bytes 131072 | tf_op jit(solution)/shard_map/all_to_all | solution.py:280
  131.2 17.1 %all-to-all-start.3 = ((bf16[16,216,128]{2,1,0:T(8,128)(2,1)}), bf16[16,216,128]{2,1,0:T(8,128)(2,1)}, u32[]{:S(2)}, u32[]{:S(2)}) async-start(bf16[16,216,128]{2,1,0:T(8,128)(2,1)} %broadcast_in_dim.2), calls=%async_computation.3 | async-start | bytes 1769472 | tf_op jit(solution)/shard_map/all_to_all | solution.py:280
  136.5 4.9 %collective-permute-start.9 = (bf16[2,8,8,128]{3,2,1,0:T(8,128)(2,1)S(1)}, bf16[2,8,8,128]{3,2,1,0:T(8,128)(2,1)S(1)}, u32[]{:S(2)}, u32[]{:S(2)}) collective-permute-start(bf16[2,8,8,128]{3,2,1,0:T(8,128)(2,1)S(1)} %get-tuple-element.55), channel_id=1, source_target_pairs={{0,128},{128,256},{256,384},{1,129},{129,257},{257,385},{2,130},{1... | collective-permute-start | bytes 98312 | tf_op jit(solution)/shard_map/ppermute | solution.py:263
  139.8 5.2 %collective-permute-start.10 = (bf16[2,8,8,128]{3,2,1,0:T(8,128)(2,1)S(1)}, bf16[2,8,8,128]{3,2,1,0:T(8,128)(2,1)S(1)}, u32[]{:S(2)}, u32[]{:S(2)}) collective-permute-start(bf16[2,8,8,128]{3,2,1,0:T(8,128)(2,1)S(1)} %get-tuple-element.54), channel_id=1, source_target_pairs={{128,0},{256,128},{384,256},{129,1},{257,129},{385,257},{130,2},{2... | collective-permute-start | bytes 98312 | tf_op jit(solution)/shard_map/ppermute | solution.py:264
  148.3 12.2 %collective-permute-start.11 = (bf16[3456,128]{1,0:T(8,128)(2,1)}, bf16[3456,128]{1,0:T(8,128)(2,1)S(1)}, u32[]{:S(2)}, u32[]{:S(2)}) collective-permute-start(bf16[3456,128]{1,0:T(8,128)(2,1)} %bitcast.26), channel_id=1, source_target_pairs={{0,1},{1,0},{2,3},{3,2},{4,5},{5,4},{6,7},{7,6},{8,9},{9,8},{10,11... | collective-permute-start | bytes 2654216 | tf_op jit(solution)/shard_map/ppermute | solution.py:408
  157.0 1.1 copy-start.4
  158.1 0.9 copy-start.6
  (3 other events, 2.2 us)

commit v13 on v12

--- a/solution.py
+++ b/solution.py
@@ -397,7 +397,7 @@
         flops=2 * 460 * 27 * C * C,
     )
     parts = exchanged(jnp.broadcast_to(part[None], (plane, length, C)), PLANE)
-    parts, fine_grad, begun = lax.optimization_barrier((parts, fine_grad, begun))
+    parts, fine_grad = lax.optimization_barrier((parts, fine_grad))
     (grad_volume,) = call(
         volume_kernel,
         [((512, C), BF16)],

time: 164 us -> 164 us (level)
  no operation moved by 1% of the time
where the time goes in v13:
time: 164 us; the launch traced here: 163 us
  starting transfers between devices  88.7 us (54%)
  waiting for transfers between devices  26.4 us (16%)
  Pallas kernels  18 us (11%)
  blocking collectives  14.2 us (9%)
  other arithmetic  7.46 us (5%)
  local copies, waits for them, and re-layouts  7.1 us (4%)
    all_to_all x3, starting transfers between devices, exchanged(): return lax.all_to_all(parts, axes, 0, 0, tiled=True)  30.3 us
    ppermute x4, starting transfers between devices, beside(): before = lax.ppermute(last, axis, line(count, 1))  23.8 us
    pallas_call x7, Pallas kernels, call(): pl.pallas_call(kernel, out_shape=[jax.ShapeDtypeStruct(s, t) for s, t in...  18 us
    ppermute x1, starting transfers between devices, along_width(): lax.ppermute(x, WIDTH, [(i, i - 1 + 2 * (i % 2)) for i in range(1, count...  16.8 us
    all_to_all x3, waiting for transfers between devices, exchanged(): return lax.all_to_all(parts, axes, 0, 0, tiled=True)  16.1 us
    all_to_all x1, blocking collectives, exchanged(): return lax.all_to_all(parts, axes, 0, 0, tiled=True)  14.2 us
    ppermute x1, starting transfers between devices, local(): other = lax.ppermute(mine, 'core', swap)  8.67 us
    ppermute x4, waiting for transfers between devices, beside(): after = lax.ppermute(leading, axis, line(count, -1))  5.5 us
  transfers between devices with their start and end apart: 15, of which 8 were waited for; matrix products, arithmetic and copies ran while one was open for 3% of the time, Pallas kernels for 5%

profile of v13, /device:TPU:1, one launch (start us, length us, event | category | flops | bytes accessed | tf_op | source)
XLA Modules:
  0.0 163.0 jit_solution(13634645577598271048)
XLA Ops:
  1.6 16.8 %collective-permute-start = (bf16[576,128]{1,0:T(8,128)(2,1)S(1)}, bf16[576,128]{1,0:T(8,128)(2,1)S(1)}, u32[]{:S(2)}, u32[]{:S(2)}) collective-permute-start(bf16[576,128]{1,0:T(8,128)(2,1)S(1)} %pad_maximum_fusion.3), channel_id=1, source_target_pairs={{1,2},{2,1},{3,4},{4,3},{5,6},{6,5},{7,8},{8,7},{9,10},{10,9},{11,... | collective-permute-start | bytes 442376 | tf_op jit(solution)/shard_map/ppermute | solution.py:269
  18.5 1.9 %collective-permute-start.1 = (bf16[576,128]{1,0:T(8,128)(2,1)S(1)}, bf16[576,128]{1,0:T(8,128)(2,1)S(1)}, u32[]{:S(2)}, u32[]{:S(2)}) collective-permute-start(bf16[576,128]{1,0:T(8,128)(2,1)S(1)} %pad_maximum_fusion.3), channel_id=1, source_target_pairs={{0,1},{1,0},{2,3},{3,2},{4,5},{5,4},{6,7},{7,6},{8,9},{9,8},{10,11... | collective-permute-start | bytes 442376 | tf_op jit(solution)/shard_map/ppermute | solution.py:270
  23.9 12.3 %collective-permute-start.2 = (bf16[8,3,24,128]{3,2,1,0:T(8,128)(2,1)S(1)}, bf16[8,3,24,128]{3,2,1,0:T(8,128)(2,1)S(1)}, u32[]{:S(2)}, u32[]{:S(2)}) collective-permute-start(bf16[8,3,24,128]{3,2,1,0:T(8,128)(2,1)S(1)} %pad_maximum_fusion.4), channel_id=1, source_target_pairs={{0,16},{16,32},{32,48},{48,64},{64,80},{80,96},{96,112},{1,17},{17... | collective-permute-start | bytes 442376 | tf_op jit(solution)/shard_map/ppermute | solution.py:263
  36.2 2.1 %shard_map.75.refs_9_ = f32[6,6,24,128]{3,2,1,0:T(8,128)S(1)} custom-call(bf16[8,192,128]{2,1,0:T(8,128)(2,1)S(1)} %bitcast.36, bf16[3456,128]{1,0:T(8,128)(2,1)S(1)} %bitcast.33), custom_call_target="tpu_custom_call" | custom-call | flops 764411904 | bytes 1720320 | tf_op jit(solution)/shard_map/pallas_call | solution.py:247
  40.1 4.0 %collective-permute-start.4 = (bf16[3,14,24,128]{3,2,1,0:T(8,128)(2,1)S(1)}, bf16[3,14,24,128]{3,2,1,0:T(8,128)(2,1)S(1)}, u32[]{:S(2)}, u32[]{:S(2)}) collective-permute-start(bf16[3,14,24,128]{3,2,1,0:T(8,128)(2,1)S(1)} %pad_maximum_fusion.1), channel_id=1, source_target_pairs={{0,128},{128,256},{256,384},{1,129},{129,257},{257,385},{2,130},{1... | collective-permute-start | bytes 774152 | tf_op jit(solution)/shard_map/ppermute | solution.py:263
  44.1 2.1 %shard_map.76.refs_10_ = f32[6,6,24,128]{3,2,1,0:T(8,128)S(1)} custom-call(bf16[8,192,128]{2,1,0:T(8,128)(2,1)S(1)} %bitcast.37, bf16[8,72,128]{2,1,0:T(8,128)(2,1)S(1)} %bitcast.45, bf16[8,72,128]{2,1,0:T(8,128)(2,1)S(1)} %bitcast.43, bf16[3456,128]{1,0:T(8,128)(2,1)S(1)} %bitcast.34), custom_call_target="tpu_custom_call" | custom-call | flops 764411904 | bytes 2015232 | tf_op jit(solution)/shard_map/pallas_call | solution.py:247
  47.3 9.6 %shard_map.77 = (f32[128,128]{1,0:T(8,128)S(1)}, bf16[128,128]{1,0:T(8,128)(2,1)S(1)}, f32[12,12,24,128]{3,2,1,0:T(8,128)S(1)}, bf16[3456,128]{1,0:T(8,128)(2,1)S(1)}, bf16[3456,128]{1,0:T(8,128)(2,1)S(1)}) custom-call(s32[3]{0:T(128)S(1)} %pad_add_fusion.refs_0_, bf16[8,192,128]{2,1,0:T(8,128)(2,1)S(1)} %bitcast.38, bf16[8,72,128]{2,1,0:T(8,128)(2,1)S(1)} %bitcast.46, ...), custom_call_target="tpu_custom_call" | custom-call | flops 3538944000 | bytes 7561228 | tf_op jit(solution)/shard_map/pallas_call | solution.py:247
  57.1 1.9 %collective-permute-start.6 = (bf16[3456,128]{1,0:T(8,128)(2,1)S(1)}, bf16[3456,128]{1,0:T(8,128)(2,1)S(1)}, u32[]{:S(2)}, u32[]{:S(2)}) collective-permute-start(bf16[3456,128]{1,0:T(8,128)(2,1)S(1)} %broadcast_select_fusion.2), channel_id=1, source_target_pairs={{0,1},{1,0},{2,3},{3,2},{4,5},{5,4},{6,7},{7,6},{8,9},{9,8},{10,11... | collective-permute-start | bytes 2654216 | tf_op jit(solution)/shard_map/ppermute | solution.py:368
  59.0 2.4 %collective-permute-done.6 = bf16[3456,128]{1,0:T(8,128)(2,1)S(1)} collective-permute-done((bf16[3456,128]{1,0:T(8,128)(2,1)S(1)}, bf16[3456,128]{1,0:T(8,128)(2,1)S(1)}, u32[]{:S(2)}, u32[]{:S(2)}) %collective-permute-start.6) | collective-permute-done | bytes 884768 | tf_op jit(solution)/shard_map/ppermute | solution.py:368
  62.7 11.6 %all-to-all-start = ((bf16[16,216,128]{2,1,0:T(8,128)(2,1)}), bf16[16,216,128]{2,1,0:T(8,128)(2,1)S(1)}, u32[]{:S(2)}, u32[]{:S(2)}) async-start(bf16[16,216,128]{2,1,0:T(8,128)(2,1)} %bitcast.52), calls=%async_computation | async-start | bytes 1769472 | tf_op jit(solution)/shard_map/all_to_all | solution.py:280
  75.1 4.3 %collective-permute-start.7 = (bf16[4,2,8,128]{3,2,1,0:T(8,128)(2,1)S(1)}, bf16[4,2,8,128]{3,2,1,0:T(8,128)(2,1)S(1)}, u32[]{:S(2)}, u32[]{:S(2)}) collective-permute-start(bf16[4,2,8,128]{3,2,1,0:T(8,128)(2,1)S(1)} %get-tuple-element.55), channel_id=1, source_target_pairs={{0,16},{16,32},{32,48},{48,64},{64,80},{80,96},{96,112},{1,17},{17... | collective-permute-start | bytes 49160 | tf_op jit(solution)/shard_map/ppermute | solution.py:263
  80.7 1.5 fusion
  82.1 2.0 %collective-permute-done.8 = bf16[4,2,8,128]{3,2,1,0:T(8,128)(2,1)} collective-permute-done((bf16[4,2,8,128]{3,2,1,0:T(8,128)(2,1)S(1)}, bf16[4,2,8,128]{3,2,1,0:T(8,128)(2,1)}, u32[]{:S(2)}, u32[]{:S(2)}) %collective-permute-start.8) | collective-permute-done | bytes 16416 | tf_op jit(solution)/shard_map/ppermute | solution.py:264
  84.1 3.9 %all-to-all-done.parts = bf16[16,216,128]{2,1,0:T(8,128)(2,1)S(1)} async-done(((bf16[16,216,128]{2,1,0:T(8,128)(2,1)}), bf16[16,216,128]{2,1,0:T(8,128)(2,1)S(1)}, u32[]{:S(2)}, u32[]{:S(2)}) %all-to-all-start) | async-done | bytes 884768 | tf_op jit(solution)/shard_map/all_to_all | solution.py:280
  88.8 14.1 %all-to-all-start.1 = ((bf16[16,16,128]{2,1,0:T(8,128)(2,1)}), bf16[16,16,128]{2,1,0:T(8,128)(2,1)}, u32[]{:S(2)}, u32[]{:S(2)}) async-start(bf16[16,16,128]{2,1,0:T(8,128)(2,1)} %bitcast.40), calls=%async_computation.1 | async-start | bytes 131072 | tf_op jit(solution)/shard_map/all_to_all | solution.py:280
  102.9 12.2 %all-to-all-done.1.parts = bf16[16,16,128]{2,1,0:T(8,128)(2,1)} async-done(((bf16[16,16,128]{2,1,0:T(8,128)(2,1)}), bf16[16,16,128]{2,1,0:T(8,128)(2,1)}, u32[]{:S(2)}, u32[]{:S(2)}) %all-to-all-start.1) | async-done | bytes 65568 | tf_op jit(solution)/shard_map/all_to_all | solution.py:280
  116.0 14.2 %all_to_all.20 = bf16[16,16,128]{2,1,0:T(8,128)(2,1)S(1)} all-to-all(bf16[16,16,128]{2,1,0:T(8,128)(2,1)S(1)} %shard_map.79), channel_id=1, replica_groups=mesh['gx'=4,'gy'=8,'y'=4,'zh'=2,'core'=2] {'gy','zh'}, dimensions={0} | all-to-all | bytes 131072 | tf_op jit(solution)/shard_map/all_to_all | solution.py:280
  131.2 4.5 %all-to-all-start.3 = ((bf16[16,216,128]{2,1,0:T(8,128)(2,1)}), bf16[16,216,128]{2,1,0:T(8,128)(2,1)}, u32[]{:S(2)}, u32[]{:S(2)}) async-start(bf16[16,216,128]{2,1,0:T(8,128)(2,1)} %broadcast_in_dim.2), calls=%async_computation.3 | async-start | bytes 1769472 | tf_op jit(solution)/shard_map/all_to_all | solution.py:280
  136.5 3.2 %collective-permute-start.9 = (bf16[2,8,8,128]{3,2,1,0:T(8,128)(2,1)S(1)}, bf16[2,8,8,128]{3,2,1,0:T(8,128)(2,1)S(1)}, u32[]{:S(2)}, u32[]{:S(2)}) collective-permute-start(bf16[2,8,8,128]{3,2,1,0:T(8,128)(2,1)S(1)} %get-tuple-element.53), channel_id=1, source_target_pairs={{0,128},{128,256},{256,384},{1,129},{129,257},{257,385},{2,130},{1... | collective-permute-start | bytes 98312 | tf_op jit(solution)/shard_map/ppermute | solution.py:263
  141.5 3.5 %collective-permute-done.10 = bf16[2,8,8,128]{3,2,1,0:T(8,128)(2,1)S(1)} collective-permute-done((bf16[2,8,8,128]{3,2,1,0:T(8,128)(2,1)S(1)}, bf16[2,8,8,128]{3,2,1,0:T(8,128)(2,1)S(1)}, u32[]{:S(2)}, u32[]{:S(2)}) %collective-permute-start.10) | collective-permute-done | bytes 32800 | tf_op jit(solution)/shard_map/ppermute | solution.py:264
  145.0 1.7 %shard_map.80 = (f32[10,10,16,128]{3,2,1,0:T(8,128)S(1)}, f32[512,128]{1,0:T(8,128)S(1)}) custom-call(bf16[128,128]{1,0:T(8,128)(2,1)S(1)} %bitcast.47, bf16[256,128]{1,0:T(8,128)(2,1)S(1)} %bitcast.39, bf16[128,128]{1,0:T(8,128)(2,1)S(1)} %bitcast.48, bf16[27,128,128]{2,1,0:T(8,128)(2,1)S(1)} %copy-done.2, f32[12,12,24,128]{3,2,1,0:T(8,128)S(1)} %get-tuple-element.31.slope, ...), custom_call_target="tpu_custom_call" | custom-call | flops 406978560 | bytes 4751360 | tf_op jit(solution)/shard_map/pallas_call | solution.py:247
  148.3 8.7 %collective-permute-start.11 = (bf16[3456,128]{1,0:T(8,128)(2,1)}, bf16[3456,128]{1,0:T(8,128)(2,1)S(1)}, u32[]{:S(2)}, u32[]{:S(2)}) collective-permute-start(bf16[3456,128]{1,0:T(8,128)(2,1)} %bitcast.26), channel_id=1, source_target_pairs={{0,1},{1,0},{2,3},{3,2},{4,5},{5,4},{6,7},{7,6},{8,9},{9,8},{10,11... | collective-permute-start | bytes 2654216 | tf_op jit(solution)/shard_map/ppermute | solution.py:408
  159.1 1.4 shard_map.81
  160.5 2.5 %broadcast_select_fusion = (bf16[3456,128]{1,0:T(8,128)(2,1)}, bf16[3456,128]{1,0:T(8,128)(2,1)}) fusion(bf16[3456,128]{1,0:T(8,128)(2,1)S(1)} %collective-permute-done.11, pred[]{:T(512)S(6)} %eq.4, bf16[16,216,128]{2,1,0:T(8,128)(2,1)} %all-to-all-done.3), kind=kLoop, calls=%fused_computation.1 | loop fusion | flops 884736 | bytes 3538945 | tf_op jit(solution)/shard_map/jit(_where)/select_n | solution.py:410
  (68 shorter events, 19.4 us)
Async XLA Ops:
  0.6 21.8 %copy-start.10 = (bf16[8,8,8,128]{3,2,1,0:T(8,128)(2,1)S(1)}, bf16[8,8,8,128]{3,2,1,0:T(8,128)(2,1)}, u32[]{:S(2)}) copy-start(bf16[8,8,8,128]{3,2,1,0:T(8,128)(2,1)} %param.4) | copy-start | bytes 393220
  1.6 20.7 %collective-permute-start = (bf16[576,128]{1,0:T(8,128)(2,1)S(1)}, bf16[576,128]{1,0:T(8,128)(2,1)S(1)}, u32[]{:S(2)}, u32[]{:S(2)}) collective-permute-start(bf16[576,128]{1,0:T(8,128)(2,1)S(1)} %pad_maximum_fusion.3), channel_id=1, source_target_pairs={{1,2},{2,1},{3,4},{4,3},{5,6},{6,5},{7,8},{8,7},{9,10},{10,9},{11,... | collective-permute-start | bytes 442376 | tf_op jit(solution)/shard_map/ppermute | solution.py:269
  18.5 3.8 %collective-permute-start.1 = (bf16[576,128]{1,0:T(8,128)(2,1)S(1)}, bf16[576,128]{1,0:T(8,128)(2,1)S(1)}, u32[]{:S(2)}, u32[]{:S(2)}) collective-permute-start(bf16[576,128]{1,0:T(8,128)(2,1)S(1)} %pad_maximum_fusion.3), channel_id=1, source_target_pairs={{0,1},{1,0},{2,3},{3,2},{4,5},{5,4},{6,7},{7,6},{8,9},{9,8},{10,11... | collective-permute-start | bytes 442376 | tf_op jit(solution)/shard_map/ppermute | solution.py:270
  21.2 15.0 %copy-start = (bf16[27,128,128]{2,1,0:T(8,128)(2,1)S(1)}, bf16[27,128,128]{2,1,0:T(8,128)(2,1)}, u32[]{:S(2)}) copy-start(bf16[27,128,128]{2,1,0:T(8,128)(2,1)} %weights.3) | copy-start | bytes 2654212
  22.5 15.9 %collective-permute-start.3 = (bf16[8,3,24,128]{3,2,1,0:T(8,128)(2,1)S(1)}, bf16[8,3,24,128]{3,2,1,0:T(8,128)(2,1)S(1)}, u32[]{:S(2)}, u32[]{:S(2)}) collective-permute-start(bf16[8,3,24,128]{3,2,1,0:T(8,128)(2,1)S(1)} %pad_maximum_fusion.5), channel_id=1, source_target_pairs={{16,0},{32,16},{48,32},{64,48},{80,64},{96,80},{112,96},{17,1},{33... | collective-permute-start | bytes 442376 | tf_op jit(solution)/shard_map/ppermute | solution.py:264
  23.9 14.6 %copy-start.11 = (bf16[4,4,4,128]{3,2,1,0:T(4,128)(2,1)S(1)}, bf16[4,4,4,128]{3,2,1,0:T(4,128)(2,1)}, u32[]{:S(2)}) copy-start(bf16[4,4,4,128]{3,2,1,0:T(4,128)(2,1)} %param.7) | copy-start | bytes 49156
  23.9 14.6 %collective-permute-start.2 = (bf16[8,3,24,128]{3,2,1,0:T(8,128)(2,1)S(1)}, bf16[8,3,24,128]{3,2,1,0:T(8,128)(2,1)S(1)}, u32[]{:S(2)}, u32[]{:S(2)}) collective-permute-start(bf16[8,3,24,128]{3,2,1,0:T(8,128)(2,1)S(1)} %pad_maximum_fusion.4), channel_id=1, source_target_pairs={{0,16},{16,32},{32,48},{48,64},{64,80},{80,96},{96,112},{1,17},{17... | collective-permute-start | bytes 442376 | tf_op jit(solution)/shard_map/ppermute | solution.py:263
  38.6 8.7 %copy-start.1 = (bf16[27,128,128]{2,1,0:T(8,128)(2,1)S(1)}, bf16[27,128,128]{2,1,0:T(8,128)(2,1)}, u32[]{:S(2)}) copy-start(bf16[27,128,128]{2,1,0:T(8,128)(2,1)} %coarse_weights.1) | copy-start | bytes 2654212
  38.6 7.6 %collective-permute-start.5 = (bf16[3,14,24,128]{3,2,1,0:T(8,128)(2,1)S(1)}, bf16[3,14,24,128]{3,2,1,0:T(8,128)(2,1)S(1)}, u32[]{:S(2)}, u32[]{:S(2)}) collective-permute-start(bf16[3,14,24,128]{3,2,1,0:T(8,128)(2,1)S(1)} %pad_maximum_fusion.2), channel_id=1, source_target_pairs={{128,0},{256,128},{384,256},{129,1},{257,129},{385,257},{130,2},{2... | collective-permute-start | bytes 774152 | tf_op jit(solution)/shard_map/ppermute | solution.py:264
  40.1 7.2 %collective-permute-start.4 = (bf16[3,14,24,128]{3,2,1,0:T(8,128)(2,1)S(1)}, bf16[3,14,24,128]{3,2,1,0:T(8,128)(2,1)S(1)}, u32[]{:S(2)}, u32[]{:S(2)}) collective-permute-start(bf16[3,14,24,128]{3,2,1,0:T(8,128)(2,1)S(1)} %pad_maximum_fusion.1), channel_id=1, source_target_pairs={{0,128},{128,256},{256,384},{1,129},{129,257},{257,385},{2,130},{1... | collective-permute-start | bytes 774152 | tf_op jit(solution)/shard_map/ppermute | solution.py:263
  57.0 5.7 %copy-start.8 = (bf16[128,128]{1,0:T(8,128)(2,1)}, bf16[128,128]{1,0:T(8,128)(2,1)S(1)}, u32[]{:S(2)}) copy-start(bf16[128,128]{1,0:T(8,128)(2,1)S(1)} %get-tuple-element.22) | copy-start | bytes 98308
  57.0 5.7 %copy-start.9 = (f32[128,128]{1,0:T(8,128)}, f32[128,128]{1,0:T(8,128)S(1)}, u32[]{:S(2)}) copy-start(f32[128,128]{1,0:T(8,128)S(1)} %get-tuple-element.23) | copy-start | bytes 196612
  57.1 4.3 %collective-permute-start.6 = (bf16[3456,128]{1,0:T(8,128)(2,1)S(1)}, bf16[3456,128]{1,0:T(8,128)(2,1)S(1)}, u32[]{:S(2)}, u32[]{:S(2)}) collective-permute-start(bf16[3456,128]{1,0:T(8,128)(2,1)S(1)} %broadcast_select_fusion.2), channel_id=1, source_target_pairs={{0,1},{1,0},{2,3},{3,2},{4,5},{5,4},{6,7},{7,6},{8,9},{9,8},{10,11... | collective-permute-start | bytes 2654216 | tf_op jit(solution)/shard_map/ppermute | solution.py:368
  62.7 25.3 %all-to-all-start = ((bf16[16,216,128]{2,1,0:T(8,128)(2,1)}), bf16[16,216,128]{2,1,0:T(8,128)(2,1)S(1)}, u32[]{:S(2)}, u32[]{:S(2)}) async-start(bf16[16,216,128]{2,1,0:T(8,128)(2,1)} %bitcast.52), calls=%async_computation | async-start | bytes 1769472 | tf_op jit(solution)/shard_map/all_to_all | solution.py:280
  75.1 7.1 %collective-permute-start.7 = (bf16[4,2,8,128]{3,2,1,0:T(8,128)(2,1)S(1)}, bf16[4,2,8,128]{3,2,1,0:T(8,128)(2,1)S(1)}, u32[]{:S(2)}, u32[]{:S(2)}) collective-permute-start(bf16[4,2,8,128]{3,2,1,0:T(8,128)(2,1)S(1)} %get-tuple-element.55), channel_id=1, source_target_pairs={{0,16},{16,32},{32,48},{48,64},{64,80},{80,96},{96,112},{1,17},{17... | collective-permute-start | bytes 49160 | tf_op jit(solution)/shard_map/ppermute | solution.py:263
  79.4 4.8 %collective-permute-start.8 = (bf16[4,2,8,128]{3,2,1,0:T(8,128)(2,1)S(1)}, bf16[4,2,8,128]{3,2,1,0:T(8,128)(2,1)}, u32[]{:S(2)}, u32[]{:S(2)}) collective-permute-start(bf16[4,2,8,128]{3,2,1,0:T(8,128)(2,1)S(1)} %get-tuple-element.54), channel_id=1, source_target_pairs={{16,0},{32,16},{48,32},{64,48},{80,64},{96,80},{112,96},{17,1},{33... | collective-permute-start | bytes 49160 | tf_op jit(solution)/shard_map/ppermute | solution.py:264
  88.8 56.2 %copy-start.2 = (bf16[27,128,128]{2,1,0:T(8,128)(2,1)S(1)}, bf16[27,128,128]{2,1,0:T(8,128)(2,1)}, u32[]{:S(2)}) copy-start(bf16[27,128,128]{2,1,0:T(8,128)(2,1)} %coarse_weights.1) | copy-start | bytes 2654212
  88.8 26.3 %all-to-all-start.1 = ((bf16[16,16,128]{2,1,0:T(8,128)(2,1)}), bf16[16,16,128]{2,1,0:T(8,128)(2,1)}, u32[]{:S(2)}, u32[]{:S(2)}) async-start(bf16[16,16,128]{2,1,0:T(8,128)(2,1)} %bitcast.40), calls=%async_computation.1 | async-start | bytes 131072 | tf_op jit(solution)/shard_map/all_to_all | solution.py:280
  131.2 17.1 %all-to-all-start.3 = ((bf16[16,216,128]{2,1,0:T(8,128)(2,1)}), bf16[16,216,128]{2,1,0:T(8,128)(2,1)}, u32[]{:S(2)}, u32[]{:S(2)}) async-start(bf16[16,216,128]{2,1,0:T(8,128)(2,1)} %broadcast_in_dim.2), calls=%async_computation.3 | async-start | bytes 1769472 | tf_op jit(solution)/shard_map/all_to_all | solution.py:280
  136.5 4.9 %collective-permute-start.9 = (bf16[2,8,8,128]{3,2,1,0:T(8,128)(2,1)S(1)}, bf16[2,8,8,128]{3,2,1,0:T(8,128)(2,1)S(1)}, u32[]{:S(2)}, u32[]{:S(2)}) collective-permute-start(bf16[2,8,8,128]{3,2,1,0:T(8,128)(2,1)S(1)} %get-tuple-element.53), channel_id=1, source_target_pairs={{0,128},{128,256},{256,384},{1,129},{129,257},{257,385},{2,130},{1... | collective-permute-start | bytes 98312 | tf_op jit(solution)/shard_map/ppermute | solution.py:263
  139.8 5.2 %collective-permute-start.10 = (bf16[2,8,8,128]{3,2,1,0:T(8,128)(2,1)S(1)}, bf16[2,8,8,128]{3,2,1,0:T(8,128)(2,1)S(1)}, u32[]{:S(2)}, u32[]{:S(2)}) collective-permute-start(bf16[2,8,8,128]{3,2,1,0:T(8,128)(2,1)S(1)} %get-tuple-element.52), channel_id=1, source_target_pairs={{128,0},{256,128},{384,256},{129,1},{257,129},{385,257},{130,2},{2... | collective-permute-start | bytes 98312 | tf_op jit(solution)/shard_map/ppermute | solution.py:264
  148.3 12.2 %collective-permute-start.11 = (bf16[3456,128]{1,0:T(8,128)(2,1)}, bf16[3456,128]{1,0:T(8,128)(2,1)S(1)}, u32[]{:S(2)}, u32[]{:S(2)}) collective-permute-start(bf16[3456,128]{1,0:T(8,128)(2,1)} %bitcast.26), channel_id=1, source_target_pairs={{0,1},{1,0},{2,3},{3,2},{4,5},{5,4},{6,7},{7,6},{8,9},{9,8},{10,11... | collective-permute-start | bytes 2654216 | tf_op jit(solution)/shard_map/ppermute | solution.py:408
  157.0 1.1 copy-start.4
  158.1 0.9 copy-start.6
  (3 other events, 2.2 us)
